TPU v7x, 128 devices: a whole 4x4x4 slice. The times are simulated.
128 devices in a mesh: dp: 64 (over z_lo, x, y, core), mp: 2 (over z_hi).
Axes of the slice: x: 4, y: 4, z: 4 (z_hi: 2, z_lo: 2; z = z_hi * 2 + z_lo), core: 2. Of those that a mesh axis runs over, the one named last changes fastest.
Arguments:
- tokens: bfloat16 [16384, 2048], P(('dp', 'mp')), may hold values from -6 to 6
- layernorm_gain: float32 [2048], replicated, may hold values from 0.5 to 1.5
- layernorm_bias: float32 [2048], replicated, may hold values from -1.75 to 1.75
- w_qkv: bfloat16 [2048, 3, 2048], P('dp', None, 'mp'), may hold values from -0.125 to 0.125
- b_qkv: float32 [3, 2048], P(None, 'mp'), may hold values from -3 to 3
- w_out: bfloat16 [2048, 2048], P('mp', 'dp'), may hold values from -0.5 to 0.5
- b_out: float32 [2048], replicated, may hold values from -1.75 to 1.75
- w_up: bfloat16 [2048, 8192], P('dp', 'mp'), may hold values from -0.125 to 0.125
- b_up: float32 [8192], P('mp'), may hold values from -3 to 3
- w_down: bfloat16 [8192, 2048], P('mp', 'dp'), may hold values from -0.0625 to 0.0625
- b_down: float32 [2048], replicated, may hold values from -1.75 to 1.75
- segments: int32 [16384], P('dp'), may hold values from 0 to 1, as said below
- cotangent: bfloat16 [16384, 2048], P(('dp', 'mp')), may hold values from -6 to 6
Outputs:
- mixed: bfloat16 [16384, 2048], P(('dp', 'mp'))
- d_tokens: float32 [16384, 2048], P(('dp', 'mp'))
- d_ln_gain: float32 [2048], replicated
- d_ln_bias: float32 [2048], replicated
- d_w_qkv: float32 [2048, 3, 2048], P('dp', None, 'mp')
- d_b_qkv: float32 [3, 2048], P(None, 'mp')
- d_w_out: float32 [2048, 2048], P('mp', 'dp')
- d_b_out: float32 [2048], replicated
- d_w_up: float32 [2048, 8192], P('dp', 'mp')
- d_b_up: float32 [8192], P('mp')
- d_w_down: float32 [8192, 2048], P('mp', 'dp')
- d_b_down: float32 [2048], replicated
Inputs may be any that keep to these rules, and one draw needn't show every extreme that they name: `segments`: each sequence of 256 tokens holds exactly 2 documents, numbered from 0 in order, so segment numbers never fall and rise by one at each document start; the tokens at positions 124 to 131 of each sequence lie in one document.
All inputs are finite; a program needn't handle non-finite values.
Results may differ from a plain program's by a relative error of at most 0.011.
Values may be sent and summed in bfloat16 or wider, within the bound.
No kernel may reach another device: no remote copies, remote signals or barrier semaphores. Data moves between devices by JAX's collectives and lax.ppermute only.
A program may use at most 256 MiB of HBM per device.

v0:
```python
import jax
import jax.numpy as jnp
from jax import lax
from jax.experimental import pallas as pl
from jax.experimental.pallas import tpu as pltpu
from jax.sharding import Mesh, PartitionSpec as P

HEAD_DIM = 64
ROT = 32
HALF = ROT // 2
LANES = 128
EPSILON = 1e-05

AXES = ("zl", "x", "y", "c", "mp")
SIZES = (2, 4, 4, 2, 2)
PLANE = ("x", "y")
PAIR = ("zl", "c")

BF16 = jnp.bfloat16
F32 = jnp.float32


def flip(value, *axes):
    count = 2 ** len(axes)
    return lax.ppermute(value, axes, [(i, count - 1 - i) for i in range(count)])


def hop(value, axis, bits):
    return lax.ppermute(value, axis, [(i, i ^ bits) for i in range(4)])


def scatter_group(partial_rows):
    rows = partial_rows.shape[0] // 8
    mine, theirs = partial_rows[: 4 * rows], partial_rows[4 * rows :]
    half = mine.astype(F32) + flip(theirs.astype(BF16), "c").astype(F32)
    low = half.astype(BF16)
    return (
        half[:rows]
        + flip(low[rows : 2 * rows], "mp").astype(F32)
        + flip(low[2 * rows : 3 * rows], "zl").astype(F32)
        + flip(low[3 * rows :], "zl", "mp").astype(F32)
    )


def sum_everywhere(vector):
    vector = vector + flip(vector, "c")
    vector = vector + flip(vector, "zl") + (flip(vector, "mp") + flip(vector, "zl", "mp"))
    for axis in PLANE:
        vector = (vector + hop(vector, axis, 2)) + (hop(vector, axis, 1) + hop(vector, axis, 3))
    return vector


def attention_kernel(
    linear_ref,
    grad_ref,
    cos_ref,
    low_ref,
    high_ref,
    segment_col,
    segment_row,
    index_col,
    index_row,
    attended_ref,
    grad_linear_ref,
    query_ref,
    key_ref,
    value_ref,
    grad_query_ref,
    grad_key_ref,
):
    width = grad_ref.shape[1]
    scale = HEAD_DIM ** (-0.5)

    def rotated(tile, lanes, sign):
        cos, low, high = cos_ref[...], low_ref[...], high_ref[...]
        ahead = pltpu.roll(tile, lanes - HALF, 1)
        behind = pltpu.roll(tile, HALF, 1)
        return tile * cos + (ahead * low + behind * high) * sign

    for start in range(0, width, LANES):
        lanes = slice(start, start + LANES)
        query_ref[:, lanes] = (rotated(linear_ref[:, lanes], LANES, 1.0) * scale).astype(BF16)
        keys = linear_ref[:, width + start : width + start + LANES]
        key_ref[:, lanes] = rotated(keys, LANES, 1.0).astype(BF16)
        value_ref[:, lanes] = linear_ref[:, 2 * width + start : 2 * width + start + LANES].astype(BF16)
    allowed = (segment_col[...] == segment_row[0]) & (index_col[...] >= index_row[0])
    for start in range(0, width, HEAD_DIM):
        lanes = slice(start, start + HEAD_DIM)
        query, key, value = query_ref[:, lanes], key_ref[:, lanes], value_ref[:, lanes]
        grad = grad_ref[:, lanes]
        scores = lax.dot_general(query, key, (((1,), (1,)), ((), ())), preferred_element_type=F32)
        scores = jnp.where(allowed, scores, -1000000000.0)
        expo = jnp.exp(scores - jnp.max(scores, axis=1, keepdims=True))
        probs = expo / jnp.sum(expo, axis=1, keepdims=True)
        low_probs = probs.astype(BF16)
        attended_ref[:, lanes] = jnp.dot(low_probs, value, preferred_element_type=F32).astype(BF16)
        grad_probs = lax.dot_general(grad, value, (((1,), (1,)), ((), ())), preferred_element_type=F32)
        grad_values = lax.dot_general(
            low_probs, grad, (((0,), (0,)), ((), ())), preferred_element_type=F32
        )
        weighted = probs * grad_probs
        delta = jnp.sum(weighted, axis=1, keepdims=True)
        grad_scores = (weighted - probs * delta).astype(BF16)
        grad_query_ref[:, lanes] = jnp.dot(grad_scores, key, preferred_element_type=F32) * scale
        grad_key_ref[:, lanes] = lax.dot_general(
            grad_scores, query, (((0,), (0,)), ((), ())), preferred_element_type=F32
        )
        grad_linear_ref[:, 2 * width + start : 2 * width + start + HEAD_DIM] = grad_values.astype(BF16)
    for start in range(0, width, LANES):
        lanes = slice(start, start + LANES)
        grad_linear_ref[:, lanes] = rotated(grad_query_ref[:, lanes], LANES, -1.0).astype(BF16)
        grad_linear_ref[:, width + start : width + start + LANES] = rotated(
            grad_key_ref[:, lanes], LANES, -1.0
        ).astype(BF16)


def attention(linear, grad_attended, tables, segments, indices, length):
    rows, width = grad_attended.shape
    count = rows // length
    blocks = lambda lanes: pl.BlockSpec((length, lanes), lambda i: (i, 0))
    rowwise = pl.BlockSpec((1, 1, length), lambda i: (i, 0, 0))
    return pl.pallas_call(
        attention_kernel,
        grid=(count,),
        in_specs=[
            blocks(3 * width),
            blocks(width),
            blocks(LANES),
            blocks(LANES),
            blocks(LANES),
            blocks(1),
            rowwise,
            blocks(1),
            rowwise,
        ],
        out_specs=[blocks(width), blocks(3 * width)],
        out_shape=[
            jax.ShapeDtypeStruct((rows, width), BF16),
            jax.ShapeDtypeStruct((rows, 3 * width), BF16),
        ],
        scratch_shapes=[pltpu.VMEM((length, width), BF16)] * 3
        + [pltpu.VMEM((length, width), F32)] * 2,
        compiler_params=pltpu.CompilerParams(vmem_limit_bytes=32 * 1024 * 1024),
        name="attention",
    )(
        linear,
        grad_attended,
        *tables,
        segments.reshape(rows, 1),
        segments.reshape(count, 1, length),
        indices.reshape(rows, 1),
        indices.reshape(count, 1, length),
    )


MIB = 1024 * 1024
ANY = pl.BlockSpec(memory_space=pl.ANY)
WHOLE = pl.BlockSpec(memory_space=pltpu.VMEM)
SCALARS = pl.BlockSpec(memory_space=pltpu.SMEM)


def like(shape, dtype=BF16):
    return jax.ShapeDtypeStruct(shape, dtype)


def params(mib):
    return pltpu.CompilerParams(vmem_limit_bytes=mib * MIB)


def cost(flops, moved):
    return pl.CostEstimate(flops=flops, bytes_accessed=moved, transcendentals=0)


def slot_of(coords, bits):
    return (coords[0] * 2 + coords[3]) ^ bits


def pack_kernel(coords, up_ref, down_ref, qkv_ref, out_ref, segment_ref, *parts):
    hidden, width = up_ref.shape[1] // 4, out_ref.shape[1] // 4
    rows = up_ref.shape[0]
    segments = segment_ref[...].astype(F32).astype(BF16)
    for bits in range(4):
        slot = slot_of(coords, bits)
        wide = pl.ds(pl.multiple_of(slot * hidden, hidden), hidden)
        narrow = pl.ds(pl.multiple_of(slot * width, width), width)
        mlp, heads = parts[2 * bits], parts[2 * bits + 1]
        mlp[:, :hidden] = up_ref[:, wide]
        mlp[:, hidden:] = down_ref[:, wide]
        for kind in range(3):
            heads[:rows, kind * width : (kind + 1) * width] = qkv_ref[kind, :, narrow]
        heads[:rows, 3 * width :] = out_ref[:, narrow]
        heads[rows:, :] = jnp.zeros((16, 4 * width), BF16)
        heads[rows:, : segments.shape[1]] = jnp.broadcast_to(segments, (16, segments.shape[1]))


def pack(coords, w_up, down_t, qkv_t, out_t, segments):
    rows, hidden, width = w_up.shape[0], w_up.shape[1] // 4, out_t.shape[1] // 4
    shapes = [like((rows, 2 * hidden)), like((rows + 16, 4 * width))] * 4
    return pl.pallas_call(
        pack_kernel,
        in_specs=[SCALARS] + [WHOLE] * 5,
        out_specs=[WHOLE] * 8,
        out_shape=shapes,
        compiler_params=params(16),
        name="pack",
    )(coords, w_up, down_t, qkv_t, out_t, segments.reshape(1, -1))


def order_kernel(coords, *refs):
    parts, outs = refs[:4], refs[4:]
    for bits in range(4):
        zl, c = coords[0] ^ (bits >> 1), coords[3] ^ (bits & 1)
        start = 0
        for out in outs:
            columns = out.shape[3]
            out[zl, c] = parts[bits][: out.shape[2], start : start + columns]
            start += columns


def order(coords, parts, columns, rows):
    return pl.pallas_call(
        order_kernel,
        in_specs=[SCALARS] + [WHOLE] * 4,
        out_specs=[WHOLE] * len(columns),
        out_shape=[like((2, 2, rows, count)) for count in columns],
        compiler_params=params(16),
        name="order",
    )(coords, *parts)


def join_kernel(*refs):
    parts, out, sem = refs[:-2], refs[-2], refs[-1]
    copies = []
    for i, part in enumerate(parts):
        copies.append(pltpu.make_async_copy(part, out.at[i], sem.at[i]))
        copies[-1].start()
    for copy in copies:
        copy.wait()


def join(*parts):
    return pl.pallas_call(
        join_kernel,
        in_specs=[ANY] * len(parts),
        out_specs=ANY,
        out_shape=like((len(parts),) + parts[0].shape),
        scratch_shapes=[pltpu.SemaphoreType.DMA((len(parts),))],
        compiler_params=params(16),
        name="join",
    )(*parts)


def gather_plane(shard, first, second):
    row = join(shard, hop(shard, first, 1), hop(shard, first, 2), hop(shard, first, 3))
    one, three = hop(row, second, 1), hop(row, second, 3)
    half = row.shape[0] // 2
    two_low, two_high = hop(three[:half], second, 1), hop(one[half:], second, 3)
    return row, one, two_low, two_high, three


def tokens_kernel(mine_ref, other_ref, rows_ref, columns_ref):
    @pl.when(pl.program_id(1) == 0)
    def _():
        rows_ref[0] = mine_ref[0, 0]
        columns_ref[0] = mine_ref[0, 0].T

    @pl.when(pl.program_id(1) == 1)
    def _():
        rows_ref[0] = other_ref[0, 0]
        columns_ref[0] = other_ref[0, 0].T


def gather_tokens(pair):
    near, far = flip(pair, "zl"), flip(pair, "zl", "mp")
    middle = join(flip(far[0], "zl"), flip(near[1], "zl", "mp"))
    mine = join(pair, middle, near, far)
    other = flip(mine, "c")
    _, _, rows, depth = mine.shape
    block = (1, 1, rows, depth)
    return pl.pallas_call(
        tokens_kernel,
        grid=(2, 2, 4),
        in_specs=[
            pl.BlockSpec(block, lambda w, c, z: (jnp.where(c == 0, z, 3), w, 0, 0)),
            pl.BlockSpec(block, lambda w, c, z: (jnp.where(c == 1, z, 0), w, 0, 0)),
        ],
        out_specs=[
            pl.BlockSpec((1, rows, depth), lambda w, c, z: (w, 4 * c + z, 0)),
            pl.BlockSpec((1, depth, rows), lambda w, c, z: (w, 0, 4 * c + z)),
        ],
        out_shape=[like((2, 8 * rows, depth)), like((2, depth, 8 * rows))],
        compiler_params=params(32),
        cost_estimate=cost(0, 8 * mine.size * 2),
        name="tokens",
    )(mine, other)


def mlp_kernel(coords, pair_ref, bias_ref, *refs):
    up_parts, down_parts = refs[:5], refs[5:10]
    hidden_ref, sums_ref, up_out, down_out = refs[10:14]
    rows_ref, up_ref, down_ref, sems = refs[14:]
    x, y = coords[1], coords[2]
    block = up_ref.shape[0] // 32

    def load(parts, target, sems, second_is_y):
        copies = []
        row, one, two_low, two_high, three = parts
        for second in range(4):
            for first in range(4):
                if second == 2:
                    source = two_low.at[first] if first < 2 else two_high.at[first - 2]
                else:
                    source = (row, one, None, three)[second].at[first]
                if second_is_y:
                    place = (x ^ first) * 4 + (y ^ second)
                else:
                    place = (x ^ second) * 4 + (y ^ first)
                for zl in range(2):
                    target_rows = pl.ds(pl.multiple_of((zl * 16 + place) * block, block), block)
                    sem = sems.at[len(copies)]
                    copies.append(pltpu.make_async_copy(source.at[zl], target.at[target_rows], sem))
        return copies

    first = [pltpu.make_async_copy(pair_ref.at[0], rows_ref.at[0], sems.at[0, 32])]
    first += load(up_parts, up_ref, sems.at[0], True)
    second = [pltpu.make_async_copy(pair_ref.at[1], rows_ref.at[1], sems.at[1, 32])]
    second += load(down_parts, down_ref, sems.at[1], False)
    for copy in first + second:
        copy.start()
    for copy in first:
        copy.wait()
    for copy in second:
        copy.wait()
    up_back = pltpu.make_async_copy(up_ref, up_out, sems.at[0, 33])
    down_back = pltpu.make_async_copy(down_ref, down_out, sems.at[1, 33])
    up_back.start()
    down_back.start()
    tile = 256
    slope = 0.7978845608028654

    def body(j, carry):
        lanes = pl.ds(pl.multiple_of(j * tile, tile), tile)
        up = jnp.dot(rows_ref[0], up_ref[:, lanes], preferred_element_type=F32) + bias_ref[:, lanes]
        square = up * up
        wave = jnp.tanh(slope * (up + 0.044715 * (square * up)))
        half = 0.5 * (1.0 + wave)
        hidden_ref[1, :, lanes] = (up * half).astype(BF16)
        rise = half + (0.5 * up) * (1.0 - wave * wave) * (slope * (1.0 + 0.134145 * square))
        grad = jnp.dot(rows_ref[1], down_ref[:, lanes], preferred_element_type=F32) * rise
        low = grad.astype(BF16)
        hidden_ref[0, :, lanes] = low
        sums_ref[:, lanes] = jnp.sum(low.astype(F32), axis=0, keepdims=True)
        return carry

    lax.fori_loop(0, up_ref.shape[1] // tile, body, 0)
    up_back.wait()
    down_back.wait()


def mlp(coords, pair, bias, up_parts, down_parts):
    rows, depth = pair.shape[1:]
    hidden = bias.shape[0]
    return pl.pallas_call(
        mlp_kernel,
        in_specs=[SCALARS, ANY, WHOLE] + [ANY] * 10,
        out_specs=[WHOLE, WHOLE, ANY, ANY],
        out_shape=[
            like((2, rows, hidden)),
            like((1, hidden), F32),
            like((depth, hidden)),
            like((depth, hidden)),
        ],
        scratch_shapes=[
            pltpu.VMEM((2, rows, depth), BF16),
            pltpu.VMEM((depth, hidden), BF16),
            pltpu.VMEM((depth, hidden), BF16),
            pltpu.SemaphoreType.DMA((2, 34)),
        ],
        compiler_params=params(48),
        cost_estimate=cost(4 * rows * depth * hidden, 24 * MIB),
        name="mlp",
    )(coords, pair, bias.reshape(1, -1), *up_parts, *down_parts)


def grads_kernel(left_ref, right_ref, out_ref):
    product = jnp.dot(left_ref[0], right_ref[0], preferred_element_type=F32).astype(BF16)
    out_ref[...] = product.reshape(out_ref.shape)


def weight_grads(pair_t, right, tile, which):
    _, depth, rows = pair_t.shape
    count, _, columns = right.shape
    tiles = columns // tile
    block = depth // 32
    return pl.pallas_call(
        grads_kernel,
        grid=(count, tiles, 2),
        in_specs=[
            pl.BlockSpec((1, depth // 2, rows), lambda i, j, zl: (which(i, j), zl, 0)),
            pl.BlockSpec((1, rows, tile), lambda i, j, zl: (i, 0, j)),
        ],
        out_specs=pl.BlockSpec((16, 1, block, tile), lambda i, j, zl: (0, zl, 0, i * tiles + j)),
        out_shape=like((16, 2, block, count * columns)),
        compiler_params=params(40),
        cost_estimate=cost(2 * depth * rows * count * columns, 2 * (pair_t.size + right.size * 2)),
        name="weight_grads",
    )(pair_t, right)


def project_kernel(pair_ref, bias_ref, weights_ref, linear_ref, grad_ref, order_ref):
    width = grad_ref.shape[1]
    columns = weights_ref[...].astype(BF16)
    columns = jnp.swapaxes(columns, 0, 1).reshape(order_ref.shape)
    order_ref[...] = columns

    @pl.when(pl.program_id(0) < 3)
    def _():
        linear_ref[...] = jnp.dot(pair_ref[0], columns, preferred_element_type=F32) + bias_ref[...]

    @pl.when(pl.program_id(0) == 3)
    def _():
        grad_ref[...] = jnp.dot(pair_ref[0], columns, preferred_element_type=F32).astype(BF16)


def project(pair, bias, weights):
    rows, depth = pair.shape[1:]
    block, width = depth // 32, weights.shape[3] // 4
    return pl.pallas_call(
        project_kernel,
        grid=(4,),
        in_specs=[
            pl.BlockSpec((1, rows, depth), lambda j: (j // 3, 0, 0)),
            pl.BlockSpec((1, width), lambda j: (0, jnp.minimum(j, 2))),
            pl.BlockSpec((16, 2, block, width), lambda j: (0, 0, 0, j)),
        ],
        out_specs=[
            pl.BlockSpec((rows, width), lambda j: (0, jnp.minimum(j, 2))),
            pl.BlockSpec((rows, width), lambda j: (0, 0)),
            pl.BlockSpec((depth, width), lambda j: (0, j)),
        ],
        out_shape=[
            like((rows, 3 * width), F32),
            like((rows, width)),
            like((depth, 4 * width)),
        ],
        compiler_params=params(40),
        cost_estimate=cost(8 * rows * depth * width, 16 * MIB),
        name="project",
    )(pair, bias.reshape(1, -1), weights)


def cut_kernel(coords, whole_ref, *outs):
    for bits in range(4):
        outs[bits][...] = whole_ref[slot_of(coords, bits)]


def cut(coords, whole):
    return pl.pallas_call(
        cut_kernel,
        in_specs=[SCALARS, WHOLE],
        out_specs=[WHOLE] * 4,
        out_shape=[like(whole.shape[1:])] * 4,
        compiler_params=params(16),
        name="cut",
    )(coords, whole)


def exchange(parts):
    return [parts[0], flip(parts[1], "c"), flip(parts[2], "zl"), flip(parts[3], "zl", "c")]


def unpack_mlp_kernel(coords, *refs):
    parts, (up_ref, down_ref) = refs[:4], refs[4:]
    hidden = up_ref.shape[1] // 4
    for bits in range(4):
        lanes = pl.ds(pl.multiple_of(slot_of(coords, bits) * hidden, hidden), hidden)
        up_ref[:, lanes] = parts[bits][:, :hidden].astype(F32)
        down_ref[:, lanes] = parts[bits][:, hidden:].astype(F32)


def unpack_heads_kernel(coords, *refs):
    parts, (qkv_ref, out_ref) = refs[:4], refs[4:]
    width = out_ref.shape[1] // 4
    for bits in range(4):
        lanes = pl.ds(pl.multiple_of(slot_of(coords, bits) * width, width), width)
        for kind in range(3):
            qkv_ref[kind, :, lanes] = parts[bits][:, kind * width : (kind + 1) * width].astype(F32)
        out_ref[:, lanes] = parts[bits][:, 3 * width :].astype(F32)


def unpack(coords, kernel, parts, shapes, name):
    return pl.pallas_call(
        kernel,
        in_specs=[SCALARS] + [WHOLE] * 4,
        out_specs=[WHOLE] * 2,
        out_shape=[like(shape, F32) for shape in shapes],
        compiler_params=params(16),
        name=name,
    )(coords, *parts)


def scatter_plane(grads):
    return lax.psum_scatter(grads.reshape(-1, grads.shape[3]), PLANE, scatter_dimension=0, tiled=True)


def per_device(
    tokens,
    layernorm_gain,
    layernorm_bias,
    w_qkv,
    b_qkv,
    w_out,
    b_out,
    w_up,
    b_up,
    w_down,
    b_down,
    segments,
    cotangent,
):
    depth = tokens.shape[1]
    length = segments.shape[0]
    half_rows = tokens.shape[0]
    width = w_out.shape[0] // 4
    hidden = w_down.shape[0] // 4
    rows = w_up.shape[0]
    coords = jnp.stack([lax.axis_index(axis) for axis in AXES]).astype(jnp.int32)
    place = coords[0] * 2 + coords[3]
    this_half = coords[4]

    packed = pack(coords, w_up, w_down.T, w_qkv.transpose(1, 0, 2), w_out.T, segments)
    mlp_parts, head_parts = exchange(packed[0::2]), exchange(packed[1::2])
    up_shard, down_shard = order(coords, mlp_parts, (hidden, hidden), rows)
    (head_shard,) = order(coords, head_parts, (4 * width,), rows)

    inputs_f = tokens.astype(F32)
    row_mean = jnp.mean(inputs_f, axis=-1, keepdims=True)
    mean_removed = inputs_f - row_mean
    variance = jnp.mean(mean_removed * mean_removed, axis=-1, keepdims=True)
    inverse_deviation = lax.rsqrt(variance + EPSILON)
    standardized_input = mean_removed * inverse_deviation
    normalized_rows = (standardized_input * layernorm_gain + layernorm_bias).astype(BF16)

    head_weights = lax.all_gather(head_shard.reshape(2, 2 * rows, 4 * width), PLANE, axis=0, tiled=False)
    head_weights = head_weights.reshape(16, 2, 2 * rows, 4 * width)
    pair, pair_t = gather_tokens(jnp.stack([normalized_rows, cotangent]))
    up_parts = gather_plane(up_shard.reshape(2, 2 * rows, hidden), "x", "y")
    down_parts = gather_plane(down_shard.reshape(2, 2 * rows, hidden), "y", "x")

    doc = jnp.stack([head_parts[k][rows, :length] for k in (0, 2, 1, 3)]).astype(jnp.int32)
    doc = doc.reshape(4, 2, half_rows)
    doc = jnp.where(this_half == 0, doc, doc[:, ::-1]).reshape(4, length)
    halves = jnp.stack([this_half, 1 - this_half]) * half_rows
    index = (halves[:, None] + jnp.arange(half_rows, dtype=jnp.int32)).reshape(1, length)
    index = jnp.broadcast_to(index, (4, length)).astype(jnp.int32)
    same_doc = doc[:, :, None] == doc[:, None, :]
    doc_start = jnp.min(jnp.where(same_doc, index[:, None, :], length), axis=2)
    positions = (index - doc_start).astype(F32).reshape(-1)
    inv_freq = 10000.0 ** (-(jnp.arange(HALF, dtype=F32) * 2.0 / ROT))
    angles = positions[:, None] * inv_freq
    cos, sin = jnp.cos(angles), jnp.sin(angles)
    nothing = jnp.zeros_like(cos)
    rest = (positions.shape[0], HEAD_DIM - ROT)
    repeat = LANES // HEAD_DIM
    cos_table = jnp.tile(jnp.concatenate([cos, cos, jnp.ones(rest, F32)], axis=1), (1, repeat))
    low_table = jnp.tile(jnp.concatenate([-sin, nothing, jnp.zeros(rest, F32)], axis=1), (1, repeat))
    high_table = jnp.tile(jnp.concatenate([nothing, sin, jnp.zeros(rest, F32)], axis=1), (1, repeat))

    b_up_here = lax.dynamic_slice_in_dim(b_up, place * hidden, hidden)
    b_qkv_here = lax.dynamic_slice_in_dim(b_qkv, place * width, width, axis=1).reshape(-1)

    hidden_pair, grad_b_up, up_w, down_w = mlp(coords, pair, b_up_here, up_parts, down_parts)
    mlp_grads = scatter_plane(weight_grads(pair_t, hidden_pair, hidden // 2, lambda i, j: i))

    linear, grad_attended, head_w = project(pair, b_qkv_here, head_weights)
    attended, grad_linear = attention(
        linear, grad_attended, (cos_table, low_table, high_table), doc, index, length
    )
    head_right = jnp.concatenate([grad_linear, attended], axis=1)[None]
    head_grads = scatter_plane(weight_grads(pair_t, head_right, width, lambda i, j: j // 3))

    out_w, qkv_w = head_w[:, 3 * width :], head_w[:, : 3 * width]
    branches = jnp.einsum("te,de->td", attended, out_w, preferred_element_type=F32) + jnp.einsum(
        "tf,df->td", hidden_pair[1], down_w, preferred_element_type=F32
    )
    mixed = (inputs_f + scatter_group(branches) + b_out + b_down).astype(BF16)
    grad_sequence = jnp.einsum(
        "te,de->td", grad_linear, qkv_w, preferred_element_type=F32
    ) + jnp.einsum("tf,df->td", hidden_pair[0], up_w, preferred_element_type=F32)
    normalized_gradient = scatter_group(grad_sequence)
    standardized_gradient = normalized_gradient * layernorm_gain
    grad_inputs = inverse_deviation * (
        standardized_gradient
        - jnp.mean(standardized_gradient, axis=-1, keepdims=True)
        - standardized_input
        * jnp.mean(standardized_gradient * standardized_input, axis=-1, keepdims=True)
    )
    cot_rows = cotangent.astype(F32)
    d_tokens = cot_rows + grad_inputs

    slices = jnp.concatenate([jnp.sum(grad_linear.astype(F32), axis=0), grad_b_up[0]])
    slot = this_half * 4 + place
    spread = jnp.zeros((8,) + slices.shape, F32)
    spread = lax.dynamic_update_slice(spread, slices[None], (slot, 0))
    vector = jnp.concatenate(
        [
            spread.reshape(-1),
            jnp.sum(cot_rows, axis=0),
            jnp.sum(normalized_gradient * standardized_input, axis=0),
            jnp.sum(normalized_gradient, axis=0),
        ]
    )
    vector = sum_everywhere(vector.reshape(-1, LANES)).reshape(-1)
    spread, whole = vector[: spread.size].reshape(8, -1), vector[spread.size :].reshape(3, depth)
    spread = lax.dynamic_slice_in_dim(spread, this_half * 4, 4)
    grad_b_qkv = spread[:, : 3 * width].reshape(4, 3, width).transpose(1, 0, 2).reshape(3, 4 * width)
    grad_b_up = spread[:, 3 * width :].reshape(-1)

    mlp_parts = exchange(cut(coords, mlp_grads.reshape(4, rows, 2 * hidden)))
    grad_up_w, grad_down_w = unpack(
        coords, unpack_mlp_kernel, mlp_parts, [w_up.shape, w_up.shape], "unpack_mlp"
    )
    head_parts = exchange(cut(coords, head_grads.reshape(4, rows, 4 * width)))
    shapes = [(3, rows, 4 * width), (rows, 4 * width)]
    grad_qkv_w, grad_out_w = unpack(coords, unpack_heads_kernel, head_parts, shapes, "unpack_heads")
    return (
        mixed,
        d_tokens,
        whole[1],
        whole[2],
        grad_qkv_w.transpose(1, 0, 2),
        grad_b_qkv,
        grad_out_w.T,
        whole[0],
        grad_up_w,
        grad_b_up,
        grad_down_w.T,
        whole[0],
    )


def solution(mesh):
    fine = Mesh(mesh.devices.reshape(SIZES), AXES)
    dp = ("zl", "x", "y", "c")
    in_specs = (
        P(AXES, None),
        P(),
        P(),
        P(dp, None, "mp"),
        P(None, "mp"),
        P("mp", dp),
        P(),
        P(dp, "mp"),
        P("mp"),
        P("mp", dp),
        P(),
        P(dp),
        P(AXES, None),
    )
    out_specs = (
        P(AXES, None),
        P(AXES, None),
        P(),
        P(),
        P(dp, None, "mp"),
        P(None, "mp"),
        P("mp", dp),
        P(),
        P(dp, "mp"),
        P("mp"),
        P("mp", dp),
        P(),
    )
    return jax.shard_map(
        per_device, mesh=fine, in_specs=in_specs, out_specs=out_specs, check_vma=False
    )
```

profile of v0, /device:TPU:1, one launch (start us, length us, event | category | flops | bytes accessed | tf_op | source)
XLA Modules:
  0.0 416.0 jit_solution(5134112328320454341)
XLA Ops:
  28.0 23.4 %collective-permute-done.refs_3_ = bf16[2,128,2048]{2,1,0:T(8,128)(2,1)S(1)} collective-permute-done((bf16[2,128,2048]{2,1,0:T(8,128)(2,1)S(1)}, bf16[2,128,2048]{2,1,0:T(8,128)(2,1)S(1)}, u32[]{:S(2)}, u32[]{:S(2)}) %collective-permute-start) | collective-permute-done | bytes 1048608 | tf_op jit(solution)/shard_map/ppermute | solution.py:25
  54.5 10.2 %collective-permute-done.1.refs_0_ = bf16[128,2048]{1,0:T(8,128)(2,1)S(1)} collective-permute-done((bf16[128,2048]{1,0:T(8,128)(2,1)S(1)}, bf16[128,2048]{1,0:T(8,128)(2,1)S(1)}, u32[]{:S(2)}, u32[]{:S(2)}) %collective-permute-start.1) | collective-permute-done | bytes 524320 | tf_op jit(solution)/shard_map/ppermute | solution.py:25
  78.1 13.4 %tokens.1 = (bf16[2,1024,2048]{2,1,0:T(8,128)(2,1)S(1)}, bf16[2,2048,1024]{2,1,0:T(8,128)(2,1)}) custom-call(bf16[4,2,128,2048]{3,2,1,0:T(8,128)(2,1)} %join.5.mine_ref, bf16[4,2,128,2048]{3,2,1,0:T(8,128)(2,1)} %collective-permute-done.4.other_ref), custom_call_target="tpu_custom_call" | custom-call | bytes 33554432 | tf_op jit(solution)/shard_map/tokens/pallas_call | solution.py:280
  97.0 9.5 %project.1 = (f32[1024,768]{1,0:T(8,128)S(1)}, bf16[1024,256]{1,0:T(8,128)(2,1)S(1)}, bf16[2048,1024]{1,0:T(8,128)(2,1)S(1)}) custom-call(bf16[2,1024,2048]{2,1,0:T(8,128)(2,1)} %copy-done.20, f32[1,768]{1,0:T(1,128)S(1)} %bitcast.111, bf16[16,2,64,1024]{3,2,1,0:T(8,128)(2,1)S(1)} %copy-done.21), custom_call_target="tpu_custom_call" | custom-call | flops 4294967296 | bytes 16777216 | tf_op jit(solution)/shard_map/project/pallas_call | solution.py:428
  106.6 15.8 %attention.1 = (bf16[1024,256]{1,0:T(8,128)(2,1)S(1)}, bf16[1024,768]{1,0:T(8,128)(2,1)S(1)}) custom-call(f32[1024,768]{1,0:T(8,128)S(1)} %get-tuple-element.50.linear_ref, bf16[1024,256]{1,0:T(8,128)(2,1)S(1)} %get-tuple-element.51.grad_ref, f32[1024,128]{1,0:T(8,128)S(1)} %copy.35.cos_ref, f32[1024,128]{1,0:T(8,128)S(1)} %copy.36.low_ref, ...), custom_call_target="tpu_custom_call" | custom-call | tf_op jit(solution)/shard_map/attention/pallas_call | solution.py:122
  122.7 10.8 %weight_grads.2 = bf16[16,2,64,1024]{3,2,1,0:T(8,128)(2,1)S(1)} custom-call(bf16[2,2048,1024]{2,1,0:T(8,128)(2,1)} %get-tuple-element.65.left_ref, bf16[1,1024,1024]{2,1,0:T(8,128)(2,1)S(1)} %maximum_bitcast_fusion.right_ref), custom_call_target="tpu_custom_call" | custom-call | flops 4294967296 | bytes 12582912 | tf_op jit(solution)/shard_map/weight_grads/pallas_call | solution.py:395
  138.4 3.9 collective-permute-done.10.refs_3_
  157.3 7.4 %collective-permute-done.12.refs_2_ = bf16[2,64,1024]{2,1,0:T(8,128)(2,1)S(1)} collective-permute-done((bf16[2,64,1024]{2,1,0:T(8,128)(2,1)S(1)}, bf16[2,64,1024]{2,1,0:T(8,128)(2,1)S(1)}, u32[]{:S(2)}, u32[]{:S(2)}) %collective-permute-start.12) | collective-permute-done | bytes 262176 | tf_op jit(solution)/shard_map/ppermute | solution.py:29
  170.3 5.1 %collective-permute-start.22 = (bf16[4,2,64,1024]{3,2,1,0:T(8,128)(2,1)S(1)}, bf16[4,2,64,1024]{3,2,1,0:T(8,128)(2,1)S(1)}, u32[]{:S(2)}, u32[]{:S(2)}) collective-permute-start(bf16[4,2,64,1024]{3,2,1,0:T(8,128)(2,1)S(1)} %join.7.refs_5_), channel_id=1, source_target_pairs={{0,48},{16,32},{32,16},{48,0},{1,49},{17,33},{33,17},{49,1},{2,50}... | collective-permute-start | bytes 3145736 | tf_op jit(solution)/shard_map/ppermute | solution.py:29
  175.7 28.2 %collective-permute-done.15.refs_4_ = bf16[4,2,64,1024]{3,2,1,0:T(8,128)(2,1)S(1)} collective-permute-done((bf16[4,2,64,1024]{3,2,1,0:T(8,128)(2,1)S(1)}, bf16[4,2,64,1024]{3,2,1,0:T(8,128)(2,1)S(1)}, u32[]{:S(2)}, u32[]{:S(2)}) %collective-permute-start.15) | collective-permute-done | bytes 1048608 | tf_op jit(solution)/shard_map/ppermute | solution.py:29
  213.6 6.8 %collective-permute-done.16.refs_2_ = bf16[2,2,64,1024]{3,2,1,0:T(8,128)(2,1)} collective-permute-done((bf16[2,2,64,1024]{3,2,1,0:T(8,128)(2,1)}, bf16[2,2,64,1024]{3,2,1,0:T(8,128)(2,1)}, u32[]{:S(2)}, u32[]{:S(2)}) %collective-permute-start.16) | collective-permute-done | bytes 524320 | tf_op jit(solution)/shard_map/ppermute | solution.py:29
  229.6 22.6 %mlp.1 = (bf16[2,1024,1024]{2,1,0:T(8,128)(2,1)}, f32[1,1024]{1,0:T(1,128)S(1)}, bf16[2048,1024]{1,0:T(8,128)(2,1)}, bf16[2048,1024]{1,0:T(8,128)(2,1)}) custom-call(s32[5]{0:T(128)S(1)} %stack.52.coords, bf16[2,1024,2048]{2,1,0:T(8,128)(2,1)} %copy-done.20, f32[1,1024]{1,0:T(1,128)S(1)} %bitcast.109, bf16[4,2,64,1024]{3,2,1,0:T(8,128)(2,1)S(1)} %join.6.refs_0_, ...), custom_call_target="tpu_custom_call" | custom-call | flops 8589934592 | bytes 25165824 | tf_op jit(solution)/shard_map/mlp/pallas_call | solution.py:363
  254.4 13.3 %weight_grads.3 = bf16[16,2,64,2048]{3,2,1,0:T(8,128)(2,1)S(1)} custom-call(bf16[2,2048,1024]{2,1,0:T(8,128)(2,1)} %get-tuple-element.65.left_ref, bf16[2,1024,1024]{2,1,0:T(8,128)(2,1)S(1)} %copy-done.26), custom_call_target="tpu_custom_call" | custom-call | flops 8589934592 | bytes 16777216 | tf_op jit(solution)/shard_map/weight_grads/pallas_call | solution.py:395
  271.0 7.7 %fusion = f32[1024,2048]{1,0:T(8,128)} fusion(bf16[1024,768]{1,0:T(8,128)(2,1)S(1)} %get-tuple-element.62, bf16[2048,1024]{1,0:T(8,128)(2,1)} %copy-done.9), kind=kOutput, calls=%fused_computation.7 | convolution fusion | flops 3221225472 | bytes 13107200 | tf_op jit(solution)/shard_map/te,de->td/dot_general | solution.py:587
  278.7 7.0 %convolution_add_fusion = f32[1024,2048]{1,0:T(8,128)S(1)} fusion(f32[1024,2048]{1,0:T(8,128)} %fusion, bf16[2048,1024]{1,0:T(8,128)(2,1)S(1)} %copy-done.39, bf16[2,1024,1024]{2,1,0:T(8,128)(2,1)S(1)} %copy-done.27), kind=kOutput, calls=%fused_computation.4 | convolution fusion | flops 4297064448 | bytes 23068672 | tf_op jit(solution)/shard_map/tf,df->td/dot_general | solution.py:589
  295.5 6.8 %convolution_add_fusion.1 = f32[1024,2048]{1,0:T(8,128)} fusion(f32[1024,2048]{1,0:T(8,128)S(1)} %fusion.26, bf16[2048,1024]{1,0:T(8,128)(2,1)S(1)} %copy-done.38, bf16[2,1024,1024]{2,1,0:T(8,128)(2,1)S(1)} %copy-done.27), kind=kOutput, calls=%fused_computation.5 | convolution fusion | flops 4297064448 | bytes 23068672 | tf_op jit(solution)/shard_map/tf,df->td/dot_general | solution.py:583
  302.2 4.0 slice.203
  306.9 3.7 fusion.32
  314.3 3.9 fusion.33
  321.3 4.2 %collective-permute-done.30 = bf16[128,2048]{1,0:T(8,128)(2,1)S(1)} collective-permute-done((bf16[128,2048]{1,0:T(8,128)(2,1)S(1)}, bf16[128,2048]{1,0:T(8,128)(2,1)S(1)}, u32[]{:S(2)}, u32[]{:S(2)}) %collective-permute-start.30) | collective-permute-done | bytes 524320 | tf_op jit(solution)/shard_map/ppermute | solution.py:25
  327.9 8.8 %collective-permute-done.31 = bf16[128,2048]{1,0:T(8,128)(2,1)S(1)} collective-permute-done((bf16[128,2048]{1,0:T(8,128)(2,1)S(1)}, bf16[128,2048]{1,0:T(8,128)(2,1)S(1)}, u32[]{:S(2)}, u32[]{:S(2)}) %collective-permute-start.31) | collective-permute-done | bytes 524320 | tf_op jit(solution)/shard_map/ppermute | solution.py:25
  338.9 9.0 %collective-permute-done.26 = bf16[128,2048]{1,0:T(8,128)(2,1)S(1)} collective-permute-done((bf16[128,2048]{1,0:T(8,128)(2,1)S(1)}, bf16[128,2048]{1,0:T(8,128)(2,1)S(1)}, u32[]{:S(2)}, u32[]{:S(2)}) %collective-permute-start.26) | collective-permute-done | bytes 524320 | tf_op jit(solution)/shard_map/ppermute | solution.py:25
  347.9 11.3 %collective-permute-done.27 = bf16[128,2048]{1,0:T(8,128)(2,1)S(1)} collective-permute-done((bf16[128,2048]{1,0:T(8,128)(2,1)S(1)}, bf16[128,2048]{1,0:T(8,128)(2,1)S(1)}, u32[]{:S(2)}, u32[]{:S(2)}) %collective-permute-start.27) | collective-permute-done | bytes 524320 | tf_op jit(solution)/shard_map/ppermute | solution.py:25
  399.4 3.8 collective-permute-done.44.refs_2_
  (262 shorter events, 160.6 us)
Async XLA Ops:
  7.2 87.6 %all-gather.2.cloned.1.call-start = ((), (), s32[]{:S(2)}) async-start(), calls=%async_computation.2 | async-start | bytes 4456448 | tf_op jit(solution)/shard_map/all_gather | solution.py:544
  21.5 366.1 %reduce-scatter.3.cloned.1.call-start = ((), (), s32[]{:S(2)}) async-start(), calls=%async_computation.3 | async-start | bytes 4456448 | tf_op jit(solution)/shard_map/reduce_scatter | solution.py:503
  24.5 26.8 %collective-permute-start = (bf16[2,128,2048]{2,1,0:T(8,128)(2,1)S(1)}, bf16[2,128,2048]{2,1,0:T(8,128)(2,1)S(1)}, u32[]{:S(2)}, u32[]{:S(2)}) collective-permute-start(bf16[2,128,2048]{2,1,0:T(8,128)(2,1)S(1)} %pad_maximum_fusion.refs_0_), channel_id=1, source_target_pairs={{0,65},{1,64},{64,1},{65,0},{2,67},{3,66},{66,3},{67,2},{4,69},{5,... | collective-permute-start | bytes 3145736 | tf_op jit(solution)/shard_map/ppermute | solution.py:25
  28.0 24.9 %collective-permute-start.2 = (bf16[2,128,2048]{2,1,0:T(8,128)(2,1)S(1)}, bf16[2,128,2048]{2,1,0:T(8,128)(2,1)S(1)}, u32[]{:S(2)}, u32[]{:S(2)}) collective-permute-start(bf16[2,128,2048]{2,1,0:T(8,128)(2,1)S(1)} %pad_maximum_fusion.refs_0_), channel_id=1, source_target_pairs={{0,64},{64,0},{1,65},{65,1},{2,66},{66,2},{3,67},{67,3},{4,68},{68... | collective-permute-start | bytes 3145736 | tf_op jit(solution)/shard_map/ppermute | solution.py:25
  135.6 257.2 %reduce-scatter.5.cloned.1.call-start = ((), (), s32[]{:S(2)}) async-start(), calls=%async_computation.4 | async-start | bytes 8912896 | tf_op jit(solution)/shard_map/reduce_scatter | solution.py:503
  146.7 18.1 %collective-permute-start.12 = (bf16[2,64,1024]{2,1,0:T(8,128)(2,1)S(1)}, bf16[2,64,1024]{2,1,0:T(8,128)(2,1)S(1)}, u32[]{:S(2)}, u32[]{:S(2)}) collective-permute-start(bf16[2,64,1024]{2,1,0:T(8,128)(2,1)S(1)} %bitcast.102), channel_id=1, source_target_pairs={{0,32},{16,48},{32,0},{48,16},{1,33},{17,49},{33,1},{49,17},{2,34}... | collective-permute-start | bytes 786440 | tf_op jit(solution)/shard_map/ppermute | solution.py:29
  149.1 18.8 %collective-permute-start.13 = (bf16[2,64,1024]{2,1,0:T(8,128)(2,1)S(1)}, bf16[2,64,1024]{2,1,0:T(8,128)(2,1)S(1)}, u32[]{:S(2)}, u32[]{:S(2)}) collective-permute-start(bf16[2,64,1024]{2,1,0:T(8,128)(2,1)S(1)} %bitcast.103), channel_id=1, source_target_pairs={{0,48},{16,32},{32,16},{48,0},{1,49},{17,33},{33,17},{49,1},{2,50}... | collective-permute-start | bytes 786440 | tf_op jit(solution)/shard_map/ppermute | solution.py:29
  149.3 19.9 %collective-permute-start.18 = (bf16[2,64,1024]{2,1,0:T(8,128)(2,1)S(1)}, bf16[2,64,1024]{2,1,0:T(8,128)(2,1)S(1)}, u32[]{:S(2)}, u32[]{:S(2)}) collective-permute-start(bf16[2,64,1024]{2,1,0:T(8,128)(2,1)S(1)} %bitcast.97), channel_id=1, source_target_pairs={{0,4},{4,0},{8,12},{12,8},{1,5},{5,1},{9,13},{13,9},{2,6},{6,2},{1... | collective-permute-start | bytes 786440 | tf_op jit(solution)/shard_map/ppermute | solution.py:29
  150.6 18.6 %collective-permute-start.19 = (bf16[2,64,1024]{2,1,0:T(8,128)(2,1)S(1)}, bf16[2,64,1024]{2,1,0:T(8,128)(2,1)S(1)}, u32[]{:S(2)}, u32[]{:S(2)}) collective-permute-start(bf16[2,64,1024]{2,1,0:T(8,128)(2,1)S(1)} %bitcast.98), channel_id=1, source_target_pairs={{0,8},{4,12},{8,0},{12,4},{1,9},{5,13},{9,1},{13,5},{2,10},{6,14},... | collective-permute-start | bytes 786440 | tf_op jit(solution)/shard_map/ppermute | solution.py:29
  154.6 15.6 %collective-permute-start.20 = (bf16[2,64,1024]{2,1,0:T(8,128)(2,1)S(1)}, bf16[2,64,1024]{2,1,0:T(8,128)(2,1)S(1)}, u32[]{:S(2)}, u32[]{:S(2)}) collective-permute-start(bf16[2,64,1024]{2,1,0:T(8,128)(2,1)S(1)} %bitcast.99), channel_id=1, source_target_pairs={{0,12},{4,8},{8,4},{12,0},{1,13},{5,9},{9,5},{13,1},{2,14},{6,10},... | collective-permute-start | bytes 786440 | tf_op jit(solution)/shard_map/ppermute | solution.py:29
  168.0 35.9 %collective-permute-start.15 = (bf16[4,2,64,1024]{3,2,1,0:T(8,128)(2,1)S(1)}, bf16[4,2,64,1024]{3,2,1,0:T(8,128)(2,1)S(1)}, u32[]{:S(2)}, u32[]{:S(2)}) collective-permute-start(bf16[4,2,64,1024]{3,2,1,0:T(8,128)(2,1)S(1)} %join.6.refs_0_), channel_id=1, source_target_pairs={{0,12},{4,8},{8,4},{12,0},{1,13},{5,9},{9,5},{13,1},{2,14},{6,10},... | collective-permute-start | bytes 3145736 | tf_op jit(solution)/shard_map/ppermute | solution.py:29
  169.2 35.6 %collective-permute-start.14 = (bf16[4,2,64,1024]{3,2,1,0:T(8,128)(2,1)S(1)}, bf16[4,2,64,1024]{3,2,1,0:T(8,128)(2,1)S(1)}, u32[]{:S(2)}, u32[]{:S(2)}) collective-permute-start(bf16[4,2,64,1024]{3,2,1,0:T(8,128)(2,1)S(1)} %join.6.refs_0_), channel_id=1, source_target_pairs={{0,4},{4,0},{8,12},{12,8},{1,5},{5,1},{9,13},{13,9},{2,6},{6,2},{1... | collective-permute-start | bytes 3145736 | tf_op jit(solution)/shard_map/ppermute | solution.py:29
  170.3 36.8 %collective-permute-start.22 = (bf16[4,2,64,1024]{3,2,1,0:T(8,128)(2,1)S(1)}, bf16[4,2,64,1024]{3,2,1,0:T(8,128)(2,1)S(1)}, u32[]{:S(2)}, u32[]{:S(2)}) collective-permute-start(bf16[4,2,64,1024]{3,2,1,0:T(8,128)(2,1)S(1)} %join.7.refs_5_), channel_id=1, source_target_pairs={{0,48},{16,32},{32,16},{48,0},{1,49},{17,33},{33,17},{49,1},{2,50}... | collective-permute-start | bytes 3145736 | tf_op jit(solution)/shard_map/ppermute | solution.py:29
  175.4 34.7 %collective-permute-start.21 = (bf16[4,2,64,1024]{3,2,1,0:T(8,128)(2,1)S(1)}, bf16[4,2,64,1024]{3,2,1,0:T(8,128)(2,1)S(1)}, u32[]{:S(2)}, u32[]{:S(2)}) collective-permute-start(bf16[4,2,64,1024]{3,2,1,0:T(8,128)(2,1)S(1)} %join.7.refs_5_), channel_id=1, source_target_pairs={{0,16},{16,0},{32,48},{48,32},{1,17},{17,1},{33,49},{49,33},{2,18}... | collective-permute-start | bytes 3145736 | tf_op jit(solution)/shard_map/ppermute | solution.py:29
  204.8 15.6 %collective-permute-start.16 = (bf16[2,2,64,1024]{3,2,1,0:T(8,128)(2,1)}, bf16[2,2,64,1024]{3,2,1,0:T(8,128)(2,1)}, u32[]{:S(2)}, u32[]{:S(2)}) collective-permute-start(bf16[2,2,64,1024]{3,2,1,0:T(8,128)(2,1)} %slice.145), channel_id=1, source_target_pairs={{0,4},{4,0},{8,12},{12,8},{1,5},{5,1},{9,13},{13,9},{2,6},{6,2},{1... | collective-permute-start | bytes 1572872 | tf_op jit(solution)/shard_map/ppermute | solution.py:29
  205.7 16.4 %collective-permute-start.17 = (bf16[2,2,64,1024]{3,2,1,0:T(8,128)(2,1)}, bf16[2,2,64,1024]{3,2,1,0:T(8,128)(2,1)}, u32[]{:S(2)}, u32[]{:S(2)}) collective-permute-start(bf16[2,2,64,1024]{3,2,1,0:T(8,128)(2,1)} %slice.146), channel_id=1, source_target_pairs={{0,12},{4,8},{8,4},{12,0},{1,13},{5,9},{9,5},{13,1},{2,14},{6,10},... | collective-permute-start | bytes 1572872 | tf_op jit(solution)/shard_map/ppermute | solution.py:29
  208.0 17.8 %collective-permute-start.23 = (bf16[2,2,64,1024]{3,2,1,0:T(8,128)(2,1)}, bf16[2,2,64,1024]{3,2,1,0:T(8,128)(2,1)}, u32[]{:S(2)}, u32[]{:S(2)}) collective-permute-start(bf16[2,2,64,1024]{3,2,1,0:T(8,128)(2,1)} %slice.147), channel_id=1, source_target_pairs={{0,16},{16,0},{32,48},{48,32},{1,17},{17,1},{33,49},{49,33},{2,18}... | collective-permute-start | bytes 1572872 | tf_op jit(solution)/shard_map/ppermute | solution.py:29
  211.2 15.9 %collective-permute-start.24 = (bf16[2,2,64,1024]{3,2,1,0:T(8,128)(2,1)}, bf16[2,2,64,1024]{3,2,1,0:T(8,128)(2,1)}, u32[]{:S(2)}, u32[]{:S(2)}) collective-permute-start(bf16[2,2,64,1024]{3,2,1,0:T(8,128)(2,1)} %slice.148), channel_id=1, source_target_pairs={{0,48},{16,32},{32,16},{48,0},{1,49},{17,33},{33,17},{49,1},{2,50}... | collective-permute-start | bytes 1572872 | tf_op jit(solution)/shard_map/ppermute | solution.py:29
  289.6 17.3 %collective-permute-start.29 = (bf16[512,2048]{1,0:T(8,128)(2,1)}, bf16[512,2048]{1,0:T(8,128)(2,1)}, u32[]{:S(2)}, u32[]{:S(2)}) collective-permute-start(bf16[512,2048]{1,0:T(8,128)(2,1)} %slice.202), channel_id=1, source_target_pairs={{0,2},{2,0},{1,3},{3,1},{4,6},{6,4},{5,7},{7,5},{8,10},{10,8},{9,1... | collective-permute-start | bytes 6291464 | tf_op jit(solution)/shard_map/ppermute | solution.py:25
  313.5 23.2 %collective-permute-start.31 = (bf16[128,2048]{1,0:T(8,128)(2,1)S(1)}, bf16[128,2048]{1,0:T(8,128)(2,1)S(1)}, u32[]{:S(2)}, u32[]{:S(2)}) collective-permute-start(bf16[128,2048]{1,0:T(8,128)(2,1)S(1)} %get-tuple-element.89), channel_id=1, source_target_pairs={{0,64},{64,0},{1,65},{65,1},{2,66},{66,2},{3,67},{67,3},{4,68},{68... | collective-permute-start | bytes 1572872 | tf_op jit(solution)/shard_map/ppermute | solution.py:25
  313.8 24.4 %collective-permute-start.32 = (bf16[128,2048]{1,0:T(8,128)(2,1)S(1)}, bf16[128,2048]{1,0:T(8,128)(2,1)S(1)}, u32[]{:S(2)}, u32[]{:S(2)}) collective-permute-start(bf16[128,2048]{1,0:T(8,128)(2,1)S(1)} %get-tuple-element.88), channel_id=1, source_target_pairs={{0,65},{1,64},{64,1},{65,0},{2,67},{3,66},{66,3},{67,2},{4,69},{5,... | collective-permute-start | bytes 1572872 | tf_op jit(solution)/shard_map/ppermute | solution.py:25
  318.4 29.6 %collective-permute-start.26 = (bf16[128,2048]{1,0:T(8,128)(2,1)S(1)}, bf16[128,2048]{1,0:T(8,128)(2,1)S(1)}, u32[]{:S(2)}, u32[]{:S(2)}) collective-permute-start(bf16[128,2048]{1,0:T(8,128)(2,1)S(1)} %get-tuple-element.90), channel_id=1, source_target_pairs={{0,1},{1,0},{2,3},{3,2},{4,5},{5,4},{6,7},{7,6},{8,9},{9,8},{10,11... | collective-permute-start | bytes 1572872 | tf_op jit(solution)/shard_map/ppermute | solution.py:25
  320.9 38.3 %collective-permute-start.27 = (bf16[128,2048]{1,0:T(8,128)(2,1)S(1)}, bf16[128,2048]{1,0:T(8,128)(2,1)S(1)}, u32[]{:S(2)}, u32[]{:S(2)}) collective-permute-start(bf16[128,2048]{1,0:T(8,128)(2,1)S(1)} %get-tuple-element.92), channel_id=1, source_target_pairs={{0,64},{64,0},{1,65},{65,1},{2,66},{66,2},{3,67},{67,3},{4,68},{68... | collective-permute-start | bytes 1572872 | tf_op jit(solution)/shard_map/ppermute | solution.py:25
  325.4 34.5 %collective-permute-start.28 = (bf16[128,2048]{1,0:T(8,128)(2,1)S(1)}, bf16[128,2048]{1,0:T(8,128)(2,1)S(1)}, u32[]{:S(2)}, u32[]{:S(2)}) collective-permute-start(bf16[128,2048]{1,0:T(8,128)(2,1)S(1)} %get-tuple-element.91), channel_id=1, source_target_pairs={{0,65},{1,64},{64,1},{65,0},{2,67},{3,66},{66,3},{67,2},{4,69},{5,... | collective-permute-start | bytes 1572872 | tf_op jit(solution)/shard_map/ppermute | solution.py:25
  (68 other events, 685.9 us)
Sparse Core Ops, SparseCore 0:
  21.6 52.9 all-gather.1
  135.8 89.2 reduce-scatter.2
  271.1 85.4 reduce-scatter.4
where the time goes:
time: 420 us; the launch traced here: 416 us
  waiting for transfers between devices  159 us (38%)
  Pallas kernels  94.3 us (22%)
  starting transfers between devices  65.8 us (16%)
  local copies, waits for them, and re-layouts  42.2 us (10%)
  matrix products  24 us (6%)
  other arithmetic  16.2 us (4%)
  between operations  14.8 us (4%)
    ppermute x29, waiting for transfers between devices, flip(): return lax.ppermute(value, axes, [(i, count - 1 - i) for i in range(count)])  97 us
    ppermute x20, waiting for transfers between devices, hop(): return lax.ppermute(value, axis, [(i, i ^ bits) for i in range(4)])  61.5 us
    ppermute x29, starting transfers between devices, flip(): return lax.ppermute(value, axes, [(i, count - 1 - i) for i in range(count)])  36.4 us
    ppermute x20, starting transfers between devices, hop(): return lax.ppermute(value, axis, [(i, i ^ bits) for i in range(4)])  29.3 us
    unnamed x90, local copies, waits for them, and re-layouts  28.1 us
    pallas_call x2, Pallas kernels, weight_grads(): pl.pallas_call(grads_kernel, grid=(count, tiles, 2), in_specs=[pl.BlockSp...  24.1 us
    pallas_call x1, Pallas kernels, mlp(): pl.pallas_call(mlp_kernel, in_specs=[SCALARS, ANY, WHOLE] + [ANY] * 10, o...  22.6 us
    pallas_call x1, Pallas kernels, attention(): pl.pallas_call(attention_kernel, grid=(count,), in_specs=[blocks(3 * widt...  15.8 us
  transfers between devices with their start and end apart: 52, of which 34 were waited for; matrix products, arithmetic and copies ran while one was open for 14% of the time, Pallas kernels for 13%

commit v1 on v0

v1 whole, which is shorter than its diff:
```python
import functools

import jax
import jax.numpy as jnp
from jax import lax
from jax.experimental import pallas as pl
from jax.experimental.pallas import tpu as pltpu
from jax.sharding import Mesh, PartitionSpec as P

HEAD_DIM = 64
ROT = 32
HALF = ROT // 2
LANES = 128
EPSILON = 1e-05

AXES = ("zl", "x", "y", "c", "mp")
SIZES = (2, 4, 4, 2, 2)
PLANE = ("x", "y")
PAIR = ("zl", "c")

BF16 = jnp.bfloat16
F32 = jnp.float32
MIB = 1024 * 1024
GIGA = 1000 * MIB


def flip(value, *axes):
    count = 2 ** len(axes)
    return lax.ppermute(value, axes, [(i, count - 1 - i) for i in range(count)])


def hop(value, axis, bits):
    return lax.ppermute(value, axis, [(i, i ^ bits) for i in range(4)])


def fold_kernel(mine_ref, theirs_ref, keep_ref, *sends):
    rows = keep_ref.shape[0]
    for i in range(4):
        block = slice(i * rows, (i + 1) * rows)
        total = mine_ref[block, :].astype(F32) + theirs_ref[block, :].astype(F32)
        if i == 0:
            keep_ref[...] = total
        else:
            sends[i - 1][...] = total.astype(BF16)


def scatter_group(mine, theirs):
    rows, depth = mine.shape[0] // 4, mine.shape[1]
    tile = depth // 4
    theirs = flip(theirs, "c")
    keep, *sends = pl.pallas_call(
        fold_kernel,
        grid=(4,),
        in_specs=[pl.BlockSpec((4 * rows, tile), lambda j: (0, j))] * 2,
        out_specs=[pl.BlockSpec((rows, tile), lambda j: (0, j))] * 4,
        out_shape=[like((rows, depth), F32)] + [like((rows, depth))] * 3,
        compiler_params=params(16),
        cost_estimate=cost(0, 13 * rows * depth),
        name="fold",
    )(mine, theirs)
    far = [flip(sends[0], "mp"), flip(sends[1], "zl"), flip(sends[2], "zl", "mp")]
    return keep + far[0].astype(F32) + (far[1].astype(F32) + far[2].astype(F32))


def sum_everywhere(vector):
    vector = vector + flip(vector, "c")
    vector = vector + flip(vector, "zl") + (flip(vector, "mp") + flip(vector, "zl", "mp"))
    for axis in PLANE:
        vector = (vector + hop(vector, axis, 2)) + (hop(vector, axis, 1) + hop(vector, axis, 3))
    return vector


def attention_kernel(
    linear_ref,
    grad_ref,
    cos_ref,
    low_ref,
    high_ref,
    segment_col,
    segment_row,
    index_col,
    index_row,
    right_ref,
    query_ref,
    key_ref,
    value_ref,
    grad_query_ref,
    grad_key_ref,
):
    width = grad_ref.shape[1]
    scale = HEAD_DIM ** (-0.5)

    def rotated(tile, lanes, sign):
        cos, low, high = cos_ref[...], low_ref[...], high_ref[...]
        ahead = pltpu.roll(tile, lanes - HALF, 1)
        behind = pltpu.roll(tile, HALF, 1)
        return tile * cos + (ahead * low + behind * high) * sign

    for start in range(0, width, LANES):
        lanes = slice(start, start + LANES)
        query_ref[:, lanes] = (rotated(linear_ref[:, lanes], LANES, 1.0) * scale).astype(BF16)
        keys = linear_ref[:, width + start : width + start + LANES]
        key_ref[:, lanes] = rotated(keys, LANES, 1.0).astype(BF16)
        value_ref[:, lanes] = linear_ref[:, 2 * width + start : 2 * width + start + LANES].astype(BF16)
    allowed = (segment_col[...] == segment_row[0]) & (index_col[...] >= index_row[0])
    for start in range(0, width, HEAD_DIM):
        lanes = slice(start, start + HEAD_DIM)
        query, key, value = query_ref[:, lanes], key_ref[:, lanes], value_ref[:, lanes]
        grad = grad_ref[:, lanes]
        scores = lax.dot_general(query, key, (((1,), (1,)), ((), ())), preferred_element_type=F32)
        scores = jnp.where(allowed, scores, -1000000000.0)
        expo = jnp.exp(scores - jnp.max(scores, axis=1, keepdims=True))
        probs = expo / jnp.sum(expo, axis=1, keepdims=True)
        low_probs = probs.astype(BF16)
        attended = jnp.dot(low_probs, value, preferred_element_type=F32)
        right_ref[:, 3 * width + start : 3 * width + start + HEAD_DIM] = attended.astype(BF16)
        grad_probs = lax.dot_general(grad, value, (((1,), (1,)), ((), ())), preferred_element_type=F32)
        grad_values = lax.dot_general(
            low_probs, grad, (((0,), (0,)), ((), ())), preferred_element_type=F32
        )
        weighted = probs * grad_probs
        delta = jnp.sum(weighted, axis=1, keepdims=True)
        grad_scores = (weighted - probs * delta).astype(BF16)
        grad_query_ref[:, lanes] = jnp.dot(grad_scores, key, preferred_element_type=F32) * scale
        grad_key_ref[:, lanes] = lax.dot_general(
            grad_scores, query, (((0,), (0,)), ((), ())), preferred_element_type=F32
        )
        right_ref[:, 2 * width + start : 2 * width + start + HEAD_DIM] = grad_values.astype(BF16)
    for start in range(0, width, LANES):
        lanes = slice(start, start + LANES)
        right_ref[:, lanes] = rotated(grad_query_ref[:, lanes], LANES, -1.0).astype(BF16)
        right_ref[:, width + start : width + start + LANES] = rotated(
            grad_key_ref[:, lanes], LANES, -1.0
        ).astype(BF16)


def attention(linear, grad_attended, tables, segments, indices, length):
    rows, width = grad_attended.shape
    count = rows // length
    blocks = lambda lanes: pl.BlockSpec((length, lanes), lambda i: (i, 0))
    rowwise = pl.BlockSpec((1, 1, length), lambda i: (i, 0, 0))
    return pl.pallas_call(
        attention_kernel,
        grid=(count,),
        in_specs=[
            blocks(3 * width),
            blocks(width),
            blocks(LANES),
            blocks(LANES),
            blocks(LANES),
            blocks(1),
            rowwise,
            blocks(1),
            rowwise,
        ],
        out_specs=blocks(4 * width),
        out_shape=jax.ShapeDtypeStruct((rows, 4 * width), BF16),
        scratch_shapes=[pltpu.VMEM((length, width), BF16)] * 3
        + [pltpu.VMEM((length, width), F32)] * 2,
        compiler_params=params(32),
        cost_estimate=cost(18 * GIGA, 8 * MIB),
        name="attention",
    )(
        linear,
        grad_attended,
        *tables,
        segments.reshape(rows, 1),
        segments.reshape(count, 1, length),
        indices.reshape(rows, 1),
        indices.reshape(count, 1, length),
    )


ANY = pl.BlockSpec(memory_space=pl.ANY)
WHOLE = pl.BlockSpec(memory_space=pltpu.VMEM)
SCALARS = pl.BlockSpec(memory_space=pltpu.SMEM)


def like(shape, dtype=BF16):
    return jax.ShapeDtypeStruct(shape, dtype)


def params(mib):
    return pltpu.CompilerParams(vmem_limit_bytes=mib * MIB)


def cost(flops, moved):
    return pl.CostEstimate(flops=flops, bytes_accessed=moved, transcendentals=0)


def slot_of(coords, bits):
    return (coords[0] * 2 + coords[3]) ^ bits


def pack_kernel(coords, up_ref, down_ref, qkv_ref, out_ref, segment_ref, *parts):
    hidden, width = up_ref.shape[1] // 4, out_ref.shape[1] // 4
    segments = segment_ref[...].astype(F32).astype(BF16)
    segments = jnp.broadcast_to(segments, (up_ref.shape[0], segments.shape[1]))
    for bits in range(4):
        slot = slot_of(coords, bits)
        wide = pl.ds(pl.multiple_of(slot * hidden, hidden), hidden)
        narrow = pl.ds(pl.multiple_of(slot * width, width), width)
        part = parts[bits]
        part[:, :hidden] = up_ref[:, wide]
        part[:, hidden : 2 * hidden] = down_ref[:, wide]
        for kind in range(3):
            start = 2 * hidden + kind * width
            part[:, start : start + width] = qkv_ref[kind, :, narrow]
        start = 2 * hidden + 3 * width
        part[:, start : start + width] = out_ref[:, narrow]
        part[:, start + width :] = segments


def pack(coords, w_up, down_t, qkv_t, out_t, segments):
    rows, hidden, width = w_up.shape[0], w_up.shape[1] // 4, out_t.shape[1] // 4
    return pl.pallas_call(
        pack_kernel,
        in_specs=[SCALARS] + [WHOLE] * 5,
        out_specs=[WHOLE] * 4,
        out_shape=[like((rows, 2 * hidden + 4 * width + segments.shape[0]))] * 4,
        compiler_params=params(16),
        name="pack",
    )(coords, w_up, down_t, qkv_t, out_t, segments.reshape(1, -1))


def order_kernel(coords, *refs):
    parts, outs = refs[:4], refs[4:]
    for bits in range(4):
        zl, c = coords[0] ^ (bits >> 1), coords[3] ^ (bits & 1)
        start = 0
        for out in outs:
            columns = out.shape[3]
            out[zl, c] = parts[bits][:, start : start + columns]
            start += columns


def order(coords, parts, columns):
    rows = parts[0].shape[0]
    outs = pl.pallas_call(
        order_kernel,
        in_specs=[SCALARS] + [WHOLE] * 4,
        out_specs=[WHOLE] * len(columns),
        out_shape=[like((2, 2, rows, count)) for count in columns],
        compiler_params=params(16),
        name="order",
    )(coords, *parts)
    return [out.reshape(2, 2 * rows, -1) for out in outs]


def join_kernel(*refs):
    parts, out, sem = refs[:-2], refs[-2], refs[-1]
    copies = []
    for i, part in enumerate(parts):
        copies.append(pltpu.make_async_copy(part, out.at[i], sem.at[i]))
        copies[-1].start()
    for copy in copies:
        copy.wait()


def join(*parts):
    return pl.pallas_call(
        join_kernel,
        in_specs=[ANY] * len(parts),
        out_specs=ANY,
        out_shape=like((len(parts),) + parts[0].shape),
        scratch_shapes=[pltpu.SemaphoreType.DMA((len(parts),))],
        compiler_params=params(16),
        name="join",
    )(*parts)


def place_kernel(entries, second_is_y, coords, *refs):
    parts, out, sems = refs[-2 - len(entries) : -2], refs[-2], refs[-1]
    x, y = coords[1], coords[2]
    copies = []
    for part, (second, start) in zip(parts, entries):
        for i in range(part.shape[0]):
            first = start + i
            if second_is_y:
                chip = (x ^ first) * 4 + (y ^ second)
            else:
                chip = (x ^ second) * 4 + (y ^ first)
            copies.append(pltpu.make_async_copy(part.at[i], out.at[:, chip], sems.at[len(copies)]))
            copies[-1].start()
    for copy in copies:
        copy.wait()


def place(coords, buffer, parts, entries, second):
    _, _, rows, columns = parts[0].shape
    count = sum(part.shape[0] for part in parts)
    buffers = [] if buffer is None else [buffer]
    return pl.pallas_call(
        functools.partial(place_kernel, entries, second == "y"),
        in_specs=[SCALARS] + [ANY] * (len(buffers) + len(parts)),
        out_specs=ANY,
        out_shape=like((2, 16, rows, columns)),
        scratch_shapes=[pltpu.SemaphoreType.DMA((count,))],
        input_output_aliases={1: 0} if buffers else {},
        compiler_params=params(16),
        cost_estimate=cost(0, 4 * count * rows * columns * 2),
        name="place",
    )(coords, *buffers, *parts)


def gather_line(shard, axis):
    return join(shard, hop(shard, axis, 1), hop(shard, axis, 2), hop(shard, axis, 3))


def gather_sides(row, axis):
    return hop(row, axis, 1), hop(row, axis, 3)


def gather_plane(coords, row, sides, second):
    one, three = sides
    buffer = place(coords, None, [row], [(0, 0)], second)
    half = row.shape[0] // 2
    two_low, two_high = hop(three[:half], second, 1), hop(one[half:], second, 3)
    buffer = place(coords, buffer, [one, three], [(1, 0), (3, 0)], second)
    buffer = place(coords, buffer, [two_low, two_high], [(2, 0), (2, half)], second)
    return buffer.reshape(-1, buffer.shape[3])


def tokens_kernel(mine_ref, other_ref, rows_ref, columns_ref):
    @pl.when(pl.program_id(1) == 0)
    def _():
        rows_ref[0] = mine_ref[0, 0]
        columns_ref[0] = mine_ref[0, 0].T

    @pl.when(pl.program_id(1) == 1)
    def _():
        rows_ref[0] = other_ref[0, 0]
        columns_ref[0] = other_ref[0, 0].T


def gather_tokens(*pairs):
    mine = join(*pairs)
    other = flip(mine, "c")
    _, _, rows, depth = mine.shape
    block = (1, 1, rows, depth)
    return pl.pallas_call(
        tokens_kernel,
        grid=(2, 2, 4),
        in_specs=[
            pl.BlockSpec(block, lambda w, c, z: (jnp.where(c == 0, z, 3), w, 0, 0)),
            pl.BlockSpec(block, lambda w, c, z: (jnp.where(c == 1, z, 0), w, 0, 0)),
        ],
        out_specs=[
            pl.BlockSpec((1, rows, depth), lambda w, c, z: (w, 4 * c + z, 0)),
            pl.BlockSpec((1, depth, rows), lambda w, c, z: (w, 0, 4 * c + z)),
        ],
        out_shape=[like((2, 8 * rows, depth)), like((2, depth, 8 * rows))],
        compiler_params=params(32),
        cost_estimate=cost(0, 8 * mine.size * 2),
        name="tokens",
    )(mine, other)


def mlp_kernel(pair_ref, bias_ref, up_ref, down_ref, hidden_ref, sums_ref):
    slope = 0.7978845608028654
    up = jnp.dot(pair_ref[0], up_ref[...], preferred_element_type=F32) + bias_ref[...]
    square = up * up
    wave = jnp.tanh(slope * (up + 0.044715 * (square * up)))
    half = 0.5 * (1.0 + wave)
    hidden_ref[1] = (up * half).astype(BF16)
    rise = half + (0.5 * up) * (1.0 - wave * wave) * (slope * (1.0 + 0.134145 * square))
    grad = jnp.dot(pair_ref[1], down_ref[...], preferred_element_type=F32) * rise
    low = grad.astype(BF16)
    hidden_ref[0] = low
    sums_ref[...] = jnp.sum(low.astype(F32), axis=0, keepdims=True)


def mlp(pair, bias, up_w, down_w):
    rows, depth = pair.shape[1:]
    hidden = bias.shape[0]
    tile = 256
    column = lambda j: (0, j)
    return pl.pallas_call(
        mlp_kernel,
        grid=(hidden // tile,),
        in_specs=[
            pl.BlockSpec((2, rows, depth), lambda j: (0, 0, 0), pipeline_mode=pl.Buffered(1)),
            pl.BlockSpec((1, tile), column),
            pl.BlockSpec((depth, tile), column),
            pl.BlockSpec((depth, tile), column),
        ],
        out_specs=[
            pl.BlockSpec((2, rows, tile), lambda j: (0, 0, j)),
            pl.BlockSpec((1, tile), column),
        ],
        out_shape=[like((2, rows, hidden)), like((1, hidden), F32)],
        compiler_params=params(32),
        cost_estimate=cost(4 * rows * depth * hidden, 20 * MIB),
        name="mlp",
    )(pair, bias.reshape(1, -1), up_w, down_w)


def grads_kernel(left_ref, right_ref, out_ref):
    product = jnp.dot(left_ref[0], right_ref[0], preferred_element_type=F32).astype(BF16)
    out_ref[...] = product.reshape(out_ref.shape)


def weight_grads(pair_t, right, tile, which):
    _, depth, rows = pair_t.shape
    count, _, columns = right.shape
    tiles = columns // tile
    block = depth // 32
    return pl.pallas_call(
        grads_kernel,
        grid=(count, tiles, 2),
        in_specs=[
            pl.BlockSpec((1, depth // 2, rows), lambda i, j, zl: (which(i, j), zl, 0)),
            pl.BlockSpec((1, rows, tile), lambda i, j, zl: (i, 0, j)),
        ],
        out_specs=pl.BlockSpec((16, 1, block, tile), lambda i, j, zl: (0, zl, 0, i * tiles + j)),
        out_shape=like((16, 2, block, count * columns)),
        compiler_params=params(40),
        cost_estimate=cost(2 * depth * rows * count * columns, 2 * (pair_t.size + right.size * 2)),
        name="weight_grads",
    )(pair_t, right)


def head_grads_kernel(coords, left_ref, right_ref, *refs):
    outs, product_ref = refs[:-1], refs[-1]
    zl, j = pl.program_id(0), pl.program_id(1)
    x, y = coords[1], coords[2]
    block, tile = product_ref.shape[1:]
    product = jnp.dot(left_ref[0], right_ref[...], preferred_element_type=F32).astype(BF16)
    product_ref[...] = product.reshape(product_ref.shape)
    for side in range(2):

        @pl.when(j // 2 == side)
        def _(side=side):
            lanes = pl.ds(pl.multiple_of((j % 2) * tile, tile), tile)
            for second in range(4):
                for first in range(4):
                    if side == 0:
                        chip = (x ^ first) * 4 + (y ^ second)
                    else:
                        chip = (x ^ second) * 4 + (y ^ first)
                    if second == 2:
                        out, i = outs[5 * side + 3 + first // 2], first % 2
                    else:
                        out, i = outs[5 * side + (0, 1, None, 2)[second]], first
                    out[i, zl, :, lanes] = product_ref[chip]


def head_grads(coords, pair_t, right):
    _, depth, rows = pair_t.shape
    columns = right.shape[1]
    tile, block = columns // 4, depth // 32
    full, half = like((4, 2, block, 2 * tile)), like((2, 2, block, 2 * tile))
    outs = pl.pallas_call(
        head_grads_kernel,
        grid=(2, 4),
        in_specs=[
            SCALARS,
            pl.BlockSpec((1, depth // 2, rows), lambda zl, j: (j // 3, zl, 0)),
            pl.BlockSpec((rows, tile), lambda zl, j: (0, j)),
        ],
        out_specs=[WHOLE] * 10,
        out_shape=[full, full, full, half, half] * 2,
        scratch_shapes=[pltpu.VMEM((16, block, tile), BF16)],
        compiler_params=params(32),
        cost_estimate=cost(2 * depth * rows * columns, 16 * MIB),
        name="head_grads",
    )(coords, pair_t, right)
    return outs[:5], outs[5:]


def bump_kernel(chunk_ref, part_ref, out_ref):
    out_ref[...] = (chunk_ref[...].astype(F32) + part_ref[...].astype(F32)).astype(BF16)


def bump(chunk, part, half):
    spec = pl.BlockSpec(part.shape, lambda i: (half, 0, 0, 0))
    return pl.pallas_call(
        bump_kernel,
        grid=(1,),
        in_specs=[spec, pl.BlockSpec(part.shape, lambda i: (0, 0, 0, 0))],
        out_specs=spec,
        out_shape=like(chunk.shape),
        input_output_aliases={0: 0},
        compiler_params=params(16),
        name="bump",
    )(chunk, part)


def near_kernel(own_ref, one_ref, three_ref, keep_ref, *sends):
    for i in range(4):
        total = own_ref[i].astype(F32) + (one_ref[i].astype(F32) + three_ref[i].astype(F32))
        if i == 0:
            keep_ref[...] = total
        else:
            sends[i - 1][...] = total.astype(BF16)


def scatter_blocks(chunks, first, second):
    own, one, three, two_low, two_high = chunks
    low, high = hop(two_low, second, 1), hop(two_high, second, 3)
    three = hop(bump(three, low, 0), second, 3)
    one = hop(bump(one, high, 1), second, 1)
    shape = own.shape[1:]
    keep, *sends = pl.pallas_call(
        near_kernel,
        in_specs=[WHOLE] * 3,
        out_specs=[WHOLE] * 4,
        out_shape=[like(shape, F32)] + [like(shape)] * 3,
        compiler_params=params(16),
        name="near",
    )(own, one, three)
    return [keep] + [hop(send, first, bits) for send, bits in zip(sends, (1, 2, 3))]


def cut_heads_kernel(coords, *refs):
    parts, outs = refs[:8], refs[8:]
    rows = outs[0].shape[0]
    half = outs[0].shape[1] // 2
    for bits in range(4):
        zl, c = coords[0] ^ (bits >> 1), coords[3] ^ (bits & 1)
        some = pl.ds(pl.multiple_of(c * rows, rows), rows)
        for side in range(2):
            keep, *others = parts[4 * side : 4 * side + 4]
            total = keep[zl, some, :]
            for other in others:
                total = total + other[zl, some, :].astype(F32)
            outs[bits][:, side * half : (side + 1) * half] = total.astype(BF16)


def cut_heads(coords, left, right, rows):
    return pl.pallas_call(
        cut_heads_kernel,
        in_specs=[SCALARS] + [WHOLE] * 8,
        out_specs=[WHOLE] * 4,
        out_shape=[like((rows, 2 * left[0].shape[2]))] * 4,
        compiler_params=params(16),
        name="cut_heads",
    )(coords, *left, *right)


def combine_kernel(products, *refs):
    mine_ref, theirs_ref = refs[2 * products : 2 * products + 2] if len(refs) == 2 * products + 2 else refs[-3:-1]
    contract = (((1,), (1,)), ((), ()))
    total = None
    for i in range(products):
        left, right = refs[2 * i], refs[2 * i + 1]
        left = left[0] if len(left.shape) == 3 else left[...]
        product = lax.dot_general(left, right[...], contract, preferred_element_type=F32)
        total = product if total is None else total + product
    half = mine_ref.shape[0]
    mine_ref[...] = total[:half].astype(BF16)
    theirs_ref[...] = total[half:].astype(BF16)
    if len(refs) > 2 * products + 2:
        rows_ref, sums_ref = refs[2 * products], refs[-1]
        sums_ref[0:1, :] = jnp.sum(total, axis=0, keepdims=True)
        sums_ref[1:2, :] = jnp.sum(total * rows_ref[0].astype(F32), axis=0, keepdims=True)


def combine(hidden_pair, side, mlp_w, right, head_parts, pair=None):
    _, rows, hidden = hidden_pair.shape
    depth = mlp_w.shape[0]
    tile = 256
    column = lambda i: (0, i)
    specs = [
        pl.BlockSpec((1, rows, hidden), lambda i: (side, 0, 0)),
        pl.BlockSpec((tile, hidden), lambda i: (i, 0)),
    ]
    arrays = [hidden_pair, mlp_w]
    total = hidden
    for start, weights, weights_start, columns in head_parts:
        left, where = start // columns, weights_start // columns
        specs.append(pl.BlockSpec((rows, columns), lambda i, left=left: (0, left)))
        specs.append(pl.BlockSpec((tile, columns), lambda i, where=where: (i, where)))
        arrays += [right, weights]
        total += columns
    out_specs = [pl.BlockSpec((rows // 2, tile), column)] * 2
    shapes = [like((rows // 2, depth))] * 2
    if pair is not None:
        specs.append(pl.BlockSpec((1, rows, tile), lambda i: (0, 0, i)))
        arrays.append(pair)
        out_specs.append(pl.BlockSpec((2, tile), column))
        shapes.append(like((2, depth), F32))
    return pl.pallas_call(
        functools.partial(combine_kernel, 1 + len(head_parts)),
        grid=(depth // tile,),
        in_specs=specs,
        out_specs=out_specs,
        out_shape=shapes,
        compiler_params=params(32),
        cost_estimate=cost(2 * rows * depth * total, 16 * MIB),
        name="combine",
    )(*arrays)


def project_kernel(pair_ref, bias_ref, first_ref, second_ref, linear_ref, grad_ref):
    step = pl.program_id(0)

    @pl.when(step < 2)
    def _():
        linear_ref[...] = jnp.dot(pair_ref[0], first_ref[...], preferred_element_type=F32) + bias_ref[...]

    @pl.when(step == 2)
    def _():
        linear_ref[...] = jnp.dot(pair_ref[0], second_ref[...], preferred_element_type=F32) + bias_ref[...]

    @pl.when(step == 3)
    def _():
        grad_ref[...] = jnp.dot(pair_ref[0], second_ref[...], preferred_element_type=F32).astype(BF16)


def project(pair, bias, first_w, second_w):
    rows, depth = pair.shape[1:]
    width = first_w.shape[1] // 2
    return pl.pallas_call(
        project_kernel,
        grid=(4,),
        in_specs=[
            pl.BlockSpec((1, rows, depth), lambda j: (j // 3, 0, 0)),
            pl.BlockSpec((1, width), lambda j: (0, jnp.minimum(j, 2))),
            pl.BlockSpec((depth, width), lambda j: (0, jnp.minimum(j, 1))),
            pl.BlockSpec((depth, width), lambda j: (0, jnp.maximum(j - 2, 0))),
        ],
        out_specs=[
            pl.BlockSpec((rows, width), lambda j: (0, jnp.minimum(j, 2))),
            pl.BlockSpec((rows, width), lambda j: (0, 0)),
        ],
        out_shape=[like((rows, 3 * width), F32), like((rows, width))],
        compiler_params=params(32),
        cost_estimate=cost(8 * rows * depth * width, 16 * MIB),
        name="project",
    )(pair, bias.reshape(1, -1), first_w, second_w)


def cut_kernel(coords, whole_ref, *outs):
    for bits in range(4):
        outs[bits][...] = whole_ref[slot_of(coords, bits)]


def cut(coords, whole):
    return pl.pallas_call(
        cut_kernel,
        in_specs=[SCALARS, WHOLE],
        out_specs=[WHOLE] * 4,
        out_shape=[like(whole.shape[1:])] * 4,
        compiler_params=params(16),
        name="cut",
    )(coords, whole)


def exchange(parts):
    return [parts[0], flip(parts[1], "c"), flip(parts[2], "zl"), flip(parts[3], "zl", "c")]


def unpack_mlp_kernel(coords, *refs):
    parts, (up_ref, down_ref) = refs[:4], refs[4:]
    hidden = up_ref.shape[1] // 4
    for bits in range(4):
        lanes = pl.ds(pl.multiple_of(slot_of(coords, bits) * hidden, hidden), hidden)
        up_ref[:, lanes] = parts[bits][:, :hidden].astype(F32)
        down_ref[:, lanes] = parts[bits][:, hidden:].astype(F32)


def unpack_heads_kernel(coords, *refs):
    parts, (qkv_ref, out_ref) = refs[:4], refs[4:]
    width = out_ref.shape[1] // 4
    for bits in range(4):
        lanes = pl.ds(pl.multiple_of(slot_of(coords, bits) * width, width), width)
        for kind in range(3):
            qkv_ref[kind, :, lanes] = parts[bits][:, kind * width : (kind + 1) * width].astype(F32)
        out_ref[:, lanes] = parts[bits][:, 3 * width :].astype(F32)


def unpack(coords, kernel, parts, shapes, name):
    return pl.pallas_call(
        kernel,
        in_specs=[SCALARS] + [WHOLE] * 4,
        out_specs=[WHOLE] * 2,
        out_shape=[like(shape, F32) for shape in shapes],
        compiler_params=params(16),
        name=name,
    )(coords, *parts)


def scatter_plane(grads):
    return lax.psum_scatter(grads.reshape(-1, grads.shape[3]), PLANE, scatter_dimension=0, tiled=True)


def per_device(
    tokens,
    layernorm_gain,
    layernorm_bias,
    w_qkv,
    b_qkv,
    w_out,
    b_out,
    w_up,
    b_up,
    w_down,
    b_down,
    segments,
    cotangent,
):
    depth = tokens.shape[1]
    length = segments.shape[0]
    half_rows = tokens.shape[0]
    width = w_out.shape[0] // 4
    hidden = w_down.shape[0] // 4
    rows = w_up.shape[0]
    coords = jnp.stack([lax.axis_index(axis) for axis in AXES]).astype(jnp.int32)
    place_here = coords[0] * 2 + coords[3]
    this_half = coords[4]

    parts = exchange(pack(coords, w_up, w_down.T, w_qkv.transpose(1, 0, 2), w_out.T, segments))
    up_shard, down_shard, first_shard, second_shard = order(
        coords, parts, (hidden, hidden, 2 * width, 2 * width)
    )

    inputs_f = tokens.astype(F32)
    row_mean = jnp.mean(inputs_f, axis=-1, keepdims=True)
    mean_removed = inputs_f - row_mean
    variance = jnp.mean(mean_removed * mean_removed, axis=-1, keepdims=True)
    inverse_deviation = lax.rsqrt(variance + EPSILON)
    standardized_input = mean_removed * inverse_deviation
    normalized_rows = (standardized_input * layernorm_gain + layernorm_bias).astype(BF16)

    pair = jnp.stack([normalized_rows, cotangent])
    up_shard, down_shard, pair = lax.optimization_barrier((up_shard, down_shard, pair))
    near, far = flip(pair, "zl"), flip(pair, "zl", "mp")
    up_row = gather_line(up_shard, "x")
    down_row = gather_line(down_shard, "y")
    up_row, down_row, pair = lax.optimization_barrier((up_row, down_row, pair))
    opposite = flip(pair, "mp")
    up_sides, down_sides = gather_sides(up_row, "y"), gather_sides(down_row, "x")
    up_sides, down_sides, opposite, near, far, first_shard, second_shard = lax.optimization_barrier(
        (up_sides, down_sides, opposite, near, far, first_shard, second_shard)
    )
    up_w = gather_plane(coords, up_row, up_sides, "y")
    down_w = gather_plane(coords, down_row, down_sides, "x")
    first_row = gather_line(first_shard, "x")
    second_row = gather_line(second_shard, "y")
    up_w, down_w, first_row, second_row = lax.optimization_barrier((up_w, down_w, first_row, second_row))
    first_sides, second_sides = gather_sides(first_row, "y"), gather_sides(second_row, "x")
    pair, pair_t = gather_tokens(pair, opposite, near, far)

    doc = jnp.stack([parts[k][0, -length:] for k in (0, 2, 1, 3)]).astype(jnp.int32)
    doc = doc.reshape(4, 2, half_rows)
    doc = jnp.where(this_half == 0, doc, doc[:, ::-1]).reshape(4, length)
    halves = jnp.stack([this_half, 1 - this_half]) * half_rows
    index = (halves[:, None] + jnp.arange(half_rows, dtype=jnp.int32)).reshape(1, length)
    index = jnp.broadcast_to(index, (4, length)).astype(jnp.int32)
    same_doc = doc[:, :, None] == doc[:, None, :]
    doc_start = jnp.min(jnp.where(same_doc, index[:, None, :], length), axis=2)
    positions = (index - doc_start).astype(F32).reshape(-1)
    inv_freq = 10000.0 ** (-(jnp.arange(HALF, dtype=F32) * 2.0 / ROT))
    angles = positions[:, None] * inv_freq
    cos, sin = jnp.cos(angles), jnp.sin(angles)
    nothing = jnp.zeros_like(cos)
    rest = (positions.shape[0], HEAD_DIM - ROT)
    repeat = LANES // HEAD_DIM
    cos_table = jnp.tile(jnp.concatenate([cos, cos, jnp.ones(rest, F32)], axis=1), (1, repeat))
    low_table = jnp.tile(jnp.concatenate([-sin, nothing, jnp.zeros(rest, F32)], axis=1), (1, repeat))
    high_table = jnp.tile(jnp.concatenate([nothing, sin, jnp.zeros(rest, F32)], axis=1), (1, repeat))

    b_up_here = lax.dynamic_slice_in_dim(b_up, place_here * hidden, hidden)
    b_qkv_here = lax.dynamic_slice_in_dim(b_qkv, place_here * width, width, axis=1).reshape(-1)

    hidden_pair, grad_b_up = mlp(pair, b_up_here, up_w, down_w)
    mlp_grads = scatter_plane(weight_grads(pair_t, hidden_pair, hidden // 2, lambda i, j: i))

    first_sides, second_sides, pair, hidden_pair = lax.optimization_barrier(
        (first_sides, second_sides, pair, hidden_pair)
    )
    first_w = gather_plane(coords, first_row, first_sides, "y")
    second_w = gather_plane(coords, second_row, second_sides, "x")
    linear, grad_attended = project(pair, b_qkv_here, first_w, second_w)
    right = attention(
        linear, grad_attended, (cos_table, low_table, high_table), doc, index, length
    )
    first_grads, second_grads = head_grads(coords, pair_t, right)
    first_grads, second_grads, hidden_pair = lax.optimization_barrier(
        (first_grads, second_grads, hidden_pair)
    )
    first_grads = scatter_blocks(first_grads, "x", "y")
    second_grads = scatter_blocks(second_grads, "y", "x")

    inner = [(0, first_w, 0, 2 * width), (2 * width, second_w, 0, width)]
    mine, theirs, sums = combine(hidden_pair, 0, up_w, right, inner, pair)
    normalized_gradient = scatter_group(mine, theirs)
    outer = [(3 * width, second_w, width, width)]
    branches = scatter_group(*combine(hidden_pair, 1, down_w, right, outer))
    mixed = (inputs_f + branches + b_out + b_down).astype(BF16)
    standardized_gradient = normalized_gradient * layernorm_gain
    grad_inputs = inverse_deviation * (
        standardized_gradient
        - jnp.mean(standardized_gradient, axis=-1, keepdims=True)
        - standardized_input
        * jnp.mean(standardized_gradient * standardized_input, axis=-1, keepdims=True)
    )
    cot_rows = cotangent.astype(F32)
    d_tokens = cot_rows + grad_inputs

    grad_b_heads = jnp.sum(right[:, : 3 * width].astype(F32), axis=0)
    slices = jnp.concatenate([grad_b_heads, grad_b_up[0]])
    slot = this_half * 4 + place_here
    spread = jnp.zeros((8,) + slices.shape, F32)
    spread = lax.dynamic_update_slice(spread, slices[None], (slot, 0))
    vector = jnp.concatenate([spread.reshape(-1), jnp.sum(cot_rows, axis=0), sums.reshape(-1)])
    vector = sum_everywhere(vector.reshape(-1, LANES)).reshape(-1)
    spread, whole = vector[: spread.size].reshape(8, -1), vector[spread.size :].reshape(3, depth)
    spread = lax.dynamic_slice_in_dim(spread, this_half * 4, 4)
    grad_b_qkv = spread[:, : 3 * width].reshape(4, 3, width).transpose(1, 0, 2).reshape(3, 4 * width)
    grad_b_up = spread[:, 3 * width :].reshape(-1)
    grad_gain = (whole[2] - layernorm_bias * whole[1]) / layernorm_gain

    mlp_parts = exchange(cut(coords, mlp_grads.reshape(4, rows, 2 * hidden)))
    grad_up_w, grad_down_w = unpack(
        coords, unpack_mlp_kernel, mlp_parts, [w_up.shape, w_up.shape], "unpack_mlp"
    )
    head_parts = exchange(cut_heads(coords, first_grads, second_grads, rows))
    shapes = [(3, rows, 4 * width), (rows, 4 * width)]
    grad_qkv_w, grad_out_w = unpack(coords, unpack_heads_kernel, head_parts, shapes, "unpack_heads")
    return (
        mixed,
        d_tokens,
        grad_gain,
        whole[1],
        grad_qkv_w.transpose(1, 0, 2),
        grad_b_qkv,
        grad_out_w.T,
        whole[0],
        grad_up_w,
        grad_b_up,
        grad_down_w.T,
        whole[0],
    )


def solution(mesh):
    fine = Mesh(mesh.devices.reshape(SIZES), AXES)
    dp = ("zl", "x", "y", "c")
    in_specs = (
        P(AXES, None),
        P(),
        P(),
        P(dp, None, "mp"),
        P(None, "mp"),
        P("mp", dp),
        P(),
        P(dp, "mp"),
        P("mp"),
        P("mp", dp),
        P(),
        P(dp),
        P(AXES, None),
    )
    out_specs = (
        P(AXES, None),
        P(AXES, None),
        P(),
        P(),
        P(dp, None, "mp"),
        P(None, "mp"),
        P("mp", dp),
        P(),
        P(dp, "mp"),
        P("mp"),
        P("mp", dp),
        P(),
    )
    return jax.shard_map(
        per_device, mesh=fine, in_specs=in_specs, out_specs=out_specs, check_vma=False
    )
```

time: 420 us -> 418 us (level); the launches traced: 416 us -> 410 us
  waiting for transfers between devices: 159 us -> 107 us
  starting transfers between devices: 65.8 us -> 102 us
  Pallas kernels: 94.3 us -> 124 us
  matrix products: 24 us -> 0 us
  local copies, waits for them, and re-layouts: 42.2 us -> 49.3 us
  other arithmetic: 16.2 us -> 11.9 us
    ppermute x29 -> x25, waiting for transfers between devices: 97 us -> 37.5 us  [flip(): return lax.ppermute(value, axes, [(i, count - 1 - i) for i in range(count)])]
    pallas_call x1 -> x25, Pallas kernels: 22.6 us -> 65.6 us  [the longest x2 19.5 us: combine(): pl.pallas_call(functools.partial(combine_kernel, 1 + len(head_parts)), gr...]
    dot_general x4 -> x0, matrix products: 24 us -> none  [the longest x1 7.7 us: per_device(): jnp.einsum('te,de->td', grad_linear, qkv_w, preferred_element_type=F32)]
    ppermute x20 -> x48, starting transfers between devices: 29.3 us -> 51.1 us  [hop(): return lax.ppermute(value, axis, [(i, i ^ bits) for i in range(4)])]
    ppermute x29 -> x25, starting transfers between devices: 36.4 us -> 50.6 us  [flip(): return lax.ppermute(value, axes, [(i, count - 1 - i) for i in range(count)])]
    pallas_call x2 -> x1, Pallas kernels: 24.1 us -> 14.8 us  [weight_grads(): pl.pallas_call(grads_kernel, grid=(count, tiles, 2), in_specs=[pl.BlockSp...]
    ppermute x20 -> x48, waiting for transfers between devices: 61.5 us -> 69.4 us  [hop(): return lax.ppermute(value, axis, [(i, i ^ bits) for i in range(4)])]
    convert_element_type x3 -> x1, other arithmetic: 7.68 us -> 0.01 us  [per_device(): jnp.stack([parts[k][0, -length:] for k in (0, 2, 1, 3)]).astype(jnp.int32)]
  transfers between devices with their start and end apart: 52 -> 74, of which waited for: 34 -> 30; matrix products, arithmetic and copies ran while one was open for 14% -> 9% of each run, Pallas kernels for 13% -> 19%
where the time goes in v1:
time: 418 us; the launch traced here: 410 us
  Pallas kernels  124 us (30%)
  waiting for transfers between devices  107 us (26%)
  starting transfers between devices  102 us (24%)
  local copies, waits for them, and re-layouts  49.3 us (12%)
  between operations  15.6 us (4%)
  other arithmetic  11.9 us (3%)
    ppermute x48, waiting for transfers between devices, hop(): return lax.ppermute(value, axis, [(i, i ^ bits) for i in range(4)])  69.4 us
    ppermute x48, starting transfers between devices, hop(): return lax.ppermute(value, axis, [(i, i ^ bits) for i in range(4)])  51.1 us
    ppermute x25, starting transfers between devices, flip(): return lax.ppermute(value, axes, [(i, count - 1 - i) for i in range(count)])  50.6 us
    ppermute x25, waiting for transfers between devices, flip(): return lax.ppermute(value, axes, [(i, count - 1 - i) for i in range(count)])  37.5 us
    unnamed x169, local copies, waits for them, and re-layouts  28.1 us
    pallas_call x2, Pallas kernels, combine(): pl.pallas_call(functools.partial(combine_kernel, 1 + len(head_parts)), gr...  19.5 us
    pallas_call x1, Pallas kernels, attention(): pl.pallas_call(attention_kernel, grid=(count,), in_specs=[blocks(3 * widt...  15.7 us
    pallas_call x1, Pallas kernels, weight_grads(): pl.pallas_call(grads_kernel, grid=(count, tiles, 2), in_specs=[pl.BlockSp...  14.8 us
  transfers between devices with their start and end apart: 74, of which 30 were waited for; matrix products, arithmetic and copies ran while one was open for 9% of the time, Pallas kernels for 19%

profile of v1, /device:TPU:1, one launch (start us, length us, event | category | flops | bytes accessed | tf_op | source)
XLA Modules:
  0.0 409.7 jit_solution(3644801688938233551)
XLA Ops:
  21.0 4.6 %collective-permute-done.2.refs_3_ = bf16[32,3328]{1,0:T(8,128)(2,1)S(1)} collective-permute-done((bf16[32,3328]{1,0:T(8,128)(2,1)S(1)}, bf16[32,3328]{1,0:T(8,128)(2,1)S(1)}, u32[]{:S(2)}, u32[]{:S(2)}) %collective-permute-start.2) | collective-permute-done | bytes 213024 | tf_op jit(solution)/shard_map/ppermute | solution.py:29
  34.0 3.1 collective-permute-done.6.refs_1_
  38.3 6.9 %collective-permute-done.7.refs_2_ = bf16[2,64,1024]{2,1,0:T(8,128)(2,1)S(1)} collective-permute-done((bf16[2,64,1024]{2,1,0:T(8,128)(2,1)S(1)}, bf16[2,64,1024]{2,1,0:T(8,128)(2,1)S(1)}, u32[]{:S(2)}, u32[]{:S(2)}) %collective-permute-start.7) | collective-permute-done | bytes 262176 | tf_op jit(solution)/shard_map/ppermute | solution.py:33
  52.8 7.8 %collective-permute-done.5.refs_3_ = bf16[2,64,1024]{2,1,0:T(8,128)(2,1)S(1)} collective-permute-done((bf16[2,64,1024]{2,1,0:T(8,128)(2,1)S(1)}, bf16[2,64,1024]{2,1,0:T(8,128)(2,1)S(1)}, u32[]{:S(2)}, u32[]{:S(2)}) %collective-permute-start.5) | collective-permute-done | bytes 262176 | tf_op jit(solution)/shard_map/ppermute | solution.py:33
  65.2 23.4 %collective-permute-done.10.refs_2_ = bf16[4,2,64,1024]{3,2,1,0:T(8,128)(2,1)S(1)} collective-permute-done((bf16[4,2,64,1024]{3,2,1,0:T(8,128)(2,1)S(1)}, bf16[4,2,64,1024]{3,2,1,0:T(8,128)(2,1)S(1)}, u32[]{:S(2)}, u32[]{:S(2)}) %collective-permute-start.10) | collective-permute-done | bytes 1048608 | tf_op jit(solution)/shard_map/ppermute | solution.py:33
  127.4 14.0 %tokens.1 = (bf16[2,1024,2048]{2,1,0:T(8,128)(2,1)S(1)}, bf16[2,2048,1024]{2,1,0:T(8,128)(2,1)}) custom-call(bf16[4,2,128,2048]{3,2,1,0:T(8,128)(2,1)} %join.7.mine_ref, bf16[4,2,128,2048]{3,2,1,0:T(8,128)(2,1)} %collective-permute-done.16.other_ref), custom_call_target="tpu_custom_call" | custom-call | bytes 33554432 | tf_op jit(solution)/shard_map/tokens/pallas_call | solution.py:341
  141.5 13.3 %mlp.1 = (bf16[2,1024,1024]{2,1,0:T(8,128)(2,1)S(1)}, f32[1,1024]{1,0:T(1,128)S(1)}) custom-call(bf16[2,1024,2048]{2,1,0:T(8,128)(2,1)S(1)} %get-tuple-element.135.pair_ref.refs_6_, f32[1,1024]{1,0:T(1,128)S(1)} %bitcast.119, bf16[2048,1024]{1,0:T(8,128)(2,1)S(1)} %bitcast.85, bf16[2048,1024]{1,0:T(8,128)(2,1)S(1)} %bitcast.87), custom_call_target="tpu_custom_call" | custom-call | flops 8589934592 | bytes 20971520 | tf_op jit(solution)/shard_map/mlp/pallas_call | solution.py:378
  154.8 14.8 %weight_grads.1 = bf16[16,2,64,2048]{3,2,1,0:T(8,128)(2,1)S(1)} custom-call(bf16[2,2048,1024]{2,1,0:T(8,128)(2,1)} %get-tuple-element.122.left_ref, bf16[2,1024,1024]{2,1,0:T(8,128)(2,1)S(1)} %get-tuple-element.153.refs_0_.right_ref), custom_call_target="tpu_custom_call" | custom-call | flops 8589934592 | bytes 16777216 | tf_op jit(solution)/shard_map/weight_grads/pallas_call | solution.py:408
  169.6 3.4 copy-done.6
  178.7 11.5 %collective-permute-done.27.refs_1_ = bf16[4,2,64,512]{3,2,1,0:T(8,128)(2,1)S(1)} collective-permute-done((bf16[4,2,64,512]{3,2,1,0:T(8,128)(2,1)S(1)}, bf16[4,2,64,512]{3,2,1,0:T(8,128)(2,1)S(1)}, u32[]{:S(2)}, u32[]{:S(2)}) %collective-permute-start.27) | collective-permute-done | bytes 524320 | tf_op jit(solution)/shard_map/ppermute | solution.py:33
  223.0 5.7 %project.1 = (f32[1024,768]{1,0:T(8,128)S(1)}, bf16[1024,256]{1,0:T(8,128)(2,1)S(1)}) custom-call(bf16[2,1024,2048]{2,1,0:T(8,128)(2,1)S(1)} %bitcast.124, f32[1,768]{1,0:T(1,128)S(1)} %bitcast.121, bf16[2048,512]{1,0:T(8,128)(2,1)S(1)} %bitcast.89, bf16[2048,512]{1,0:T(8,128)(2,1)S(1)} %bitcast.91), custom_call_target="tpu_custom_call" | custom-call | flops 4294967296 | bytes 16777216 | tf_op jit(solution)/shard_map/project/pallas_call | solution.py:614
  228.8 15.7 %attention.1.right_ref.refs_2_.refs_4_ = bf16[1024,1024]{1,0:T(8,128)(2,1)S(1)} custom-call(f32[1024,768]{1,0:T(8,128)S(1)} %get-tuple-element.140.linear_ref, bf16[1024,256]{1,0:T(8,128)(2,1)S(1)} %get-tuple-element.141.grad_ref, f32[1024,128]{1,0:T(8,128)S(1)} %copy-done.26, f32[1024,128]{1,0:T(8,128)S(1)} %copy-done.27, f32[1024,128]{1,0:T(8,128)S(1)} %copy-done.28, ...), custom_call_target="tpu_custom_call" | custom-call | flops 18874368000 | bytes 8388608 | tf_op jit(solution)/shard_map/attention/pallas_call | solution.py:142
  244.5 8.2 %head_grads.1 = (bf16[4,2,64,512]{3,2,1,0:T(8,128)(2,1)S(1)}, bf16[4,2,64,512]{3,2,1,0:T(8,128)(2,1)S(1)}, bf16[4,2,64,512]{3,2,1,0:T(8,128)(2,1)S(1)}, bf16[2,2...) custom-call(s32[5]{0:T(128)S(1)} %stack.49.coords, ...), custom_call_target="tpu_custom_call" | custom-call | flops 4294967296 | bytes 16777216 | tf_op jit(solution)/shard_map/head_grads/pallas_call | solution.py:453
  261.2 11.3 %combine.3 = (bf16[512,2048]{1,0:T(8,128)(2,1)S(1)}, bf16[512,2048]{1,0:T(8,128)(2,1)S(1)}, f32[2,2048]{1,0:T(2,128)S(1)}) custom-call(bf16[2,1024,1024]{2,1,0:T(8,128)(2,1)S(1)} %copy-done.64, bf16[2048,1024]{1,0:T(8,128)(2,1)S(1)} %bitcast.86, bf16[1024,1024]{1,0:T(8,128)(2,1)S(1)} %attention.1.right_ref.refs_2_.refs_4_, bf16[2048,512]{1,0:T(8,128)(2,1)S(1)} %bitcast.90, ...), custom_call_target="tpu_custom_call" | custom-call | flops 7516192768 | bytes 16777216 | tf_op jit(solution)/shard_map/combine/pallas_call | solution.py:583
  272.5 11.5 %collective-permute-start.39 = (bf16[512,2048]{1,0:T(8,128)(2,1)S(1)}, bf16[512,2048]{1,0:T(8,128)(2,1)S(1)}, u32[]{:S(2)}, u32[]{:S(2)}) collective-permute-start(bf16[512,2048]{1,0:T(8,128)(2,1)S(1)} %get-tuple-element.161), channel_id=1, source_target_pairs={{0,2},{2,0},{1,3},{3,1},{4,6},{6,4},{5,7},{7,5},{8,10},{10,8},{9,1... | collective-permute-start | bytes 6291464 | tf_op jit(solution)/shard_map/ppermute | solution.py:29
  284.0 8.2 %combine.2 = (bf16[512,2048]{1,0:T(8,128)(2,1)S(1)}, bf16[512,2048]{1,0:T(8,128)(2,1)}) custom-call(bf16[2,1024,1024]{2,1,0:T(8,128)(2,1)S(1)} %copy-done.65, bf16[2048,1024]{1,0:T(8,128)(2,1)S(1)} %bitcast.88, bf16[1024,1024]{1,0:T(8,128)(2,1)S(1)} %attention.1.right_ref.refs_2_.refs_4_, bf16[2048,512]{1,0:T(8,128)(2,1)S(1)} %bitcast.93), custom_call_target="tpu_custom_call" | custom-call | flops 5368709120 | bytes 16777216 | tf_op jit(solution)/shard_map/combine/pallas_call | solution.py:583
  319.4 2.9 collective-permute-done.41
  322.9 3.5 collective-permute-done.42
  330.1 4.2 %collective-permute-done.36 = bf16[128,2048]{1,0:T(8,128)(2,1)S(1)} collective-permute-done((bf16[128,2048]{1,0:T(8,128)(2,1)S(1)}, bf16[128,2048]{1,0:T(8,128)(2,1)S(1)}, u32[]{:S(2)}, u32[]{:S(2)}) %collective-permute-start.36) | collective-permute-done | bytes 524320 | tf_op jit(solution)/shard_map/ppermute | solution.py:29
  334.2 10.5 %collective-permute-done.37 = bf16[128,2048]{1,0:T(8,128)(2,1)S(1)} collective-permute-done((bf16[128,2048]{1,0:T(8,128)(2,1)S(1)}, bf16[128,2048]{1,0:T(8,128)(2,1)S(1)}, u32[]{:S(2)}, u32[]{:S(2)}) %collective-permute-start.37) | collective-permute-done | bytes 524320 | tf_op jit(solution)/shard_map/ppermute | solution.py:29
  368.0 8.2 %collective-permute-start.67 = (bf16[32,1024]{1,0:T(8,128)(2,1)S(1)}, bf16[32,1024]{1,0:T(8,128)(2,1)S(1)}, u32[]{:S(2)}, u32[]{:S(2)}) collective-permute-start(bf16[32,1024]{1,0:T(8,128)(2,1)S(1)} %get-tuple-element.187), channel_id=1, source_target_pairs={{0,2},{2,0},{1,3},{3,1},{4,6},{6,4},{5,7},{7,5},{8,10},{10,8},{9,1... | collective-permute-start | bytes 196616 | tf_op jit(solution)/shard_map/ppermute | solution.py:29
  379.9 4.4 %collective-permute-start.69 = (bf16[32,1024]{1,0:T(8,128)(2,1)S(1)}, bf16[32,1024]{1,0:T(8,128)(2,1)S(1)}, u32[]{:S(2)}, u32[]{:S(2)}) collective-permute-start(bf16[32,1024]{1,0:T(8,128)(2,1)S(1)} %get-tuple-element.189), channel_id=1, source_target_pairs={{0,66},{2,64},{64,2},{66,0},{1,67},{3,65},{65,3},{67,1},{4,70},{6,... | collective-permute-start | bytes 196616 | tf_op jit(solution)/shard_map/ppermute | solution.py:29
  384.3 3.3 collective-permute-done.69.refs_3_
  396.9 3.4 collective-permute-done.72.refs_3_
  (399 shorter events, 190.4 us)
Async XLA Ops:
  7.2 383.2 %reduce-scatter.2.cloned.1.call-start = ((), (), s32[]{:S(2)}) async-start(), calls=%async_computation.1 | async-start | bytes 8912896 | tf_op jit(solution)/shard_map/reduce_scatter | solution.py:685
  26.3 37.5 %collective-permute-start.14 = (bf16[2,128,2048]{2,1,0:T(8,128)(2,1)S(1)}, bf16[2,128,2048]{2,1,0:T(8,128)(2,1)S(1)}, u32[]{:S(2)}, u32[]{:S(2)}) collective-permute-start(bf16[2,128,2048]{2,1,0:T(8,128)(2,1)S(1)} %pad_maximum_fusion.refs_0_), channel_id=1, source_target_pairs={{0,64},{64,0},{1,65},{65,1},{2,66},{66,2},{3,67},{67,3},{4,68},{68... | collective-permute-start | bytes 3145736 | tf_op jit(solution)/shard_map/ppermute | solution.py:29
  27.8 37.4 %collective-permute-start.15 = (bf16[2,128,2048]{2,1,0:T(8,128)(2,1)S(1)}, bf16[2,128,2048]{2,1,0:T(8,128)(2,1)S(1)}, u32[]{:S(2)}, u32[]{:S(2)}) collective-permute-start(bf16[2,128,2048]{2,1,0:T(8,128)(2,1)S(1)} %pad_maximum_fusion.refs_0_), channel_id=1, source_target_pairs={{0,65},{1,64},{64,1},{65,0},{2,67},{3,66},{66,3},{67,2},{4,69},{5,... | collective-permute-start | bytes 3145736 | tf_op jit(solution)/shard_map/ppermute | solution.py:29
  60.7 27.9 %collective-permute-start.11 = (bf16[4,2,64,1024]{3,2,1,0:T(8,128)(2,1)S(1)}, bf16[4,2,64,1024]{3,2,1,0:T(8,128)(2,1)S(1)}, u32[]{:S(2)}, u32[]{:S(2)}) collective-permute-start(bf16[4,2,64,1024]{3,2,1,0:T(8,128)(2,1)S(1)} %join.6.refs_0_), channel_id=1, source_target_pairs={{0,16},{16,0},{32,48},{48,32},{1,17},{17,1},{33,49},{49,33},{2,18}... | collective-permute-start | bytes 3145736 | tf_op jit(solution)/shard_map/ppermute | solution.py:33
  62.0 26.6 %collective-permute-start.12 = (bf16[4,2,64,1024]{3,2,1,0:T(8,128)(2,1)S(1)}, bf16[4,2,64,1024]{3,2,1,0:T(8,128)(2,1)S(1)}, u32[]{:S(2)}, u32[]{:S(2)}) collective-permute-start(bf16[4,2,64,1024]{3,2,1,0:T(8,128)(2,1)S(1)} %join.6.refs_0_), channel_id=1, source_target_pairs={{0,48},{16,32},{32,16},{48,0},{1,49},{17,33},{33,17},{49,1},{2,50}... | collective-permute-start | bytes 3145736 | tf_op jit(solution)/shard_map/ppermute | solution.py:33
  63.8 24.8 %collective-permute-start.10 = (bf16[4,2,64,1024]{3,2,1,0:T(8,128)(2,1)S(1)}, bf16[4,2,64,1024]{3,2,1,0:T(8,128)(2,1)S(1)}, u32[]{:S(2)}, u32[]{:S(2)}) collective-permute-start(bf16[4,2,64,1024]{3,2,1,0:T(8,128)(2,1)S(1)} %join.5.refs_0_), channel_id=1, source_target_pairs={{0,12},{4,8},{8,4},{12,0},{1,13},{5,9},{9,5},{13,1},{2,14},{6,10},... | collective-permute-start | bytes 3145736 | tf_op jit(solution)/shard_map/ppermute | solution.py:33
  63.8 24.9 %collective-permute-start.13 = (bf16[2,128,2048]{2,1,0:T(8,128)(2,1)S(1)}, bf16[2,128,2048]{2,1,0:T(8,128)(2,1)S(1)}, u32[]{:S(2)}, u32[]{:S(2)}) collective-permute-start(bf16[2,128,2048]{2,1,0:T(8,128)(2,1)S(1)} %pad_maximum_fusion.refs_0_), channel_id=1, source_target_pairs={{0,1},{1,0},{2,3},{3,2},{4,5},{5,4},{6,7},{7,6},{8,9},{9,8},{10,11... | collective-permute-start | bytes 3145736 | tf_op jit(solution)/shard_map/ppermute | solution.py:29
  65.2 23.5 %collective-permute-start.9 = (bf16[4,2,64,1024]{3,2,1,0:T(8,128)(2,1)S(1)}, bf16[4,2,64,1024]{3,2,1,0:T(8,128)(2,1)S(1)}, u32[]{:S(2)}, u32[]{:S(2)}) collective-permute-start(bf16[4,2,64,1024]{3,2,1,0:T(8,128)(2,1)S(1)} %join.5.refs_0_), channel_id=1, source_target_pairs={{0,4},{4,0},{8,12},{12,8},{1,5},{5,1},{9,13},{13,9},{2,6},{6,2},{1... | collective-permute-start | bytes 3145736 | tf_op jit(solution)/shard_map/ppermute | solution.py:33
  90.9 36.6 %collective-permute-start.16 = (bf16[4,2,128,2048]{3,2,1,0:T(8,128)(2,1)}, bf16[4,2,128,2048]{3,2,1,0:T(8,128)(2,1)}, u32[]{:S(2)}, u32[]{:S(2)}) collective-permute-start(bf16[4,2,128,2048]{3,2,1,0:T(8,128)(2,1)} %join.7.mine_ref), channel_id=1, source_target_pairs={{0,2},{2,0},{1,3},{3,1},{4,6},{6,4},{5,7},{7,5},{8,10},{10,8},{9,1... | collective-permute-start | bytes 12582920 | tf_op jit(solution)/shard_map/ppermute | solution.py:29
  177.1 16.5 %collective-permute-start.30 = (bf16[4,2,64,512]{3,2,1,0:T(8,128)(2,1)S(1)}, bf16[4,2,64,512]{3,2,1,0:T(8,128)(2,1)S(1)}, u32[]{:S(2)}, u32[]{:S(2)}) collective-permute-start(bf16[4,2,64,512]{3,2,1,0:T(8,128)(2,1)S(1)} %join.9.refs_0_), channel_id=1, source_target_pairs={{0,48},{16,32},{32,16},{48,0},{1,49},{17,33},{33,17},{49,1},{2,50}... | collective-permute-start | bytes 1572872 | tf_op jit(solution)/shard_map/ppermute | solution.py:33
  194.3 25.1 %collective-permute-start.33 = (bf16[2,2,64,512]{3,2,1,0:T(8,128)(2,1)}, bf16[2,2,64,512]{3,2,1,0:T(8,128)(2,1)}, u32[]{:S(2)}, u32[]{:S(2)}) collective-permute-start(bf16[2,2,64,512]{3,2,1,0:T(8,128)(2,1)} %slice.74), channel_id=1, source_target_pairs={{0,16},{16,0},{32,48},{48,32},{1,17},{17,1},{33,49},{49,33},{2,18}... | collective-permute-start | bytes 786440 | tf_op jit(solution)/shard_map/ppermute | solution.py:33
  195.1 24.4 %collective-permute-start.34 = (bf16[2,2,64,512]{3,2,1,0:T(8,128)(2,1)}, bf16[2,2,64,512]{3,2,1,0:T(8,128)(2,1)}, u32[]{:S(2)}, u32[]{:S(2)}) collective-permute-start(bf16[2,2,64,512]{3,2,1,0:T(8,128)(2,1)} %slice.75), channel_id=1, source_target_pairs={{0,48},{16,32},{32,16},{48,0},{1,49},{17,33},{33,17},{49,1},{2,50}... | collective-permute-start | bytes 786440 | tf_op jit(solution)/shard_map/ppermute | solution.py:33
  198.2 22.9 %collective-permute-start.31 = (bf16[2,2,64,512]{3,2,1,0:T(8,128)(2,1)}, bf16[2,2,64,512]{3,2,1,0:T(8,128)(2,1)S(1)}, u32[]{:S(2)}, u32[]{:S(2)}) collective-permute-start(bf16[2,2,64,512]{3,2,1,0:T(8,128)(2,1)} %slice.72), channel_id=1, source_target_pairs={{0,4},{4,0},{8,12},{12,8},{1,5},{5,1},{9,13},{13,9},{2,6},{6,2},{1... | collective-permute-start | bytes 786440 | tf_op jit(solution)/shard_map/ppermute | solution.py:33
  199.0 22.2 %collective-permute-start.32 = (bf16[2,2,64,512]{3,2,1,0:T(8,128)(2,1)}, bf16[2,2,64,512]{3,2,1,0:T(8,128)(2,1)}, u32[]{:S(2)}, u32[]{:S(2)}) collective-permute-start(bf16[2,2,64,512]{3,2,1,0:T(8,128)(2,1)} %slice.73), channel_id=1, source_target_pairs={{0,12},{4,8},{8,4},{12,0},{1,13},{5,9},{9,5},{13,1},{2,14},{6,10},... | collective-permute-start | bytes 786440 | tf_op jit(solution)/shard_map/ppermute | solution.py:33
  272.5 22.9 %collective-permute-start.39 = (bf16[512,2048]{1,0:T(8,128)(2,1)S(1)}, bf16[512,2048]{1,0:T(8,128)(2,1)S(1)}, u32[]{:S(2)}, u32[]{:S(2)}) collective-permute-start(bf16[512,2048]{1,0:T(8,128)(2,1)S(1)} %get-tuple-element.161), channel_id=1, source_target_pairs={{0,2},{2,0},{1,3},{3,1},{4,6},{6,4},{5,7},{7,5},{8,10},{10,8},{9,1... | collective-permute-start | bytes 6291464 | tf_op jit(solution)/shard_map/ppermute | solution.py:29
  292.2 23.0 %collective-permute-start.35 = (bf16[512,2048]{1,0:T(8,128)(2,1)}, bf16[512,2048]{1,0:T(8,128)(2,1)}, u32[]{:S(2)}, u32[]{:S(2)}) collective-permute-start(bf16[512,2048]{1,0:T(8,128)(2,1)} %get-tuple-element.155), channel_id=1, source_target_pairs={{0,2},{2,0},{1,3},{3,1},{4,6},{6,4},{5,7},{7,5},{8,10},{10,8},{9,1... | collective-permute-start | bytes 6291464 | tf_op jit(solution)/shard_map/ppermute | solution.py:29
  297.6 20.5 %collective-permute-start.40 = (bf16[128,2048]{1,0:T(8,128)(2,1)}, bf16[128,2048]{1,0:T(8,128)(2,1)}, u32[]{:S(2)}, u32[]{:S(2)}) collective-permute-start(bf16[128,2048]{1,0:T(8,128)(2,1)} %get-tuple-element.163), channel_id=1, source_target_pairs={{0,1},{1,0},{2,3},{3,2},{4,5},{5,4},{6,7},{7,6},{8,9},{9,8},{10,11... | collective-permute-start | bytes 1572872 | tf_op jit(solution)/shard_map/ppermute | solution.py:29
  299.8 22.5 %collective-permute-start.41 = (bf16[128,2048]{1,0:T(8,128)(2,1)}, bf16[128,2048]{1,0:T(8,128)(2,1)}, u32[]{:S(2)}, u32[]{:S(2)}) collective-permute-start(bf16[128,2048]{1,0:T(8,128)(2,1)} %get-tuple-element.164), channel_id=1, source_target_pairs={{0,64},{64,0},{1,65},{65,1},{2,66},{66,2},{3,67},{67,3},{4,68},{68... | collective-permute-start | bytes 1572872 | tf_op jit(solution)/shard_map/ppermute | solution.py:29
  301.9 24.5 %collective-permute-start.42 = (bf16[128,2048]{1,0:T(8,128)(2,1)}, bf16[128,2048]{1,0:T(8,128)(2,1)}, u32[]{:S(2)}, u32[]{:S(2)}) collective-permute-start(bf16[128,2048]{1,0:T(8,128)(2,1)} %get-tuple-element.165), channel_id=1, source_target_pairs={{0,65},{1,64},{64,1},{65,0},{2,67},{3,66},{66,3},{67,2},{4,69},{5,... | collective-permute-start | bytes 1572872 | tf_op jit(solution)/shard_map/ppermute | solution.py:29
  311.6 39.1 %collective-permute-start.63 = (bf16[4,2,64,512]{3,2,1,0:T(8,128)(2,1)}, bf16[4,2,64,512]{3,2,1,0:T(8,128)(2,1)S(1)}, u32[]{:S(2)}, u32[]{:S(2)}) collective-permute-start(bf16[4,2,64,512]{3,2,1,0:T(8,128)(2,1)} %copy-done.25), channel_id=1, source_target_pairs={{0,48},{16,32},{32,16},{48,0},{1,49},{17,33},{33,17},{49,1},{2,50}... | collective-permute-start | bytes 1572872 | tf_op jit(solution)/shard_map/ppermute | solution.py:33
  315.2 35.6 %collective-permute-start.61 = (bf16[4,2,64,512]{3,2,1,0:T(8,128)(2,1)}, bf16[4,2,64,512]{3,2,1,0:T(8,128)(2,1)S(1)}, u32[]{:S(2)}, u32[]{:S(2)}) collective-permute-start(bf16[4,2,64,512]{3,2,1,0:T(8,128)(2,1)} %bump.6), channel_id=1, source_target_pairs={{0,16},{16,0},{32,48},{48,32},{1,17},{17,1},{33,49},{49,33},{2,18}... | collective-permute-start | bytes 1572872 | tf_op jit(solution)/shard_map/ppermute | solution.py:33
  322.3 22.4 %collective-permute-start.37 = (bf16[128,2048]{1,0:T(8,128)(2,1)S(1)}, bf16[128,2048]{1,0:T(8,128)(2,1)S(1)}, u32[]{:S(2)}, u32[]{:S(2)}) collective-permute-start(bf16[128,2048]{1,0:T(8,128)(2,1)S(1)} %get-tuple-element.158), channel_id=1, source_target_pairs={{0,64},{64,0},{1,65},{65,1},{2,66},{66,2},{3,67},{67,3},{4,68},{68... | collective-permute-start | bytes 1572872 | tf_op jit(solution)/shard_map/ppermute | solution.py:29
  326.4 20.7 %collective-permute-start.38 = (bf16[128,2048]{1,0:T(8,128)(2,1)S(1)}, bf16[128,2048]{1,0:T(8,128)(2,1)S(1)}, u32[]{:S(2)}, u32[]{:S(2)}) collective-permute-start(bf16[128,2048]{1,0:T(8,128)(2,1)S(1)} %get-tuple-element.159), channel_id=1, source_target_pairs={{0,65},{1,64},{64,1},{65,0},{2,67},{3,66},{66,3},{67,2},{4,69},{5,... | collective-permute-start | bytes 1572872 | tf_op jit(solution)/shard_map/ppermute | solution.py:29
  334.2 20.1 %collective-permute-start.56 = (bf16[4,2,64,512]{3,2,1,0:T(8,128)(2,1)S(1)}, bf16[4,2,64,512]{3,2,1,0:T(8,128)(2,1)S(1)}, u32[]{:S(2)}, u32[]{:S(2)}) collective-permute-start(bf16[4,2,64,512]{3,2,1,0:T(8,128)(2,1)S(1)} %bump.5), channel_id=1, source_target_pairs={{0,12},{4,8},{8,4},{12,0},{1,13},{5,9},{9,5},{13,1},{2,14},{6,10},... | collective-permute-start | bytes 1572872 | tf_op jit(solution)/shard_map/ppermute | solution.py:33
  (129 other events, 1405.1 us)
Sparse Core Ops, SparseCore 0:
  173.1 87.4 reduce-scatter.1

commit v2 on v1

--- a/solution.py
+++ b/solution.py
@@ -58,8 +58,7 @@
         cost_estimate=cost(0, 13 * rows * depth),
         name="fold",
     )(mine, theirs)
-    far = [flip(sends[0], "mp"), flip(sends[1], "zl"), flip(sends[2], "zl", "mp")]
-    return keep + far[0].astype(F32) + (far[1].astype(F32) + far[2].astype(F32))
+    return [keep, flip(sends[0], "mp"), flip(sends[1], "zl"), flip(sends[2], "zl", "mp")]
 
 
 def sum_everywhere(vector):
@@ -269,36 +268,30 @@
     )(*parts)
 
 
-def place_kernel(entries, second_is_y, coords, *refs):
+def place_kernel(entries, coords, *refs):
     parts, out, sems = refs[-2 - len(entries) : -2], refs[-2], refs[-1]
-    x, y = coords[1], coords[2]
     copies = []
-    for part, (second, start) in zip(parts, entries):
+    for part, (y_bits, start) in zip(parts, entries):
         for i in range(part.shape[0]):
-            first = start + i
-            if second_is_y:
-                chip = (x ^ first) * 4 + (y ^ second)
-            else:
-                chip = (x ^ second) * 4 + (y ^ first)
-            copies.append(pltpu.make_async_copy(part.at[i], out.at[:, chip], sems.at[len(copies)]))
+            chip = (coords[1] ^ (start + i)) * 4 + (coords[2] ^ y_bits)
+            copies.append(pltpu.make_async_copy(part.at[i], out.at[chip], sems.at[len(copies)]))
             copies[-1].start()
     for copy in copies:
         copy.wait()
 
 
-def place(coords, buffer, parts, entries, second):
-    _, _, rows, columns = parts[0].shape
+def place(coords, buffer, parts, entries):
     count = sum(part.shape[0] for part in parts)
     buffers = [] if buffer is None else [buffer]
     return pl.pallas_call(
-        functools.partial(place_kernel, entries, second == "y"),
+        functools.partial(place_kernel, entries),
         in_specs=[SCALARS] + [ANY] * (len(buffers) + len(parts)),
         out_specs=ANY,
-        out_shape=like((2, 16, rows, columns)),
+        out_shape=like((16,) + parts[0].shape[1:]),
         scratch_shapes=[pltpu.SemaphoreType.DMA((count,))],
         input_output_aliases={1: 0} if buffers else {},
         compiler_params=params(16),
-        cost_estimate=cost(0, 4 * count * rows * columns * 2),
+        cost_estimate=cost(0, 4 * count * parts[0][0].size),
         name="place",
     )(coords, *buffers, *parts)
 
@@ -307,17 +300,14 @@
     return join(shard, hop(shard, axis, 1), hop(shard, axis, 2), hop(shard, axis, 3))
 
 
-def gather_sides(row, axis):
-    return hop(row, axis, 1), hop(row, axis, 3)
-
-
-def gather_plane(coords, row, sides, second):
-    one, three = sides
-    buffer = place(coords, None, [row], [(0, 0)], second)
+def gather_plane(coords, shard):
+    row = gather_line(shard, "x")
+    one, three = hop(row, "y", 1), hop(row, "y", 3)
     half = row.shape[0] // 2
-    two_low, two_high = hop(three[:half], second, 1), hop(one[half:], second, 3)
-    buffer = place(coords, buffer, [one, three], [(1, 0), (3, 0)], second)
-    buffer = place(coords, buffer, [two_low, two_high], [(2, 0), (2, half)], second)
+    two_low, two_high = hop(three[:half], "y", 1), hop(one[half:], "y", 3)
+    buffer = place(coords, None, [row], [(0, 0)])
+    buffer = place(coords, buffer, [one, three], [(1, 0), (3, 0)])
+    buffer = place(coords, buffer, [two_low, two_high], [(2, 0), (2, half)])
     return buffer.reshape(-1, buffer.shape[3])
 
 
@@ -370,19 +360,20 @@
     sums_ref[...] = jnp.sum(low.astype(F32), axis=0, keepdims=True)
 
 
-def mlp(pair, bias, up_w, down_w):
+def mlp(pair, bias, weights):
     rows, depth = pair.shape[1:]
     hidden = bias.shape[0]
     tile = 256
+    tiles = hidden // tile
     column = lambda j: (0, j)
     return pl.pallas_call(
         mlp_kernel,
-        grid=(hidden // tile,),
+        grid=(tiles,),
         in_specs=[
             pl.BlockSpec((2, rows, depth), lambda j: (0, 0, 0), pipeline_mode=pl.Buffered(1)),
             pl.BlockSpec((1, tile), column),
             pl.BlockSpec((depth, tile), column),
-            pl.BlockSpec((depth, tile), column),
+            pl.BlockSpec((depth, tile), lambda j: (0, tiles + j)),
         ],
         out_specs=[
             pl.BlockSpec((2, rows, tile), lambda j: (0, 0, j)),
@@ -392,28 +383,26 @@
         compiler_params=params(32),
         cost_estimate=cost(4 * rows * depth * hidden, 20 * MIB),
         name="mlp",
-    )(pair, bias.reshape(1, -1), up_w, down_w)
+    )(pair, bias.reshape(1, -1), weights, weights)
 
 
 def grads_kernel(left_ref, right_ref, out_ref):
-    product = jnp.dot(left_ref[0], right_ref[0], preferred_element_type=F32).astype(BF16)
-    out_ref[...] = product.reshape(out_ref.shape)
-
-
-def weight_grads(pair_t, right, tile, which):
+    out_ref[...] = jnp.dot(left_ref[0], right_ref[0], preferred_element_type=F32).astype(BF16)
+
+
+def weight_grads(pair_t, right, tile):
     _, depth, rows = pair_t.shape
     count, _, columns = right.shape
     tiles = columns // tile
-    block = depth // 32
     return pl.pallas_call(
         grads_kernel,
         grid=(count, tiles, 2),
         in_specs=[
-            pl.BlockSpec((1, depth // 2, rows), lambda i, j, zl: (which(i, j), zl, 0)),
-            pl.BlockSpec((1, rows, tile), lambda i, j, zl: (i, 0, j)),
+            pl.BlockSpec((1, depth // 2, rows), lambda i, j, k: (i, k, 0)),
+            pl.BlockSpec((1, rows, tile), lambda i, j, k: (i, 0, j)),
         ],
-        out_specs=pl.BlockSpec((16, 1, block, tile), lambda i, j, zl: (0, zl, 0, i * tiles + j)),
-        out_shape=like((16, 2, block, count * columns)),
+        out_specs=pl.BlockSpec((depth // 2, tile), lambda i, j, k: (k, i * tiles + j)),
+        out_shape=like((depth, count * columns)),
         compiler_params=params(40),
         cost_estimate=cost(2 * depth * rows * count * columns, 2 * (pair_t.size + right.size * 2)),
         name="weight_grads",
@@ -422,50 +411,41 @@
 
 def head_grads_kernel(coords, left_ref, right_ref, *refs):
     outs, product_ref = refs[:-1], refs[-1]
-    zl, j = pl.program_id(0), pl.program_id(1)
     x, y = coords[1], coords[2]
-    block, tile = product_ref.shape[1:]
+    tile = product_ref.shape[3]
+    lanes = pl.ds(pl.multiple_of(pl.program_id(0) * tile, tile), tile)
     product = jnp.dot(left_ref[0], right_ref[...], preferred_element_type=F32).astype(BF16)
     product_ref[...] = product.reshape(product_ref.shape)
-    for side in range(2):
-
-        @pl.when(j // 2 == side)
-        def _(side=side):
-            lanes = pl.ds(pl.multiple_of((j % 2) * tile, tile), tile)
-            for second in range(4):
-                for first in range(4):
-                    if side == 0:
-                        chip = (x ^ first) * 4 + (y ^ second)
-                    else:
-                        chip = (x ^ second) * 4 + (y ^ first)
-                    if second == 2:
-                        out, i = outs[5 * side + 3 + first // 2], first % 2
-                    else:
-                        out, i = outs[5 * side + (0, 1, None, 2)[second]], first
-                    out[i, zl, :, lanes] = product_ref[chip]
+    for y_bits in range(4):
+        for x_bits in range(4):
+            chip = (x ^ x_bits) * 4 + (y ^ y_bits)
+            if y_bits == 2:
+                out, i = outs[3 + x_bits // 2], x_bits % 2
+            else:
+                out, i = outs[(0, 1, None, 2)[y_bits]], x_bits
+            out[i, :, :, lanes] = product_ref[chip]
 
 
 def head_grads(coords, pair_t, right):
     _, depth, rows = pair_t.shape
     columns = right.shape[1]
     tile, block = columns // 4, depth // 32
-    full, half = like((4, 2, block, 2 * tile)), like((2, 2, block, 2 * tile))
-    outs = pl.pallas_call(
+    full, half = like((4, 2, block, columns)), like((2, 2, block, columns))
+    return pl.pallas_call(
         head_grads_kernel,
-        grid=(2, 4),
+        grid=(4,),
         in_specs=[
             SCALARS,
-            pl.BlockSpec((1, depth // 2, rows), lambda zl, j: (j // 3, zl, 0)),
-            pl.BlockSpec((rows, tile), lambda zl, j: (0, j)),
+            pl.BlockSpec((1, depth, rows), lambda j: (j // 3, 0, 0)),
+            pl.BlockSpec((rows, tile), lambda j: (0, j)),
         ],
-        out_specs=[WHOLE] * 10,
-        out_shape=[full, full, full, half, half] * 2,
-        scratch_shapes=[pltpu.VMEM((16, block, tile), BF16)],
+        out_specs=[WHOLE] * 5,
+        out_shape=[full, full, full, half, half],
+        scratch_shapes=[pltpu.VMEM((16, 2, block, tile), BF16)],
         compiler_params=params(32),
         cost_estimate=cost(2 * depth * rows * columns, 16 * MIB),
         name="head_grads",
     )(coords, pair_t, right)
-    return outs[:5], outs[5:]
 
 
 def bump_kernel(chunk_ref, part_ref, out_ref):
@@ -495,11 +475,11 @@
             sends[i - 1][...] = total.astype(BF16)
 
 
-def scatter_blocks(chunks, first, second):
+def scatter_blocks(chunks):
     own, one, three, two_low, two_high = chunks
-    low, high = hop(two_low, second, 1), hop(two_high, second, 3)
-    three = hop(bump(three, low, 0), second, 3)
-    one = hop(bump(one, high, 1), second, 1)
+    low, high = hop(two_low, "y", 1), hop(two_high, "y", 3)
+    three = hop(bump(three, low, 0), "y", 3)
+    one = hop(bump(one, high, 1), "y", 1)
     shape = own.shape[1:]
     keep, *sends = pl.pallas_call(
         near_kernel,
@@ -509,33 +489,34 @@
         compiler_params=params(16),
         name="near",
     )(own, one, three)
-    return [keep] + [hop(send, first, bits) for send, bits in zip(sends, (1, 2, 3))]
-
-
-def cut_heads_kernel(coords, *refs):
-    parts, outs = refs[:8], refs[8:]
-    rows = outs[0].shape[0]
-    half = outs[0].shape[1] // 2
+    return [keep] + [hop(send, "x", bits) for send, bits in zip(sends, (1, 2, 3))]
+
+
+def cut_kernel(coords, mlp_ref, *refs):
+    heads, outs = refs[:4], refs[4:]
+    rows, columns = outs[0].shape[0], mlp_ref.shape[1]
     for bits in range(4):
-        zl, c = coords[0] ^ (bits >> 1), coords[3] ^ (bits & 1)
-        some = pl.ds(pl.multiple_of(c * rows, rows), rows)
-        for side in range(2):
-            keep, *others = parts[4 * side : 4 * side + 4]
-            total = keep[zl, some, :]
-            for other in others:
-                total = total + other[zl, some, :].astype(F32)
-            outs[bits][:, side * half : (side + 1) * half] = total.astype(BF16)
-
-
-def cut_heads(coords, left, right, rows):
-    return pl.pallas_call(
-        cut_heads_kernel,
-        in_specs=[SCALARS] + [WHOLE] * 8,
+        start = pl.multiple_of(slot_of(coords, bits) * rows, rows)
+        some = pl.ds(start, rows)
+        outs[bits][:, :columns] = mlp_ref[some, :]
+        total = heads[0][some, :]
+        for head in heads[1:]:
+            total = total + head[some, :].astype(F32)
+        outs[bits][:, columns:] = total.astype(BF16)
+
+
+def cut(coords, mlp_grads, heads):
+    rows = mlp_grads.shape[0]
+    heads = [head.reshape(rows, -1) for head in heads]
+    columns = mlp_grads.shape[1] + heads[0].shape[1]
+    return pl.pallas_call(
+        cut_kernel,
+        in_specs=[SCALARS] + [WHOLE] * 5,
         out_specs=[WHOLE] * 4,
-        out_shape=[like((rows, 2 * left[0].shape[2]))] * 4,
-        compiler_params=params(16),
-        name="cut_heads",
-    )(coords, *left, *right)
+        out_shape=[like((rows // 4, columns))] * 4,
+        compiler_params=params(16),
+        name="cut",
+    )(coords, mlp_grads, *heads)
 
 
 def combine_kernel(products, *refs):
@@ -556,23 +537,19 @@
         sums_ref[1:2, :] = jnp.sum(total * rows_ref[0].astype(F32), axis=0, keepdims=True)
 
 
-def combine(hidden_pair, side, mlp_w, right, head_parts, pair=None):
+def combine(hidden_pair, side, right, start, stop, mlp_w, head_w, pair=None):
     _, rows, hidden = hidden_pair.shape
     depth = mlp_w.shape[0]
-    tile = 256
+    width, tile = stop - start, 256
+    where = start // width
     column = lambda i: (0, i)
     specs = [
         pl.BlockSpec((1, rows, hidden), lambda i: (side, 0, 0)),
-        pl.BlockSpec((tile, hidden), lambda i: (i, 0)),
+        pl.BlockSpec((tile, hidden), lambda i: (i, side)),
+        pl.BlockSpec((rows, width), lambda i: (0, where)),
+        pl.BlockSpec((tile, width), lambda i: (i, where)),
     ]
-    arrays = [hidden_pair, mlp_w]
-    total = hidden
-    for start, weights, weights_start, columns in head_parts:
-        left, where = start // columns, weights_start // columns
-        specs.append(pl.BlockSpec((rows, columns), lambda i, left=left: (0, left)))
-        specs.append(pl.BlockSpec((tile, columns), lambda i, where=where: (i, where)))
-        arrays += [right, weights]
-        total += columns
+    arrays = [hidden_pair, mlp_w, right, head_w]
     out_specs = [pl.BlockSpec((rows // 2, tile), column)] * 2
     shapes = [like((rows // 2, depth))] * 2
     if pair is not None:
@@ -581,44 +558,39 @@
         out_specs.append(pl.BlockSpec((2, tile), column))
         shapes.append(like((2, depth), F32))
     return pl.pallas_call(
-        functools.partial(combine_kernel, 1 + len(head_parts)),
+        functools.partial(combine_kernel, 2),
         grid=(depth // tile,),
         in_specs=specs,
         out_specs=out_specs,
         out_shape=shapes,
         compiler_params=params(32),
-        cost_estimate=cost(2 * rows * depth * total, 16 * MIB),
+        cost_estimate=cost(2 * rows * depth * (hidden + width), 16 * MIB),
         name="combine",
     )(*arrays)
 
 
-def project_kernel(pair_ref, bias_ref, first_ref, second_ref, linear_ref, grad_ref):
-    step = pl.program_id(0)
-
-    @pl.when(step < 2)
+def project_kernel(pair_ref, bias_ref, weights_ref, linear_ref, grad_ref):
+    product = jnp.dot(pair_ref[0], weights_ref[...], preferred_element_type=F32)
+
+    @pl.when(pl.program_id(0) < 3)
     def _():
-        linear_ref[...] = jnp.dot(pair_ref[0], first_ref[...], preferred_element_type=F32) + bias_ref[...]
-
-    @pl.when(step == 2)
+        linear_ref[...] = product + bias_ref[...]
+
+    @pl.when(pl.program_id(0) == 3)
     def _():
-        linear_ref[...] = jnp.dot(pair_ref[0], second_ref[...], preferred_element_type=F32) + bias_ref[...]
-
-    @pl.when(step == 3)
-    def _():
-        grad_ref[...] = jnp.dot(pair_ref[0], second_ref[...], preferred_element_type=F32).astype(BF16)
-
-
-def project(pair, bias, first_w, second_w):
+        grad_ref[...] = product.astype(BF16)
+
+
+def project(pair, bias, weights):
     rows, depth = pair.shape[1:]
-    width = first_w.shape[1] // 2
+    width = weights.shape[1] // 4
     return pl.pallas_call(
         project_kernel,
         grid=(4,),
         in_specs=[
             pl.BlockSpec((1, rows, depth), lambda j: (j // 3, 0, 0)),
             pl.BlockSpec((1, width), lambda j: (0, jnp.minimum(j, 2))),
-            pl.BlockSpec((depth, width), lambda j: (0, jnp.minimum(j, 1))),
-            pl.BlockSpec((depth, width), lambda j: (0, jnp.maximum(j - 2, 0))),
+            pl.BlockSpec((depth, width), lambda j: (0, j)),
         ],
         out_specs=[
             pl.BlockSpec((rows, width), lambda j: (0, jnp.minimum(j, 2))),
@@ -628,61 +600,110 @@
         compiler_params=params(32),
         cost_estimate=cost(8 * rows * depth * width, 16 * MIB),
         name="project",
-    )(pair, bias.reshape(1, -1), first_w, second_w)
-
-
-def cut_kernel(coords, whole_ref, *outs):
-    for bits in range(4):
-        outs[bits][...] = whole_ref[slot_of(coords, bits)]
-
-
-def cut(coords, whole):
-    return pl.pallas_call(
-        cut_kernel,
-        in_specs=[SCALARS, WHOLE],
-        out_specs=[WHOLE] * 4,
-        out_shape=[like(whole.shape[1:])] * 4,
-        compiler_params=params(16),
-        name="cut",
-    )(coords, whole)
+    )(pair, bias.reshape(1, -1), weights)
 
 
 def exchange(parts):
     return [parts[0], flip(parts[1], "c"), flip(parts[2], "zl"), flip(parts[3], "zl", "c")]
 
 
-def unpack_mlp_kernel(coords, *refs):
-    parts, (up_ref, down_ref) = refs[:4], refs[4:]
-    hidden = up_ref.shape[1] // 4
+def unpack_kernel(coords, *refs):
+    parts, (up_ref, down_ref, qkv_ref, out_ref) = refs[:4], refs[4:]
+    hidden, width = up_ref.shape[1] // 4, out_ref.shape[1] // 4
     for bits in range(4):
-        lanes = pl.ds(pl.multiple_of(slot_of(coords, bits) * hidden, hidden), hidden)
-        up_ref[:, lanes] = parts[bits][:, :hidden].astype(F32)
-        down_ref[:, lanes] = parts[bits][:, hidden:].astype(F32)
-
-
-def unpack_heads_kernel(coords, *refs):
-    parts, (qkv_ref, out_ref) = refs[:4], refs[4:]
-    width = out_ref.shape[1] // 4
-    for bits in range(4):
-        lanes = pl.ds(pl.multiple_of(slot_of(coords, bits) * width, width), width)
+        slot = slot_of(coords, bits)
+        wide = pl.ds(pl.multiple_of(slot * hidden, hidden), hidden)
+        narrow = pl.ds(pl.multiple_of(slot * width, width), width)
+        part = parts[bits]
+        up_ref[:, wide] = part[:, :hidden].astype(F32)
+        down_ref[:, wide] = part[:, hidden : 2 * hidden].astype(F32)
         for kind in range(3):
-            qkv_ref[kind, :, lanes] = parts[bits][:, kind * width : (kind + 1) * width].astype(F32)
-        out_ref[:, lanes] = parts[bits][:, 3 * width :].astype(F32)
-
-
-def unpack(coords, kernel, parts, shapes, name):
-    return pl.pallas_call(
-        kernel,
+            start = 2 * hidden + kind * width
+            qkv_ref[kind, :, narrow] = part[:, start : start + width].astype(F32)
+        out_ref[:, narrow] = part[:, 2 * hidden + 3 * width :].astype(F32)
+
+
+def unpack(coords, parts, hidden, width):
+    rows = parts[0].shape[0]
+    wide, narrow = (rows, 4 * hidden), (rows, 4 * width)
+    return pl.pallas_call(
+        unpack_kernel,
         in_specs=[SCALARS] + [WHOLE] * 4,
+        out_specs=[WHOLE] * 4,
+        out_shape=[like(shape, F32) for shape in (wide, wide, (3,) + narrow, narrow)],
+        compiler_params=params(16),
+        name="unpack",
+    )(coords, *parts)
+
+
+def turn(dest, value, back):
+    block = value.shape[1] // 32
+    for chip in range(16):
+        for zl in range(2):
+            natural, inside = (zl * 16 + chip) * block, (chip * 2 + zl) * block
+            source, target = (inside, natural) if back else (natural, inside)
+            dest[:, target : target + block] = value[:, source : source + block].astype(dest.dtype)
+
+
+def standardize(tokens):
+    rows = tokens.astype(F32)
+    centered = rows - jnp.mean(rows, axis=1, keepdims=True)
+    scale = lax.rsqrt(jnp.mean(centered * centered, axis=1, keepdims=True) + EPSILON)
+    return rows, centered * scale, scale
+
+
+def enter_kernel(tokens_ref, cot_ref, gain_ref, bias_ref, pair_ref, sums_ref):
+    _, standard, _ = standardize(tokens_ref[...])
+    turn(pair_ref.at[0], (standard * gain_ref[...] + bias_ref[...]).astype(BF16), False)
+    turn(pair_ref.at[1], cot_ref[...], False)
+    sums_ref[...] = jnp.sum(cot_ref[...].astype(F32), axis=0, keepdims=True)
+
+
+def enter(tokens, cotangent, gain, bias):
+    return pl.pallas_call(
+        enter_kernel,
+        in_specs=[WHOLE] * 4,
         out_specs=[WHOLE] * 2,
-        out_shape=[like(shape, F32) for shape in shapes],
-        compiler_params=params(16),
-        name=name,
-    )(coords, *parts)
+        out_shape=[like((2,) + tokens.shape), like((1, tokens.shape[1]), F32)],
+        compiler_params=params(16),
+        name="enter",
+    )(tokens, cotangent, gain.reshape(1, -1), bias.reshape(1, -1))
+
+
+def leave_kernel(tokens_ref, cot_ref, gain_ref, bias_ref, *refs):
+    mixed_ref, grad_ref, branch_ref, normed_ref = refs[-4:]
+    branch, normed = refs[:4], refs[4:8]
+    total = branch[0][...]
+    for part in branch[1:]:
+        total = total + part[...].astype(F32)
+    turn(branch_ref, total, True)
+    total = normed[0][...]
+    for part in normed[1:]:
+        total = total + part[...].astype(F32)
+    turn(normed_ref, total, True)
+    rows, standard, scale = standardize(tokens_ref[...])
+    mixed_ref[...] = (rows + branch_ref[...] + bias_ref[...]).astype(BF16)
+    grad = normed_ref[...] * gain_ref[...]
+    level = jnp.mean(grad, axis=1, keepdims=True)
+    slope = jnp.mean(grad * standard, axis=1, keepdims=True)
+    grad_ref[...] = cot_ref[...].astype(F32) + scale * (grad - level - standard * slope)
+
+
+def leave(tokens, cotangent, gain, bias, branches, normed):
+    shape = tokens.shape
+    return pl.pallas_call(
+        leave_kernel,
+        in_specs=[WHOLE] * 12,
+        out_specs=[WHOLE] * 2,
+        out_shape=[like(shape), like(shape, F32)],
+        scratch_shapes=[pltpu.VMEM(shape, F32)] * 2,
+        compiler_params=params(24),
+        name="leave",
+    )(tokens, cotangent, gain.reshape(1, -1), bias.reshape(1, -1), *branches, *normed)
 
 
 def scatter_plane(grads):
-    return lax.psum_scatter(grads.reshape(-1, grads.shape[3]), PLANE, scatter_dimension=0, tiled=True)
+    return lax.psum_scatter(grads, PLANE, scatter_dimension=0, tiled=True)
 
 
 def per_device(
@@ -711,35 +732,13 @@
     this_half = coords[4]
 
     parts = exchange(pack(coords, w_up, w_down.T, w_qkv.transpose(1, 0, 2), w_out.T, segments))
-    up_shard, down_shard, first_shard, second_shard = order(
-        coords, parts, (hidden, hidden, 2 * width, 2 * width)
-    )
-
-    inputs_f = tokens.astype(F32)
-    row_mean = jnp.mean(inputs_f, axis=-1, keepdims=True)
-    mean_removed = inputs_f - row_mean
-    variance = jnp.mean(mean_removed * mean_removed, axis=-1, keepdims=True)
-    inverse_deviation = lax.rsqrt(variance + EPSILON)
-    standardized_input = mean_removed * inverse_deviation
-    normalized_rows = (standardized_input * layernorm_gain + layernorm_bias).astype(BF16)
-
-    pair = jnp.stack([normalized_rows, cotangent])
-    up_shard, down_shard, pair = lax.optimization_barrier((up_shard, down_shard, pair))
-    near, far = flip(pair, "zl"), flip(pair, "zl", "mp")
-    up_row = gather_line(up_shard, "x")
-    down_row = gather_line(down_shard, "y")
-    up_row, down_row, pair = lax.optimization_barrier((up_row, down_row, pair))
-    opposite = flip(pair, "mp")
-    up_sides, down_sides = gather_sides(up_row, "y"), gather_sides(down_row, "x")
-    up_sides, down_sides, opposite, near, far, first_shard, second_shard = lax.optimization_barrier(
-        (up_sides, down_sides, opposite, near, far, first_shard, second_shard)
-    )
-    up_w = gather_plane(coords, up_row, up_sides, "y")
-    down_w = gather_plane(coords, down_row, down_sides, "x")
-    first_row = gather_line(first_shard, "x")
-    second_row = gather_line(second_shard, "y")
-    up_w, down_w, first_row, second_row = lax.optimization_barrier((up_w, down_w, first_row, second_row))
-    first_sides, second_sides = gather_sides(first_row, "y"), gather_sides(second_row, "x")
+    mlp_shard, head_shard = order(coords, parts, (2 * hidden, 4 * width))
+    mlp_w = lax.all_gather(mlp_shard, PLANE, axis=0, tiled=False).reshape(depth, 2 * hidden)
+
+    pair, grad_b_out = enter(tokens, cotangent, layernorm_gain, layernorm_bias)
+    head_shard, pair = lax.optimization_barrier((head_shard, pair))
+    near, far, opposite = flip(pair, "zl"), flip(pair, "zl", "mp"), flip(pair, "mp")
+    head_w = gather_plane(coords, head_shard)
     pair, pair_t = gather_tokens(pair, opposite, near, far)
 
     doc = jnp.stack([parts[k][0, -length:] for k in (0, 2, 1, 3)]).astype(jnp.int32)
@@ -764,66 +763,46 @@
     b_up_here = lax.dynamic_slice_in_dim(b_up, place_here * hidden, hidden)
     b_qkv_here = lax.dynamic_slice_in_dim(b_qkv, place_here * width, width, axis=1).reshape(-1)
 
-    hidden_pair, grad_b_up = mlp(pair, b_up_here, up_w, down_w)
-    mlp_grads = scatter_plane(weight_grads(pair_t, hidden_pair, hidden // 2, lambda i, j: i))
-
-    first_sides, second_sides, pair, hidden_pair = lax.optimization_barrier(
-        (first_sides, second_sides, pair, hidden_pair)
-    )
-    first_w = gather_plane(coords, first_row, first_sides, "y")
-    second_w = gather_plane(coords, second_row, second_sides, "x")
-    linear, grad_attended = project(pair, b_qkv_here, first_w, second_w)
+    pair, head_w = lax.optimization_barrier((pair, head_w))
+    hidden_pair, grad_b_up = mlp(pair, b_up_here, mlp_w)
+    mlp_grads = scatter_plane(weight_grads(pair_t, hidden_pair, hidden // 2))
+
+    pair, hidden_pair = lax.optimization_barrier((pair, hidden_pair))
+    linear, grad_attended = project(pair, b_qkv_here, head_w)
     right = attention(
         linear, grad_attended, (cos_table, low_table, high_table), doc, index, length
     )
-    first_grads, second_grads = head_grads(coords, pair_t, right)
-    first_grads, second_grads, hidden_pair = lax.optimization_barrier(
-        (first_grads, second_grads, hidden_pair)
+    heads, hidden_pair = lax.optimization_barrier((head_grads(coords, pair_t, right), hidden_pair))
+    heads = scatter_blocks(heads)
+
+    mine, theirs, sums = combine(hidden_pair, 0, right, 0, 3 * width, mlp_w, head_w, pair)
+    normed = scatter_group(mine, theirs)
+    branches = scatter_group(*combine(hidden_pair, 1, right, 3 * width, 4 * width, mlp_w, head_w))
+    mixed, d_tokens = leave(
+        tokens, cotangent, layernorm_gain, b_out + b_down, branches, normed
     )
-    first_grads = scatter_blocks(first_grads, "x", "y")
-    second_grads = scatter_blocks(second_grads, "y", "x")
-
-    inner = [(0, first_w, 0, 2 * width), (2 * width, second_w, 0, width)]
-    mine, theirs, sums = combine(hidden_pair, 0, up_w, right, inner, pair)
-    normalized_gradient = scatter_group(mine, theirs)
-    outer = [(3 * width, second_w, width, width)]
-    branches = scatter_group(*combine(hidden_pair, 1, down_w, right, outer))
-    mixed = (inputs_f + branches + b_out + b_down).astype(BF16)
-    standardized_gradient = normalized_gradient * layernorm_gain
-    grad_inputs = inverse_deviation * (
-        standardized_gradient
-        - jnp.mean(standardized_gradient, axis=-1, keepdims=True)
-        - standardized_input
-        * jnp.mean(standardized_gradient * standardized_input, axis=-1, keepdims=True)
-    )
-    cot_rows = cotangent.astype(F32)
-    d_tokens = cot_rows + grad_inputs
 
     grad_b_heads = jnp.sum(right[:, : 3 * width].astype(F32), axis=0)
     slices = jnp.concatenate([grad_b_heads, grad_b_up[0]])
     slot = this_half * 4 + place_here
     spread = jnp.zeros((8,) + slices.shape, F32)
     spread = lax.dynamic_update_slice(spread, slices[None], (slot, 0))
-    vector = jnp.concatenate([spread.reshape(-1), jnp.sum(cot_rows, axis=0), sums.reshape(-1)])
+    vector = jnp.concatenate([spread.reshape(-1), grad_b_out[0], sums.reshape(-1)])
     vector = sum_everywhere(vector.reshape(-1, LANES)).reshape(-1)
     spread, whole = vector[: spread.size].reshape(8, -1), vector[spread.size :].reshape(3, depth)
     spread = lax.dynamic_slice_in_dim(spread, this_half * 4, 4)
     grad_b_qkv = spread[:, : 3 * width].reshape(4, 3, width).transpose(1, 0, 2).reshape(3, 4 * width)
     grad_b_up = spread[:, 3 * width :].reshape(-1)
-    grad_gain = (whole[2] - layernorm_bias * whole[1]) / layernorm_gain
-
-    mlp_parts = exchange(cut(coords, mlp_grads.reshape(4, rows, 2 * hidden)))
-    grad_up_w, grad_down_w = unpack(
-        coords, unpack_mlp_kernel, mlp_parts, [w_up.shape, w_up.shape], "unpack_mlp"
-    )
-    head_parts = exchange(cut_heads(coords, first_grads, second_grads, rows))
-    shapes = [(3, rows, 4 * width), (rows, 4 * width)]
-    grad_qkv_w, grad_out_w = unpack(coords, unpack_heads_kernel, head_parts, shapes, "unpack_heads")
+    sums = whole[1:].reshape(2, 16, 2, depth // 32).transpose(0, 2, 1, 3).reshape(2, depth)
+    grad_gain = (sums[1] - layernorm_bias * sums[0]) / layernorm_gain
+
+    parts = exchange(cut(coords, mlp_grads, heads))
+    grad_up_w, grad_down_w, grad_qkv_w, grad_out_w = unpack(coords, parts, hidden, width)
     return (
         mixed,
         d_tokens,
         grad_gain,
-        whole[1],
+        sums[0],
         grad_qkv_w.transpose(1, 0, 2),
         grad_b_qkv,
         grad_out_w.T,

time: 418 us -> 404 us (0.967); the launches traced: 410 us -> 400 us
  starting transfers between devices: 102 us -> 72.4 us
  waiting for transfers between devices: 107 us -> 133 us
  other arithmetic: 11.9 us -> 4.37 us
  local copies, waits for them, and re-layouts: 49.3 us -> 56.4 us
  Pallas kernels: 124 us -> 119 us
    ppermute x48 -> x20, starting transfers between devices: 51.1 us -> 21.4 us  [hop(): return lax.ppermute(value, axis, [(i, i ^ bits) for i in range(4)])]
    ppermute x25 -> x22, waiting for transfers between devices: 37.5 us -> 65.6 us  [flip(): return lax.ppermute(value, axes, [(i, count - 1 - i) for i in range(count)])]
    unnamed x169 -> x117, local copies, waits for them, and re-layouts: 28.1 us -> 47 us
    reduce_sum x4 -> x0, other arithmetic: 6.46 us -> none  [the longest x1 1.97 us: per_device(): jnp.sum(cot_rows, axis=0)]
    pallas_call x20 -> x11, Pallas kernels: 59.5 us -> 53.4 us  [the longest x2 21.8 us: combine(): pl.pallas_call(functools.partial(combine_kernel, 2), grid=(depth // tile,...]
    ppermute x48 -> x20, waiting for transfers between devices: 69.4 us -> 67.7 us  [hop(): return lax.ppermute(value, axis, [(i, i ^ bits) for i in range(4)])]
    ppermute x25 -> x22, starting transfers between devices: 50.6 us -> 50.9 us  [flip(): return lax.ppermute(value, axes, [(i, count - 1 - i) for i in range(count)])]
  transfers between devices with their start and end apart: 74 -> 44, of which waited for: 30 -> 18; matrix products, arithmetic and copies ran while one was open for 9% -> 4% of each run, Pallas kernels for 19% -> 22%
where the time goes in v2:
time: 404 us; the launch traced here: 400 us
  waiting for transfers between devices  133 us (33%)
  Pallas kernels  119 us (29%)
  starting transfers between devices  72.4 us (18%)
  local copies, waits for them, and re-layouts  56.4 us (14%)
  between operations  14.7 us (4%)
  other arithmetic  4.37 us (1%)
    ppermute x20, waiting for transfers between devices, hop(): return lax.ppermute(value, axis, [(i, i ^ bits) for i in range(4)])  67.7 us
    ppermute x22, waiting for transfers between devices, flip(): return lax.ppermute(value, axes, [(i, count - 1 - i) for i in range(count)])  65.6 us
    ppermute x22, starting transfers between devices, flip(): return lax.ppermute(value, axes, [(i, count - 1 - i) for i in range(count)])  50.9 us
    unnamed x117, local copies, waits for them, and re-layouts  47 us
    pallas_call x2, Pallas kernels, combine(): pl.pallas_call(functools.partial(combine_kernel, 2), grid=(depth // tile,...  21.8 us
    ppermute x20, starting transfers between devices, hop(): return lax.ppermute(value, axis, [(i, i ^ bits) for i in range(4)])  21.4 us
    pallas_call x1, Pallas kernels, attention(): pl.pallas_call(attention_kernel, grid=(count,), in_specs=[blocks(3 * widt...  15.7 us
    pallas_call x1, Pallas kernels, gather_tokens(): pl.pallas_call(tokens_kernel, grid=(2, 2, 4), in_specs=[pl.BlockSpec(bloc...  14 us
  transfers between devices with their start and end apart: 44, of which 18 were waited for; matrix products, arithmetic and copies ran while one was open for 4% of the time, Pallas kernels for 22%

profile of v2, /device:TPU:1, one launch (start us, length us, event | category | flops | bytes accessed | tf_op | source)
XLA Modules:
  0.0 400.1 jit_solution(4426229263021462593)
XLA Ops:
  15.6 5.4 %collective-permute-done.1.refs_2_ = bf16[32,3328]{1,0:T(8,128)(2,1)S(1)} collective-permute-done((bf16[32,3328]{1,0:T(8,128)(2,1)S(1)}, bf16[32,3328]{1,0:T(8,128)(2,1)S(1)}, u32[]{:S(2)}, u32[]{:S(2)}) %collective-permute-start.1) | collective-permute-done | bytes 213024 | tf_op jit(solution)/shard_map/ppermute | solution.py:29
  21.0 4.6 %collective-permute-done.2.refs_3_ = bf16[32,3328]{1,0:T(8,128)(2,1)S(1)} collective-permute-done((bf16[32,3328]{1,0:T(8,128)(2,1)S(1)}, bf16[32,3328]{1,0:T(8,128)(2,1)S(1)}, u32[]{:S(2)}, u32[]{:S(2)}) %collective-permute-start.2) | collective-permute-done | bytes 213024 | tf_op jit(solution)/shard_map/ppermute | solution.py:29
  36.4 22.7 %collective-permute-done.3.refs_1_ = bf16[2,128,2048]{2,1,0:T(8,128)(2,1)S(1)} collective-permute-done((bf16[2,128,2048]{2,1,0:T(8,128)(2,1)S(1)}, bf16[2,128,2048]{2,1,0:T(8,128)(2,1)S(1)}, u32[]{:S(2)}, u32[]{:S(2)}) %collective-permute-start.3) | collective-permute-done | bytes 1048608 | tf_op jit(solution)/shard_map/ppermute | solution.py:29
  59.1 23.0 %collective-permute-done.4.refs_2_ = bf16[2,128,2048]{2,1,0:T(8,128)(2,1)S(1)} collective-permute-done((bf16[2,128,2048]{2,1,0:T(8,128)(2,1)S(1)}, bf16[2,128,2048]{2,1,0:T(8,128)(2,1)S(1)}, u32[]{:S(2)}, u32[]{:S(2)}) %collective-permute-start.4) | collective-permute-done | bytes 1048608 | tf_op jit(solution)/shard_map/ppermute | solution.py:29
  89.1 10.0 %collective-permute-done.7.refs_1_ = bf16[2,64,1024]{2,1,0:T(8,128)(2,1)S(1)} collective-permute-done((bf16[2,64,1024]{2,1,0:T(8,128)(2,1)S(1)}, bf16[2,64,1024]{2,1,0:T(8,128)(2,1)S(1)}, u32[]{:S(2)}, u32[]{:S(2)}) %collective-permute-start.7) | collective-permute-done | bytes 262176 | tf_op jit(solution)/shard_map/ppermute | solution.py:33
  99.0 12.3 %collective-permute-done.8.refs_2_ = bf16[2,64,1024]{2,1,0:T(8,128)(2,1)S(1)} collective-permute-done((bf16[2,64,1024]{2,1,0:T(8,128)(2,1)S(1)}, bf16[2,64,1024]{2,1,0:T(8,128)(2,1)S(1)}, u32[]{:S(2)}, u32[]{:S(2)}) %collective-permute-start.8) | collective-permute-done | bytes 262176 | tf_op jit(solution)/shard_map/ppermute | solution.py:33
  114.0 22.9 %collective-permute-done.11.refs_2_ = bf16[4,2,64,1024]{3,2,1,0:T(8,128)(2,1)S(1)} collective-permute-done((bf16[4,2,64,1024]{3,2,1,0:T(8,128)(2,1)S(1)}, bf16[4,2,64,1024]{3,2,1,0:T(8,128)(2,1)S(1)}, u32[]{:S(2)}, u32[]{:S(2)}) %collective-permute-start.11) | collective-permute-done | bytes 1048608 | tf_op jit(solution)/shard_map/ppermute | solution.py:33
  143.2 6.8 %collective-permute-done.12.refs_1_ = bf16[2,2,64,1024]{3,2,1,0:T(8,128)(2,1)} collective-permute-done((bf16[2,2,64,1024]{3,2,1,0:T(8,128)(2,1)}, bf16[2,2,64,1024]{3,2,1,0:T(8,128)(2,1)}, u32[]{:S(2)}, u32[]{:S(2)}) %collective-permute-start.12) | collective-permute-done | bytes 524320 | tf_op jit(solution)/shard_map/ppermute | solution.py:33
  153.6 14.0 %tokens.1 = (bf16[2,1024,2048]{2,1,0:T(8,128)(2,1)S(1)}, bf16[2,2048,1024]{2,1,0:T(8,128)(2,1)}) custom-call(bf16[4,2,128,2048]{3,2,1,0:T(8,128)(2,1)} %join.2.mine_ref, bf16[4,2,128,2048]{3,2,1,0:T(8,128)(2,1)} %collective-permute-done.6.other_ref), custom_call_target="tpu_custom_call" | custom-call | bytes 33554432 | tf_op jit(solution)/shard_map/tokens/pallas_call | solution.py:331
  177.7 13.4 %mlp.1 = (bf16[2,1024,1024]{2,1,0:T(8,128)(2,1)S(1)}, f32[1,1024]{1,0:T(1,128)S(1)}) custom-call(bf16[2,1024,2048]{2,1,0:T(8,128)(2,1)S(1)} %copy-done.41, f32[1,1024]{1,0:T(1,128)S(1)} %bitcast.103, bf16[2048,2048]{1,0:T(8,128)(2,1)S(1)} %bitcast.109, bf16[2048,2048]{1,0:T(8,128)(2,1)S(1)} %bitcast.110), custom_call_target="tpu_custom_call" | custom-call | flops 8589934592 | bytes 20971520 | tf_op jit(solution)/shard_map/mlp/pallas_call | solution.py:369
  191.1 13.3 %weight_grads.1 = bf16[2048,2048]{1,0:T(8,128)(2,1)S(1)} custom-call(bf16[2,2048,1024]{2,1,0:T(8,128)(2,1)} %get-tuple-element.77.left_ref, bf16[2,1024,1024]{2,1,0:T(8,128)(2,1)S(1)} %get-tuple-element.93.refs_0_.right_ref), custom_call_target="tpu_custom_call" | custom-call | flops 8589934592 | bytes 16777216 | tf_op jit(solution)/shard_map/weight_grads/pallas_call | solution.py:397
  220.0 6.1 %project.1 = (f32[1024,768]{1,0:T(8,128)S(1)}, bf16[1024,256]{1,0:T(8,128)(2,1)S(1)}) custom-call(bf16[2,1024,2048]{2,1,0:T(8,128)(2,1)S(1)} %copy-done.42, f32[1,768]{1,0:T(1,128)S(1)} %bitcast.105, bf16[2048,1024]{1,0:T(8,128)(2,1)S(1)} %bitcast.80), custom_call_target="tpu_custom_call" | custom-call | flops 4294967296 | bytes 16777216 | tf_op jit(solution)/shard_map/project/pallas_call | solution.py:587
  226.2 15.7 %attention.1.right_ref.refs_2_ = bf16[1024,1024]{1,0:T(8,128)(2,1)S(1)} custom-call(f32[1024,768]{1,0:T(8,128)S(1)} %get-tuple-element.85.linear_ref, bf16[1024,256]{1,0:T(8,128)(2,1)S(1)} %get-tuple-element.86.grad_ref, f32[1024,128]{1,0:T(8,128)S(1)} %copy.48.cos_ref, f32[1024,128]{1,0:T(8,128)S(1)} %copy.49.low_ref, f32[1024,128]{1,0:T(8,128)S(1)} %copy.50.high_ref, ...), custom_call_target="tpu_custom_call" | custom-call | flops 18874368000 | bytes 8388608 | tf_op jit(solution)/shard_map/attention/pallas_call | solution.py:141
  241.9 7.4 %head_grads.1 = (bf16[4,2,64,1024]{3,2,1,0:T(8,128)(2,1)S(1)}, bf16[4,2,64,1024]{3,2,1,0:T(8,128)(2,1)S(1)}, bf16[4,2,64,1024]{3,2,1,0:T(8,128)(2,1)S(1)}, bf16[...) custom-call(s32[5]{0:T(128)S(1)} %stack.40.coords, bf16[2,2048,1024]{2,1,0:T(8,128)(2,1)S(1)} %bitcast.112, ...), custom_call_target="tpu_custom_call" | custom-call | flops 4294967296 | bytes 16777216 | tf_op jit(solution)/shard_map/head_grads/pallas_call | solution.py:434
  254.0 12.0 %combine.3 = (bf16[512,2048]{1,0:T(8,128)(2,1)S(1)}, bf16[512,2048]{1,0:T(8,128)(2,1)}, f32[2,2048]{1,0:T(2,128)S(1)}) custom-call(bf16[2,1024,1024]{2,1,0:T(8,128)(2,1)S(1)} %copy-done.44, bf16[2048,2048]{1,0:T(8,128)(2,1)} %bitcast.107, bf16[1024,1024]{1,0:T(8,128)(2,1)S(1)} %attention.1.right_ref.refs_2_, bf16[2048,1024]{1,0:T(8,128)(2,1)S(1)} %bitcast.81, ...), custom_call_target="tpu_custom_call" | custom-call | flops 7516192768 | bytes 16777216 | tf_op jit(solution)/shard_map/combine/pallas_call | solution.py:560
  265.9 3.6 collective-permute-start.18
  269.5 9.9 %combine.2 = (bf16[512,2048]{1,0:T(8,128)(2,1)S(1)}, bf16[512,2048]{1,0:T(8,128)(2,1)}) custom-call(bf16[2,1024,1024]{2,1,0:T(8,128)(2,1)S(1)} %copy-done.44, bf16[2048,2048]{1,0:T(8,128)(2,1)} %bitcast.108, bf16[1024,1024]{1,0:T(8,128)(2,1)S(1)} %attention.1.right_ref.refs_2_, bf16[2048,1024]{1,0:T(8,128)(2,1)S(1)} %bitcast.82), custom_call_target="tpu_custom_call" | custom-call | flops 5368709120 | bytes 16777216 | tf_op jit(solution)/shard_map/combine/pallas_call | solution.py:560
  299.4 5.2 %collective-permute-done.26 = f32[160,128]{1,0:T(8,128)S(1)} collective-permute-done((f32[160,128]{1,0:T(8,128)S(1)}, f32[160,128]{1,0:T(8,128)S(1)}, u32[]{:S(2)}, u32[]{:S(2)}) %collective-permute-start.26) | collective-permute-done | bytes 81952 | tf_op jit(solution)/shard_map/ppermute | solution.py:33
  309.3 3.7 collective-permute-done.28
  325.4 4.0 %fold.3 = (f32[128,2048]{1,0:T(8,128)S(1)}, bf16[128,2048]{1,0:T(8,128)(2,1)}, bf16[128,2048]{1,0:T(8,128)(2,1)}, bf16[128,2048]{1,0:T(8,128)(2,1)}) custom-call(bf16[512,2048]{1,0:T(8,128)(2,1)S(1)} %copy-done.11, bf16[512,2048]{1,0:T(8,128)(2,1)} %collective-permute-done.18.theirs_ref), custom_call_target="tpu_custom_call" | custom-call | bytes 3407872 | tf_op jit(solution)/shard_map/fold/pallas_call | solution.py:51
  340.0 4.0 %fold.2 = (f32[128,2048]{1,0:T(8,128)S(1)}, bf16[128,2048]{1,0:T(8,128)(2,1)}, bf16[128,2048]{1,0:T(8,128)(2,1)}, bf16[128,2048]{1,0:T(8,128)(2,1)}) custom-call(bf16[512,2048]{1,0:T(8,128)(2,1)S(1)} %get-tuple-element.94.mine_ref, bf16[512,2048]{1,0:T(8,128)(2,1)} %collective-permute-done.14.theirs_ref), custom_call_target="tpu_custom_call" | custom-call | bytes 3407872 | tf_op jit(solution)/shard_map/fold/pallas_call | solution.py:51
  355.5 10.2 %collective-permute-start.39 = (bf16[32,3072]{1,0:T(8,128)(2,1)S(1)}, bf16[32,3072]{1,0:T(8,128)(2,1)S(1)}, u32[]{:S(2)}, u32[]{:S(2)}) collective-permute-start(bf16[32,3072]{1,0:T(8,128)(2,1)S(1)} %get-tuple-element.121), channel_id=1, source_target_pairs={{0,2},{2,0},{1,3},{3,1},{4,6},{6,4},{5,7},{7,5},{8,10},{10,8},{9,1... | collective-permute-start | bytes 589832 | tf_op jit(solution)/shard_map/ppermute | solution.py:29
  366.0 14.1 %collective-permute-start.41 = (bf16[32,3072]{1,0:T(8,128)(2,1)S(1)}, bf16[32,3072]{1,0:T(8,128)(2,1)S(1)}, u32[]{:S(2)}, u32[]{:S(2)}) collective-permute-start(bf16[32,3072]{1,0:T(8,128)(2,1)S(1)} %get-tuple-element.123), channel_id=1, source_target_pairs={{0,66},{2,64},{64,2},{66,0},{1,67},{3,65},{65,3},{67,1},{4,70},{6,... | collective-permute-start | bytes 589832 | tf_op jit(solution)/shard_map/ppermute | solution.py:29
  383.9 3.8 leave.1
  (264 shorter events, 137.4 us)
Async XLA Ops:
  7.2 163.8 %all-gather.2.cloned.1.call-start = ((), (), s32[]{:S(2)}) async-start(), calls=%async_computation.1 | async-start | bytes 8912896 | tf_op jit(solution)/shard_map/all_gather | solution.py:736
  27.7 324.6 %reduce-scatter.2.cloned.1.call-start = ((), (), s32[]{:S(2)}) async-start(), calls=%async_computation.2 | async-start | bytes 8912896 | tf_op jit(solution)/shard_map/reduce_scatter | solution.py:706
  32.1 27.0 %collective-permute-start.3 = (bf16[2,128,2048]{2,1,0:T(8,128)(2,1)S(1)}, bf16[2,128,2048]{2,1,0:T(8,128)(2,1)S(1)}, u32[]{:S(2)}, u32[]{:S(2)}) collective-permute-start(bf16[2,128,2048]{2,1,0:T(8,128)(2,1)S(1)} %get-tuple-element.76.refs_0_), channel_id=1, source_target_pairs={{0,1},{1,0},{2,3},{3,2},{4,5},{5,4},{6,7},{7,6},{8,9},{9,8},{10,11... | collective-permute-start | bytes 3145736 | tf_op jit(solution)/shard_map/ppermute | solution.py:29
  35.7 46.4 %collective-permute-start.4 = (bf16[2,128,2048]{2,1,0:T(8,128)(2,1)S(1)}, bf16[2,128,2048]{2,1,0:T(8,128)(2,1)S(1)}, u32[]{:S(2)}, u32[]{:S(2)}) collective-permute-start(bf16[2,128,2048]{2,1,0:T(8,128)(2,1)S(1)} %get-tuple-element.76.refs_0_), channel_id=1, source_target_pairs={{0,64},{64,0},{1,65},{65,1},{2,66},{66,2},{3,67},{67,3},{4,68},{68... | collective-permute-start | bytes 3145736 | tf_op jit(solution)/shard_map/ppermute | solution.py:29
  36.4 45.7 %collective-permute-start.5 = (bf16[2,128,2048]{2,1,0:T(8,128)(2,1)S(1)}, bf16[2,128,2048]{2,1,0:T(8,128)(2,1)S(1)}, u32[]{:S(2)}, u32[]{:S(2)}) collective-permute-start(bf16[2,128,2048]{2,1,0:T(8,128)(2,1)S(1)} %get-tuple-element.76.refs_0_), channel_id=1, source_target_pairs={{0,65},{1,64},{64,1},{65,0},{2,67},{3,66},{66,3},{67,2},{4,69},{5,... | collective-permute-start | bytes 3145736 | tf_op jit(solution)/shard_map/ppermute | solution.py:29
  84.2 69.4 %collective-permute-start.6 = (bf16[4,2,128,2048]{3,2,1,0:T(8,128)(2,1)}, bf16[4,2,128,2048]{3,2,1,0:T(8,128)(2,1)}, u32[]{:S(2)}, u32[]{:S(2)}) collective-permute-start(bf16[4,2,128,2048]{3,2,1,0:T(8,128)(2,1)} %join.2.mine_ref), channel_id=1, source_target_pairs={{0,2},{2,0},{1,3},{3,1},{4,6},{6,4},{5,7},{7,5},{8,10},{10,8},{9,1... | collective-permute-start | bytes 12582920 | tf_op jit(solution)/shard_map/ppermute | solution.py:29
  86.4 24.9 %collective-permute-start.8 = (bf16[2,64,1024]{2,1,0:T(8,128)(2,1)S(1)}, bf16[2,64,1024]{2,1,0:T(8,128)(2,1)S(1)}, u32[]{:S(2)}, u32[]{:S(2)}) collective-permute-start(bf16[2,64,1024]{2,1,0:T(8,128)(2,1)S(1)} %bitcast.88), channel_id=1, source_target_pairs={{0,32},{16,48},{32,0},{48,16},{1,33},{17,49},{33,1},{49,17},{2,34}... | collective-permute-start | bytes 786440 | tf_op jit(solution)/shard_map/ppermute | solution.py:33
  88.9 22.4 %collective-permute-start.9 = (bf16[2,64,1024]{2,1,0:T(8,128)(2,1)S(1)}, bf16[2,64,1024]{2,1,0:T(8,128)(2,1)S(1)}, u32[]{:S(2)}, u32[]{:S(2)}) collective-permute-start(bf16[2,64,1024]{2,1,0:T(8,128)(2,1)S(1)} %bitcast.89), channel_id=1, source_target_pairs={{0,48},{16,32},{32,16},{48,0},{1,49},{17,33},{33,17},{49,1},{2,50}... | collective-permute-start | bytes 786440 | tf_op jit(solution)/shard_map/ppermute | solution.py:33
  111.4 25.4 %collective-permute-start.11 = (bf16[4,2,64,1024]{3,2,1,0:T(8,128)(2,1)S(1)}, bf16[4,2,64,1024]{3,2,1,0:T(8,128)(2,1)S(1)}, u32[]{:S(2)}, u32[]{:S(2)}) collective-permute-start(bf16[4,2,64,1024]{3,2,1,0:T(8,128)(2,1)S(1)} %join.3.refs_0_), channel_id=1, source_target_pairs={{0,12},{4,8},{8,4},{12,0},{1,13},{5,9},{9,5},{13,1},{2,14},{6,10},... | collective-permute-start | bytes 3145736 | tf_op jit(solution)/shard_map/ppermute | solution.py:33
  114.0 23.8 %collective-permute-start.10 = (bf16[4,2,64,1024]{3,2,1,0:T(8,128)(2,1)S(1)}, bf16[4,2,64,1024]{3,2,1,0:T(8,128)(2,1)S(1)}, u32[]{:S(2)}, u32[]{:S(2)}) collective-permute-start(bf16[4,2,64,1024]{3,2,1,0:T(8,128)(2,1)S(1)} %join.3.refs_0_), channel_id=1, source_target_pairs={{0,4},{4,0},{8,12},{12,8},{1,5},{5,1},{9,13},{13,9},{2,6},{6,2},{1... | collective-permute-start | bytes 3145736 | tf_op jit(solution)/shard_map/ppermute | solution.py:33
  251.2 29.3 %collective-permute-start.34 = (bf16[2,2,64,1024]{3,2,1,0:T(8,128)(2,1)}, bf16[2,2,64,1024]{3,2,1,0:T(8,128)(2,1)}, u32[]{:S(2)}, u32[]{:S(2)}) collective-permute-start(bf16[2,2,64,1024]{3,2,1,0:T(8,128)(2,1)} %get-tuple-element.115), channel_id=1, source_target_pairs={{0,4},{4,0},{8,12},{12,8},{1,5},{5,1},{9,13},{13,9},{2,6},{6,2},{1... | collective-permute-start | bytes 1572872 | tf_op jit(solution)/shard_map/ppermute | solution.py:33
  252.1 31.9 %collective-permute-start.32 = (bf16[2,2,64,1024]{3,2,1,0:T(8,128)(2,1)}, bf16[2,2,64,1024]{3,2,1,0:T(8,128)(2,1)}, u32[]{:S(2)}, u32[]{:S(2)}) collective-permute-start(bf16[2,2,64,1024]{3,2,1,0:T(8,128)(2,1)} %get-tuple-element.113), channel_id=1, source_target_pairs={{0,12},{4,8},{8,4},{12,0},{1,13},{5,9},{9,5},{13,1},{2,14},{6,10},... | collective-permute-start | bytes 1572872 | tf_op jit(solution)/shard_map/ppermute | solution.py:33
  265.9 59.1 %collective-permute-start.18 = (bf16[512,2048]{1,0:T(8,128)(2,1)}, bf16[512,2048]{1,0:T(8,128)(2,1)}, u32[]{:S(2)}, u32[]{:S(2)}) collective-permute-start(bf16[512,2048]{1,0:T(8,128)(2,1)} %get-tuple-element.101), channel_id=1, source_target_pairs={{0,2},{2,0},{1,3},{3,1},{4,6},{6,4},{5,7},{7,5},{8,10},{10,8},{9,1... | collective-permute-start | bytes 6291464 | tf_op jit(solution)/shard_map/ppermute | solution.py:29
  279.4 60.2 %collective-permute-start.14 = (bf16[512,2048]{1,0:T(8,128)(2,1)}, bf16[512,2048]{1,0:T(8,128)(2,1)}, u32[]{:S(2)}, u32[]{:S(2)}) collective-permute-start(bf16[512,2048]{1,0:T(8,128)(2,1)} %get-tuple-element.95), channel_id=1, source_target_pairs={{0,2},{2,0},{1,3},{3,1},{4,6},{6,4},{5,7},{7,5},{8,10},{10,8},{9,1... | collective-permute-start | bytes 6291464 | tf_op jit(solution)/shard_map/ppermute | solution.py:29
  283.4 34.5 %collective-permute-start.35 = (bf16[4,2,64,1024]{3,2,1,0:T(8,128)(2,1)S(1)}, bf16[4,2,64,1024]{3,2,1,0:T(8,128)(2,1)S(1)}, u32[]{:S(2)}, u32[]{:S(2)}) collective-permute-start(bf16[4,2,64,1024]{3,2,1,0:T(8,128)(2,1)S(1)} %bump.3), channel_id=1, source_target_pairs={{0,12},{4,8},{8,4},{12,0},{1,13},{5,9},{9,5},{13,1},{2,14},{6,10},... | collective-permute-start | bytes 3145736 | tf_op jit(solution)/shard_map/ppermute | solution.py:33
  285.7 33.3 %collective-permute-start.33 = (bf16[4,2,64,1024]{3,2,1,0:T(8,128)(2,1)S(1)}, bf16[4,2,64,1024]{3,2,1,0:T(8,128)(2,1)S(1)}, u32[]{:S(2)}, u32[]{:S(2)}) collective-permute-start(bf16[4,2,64,1024]{3,2,1,0:T(8,128)(2,1)S(1)} %bump.2), channel_id=1, source_target_pairs={{0,4},{4,0},{8,12},{12,8},{1,5},{5,1},{9,13},{13,9},{2,6},{6,2},{1... | collective-permute-start | bytes 3145736 | tf_op jit(solution)/shard_map/ppermute | solution.py:33
  325.0 20.0 %collective-permute-start.36 = (bf16[2,64,1024]{2,1,0:T(8,128)(2,1)}, bf16[2,64,1024]{2,1,0:T(8,128)(2,1)S(1)}, u32[]{:S(2)}, u32[]{:S(2)}) collective-permute-start(bf16[2,64,1024]{2,1,0:T(8,128)(2,1)} %get-tuple-element.117), channel_id=1, source_target_pairs={{0,16},{16,0},{32,48},{48,32},{1,17},{17,1},{33,49},{49,33},{2,18}... | collective-permute-start | bytes 786440 | tf_op jit(solution)/shard_map/ppermute | solution.py:33
  345.0 20.7 %collective-permute-start.21 = (bf16[128,2048]{1,0:T(8,128)(2,1)}, bf16[128,2048]{1,0:T(8,128)(2,1)S(1)}, u32[]{:S(2)}, u32[]{:S(2)}) collective-permute-start(bf16[128,2048]{1,0:T(8,128)(2,1)} %get-tuple-element.105), channel_id=1, source_target_pairs={{0,65},{1,64},{64,1},{65,0},{2,67},{3,66},{66,3},{67,2},{4,69},{5,... | collective-permute-start | bytes 1572872 | tf_op jit(solution)/shard_map/ppermute | solution.py:29
  345.5 20.5 %collective-permute-start.15 = (bf16[128,2048]{1,0:T(8,128)(2,1)}, bf16[128,2048]{1,0:T(8,128)(2,1)S(1)}, u32[]{:S(2)}, u32[]{:S(2)}) collective-permute-start(bf16[128,2048]{1,0:T(8,128)(2,1)} %get-tuple-element.97), channel_id=1, source_target_pairs={{0,1},{1,0},{2,3},{3,2},{4,5},{5,4},{6,7},{7,6},{8,9},{9,8},{10,11... | collective-permute-start | bytes 1572872 | tf_op jit(solution)/shard_map/ppermute | solution.py:29
  348.5 32.9 %collective-permute-start.16 = (bf16[128,2048]{1,0:T(8,128)(2,1)}, bf16[128,2048]{1,0:T(8,128)(2,1)S(1)}, u32[]{:S(2)}, u32[]{:S(2)}) collective-permute-start(bf16[128,2048]{1,0:T(8,128)(2,1)} %get-tuple-element.98), channel_id=1, source_target_pairs={{0,64},{64,0},{1,65},{65,1},{2,66},{66,2},{3,67},{67,3},{4,68},{68... | collective-permute-start | bytes 1572872 | tf_op jit(solution)/shard_map/ppermute | solution.py:29
  348.9 32.5 %collective-permute-start.17 = (bf16[128,2048]{1,0:T(8,128)(2,1)}, bf16[128,2048]{1,0:T(8,128)(2,1)S(1)}, u32[]{:S(2)}, u32[]{:S(2)}) collective-permute-start(bf16[128,2048]{1,0:T(8,128)(2,1)} %get-tuple-element.99), channel_id=1, source_target_pairs={{0,65},{1,64},{64,1},{65,0},{2,67},{3,66},{66,3},{67,2},{4,69},{5,... | collective-permute-start | bytes 1572872 | tf_op jit(solution)/shard_map/ppermute | solution.py:29
  355.5 32.1 %collective-permute-start.39 = (bf16[32,3072]{1,0:T(8,128)(2,1)S(1)}, bf16[32,3072]{1,0:T(8,128)(2,1)S(1)}, u32[]{:S(2)}, u32[]{:S(2)}) collective-permute-start(bf16[32,3072]{1,0:T(8,128)(2,1)S(1)} %get-tuple-element.121), channel_id=1, source_target_pairs={{0,2},{2,0},{1,3},{3,1},{4,6},{6,4},{5,7},{7,5},{8,10},{10,8},{9,1... | collective-permute-start | bytes 589832 | tf_op jit(solution)/shard_map/ppermute | solution.py:29
  365.7 21.9 %collective-permute-start.40 = (bf16[32,3072]{1,0:T(8,128)(2,1)S(1)}, bf16[32,3072]{1,0:T(8,128)(2,1)S(1)}, u32[]{:S(2)}, u32[]{:S(2)}) collective-permute-start(bf16[32,3072]{1,0:T(8,128)(2,1)S(1)} %get-tuple-element.122), channel_id=1, source_target_pairs={{0,64},{64,0},{1,65},{65,1},{2,66},{66,2},{3,67},{67,3},{4,68},{68... | collective-permute-start | bytes 589832 | tf_op jit(solution)/shard_map/ppermute | solution.py:29
  366.0 24.9 %collective-permute-start.41 = (bf16[32,3072]{1,0:T(8,128)(2,1)S(1)}, bf16[32,3072]{1,0:T(8,128)(2,1)S(1)}, u32[]{:S(2)}, u32[]{:S(2)}) collective-permute-start(bf16[32,3072]{1,0:T(8,128)(2,1)S(1)} %get-tuple-element.123), channel_id=1, source_target_pairs={{0,66},{2,64},{64,2},{66,0},{1,67},{3,65},{65,3},{67,1},{4,70},{6,... | collective-permute-start | bytes 589832 | tf_op jit(solution)/shard_map/ppermute | solution.py:29
  (73 other events, 890.4 us)
Sparse Core Ops, SparseCore 0:
  27.8 81.7 all-gather.1
  209.9 95.6 reduce-scatter.1

commit v3 on v2

--- a/solution.py
+++ b/solution.py
@@ -33,37 +33,41 @@
     return lax.ppermute(value, axis, [(i, i ^ bits) for i in range(4)])
 
 
-def fold_kernel(mine_ref, theirs_ref, keep_ref, *sends):
-    rows = keep_ref.shape[0]
-    for i in range(4):
-        block = slice(i * rows, (i + 1) * rows)
-        total = mine_ref[block, :].astype(F32) + theirs_ref[block, :].astype(F32)
-        if i == 0:
-            keep_ref[...] = total
-        else:
-            sends[i - 1][...] = total.astype(BF16)
-
-
-def scatter_group(mine, theirs):
-    rows, depth = mine.shape[0] // 4, mine.shape[1]
+def fold_kernel(*refs):
+    inputs, keep_ref, sends = refs[:4], refs[4], refs[5:]
+    rows = keep_ref.shape[1]
+    for which in range(2):
+        mine_ref, theirs_ref = inputs[2 * which : 2 * which + 2]
+        for i in range(4):
+            block = slice(i * rows, (i + 1) * rows)
+            total = mine_ref[block, :].astype(F32) + theirs_ref[block, :].astype(F32)
+            if i == 0:
+                keep_ref[which] = total
+            else:
+                sends[i - 1][which] = total.astype(BF16)
+
+
+def fold(*sums):
+    rows, depth = sums[0].shape[0] // 4, sums[0].shape[1]
     tile = depth // 4
-    theirs = flip(theirs, "c")
     keep, *sends = pl.pallas_call(
         fold_kernel,
         grid=(4,),
-        in_specs=[pl.BlockSpec((4 * rows, tile), lambda j: (0, j))] * 2,
-        out_specs=[pl.BlockSpec((rows, tile), lambda j: (0, j))] * 4,
-        out_shape=[like((rows, depth), F32)] + [like((rows, depth))] * 3,
+        in_specs=[pl.BlockSpec((4 * rows, tile), lambda j: (0, j))] * 4,
+        out_specs=[pl.BlockSpec((2, rows, tile), lambda j: (0, 0, j))] * 4,
+        out_shape=[like((2, rows, depth), F32)] + [like((2, rows, depth))] * 3,
         compiler_params=params(16),
-        cost_estimate=cost(0, 13 * rows * depth),
+        cost_estimate=cost(0, 26 * rows * depth),
         name="fold",
-    )(mine, theirs)
-    return [keep, flip(sends[0], "mp"), flip(sends[1], "zl"), flip(sends[2], "zl", "mp")]
-
-
-def sum_everywhere(vector):
-    vector = vector + flip(vector, "c")
-    vector = vector + flip(vector, "zl") + (flip(vector, "mp") + flip(vector, "zl", "mp"))
+    )(*sums)
+    return keep, sends
+
+
+def sum_along_z(vector):
+    return vector + flip(vector, "zl") + (flip(vector, "mp") + flip(vector, "zl", "mp"))
+
+
+def sum_plane(vector):
     for axis in PLANE:
         vector = (vector + hop(vector, axis, 2)) + (hop(vector, axis, 1) + hop(vector, axis, 3))
     return vector
@@ -156,7 +160,7 @@
         out_shape=jax.ShapeDtypeStruct((rows, 4 * width), BF16),
         scratch_shapes=[pltpu.VMEM((length, width), BF16)] * 3
         + [pltpu.VMEM((length, width), F32)] * 2,
-        compiler_params=params(32),
+        compiler_params=params(60),
         cost_estimate=cost(18 * GIGA, 8 * MIB),
         name="attention",
     )(
@@ -200,14 +204,13 @@
         wide = pl.ds(pl.multiple_of(slot * hidden, hidden), hidden)
         narrow = pl.ds(pl.multiple_of(slot * width, width), width)
         part = parts[bits]
-        part[:, :hidden] = up_ref[:, wide]
-        part[:, hidden : 2 * hidden] = down_ref[:, wide]
         for kind in range(3):
-            start = 2 * hidden + kind * width
-            part[:, start : start + width] = qkv_ref[kind, :, narrow]
-        start = 2 * hidden + 3 * width
-        part[:, start : start + width] = out_ref[:, narrow]
-        part[:, start + width :] = segments
+            part[:, kind * width : (kind + 1) * width] = qkv_ref[kind, :, narrow]
+        start = 4 * width
+        part[:, start - width : start] = out_ref[:, narrow]
+        part[:, start : start + hidden] = up_ref[:, wide]
+        part[:, start + hidden : start + 2 * hidden] = down_ref[:, wide]
+        part[:, start + 2 * hidden :] = segments
 
 
 def pack(coords, w_up, down_t, qkv_t, out_t, segments):
@@ -223,27 +226,22 @@
 
 
 def order_kernel(coords, *refs):
-    parts, outs = refs[:4], refs[4:]
+    parts, out = refs[:4], refs[4]
     for bits in range(4):
-        zl, c = coords[0] ^ (bits >> 1), coords[3] ^ (bits & 1)
-        start = 0
-        for out in outs:
-            columns = out.shape[3]
-            out[zl, c] = parts[bits][:, start : start + columns]
-            start += columns
+        out[coords[0] ^ (bits >> 1), coords[3] ^ (bits & 1)] = parts[bits][:, : out.shape[3]]
 
 
 def order(coords, parts, columns):
     rows = parts[0].shape[0]
-    outs = pl.pallas_call(
+    out = pl.pallas_call(
         order_kernel,
         in_specs=[SCALARS] + [WHOLE] * 4,
-        out_specs=[WHOLE] * len(columns),
-        out_shape=[like((2, 2, rows, count)) for count in columns],
+        out_specs=WHOLE,
+        out_shape=like((2, 2, rows, columns)),
         compiler_params=params(16),
         name="order",
     )(coords, *parts)
-    return [out.reshape(2, 2 * rows, -1) for out in outs]
+    return out.reshape(4 * rows, columns)
 
 
 def join_kernel(*refs):
@@ -266,49 +264,6 @@
         compiler_params=params(16),
         name="join",
     )(*parts)
-
-
-def place_kernel(entries, coords, *refs):
-    parts, out, sems = refs[-2 - len(entries) : -2], refs[-2], refs[-1]
-    copies = []
-    for part, (y_bits, start) in zip(parts, entries):
-        for i in range(part.shape[0]):
-            chip = (coords[1] ^ (start + i)) * 4 + (coords[2] ^ y_bits)
-            copies.append(pltpu.make_async_copy(part.at[i], out.at[chip], sems.at[len(copies)]))
-            copies[-1].start()
-    for copy in copies:
-        copy.wait()
-
-
-def place(coords, buffer, parts, entries):
-    count = sum(part.shape[0] for part in parts)
-    buffers = [] if buffer is None else [buffer]
-    return pl.pallas_call(
-        functools.partial(place_kernel, entries),
-        in_specs=[SCALARS] + [ANY] * (len(buffers) + len(parts)),
-        out_specs=ANY,
-        out_shape=like((16,) + parts[0].shape[1:]),
-        scratch_shapes=[pltpu.SemaphoreType.DMA((count,))],
-        input_output_aliases={1: 0} if buffers else {},
-        compiler_params=params(16),
-        cost_estimate=cost(0, 4 * count * parts[0][0].size),
-        name="place",
-    )(coords, *buffers, *parts)
-
-
-def gather_line(shard, axis):
-    return join(shard, hop(shard, axis, 1), hop(shard, axis, 2), hop(shard, axis, 3))
-
-
-def gather_plane(coords, shard):
-    row = gather_line(shard, "x")
-    one, three = hop(row, "y", 1), hop(row, "y", 3)
-    half = row.shape[0] // 2
-    two_low, two_high = hop(three[:half], "y", 1), hop(one[half:], "y", 3)
-    buffer = place(coords, None, [row], [(0, 0)])
-    buffer = place(coords, buffer, [one, three], [(1, 0), (3, 0)])
-    buffer = place(coords, buffer, [two_low, two_high], [(2, 0), (2, half)])
-    return buffer.reshape(-1, buffer.shape[3])
 
 
 def tokens_kernel(mine_ref, other_ref, rows_ref, columns_ref):
@@ -365,6 +320,7 @@
     hidden = bias.shape[0]
     tile = 256
     tiles = hidden // tile
+    start = (weights.shape[1] - 2 * hidden) // tile
     column = lambda j: (0, j)
     return pl.pallas_call(
         mlp_kernel,
@@ -372,15 +328,15 @@
         in_specs=[
             pl.BlockSpec((2, rows, depth), lambda j: (0, 0, 0), pipeline_mode=pl.Buffered(1)),
             pl.BlockSpec((1, tile), column),
-            pl.BlockSpec((depth, tile), column),
-            pl.BlockSpec((depth, tile), lambda j: (0, tiles + j)),
+            pl.BlockSpec((depth, tile), lambda j: (0, start + j)),
+            pl.BlockSpec((depth, tile), lambda j: (0, start + tiles + j)),
         ],
         out_specs=[
             pl.BlockSpec((2, rows, tile), lambda j: (0, 0, j)),
             pl.BlockSpec((1, tile), column),
         ],
         out_shape=[like((2, rows, hidden)), like((1, hidden), F32)],
-        compiler_params=params(32),
+        compiler_params=params(60),
         cost_estimate=cost(4 * rows * depth * hidden, 20 * MIB),
         name="mlp",
     )(pair, bias.reshape(1, -1), weights, weights)
@@ -403,7 +359,7 @@
         ],
         out_specs=pl.BlockSpec((depth // 2, tile), lambda i, j, k: (k, i * tiles + j)),
         out_shape=like((depth, count * columns)),
-        compiler_params=params(40),
+        compiler_params=params(60),
         cost_estimate=cost(2 * depth * rows * count * columns, 2 * (pair_t.size + right.size * 2)),
         name="weight_grads",
     )(pair_t, right)
@@ -442,7 +398,7 @@
         out_specs=[WHOLE] * 5,
         out_shape=[full, full, full, half, half],
         scratch_shapes=[pltpu.VMEM((16, 2, block, tile), BF16)],
-        compiler_params=params(32),
+        compiler_params=params(60),
         cost_estimate=cost(2 * depth * rows * columns, 16 * MIB),
         name="head_grads",
     )(coords, pair_t, right)
@@ -475,13 +431,9 @@
             sends[i - 1][...] = total.astype(BF16)
 
 
-def scatter_blocks(chunks):
-    own, one, three, two_low, two_high = chunks
-    low, high = hop(two_low, "y", 1), hop(two_high, "y", 3)
-    three = hop(bump(three, low, 0), "y", 3)
-    one = hop(bump(one, high, 1), "y", 1)
+def near_sums(own, one, three):
     shape = own.shape[1:]
-    keep, *sends = pl.pallas_call(
+    return pl.pallas_call(
         near_kernel,
         in_specs=[WHOLE] * 3,
         out_specs=[WHOLE] * 4,
@@ -489,7 +441,6 @@
         compiler_params=params(16),
         name="near",
     )(own, one, three)
-    return [keep] + [hop(send, "x", bits) for send, bits in zip(sends, (1, 2, 3))]
 
 
 def cut_kernel(coords, mlp_ref, *refs):
@@ -537,19 +488,19 @@
         sums_ref[1:2, :] = jnp.sum(total * rows_ref[0].astype(F32), axis=0, keepdims=True)
 
 
-def combine(hidden_pair, side, right, start, stop, mlp_w, head_w, pair=None):
+def combine(hidden_pair, side, right, weights, width, pair=None):
     _, rows, hidden = hidden_pair.shape
-    depth = mlp_w.shape[0]
-    width, tile = stop - start, 256
-    where = start // width
+    depth, tile = weights.shape[0], 256
+    where = 0 if side == 0 else right.shape[1] // width - 1
+    first = right.shape[1] // hidden
     column = lambda i: (0, i)
     specs = [
         pl.BlockSpec((1, rows, hidden), lambda i: (side, 0, 0)),
-        pl.BlockSpec((tile, hidden), lambda i: (i, side)),
+        pl.BlockSpec((tile, hidden), lambda i: (i, first + side)),
         pl.BlockSpec((rows, width), lambda i: (0, where)),
         pl.BlockSpec((tile, width), lambda i: (i, where)),
     ]
-    arrays = [hidden_pair, mlp_w, right, head_w]
+    arrays = [hidden_pair, weights, right, weights]
     out_specs = [pl.BlockSpec((rows // 2, tile), column)] * 2
     shapes = [like((rows // 2, depth))] * 2
     if pair is not None:
@@ -563,7 +514,7 @@
         in_specs=specs,
         out_specs=out_specs,
         out_shape=shapes,
-        compiler_params=params(32),
+        compiler_params=params(60),
         cost_estimate=cost(2 * rows * depth * (hidden + width), 16 * MIB),
         name="combine",
     )(*arrays)
@@ -583,7 +534,7 @@
 
 def project(pair, bias, weights):
     rows, depth = pair.shape[1:]
-    width = weights.shape[1] // 4
+    width = bias.shape[0] // 3
     return pl.pallas_call(
         project_kernel,
         grid=(4,),
@@ -597,7 +548,7 @@
             pl.BlockSpec((rows, width), lambda j: (0, 0)),
         ],
         out_shape=[like((rows, 3 * width), F32), like((rows, width))],
-        compiler_params=params(32),
+        compiler_params=params(60),
         cost_estimate=cost(8 * rows * depth * width, 16 * MIB),
         name="project",
     )(pair, bias.reshape(1, -1), weights)
@@ -672,15 +623,11 @@
 
 def leave_kernel(tokens_ref, cot_ref, gain_ref, bias_ref, *refs):
     mixed_ref, grad_ref, branch_ref, normed_ref = refs[-4:]
-    branch, normed = refs[:4], refs[4:8]
-    total = branch[0][...]
-    for part in branch[1:]:
-        total = total + part[...].astype(F32)
-    turn(branch_ref, total, True)
-    total = normed[0][...]
-    for part in normed[1:]:
-        total = total + part[...].astype(F32)
-    turn(normed_ref, total, True)
+    for which, target in ((0, normed_ref), (1, branch_ref)):
+        total = refs[0][which]
+        for part in refs[1:4]:
+            total = total + part[which].astype(F32)
+        turn(target, total, True)
     rows, standard, scale = standardize(tokens_ref[...])
     mixed_ref[...] = (rows + branch_ref[...] + bias_ref[...]).astype(BF16)
     grad = normed_ref[...] * gain_ref[...]
@@ -689,17 +636,17 @@
     grad_ref[...] = cot_ref[...].astype(F32) + scale * (grad - level - standard * slope)
 
 
-def leave(tokens, cotangent, gain, bias, branches, normed):
+def leave(tokens, cotangent, gain, bias, sums):
     shape = tokens.shape
     return pl.pallas_call(
         leave_kernel,
-        in_specs=[WHOLE] * 12,
+        in_specs=[WHOLE] * 8,
         out_specs=[WHOLE] * 2,
         out_shape=[like(shape), like(shape, F32)],
         scratch_shapes=[pltpu.VMEM(shape, F32)] * 2,
         compiler_params=params(24),
         name="leave",
-    )(tokens, cotangent, gain.reshape(1, -1), bias.reshape(1, -1), *branches, *normed)
+    )(tokens, cotangent, gain.reshape(1, -1), bias.reshape(1, -1), *sums)
 
 
 def scatter_plane(grads):
@@ -732,13 +679,12 @@
     this_half = coords[4]
 
     parts = exchange(pack(coords, w_up, w_down.T, w_qkv.transpose(1, 0, 2), w_out.T, segments))
-    mlp_shard, head_shard = order(coords, parts, (2 * hidden, 4 * width))
-    mlp_w = lax.all_gather(mlp_shard, PLANE, axis=0, tiled=False).reshape(depth, 2 * hidden)
+    shard = order(coords, parts, 2 * hidden + 4 * width)
+    weights = lax.all_gather(shard, PLANE, axis=0, tiled=True)
 
     pair, grad_b_out = enter(tokens, cotangent, layernorm_gain, layernorm_bias)
-    head_shard, pair = lax.optimization_barrier((head_shard, pair))
+    _, pair = lax.optimization_barrier((shard, pair))
     near, far, opposite = flip(pair, "zl"), flip(pair, "zl", "mp"), flip(pair, "mp")
-    head_w = gather_plane(coords, head_shard)
     pair, pair_t = gather_tokens(pair, opposite, near, far)
 
     doc = jnp.stack([parts[k][0, -length:] for k in (0, 2, 1, 3)]).astype(jnp.int32)
@@ -763,24 +709,22 @@
     b_up_here = lax.dynamic_slice_in_dim(b_up, place_here * hidden, hidden)
     b_qkv_here = lax.dynamic_slice_in_dim(b_qkv, place_here * width, width, axis=1).reshape(-1)
 
-    pair, head_w = lax.optimization_barrier((pair, head_w))
-    hidden_pair, grad_b_up = mlp(pair, b_up_here, mlp_w)
+    tables = (cos_table, low_table, high_table, doc, index)
+    pair, tables = lax.optimization_barrier((pair, tables))
+    hidden_pair, grad_b_up = mlp(pair, b_up_here, weights)
     mlp_grads = scatter_plane(weight_grads(pair_t, hidden_pair, hidden // 2))
 
     pair, hidden_pair = lax.optimization_barrier((pair, hidden_pair))
-    linear, grad_attended = project(pair, b_qkv_here, head_w)
-    right = attention(
-        linear, grad_attended, (cos_table, low_table, high_table), doc, index, length
-    )
-    heads, hidden_pair = lax.optimization_barrier((head_grads(coords, pair_t, right), hidden_pair))
-    heads = scatter_blocks(heads)
-
-    mine, theirs, sums = combine(hidden_pair, 0, right, 0, 3 * width, mlp_w, head_w, pair)
-    normed = scatter_group(mine, theirs)
-    branches = scatter_group(*combine(hidden_pair, 1, right, 3 * width, 4 * width, mlp_w, head_w))
-    mixed, d_tokens = leave(
-        tokens, cotangent, layernorm_gain, b_out + b_down, branches, normed
-    )
+    linear, grad_attended = project(pair, b_qkv_here, weights)
+    right = attention(linear, grad_attended, tables[:3], *tables[3:], length)
+
+    chunks = head_grads(coords, pair_t, right)
+    chunks, hidden_pair = lax.optimization_barrier((chunks, hidden_pair))
+    own, one, three, two_low, two_high = chunks
+    low, high = hop(two_low, "y", 1), hop(two_high, "y", 3)
+    normed, normed_theirs, sums = combine(hidden_pair, 0, right, weights, 3 * width, pair)
+    normed_theirs = flip(normed_theirs, "c")
+    branch, branch_theirs = combine(hidden_pair, 1, right, weights, width)
 
     grad_b_heads = jnp.sum(right[:, : 3 * width].astype(F32), axis=0)
     slices = jnp.concatenate([grad_b_heads, grad_b_up[0]])
@@ -788,7 +732,25 @@
     spread = jnp.zeros((8,) + slices.shape, F32)
     spread = lax.dynamic_update_slice(spread, slices[None], (slot, 0))
     vector = jnp.concatenate([spread.reshape(-1), grad_b_out[0], sums.reshape(-1)])
-    vector = sum_everywhere(vector.reshape(-1, LANES)).reshape(-1)
+    vector = vector.reshape(-1, LANES)
+    vector = vector + flip(vector, "c")
+
+    low, high, normed_theirs, branch, branch_theirs, vector = lax.optimization_barrier(
+        (low, high, normed_theirs, branch, branch_theirs, vector)
+    )
+    branch_theirs = flip(branch_theirs, "c")
+    one, three = hop(bump(one, high, 1), "y", 1), hop(bump(three, low, 0), "y", 3)
+    keep, sends = fold(normed, normed_theirs, branch, branch_theirs)
+    along_z = [flip(sends[1], "zl"), flip(sends[2], "zl", "mp"), flip(sends[0], "mp")]
+    one, three, keep, vector = lax.optimization_barrier((one, three, keep, vector))
+    heads = near_sums(own, one, three)
+    heads = [heads[0]] + [hop(part, "x", bits) for part, bits in zip(heads[1:], (1, 2, 3))]
+    parts, vector = lax.optimization_barrier((cut(coords, mlp_grads, heads), vector))
+    parts = exchange(parts)
+    vector = sum_plane(sum_along_z(vector)).reshape(-1)
+    mixed, d_tokens = leave(
+        tokens, cotangent, layernorm_gain, b_out + b_down, [keep] + along_z
+    )
     spread, whole = vector[: spread.size].reshape(8, -1), vector[spread.size :].reshape(3, depth)
     spread = lax.dynamic_slice_in_dim(spread, this_half * 4, 4)
     grad_b_qkv = spread[:, : 3 * width].reshape(4, 3, width).transpose(1, 0, 2).reshape(3, 4 * width)
@@ -796,7 +758,6 @@
     sums = whole[1:].reshape(2, 16, 2, depth // 32).transpose(0, 2, 1, 3).reshape(2, depth)
     grad_gain = (sums[1] - layernorm_bias * sums[0]) / layernorm_gain
 
-    parts = exchange(cut(coords, mlp_grads, heads))
     grad_up_w, grad_down_w, grad_qkv_w, grad_out_w = unpack(coords, parts, hidden, width)
     return (
         mixed,

time: 404 us -> 358 us (0.89)
  starting transfers between devices: 72.4 us -> 45.1 us
  local copies, waits for them, and re-layouts: 56.4 us -> 29.4 us
  Pallas kernels: 119 us -> 132 us
  waiting for transfers between devices: 133 us -> 128 us
    ppermute x20 -> x13, waiting for transfers between devices: 67.7 us -> 30.7 us  [hop(): return lax.ppermute(value, axis, [(i, i ^ bits) for i in range(4)])]
    unnamed x117 -> x85, local copies, waits for them, and re-layouts: 47 us -> 23 us
    ppermute x22 -> x19, starting transfers between devices: 50.9 us -> 31 us  [flip(): return lax.ppermute(value, axes, [(i, count - 1 - i) for i in range(count)])]
    ppermute x22 -> x19, waiting for transfers between devices: 65.6 us -> 83.8 us  [flip(): return lax.ppermute(value, axes, [(i, count - 1 - i) for i in range(count)])]
    all_gather x1, waiting for transfers between devices: 0.01 us -> 13.4 us  [per_device(): weights = lax.all_gather(shard, PLANE, axis=0, tiled=True)]
    pallas_call x7 -> x3, Pallas kernels: 16.1 us -> 8.14 us  [the longest x1 4.63 us: leave(): pl.pallas_call(leave_kernel, in_specs=[WHOLE] * 8, out_specs=[WHOLE] * 2,...]
    ppermute x20 -> x13, starting transfers between devices: 21.4 us -> 14 us  [hop(): return lax.ppermute(value, axis, [(i, i ^ bits) for i in range(4)])]
    pallas_call x1, Pallas kernels: 6.09 us -> 10.6 us  [project(): pl.pallas_call(project_kernel, grid=(4,), in_specs=[pl.BlockSpec((1, rows...]
  transfers between devices with their start and end apart: 44 -> 34, of which waited for: 18 -> 14; matrix products, arithmetic and copies ran while one was open for 4% -> 4% of each run, Pallas kernels for 22% -> 27%
where the time goes in v3:
time: 358 us; the launch traced here: 356 us
  Pallas kernels  132 us (37%)
  waiting for transfers between devices  128 us (36%)
  starting transfers between devices  45.1 us (13%)
  local copies, waits for them, and re-layouts  29.4 us (8%)
  between operations  14.5 us (4%)
  other arithmetic  7.06 us (2%)
    ppermute x19, waiting for transfers between devices, flip(): return lax.ppermute(value, axes, [(i, count - 1 - i) for i in range(count)])  83.8 us
    ppermute x19, starting transfers between devices, flip(): return lax.ppermute(value, axes, [(i, count - 1 - i) for i in range(count)])  31 us
    ppermute x13, waiting for transfers between devices, hop(): return lax.ppermute(value, axis, [(i, i ^ bits) for i in range(4)])  30.7 us
    pallas_call x2, Pallas kernels, combine(): pl.pallas_call(functools.partial(combine_kernel, 2), grid=(depth // tile,...  25 us
    unnamed x85, local copies, waits for them, and re-layouts  23 us
    pallas_call x1, Pallas kernels, attention(): pl.pallas_call(attention_kernel, grid=(count,), in_specs=[blocks(3 * widt...  18 us
    pallas_call x1, Pallas kernels, mlp(): pl.pallas_call(mlp_kernel, grid=(tiles,), in_specs=[pl.BlockSpec((2, rows...  17.2 us
    pallas_call x1, Pallas kernels, weight_grads(): pl.pallas_call(grads_kernel, grid=(count, tiles, 2), in_specs=[pl.BlockSp...  16.3 us
  transfers between devices with their start and end apart: 34, of which 14 were waited for; matrix products, arithmetic and copies ran while one was open for 4% of the time, Pallas kernels for 27%

profile of v3, /device:TPU:1, one launch (start us, length us, event | category | flops | bytes accessed | tf_op | source)
XLA Modules:
  0.0 356.2 jit_solution(7975968070430012660)
XLA Ops:
  15.7 5.4 %collective-permute-done.1.refs_2_ = bf16[32,3328]{1,0:T(8,128)(2,1)S(1)} collective-permute-done((bf16[32,3328]{1,0:T(8,128)(2,1)S(1)}, bf16[32,3328]{1,0:T(8,128)(2,1)S(1)}, u32[]{:S(2)}, u32[]{:S(2)}) %collective-permute-start.1) | collective-permute-done | bytes 213024 | tf_op jit(solution)/shard_map/ppermute | solution.py:29
  21.1 4.6 %collective-permute-done.2.refs_3_ = bf16[32,3328]{1,0:T(8,128)(2,1)S(1)} collective-permute-done((bf16[32,3328]{1,0:T(8,128)(2,1)S(1)}, bf16[32,3328]{1,0:T(8,128)(2,1)S(1)}, u32[]{:S(2)}, u32[]{:S(2)}) %collective-permute-start.2) | collective-permute-done | bytes 213024 | tf_op jit(solution)/shard_map/ppermute | solution.py:29
  28.2 3.5 collective-permute-start.3
  32.5 22.7 %collective-permute-done.3.refs_1_ = bf16[2,128,2048]{2,1,0:T(8,128)(2,1)S(1)} collective-permute-done((bf16[2,128,2048]{2,1,0:T(8,128)(2,1)S(1)}, bf16[2,128,2048]{2,1,0:T(8,128)(2,1)S(1)}, u32[]{:S(2)}, u32[]{:S(2)}) %collective-permute-start.3) | collective-permute-done | bytes 1048608 | tf_op jit(solution)/shard_map/ppermute | solution.py:29
  55.2 23.0 %collective-permute-done.4.refs_2_ = bf16[2,128,2048]{2,1,0:T(8,128)(2,1)S(1)} collective-permute-done((bf16[2,128,2048]{2,1,0:T(8,128)(2,1)S(1)}, bf16[2,128,2048]{2,1,0:T(8,128)(2,1)S(1)}, u32[]{:S(2)}, u32[]{:S(2)}) %collective-permute-start.4) | collective-permute-done | bytes 1048608 | tf_op jit(solution)/shard_map/ppermute | solution.py:29
  84.0 4.5 %collective-permute-done.6.other_ref = bf16[4,2,128,2048]{3,2,1,0:T(8,128)(2,1)} collective-permute-done((bf16[4,2,128,2048]{3,2,1,0:T(8,128)(2,1)}, bf16[4,2,128,2048]{3,2,1,0:T(8,128)(2,1)}, u32[]{:S(2)}, u32[]{:S(2)}) %collective-permute-start.6) | collective-permute-done | bytes 4194336 | tf_op jit(solution)/shard_map/ppermute | solution.py:29
  88.5 13.5 %tokens.1 = (bf16[2,1024,2048]{2,1,0:T(8,128)(2,1)S(1)}, bf16[2,2048,1024]{2,1,0:T(8,128)(2,1)}) custom-call(bf16[4,2,128,2048]{3,2,1,0:T(8,128)(2,1)} %join.1.mine_ref, bf16[4,2,128,2048]{3,2,1,0:T(8,128)(2,1)} %collective-permute-done.6.other_ref), custom_call_target="tpu_custom_call" | custom-call | bytes 33554432 | tf_op jit(solution)/shard_map/tokens/pallas_call | solution.py:286
  105.6 13.4 %all-gather.2.cloned.1.call-done.up_ref.down_ref.weights_ref.refs_1_.refs_3_ = bf16[2048,3072]{1,0:T(8,128)(2,1)} async-done(((bf16[128,3072]{1,0:T(8,128)(2,1)}), bf16[2048,3072]{1,0:T(8,128)(2,1)}) %all-gather.2.cloned.1.call-update) | async-done | bytes 12582928 | tf_op jit(solution)/shard_map/all_gather | solution.py:683
  119.0 17.2 %mlp.1 = (bf16[2,1024,1024]{2,1,0:T(8,128)(2,1)}, f32[1,1024]{1,0:T(1,128)}) custom-call(bf16[2,1024,2048]{2,1,0:T(8,128)(2,1)} %copy-done.2, f32[1,1024]{1,0:T(1,128)} %bitcast.103, bf16[2048,3072]{1,0:T(8,128)(2,1)} %all-gather.2.cloned.1.call-done.up_ref.down_ref.weights_ref.refs_1_.refs_3_, ...), custom_call_target="tpu_custom_call" | custom-call | flops 8589934592 | bytes 20971520 | tf_op jit(solution)/shard_map/mlp/pallas_call | solution.py:325
  136.2 16.3 %weight_grads.1 = bf16[2048,2048]{1,0:T(8,128)(2,1)} custom-call(bf16[2,2048,1024]{2,1,0:T(8,128)(2,1)} %get-tuple-element.88.left_ref, bf16[2,1024,1024]{2,1,0:T(8,128)(2,1)} %get-tuple-element.109.refs_0_.right_ref), custom_call_target="tpu_custom_call" | custom-call | flops 8589934592 | bytes 16777216 | tf_op jit(solution)/shard_map/weight_grads/pallas_call | solution.py:353
  159.4 10.6 %project.1 = (f32[1024,768]{1,0:T(8,128)}, bf16[1024,256]{1,0:T(8,128)(2,1)}) custom-call(bf16[2,1024,2048]{2,1,0:T(8,128)(2,1)} %copy-done.2, f32[1,768]{1,0:T(1,128)} %bitcast.110, bf16[2048,3072]{1,0:T(8,128)(2,1)} %all-gather.2.cloned.1.call-done.up_ref.down_ref.weights_ref.refs_1_.refs_3_), custom_call_target="tpu_custom_call" | custom-call | flops 4294967296 | bytes 16777216 | tf_op jit(solution)/shard_map/project/pallas_call | solution.py:538
  170.0 18.0 %attention.1.right_ref.refs_2_ = bf16[1024,1024]{1,0:T(8,128)(2,1)} custom-call(f32[1024,768]{1,0:T(8,128)} %get-tuple-element.93.linear_ref, bf16[1024,256]{1,0:T(8,128)(2,1)} %get-tuple-element.94.grad_ref, f32[1024,128]{1,0:T(8,128)} %copy.41.cos_ref, f32[1024,128]{1,0:T(8,128)} %copy.42.low_ref, f32[1024,128]{1,0:T(8,128)} %copy.43.high_ref, ...), custom_call_target="tpu_custom_call" | custom-call | flops 18874368000 | bytes 8388608 | tf_op jit(solution)/shard_map/attention/pallas_call | solution.py:145
  188.1 11.1 %head_grads.1 = (bf16[4,2,64,1024]{3,2,1,0:T(8,128)(2,1)}, bf16[4,2,64,1024]{3,2,1,0:T(8,128)(2,1)}, bf16[4,2,64,1024]{3,2,1,0:T(8,128)(2,1)}, bf16[2,2,64,1024]{3,2,1,0:T(8,128)(2,1)}, bf16[2,2,64,1024]{3,2,1,0:T(8,128)(2,1)}) custom-call(s32[5]{0:T(128)} %copy-done.28, bf16[2,2048,1024]{2,1,0:T(8,128)(2,1)} %get-tuple-element.88.left_ref, ...), custom_call_target="tpu_custom_call" | custom-call | flops 4294967296 | bytes 16777216 | tf_op jit(solution)/shard_map/head_grads/pallas_call | solution.py:390
  199.2 13.9 %combine.2 = (bf16[512,2048]{1,0:T(8,128)(2,1)}, bf16[512,2048]{1,0:T(8,128)(2,1)}, f32[2,2048]{1,0:T(2,128)}) custom-call(bf16[2,1024,1024]{2,1,0:T(8,128)(2,1)} %get-tuple-element.109.refs_0_.right_ref, bf16[2048,3072]{1,0:T(8,128)(2,1)} %all-gather.2.cloned.1.call-done.up_ref.down_ref.weights_ref.refs_1_.refs_3_, ...), custom_call_target="tpu_custom_call" | custom-call | flops 7516192768 | bytes 16777216 | tf_op jit(solution)/shard_map/combine/pallas_call | solution.py:511
  220.5 11.1 %combine.3 = (bf16[512,2048]{1,0:T(8,128)(2,1)}, bf16[512,2048]{1,0:T(8,128)(2,1)}) custom-call(bf16[2,1024,1024]{2,1,0:T(8,128)(2,1)} %get-tuple-element.109.refs_0_.right_ref, bf16[2048,3072]{1,0:T(8,128)(2,1)} %all-gather.2.cloned.1.call-done.up_ref.down_ref.weights_ref.refs_1_.refs_3_, bf16[1024,1024]{1,0:T(8,128)(2,1)} %attention.1.right_ref.refs_2_, ...), custom_call_target="tpu_custom_call" | custom-call | flops 5368709120 | bytes 16777216 | tf_op jit(solution)/shard_map/combine/pallas_call | solution.py:511
  233.5 3.6 %collective-permute-start.13 = (bf16[512,2048]{1,0:T(8,128)(2,1)}, bf16[512,2048]{1,0:T(8,128)(2,1)S(1)}, u32[]{:S(2)}, u32[]{:S(2)}) collective-permute-start(bf16[512,2048]{1,0:T(8,128)(2,1)} %get-tuple-element.122), channel_id=1, source_target_pairs={{0,2},{2,0},{1,3},{3,1},{4,6},{6,4},{5,7},{7,5},{8,10},{10,8},{9,1... | collective-permute-start | bytes 6291464 | tf_op jit(solution)/shard_map/ppermute | solution.py:29
  249.9 13.6 %collective-permute-done.11.one_ref = bf16[4,2,64,1024]{3,2,1,0:T(8,128)(2,1)S(1)} collective-permute-done((bf16[4,2,64,1024]{3,2,1,0:T(8,128)(2,1)}, bf16[4,2,64,1024]{3,2,1,0:T(8,128)(2,1)S(1)}, u32[]{:S(2)}, u32[]{:S(2)}) %collective-permute-start.11) | collective-permute-done | bytes 1048608 | tf_op jit(solution)/shard_map/ppermute | solution.py:33
  274.7 4.1 %collective-permute-done.18 = bf16[2,64,1024]{2,1,0:T(8,128)(2,1)S(1)} collective-permute-done((bf16[2,64,1024]{2,1,0:T(8,128)(2,1)S(1)}, bf16[2,64,1024]{2,1,0:T(8,128)(2,1)S(1)}, u32[]{:S(2)}, u32[]{:S(2)}) %collective-permute-start.18) | collective-permute-done | bytes 262176 | tf_op jit(solution)/shard_map/ppermute | solution.py:33
  279.5 5.1 %collective-permute-done.19 = bf16[2,64,1024]{2,1,0:T(8,128)(2,1)S(1)} collective-permute-done((bf16[2,64,1024]{2,1,0:T(8,128)(2,1)S(1)}, bf16[2,64,1024]{2,1,0:T(8,128)(2,1)S(1)}, u32[]{:S(2)}, u32[]{:S(2)}) %collective-permute-start.19) | collective-permute-done | bytes 262176 | tf_op jit(solution)/shard_map/ppermute | solution.py:33
  295.0 4.1 %collective-permute-done.21 = f32[160,128]{1,0:T(8,128)S(1)} collective-permute-done((f32[160,128]{1,0:T(8,128)S(1)}, f32[160,128]{1,0:T(8,128)S(1)}, u32[]{:S(2)}, u32[]{:S(2)}) %collective-permute-start.21) | collective-permute-done | bytes 81952 | tf_op jit(solution)/shard_map/ppermute | solution.py:29
  299.2 19.5 %collective-permute-done.22 = f32[160,128]{1,0:T(8,128)S(1)} collective-permute-done((f32[160,128]{1,0:T(8,128)S(1)}, f32[160,128]{1,0:T(8,128)S(1)}, u32[]{:S(2)}, u32[]{:S(2)}) %collective-permute-start.22) | collective-permute-done | bytes 81952 | tf_op jit(solution)/shard_map/ppermute | solution.py:29
  322.0 4.0 %collective-permute-start.29 = (bf16[32,3072]{1,0:T(8,128)(2,1)S(1)}, bf16[32,3072]{1,0:T(8,128)(2,1)S(1)}, u32[]{:S(2)}, u32[]{:S(2)}) collective-permute-start(bf16[32,3072]{1,0:T(8,128)(2,1)S(1)} %get-tuple-element.145), channel_id=1, source_target_pairs={{0,2},{2,0},{1,3},{3,1},{4,6},{6,4},{5,7},{7,5},{8,10},{10,8},{9,1... | collective-permute-start | bytes 589832 | tf_op jit(solution)/shard_map/ppermute | solution.py:29
  326.0 4.9 %collective-permute-start.31 = (bf16[32,3072]{1,0:T(8,128)(2,1)}, bf16[32,3072]{1,0:T(8,128)(2,1)}, u32[]{:S(2)}, u32[]{:S(2)}) collective-permute-start(bf16[32,3072]{1,0:T(8,128)(2,1)} %get-tuple-element.147), channel_id=1, source_target_pairs={{0,66},{2,64},{64,2},{66,0},{1,67},{3,65},{65,3},{67,1},{4,70},{6,... | collective-permute-start | bytes 589832 | tf_op jit(solution)/shard_map/ppermute | solution.py:29
  337.9 4.6 %leave.1 = (bf16[128,2048]{1,0:T(8,128)(2,1)}, f32[128,2048]{1,0:T(8,128)}) custom-call(bf16[128,2048]{1,0:T(8,128)(2,1)S(1)} %copy-done.3, bf16[128,2048]{1,0:T(8,128)(2,1)S(1)} %copy-done.4, f32[1,2048]{1,0:T(1,128)S(1)} %bitcast.83, f32[1,2048]{1,0:T(1,128)S(1)} %bitcast.86, f32[2,128,2048]{2,1,0:T(8,128)S(1)} %get-tuple-element.125.refs_0_, ...), custom_call_target="tpu_custom_call" | custom-call | tf_op jit(solution)/shard_map/leave/pallas_call | solution.py:641
  (204 shorter events, 89.3 us)
Async XLA Ops:
  7.2 111.8 %all-gather.2.cloned.1.call-start = ((), (), s32[]{:S(2)}) async-start(), calls=%async_computation.1 | async-start | bytes 13369344 | tf_op jit(solution)/shard_map/all_gather | solution.py:683
  27.2 258.1 %reduce-scatter.2.cloned.1.call-start = ((), (), s32[]{:S(2)}) async-start(), calls=%async_computation.2 | async-start | bytes 8912896 | tf_op jit(solution)/shard_map/reduce_scatter | solution.py:653
  28.2 27.0 %collective-permute-start.3 = (bf16[2,128,2048]{2,1,0:T(8,128)(2,1)S(1)}, bf16[2,128,2048]{2,1,0:T(8,128)(2,1)S(1)}, u32[]{:S(2)}, u32[]{:S(2)}) collective-permute-start(bf16[2,128,2048]{2,1,0:T(8,128)(2,1)S(1)} %get-tuple-element.87.refs_0_), channel_id=1, source_target_pairs={{0,1},{1,0},{2,3},{3,2},{4,5},{5,4},{6,7},{7,6},{8,9},{9,8},{10,11... | collective-permute-start | bytes 3145736 | tf_op jit(solution)/shard_map/ppermute | solution.py:29
  31.7 46.4 %collective-permute-start.4 = (bf16[2,128,2048]{2,1,0:T(8,128)(2,1)S(1)}, bf16[2,128,2048]{2,1,0:T(8,128)(2,1)S(1)}, u32[]{:S(2)}, u32[]{:S(2)}) collective-permute-start(bf16[2,128,2048]{2,1,0:T(8,128)(2,1)S(1)} %get-tuple-element.87.refs_0_), channel_id=1, source_target_pairs={{0,64},{64,0},{1,65},{65,1},{2,66},{66,2},{3,67},{67,3},{4,68},{68... | collective-permute-start | bytes 3145736 | tf_op jit(solution)/shard_map/ppermute | solution.py:29
  32.5 45.7 %collective-permute-start.5 = (bf16[2,128,2048]{2,1,0:T(8,128)(2,1)S(1)}, bf16[2,128,2048]{2,1,0:T(8,128)(2,1)S(1)}, u32[]{:S(2)}, u32[]{:S(2)}) collective-permute-start(bf16[2,128,2048]{2,1,0:T(8,128)(2,1)S(1)} %get-tuple-element.87.refs_0_), channel_id=1, source_target_pairs={{0,65},{1,64},{64,1},{65,0},{2,67},{3,66},{66,3},{67,2},{4,69},{5,... | collective-permute-start | bytes 3145736 | tf_op jit(solution)/shard_map/ppermute | solution.py:29
  213.0 20.4 %collective-permute-start.9 = (bf16[512,2048]{1,0:T(8,128)(2,1)}, bf16[512,2048]{1,0:T(8,128)(2,1)S(1)}, u32[]{:S(2)}, u32[]{:S(2)}) collective-permute-start(bf16[512,2048]{1,0:T(8,128)(2,1)} %get-tuple-element.110), channel_id=1, source_target_pairs={{0,2},{2,0},{1,3},{3,1},{4,6},{6,4},{5,7},{7,5},{8,10},{10,8},{9,1... | collective-permute-start | bytes 6291464 | tf_op jit(solution)/shard_map/ppermute | solution.py:29
  214.0 17.6 %collective-permute-start.7 = (bf16[2,2,64,1024]{3,2,1,0:T(8,128)(2,1)}, bf16[2,2,64,1024]{3,2,1,0:T(8,128)(2,1)}, u32[]{:S(2)}, u32[]{:S(2)}) collective-permute-start(bf16[2,2,64,1024]{3,2,1,0:T(8,128)(2,1)} %get-tuple-element.107), channel_id=1, source_target_pairs={{0,4},{4,0},{8,12},{12,8},{1,5},{5,1},{9,13},{13,9},{2,6},{6,2},{1... | collective-permute-start | bytes 1572872 | tf_op jit(solution)/shard_map/ppermute | solution.py:33
  215.0 18.5 %collective-permute-start.8 = (bf16[2,2,64,1024]{3,2,1,0:T(8,128)(2,1)}, bf16[2,2,64,1024]{3,2,1,0:T(8,128)(2,1)}, u32[]{:S(2)}, u32[]{:S(2)}) collective-permute-start(bf16[2,2,64,1024]{3,2,1,0:T(8,128)(2,1)} %get-tuple-element.108), channel_id=1, source_target_pairs={{0,12},{4,8},{8,4},{12,0},{1,13},{5,9},{9,5},{13,1},{2,14},{6,10},... | collective-permute-start | bytes 1572872 | tf_op jit(solution)/shard_map/ppermute | solution.py:33
  219.5 12.1 %collective-permute-start.10 = (f32[160,128]{1,0:T(8,128)S(1)}, f32[160,128]{1,0:T(8,128)S(1)}, u32[]{:S(2)}, u32[]{:S(2)}) collective-permute-start(f32[160,128]{1,0:T(8,128)S(1)} %maximum_bitcast_fusion), channel_id=1, source_target_pairs={{0,2},{2,0},{1,3},{3,1},{4,6},{6,4},{5,7},{7,5},{8,10},{10,8},{9,1... | collective-permute-start | bytes 245768 | tf_op jit(solution)/shard_map/ppermute | solution.py:29
  233.5 10.5 %collective-permute-start.13 = (bf16[512,2048]{1,0:T(8,128)(2,1)}, bf16[512,2048]{1,0:T(8,128)(2,1)S(1)}, u32[]{:S(2)}, u32[]{:S(2)}) collective-permute-start(bf16[512,2048]{1,0:T(8,128)(2,1)} %get-tuple-element.122), channel_id=1, source_target_pairs={{0,2},{2,0},{1,3},{3,1},{4,6},{6,4},{5,7},{7,5},{8,10},{10,8},{9,1... | collective-permute-start | bytes 6291464 | tf_op jit(solution)/shard_map/ppermute | solution.py:29
  239.3 24.2 %collective-permute-start.11 = (bf16[4,2,64,1024]{3,2,1,0:T(8,128)(2,1)}, bf16[4,2,64,1024]{3,2,1,0:T(8,128)(2,1)S(1)}, u32[]{:S(2)}, u32[]{:S(2)}) collective-permute-start(bf16[4,2,64,1024]{3,2,1,0:T(8,128)(2,1)} %bump.2), channel_id=1, source_target_pairs={{0,4},{4,0},{8,12},{12,8},{1,5},{5,1},{9,13},{13,9},{2,6},{6,2},{1... | collective-permute-start | bytes 3145736 | tf_op jit(solution)/shard_map/ppermute | solution.py:33
  240.7 26.0 %collective-permute-start.12 = (bf16[4,2,64,1024]{3,2,1,0:T(8,128)(2,1)S(1)}, bf16[4,2,64,1024]{3,2,1,0:T(8,128)(2,1)S(1)}, u32[]{:S(2)}, u32[]{:S(2)}) collective-permute-start(bf16[4,2,64,1024]{3,2,1,0:T(8,128)(2,1)S(1)} %bump.3), channel_id=1, source_target_pairs={{0,12},{4,8},{8,4},{12,0},{1,13},{5,9},{9,5},{13,1},{2,14},{6,10},... | collective-permute-start | bytes 3145736 | tf_op jit(solution)/shard_map/ppermute | solution.py:33
  248.7 71.8 %collective-permute-start.14 = (bf16[2,128,2048]{2,1,0:T(8,128)(2,1)}, bf16[2,128,2048]{2,1,0:T(8,128)(2,1)}, u32[]{:S(2)}, u32[]{:S(2)}) collective-permute-start(bf16[2,128,2048]{2,1,0:T(8,128)(2,1)} %get-tuple-element.126), channel_id=1, source_target_pairs={{0,64},{64,0},{1,65},{65,1},{2,66},{66,2},{3,67},{67,3},{4,68},{68... | collective-permute-start | bytes 3145736 | tf_op jit(solution)/shard_map/ppermute | solution.py:29
  267.9 63.7 %collective-permute-start.15 = (bf16[2,128,2048]{2,1,0:T(8,128)(2,1)}, bf16[2,128,2048]{2,1,0:T(8,128)(2,1)}, u32[]{:S(2)}, u32[]{:S(2)}) collective-permute-start(bf16[2,128,2048]{2,1,0:T(8,128)(2,1)} %get-tuple-element.127), channel_id=1, source_target_pairs={{0,65},{1,64},{64,1},{65,0},{2,67},{3,66},{66,3},{67,2},{4,69},{5,... | collective-permute-start | bytes 3145736 | tf_op jit(solution)/shard_map/ppermute | solution.py:29
  270.1 62.0 %collective-permute-start.16 = (bf16[2,128,2048]{2,1,0:T(8,128)(2,1)}, bf16[2,128,2048]{2,1,0:T(8,128)(2,1)}, u32[]{:S(2)}, u32[]{:S(2)}) collective-permute-start(bf16[2,128,2048]{2,1,0:T(8,128)(2,1)} %get-tuple-element.128), channel_id=1, source_target_pairs={{0,1},{1,0},{2,3},{3,2},{4,5},{5,4},{6,7},{7,6},{8,9},{9,8},{10,11... | collective-permute-start | bytes 3145736 | tf_op jit(solution)/shard_map/ppermute | solution.py:29
  274.4 10.2 %collective-permute-start.19 = (bf16[2,64,1024]{2,1,0:T(8,128)(2,1)S(1)}, bf16[2,64,1024]{2,1,0:T(8,128)(2,1)S(1)}, u32[]{:S(2)}, u32[]{:S(2)}) collective-permute-start(bf16[2,64,1024]{2,1,0:T(8,128)(2,1)S(1)} %get-tuple-element.137), channel_id=1, source_target_pairs={{0,48},{16,32},{32,16},{48,0},{1,49},{17,33},{33,17},{49,1},{2,50}... | collective-permute-start | bytes 786440 | tf_op jit(solution)/shard_map/ppermute | solution.py:33
  294.6 24.1 %collective-permute-start.22 = (f32[160,128]{1,0:T(8,128)S(1)}, f32[160,128]{1,0:T(8,128)S(1)}, u32[]{:S(2)}, u32[]{:S(2)}) collective-permute-start(f32[160,128]{1,0:T(8,128)S(1)} %fusion.1), channel_id=1, source_target_pairs={{0,65},{1,64},{64,1},{65,0},{2,67},{3,66},{66,3},{67,2},{4,69},{5,... | collective-permute-start | bytes 245768 | tf_op jit(solution)/shard_map/ppermute | solution.py:29
  299.2 19.5 %collective-permute-start.20 = (f32[160,128]{1,0:T(8,128)S(1)}, f32[160,128]{1,0:T(8,128)S(1)}, u32[]{:S(2)}, u32[]{:S(2)}) collective-permute-start(f32[160,128]{1,0:T(8,128)S(1)} %fusion.1), channel_id=1, source_target_pairs={{0,64},{64,0},{1,65},{65,1},{2,66},{66,2},{3,67},{67,3},{4,68},{68... | collective-permute-start | bytes 245768 | tf_op jit(solution)/shard_map/ppermute | solution.py:29
  322.0 11.9 %collective-permute-start.29 = (bf16[32,3072]{1,0:T(8,128)(2,1)S(1)}, bf16[32,3072]{1,0:T(8,128)(2,1)S(1)}, u32[]{:S(2)}, u32[]{:S(2)}) collective-permute-start(bf16[32,3072]{1,0:T(8,128)(2,1)S(1)} %get-tuple-element.145), channel_id=1, source_target_pairs={{0,2},{2,0},{1,3},{3,1},{4,6},{6,4},{5,7},{7,5},{8,10},{10,8},{9,1... | collective-permute-start | bytes 589832 | tf_op jit(solution)/shard_map/ppermute | solution.py:29
  326.0 16.5 %collective-permute-start.30 = (bf16[32,3072]{1,0:T(8,128)(2,1)}, bf16[32,3072]{1,0:T(8,128)(2,1)S(1)}, u32[]{:S(2)}, u32[]{:S(2)}) collective-permute-start(bf16[32,3072]{1,0:T(8,128)(2,1)} %get-tuple-element.146), channel_id=1, source_target_pairs={{0,64},{64,0},{1,65},{65,1},{2,66},{66,2},{3,67},{67,3},{4,68},{68... | collective-permute-start | bytes 589832 | tf_op jit(solution)/shard_map/ppermute | solution.py:29
  326.0 16.5 %collective-permute-start.31 = (bf16[32,3072]{1,0:T(8,128)(2,1)}, bf16[32,3072]{1,0:T(8,128)(2,1)}, u32[]{:S(2)}, u32[]{:S(2)}) collective-permute-start(bf16[32,3072]{1,0:T(8,128)(2,1)} %get-tuple-element.147), channel_id=1, source_target_pairs={{0,66},{2,64},{64,2},{66,0},{1,67},{3,65},{65,3},{67,1},{4,70},{6,... | collective-permute-start | bytes 589832 | tf_op jit(solution)/shard_map/ppermute | solution.py:29
  331.5 13.2 %collective-permute-start.27 = (f32[160,128]{1,0:T(8,128)}, f32[160,128]{1,0:T(8,128)}, u32[]{:S(2)}, u32[]{:S(2)}) collective-permute-start(f32[160,128]{1,0:T(8,128)} %add_add_fusion.1), channel_id=1, source_target_pairs={{0,4},{4,0},{8,12},{12,8},{1,5},{5,1},{9,13},{13,9},{2,6},{6,2},{1... | collective-permute-start | bytes 245768 | tf_op jit(solution)/shard_map/ppermute | solution.py:33
  332.2 12.5 %collective-permute-start.28 = (f32[160,128]{1,0:T(8,128)}, f32[160,128]{1,0:T(8,128)}, u32[]{:S(2)}, u32[]{:S(2)}) collective-permute-start(f32[160,128]{1,0:T(8,128)} %add_add_fusion.1), channel_id=1, source_target_pairs={{0,12},{4,8},{8,4},{12,0},{1,13},{5,9},{9,5},{13,1},{2,14},{6,10},... | collective-permute-start | bytes 245768 | tf_op jit(solution)/shard_map/ppermute | solution.py:33
  334.0 10.7 %collective-permute-start.26 = (f32[160,128]{1,0:T(8,128)}, f32[160,128]{1,0:T(8,128)}, u32[]{:S(2)}, u32[]{:S(2)}) collective-permute-start(f32[160,128]{1,0:T(8,128)} %add_add_fusion.1), channel_id=1, source_target_pairs={{0,8},{4,12},{8,0},{12,4},{1,9},{5,13},{9,1},{13,5},{2,10},{6,14},... | collective-permute-start | bytes 245768 | tf_op jit(solution)/shard_map/ppermute | solution.py:33
  (46 other events, 529.6 us)
Sparse Core Ops, SparseCore 0:
  27.3 91.6 all-gather.1
  152.6 87.6 reduce-scatter.1

commit v4 on v3

v4 whole, which is shorter than its diff:
```python
import functools

import jax
import jax.numpy as jnp
from jax import lax
from jax.experimental import pallas as pl
from jax.experimental.pallas import tpu as pltpu
from jax.sharding import Mesh, PartitionSpec as P

HEAD_DIM = 64
ROT = 32
HALF = ROT // 2
LANES = 128
EPSILON = 1e-05

AXES = ("zl", "x", "y", "c", "mp")
SIZES = (2, 4, 4, 2, 2)
PLANE = ("x", "y")
PAIR = ("zl", "c")

BF16 = jnp.bfloat16
F32 = jnp.float32
MIB = 1024 * 1024
GIGA = 1000 * MIB
ANY = pl.BlockSpec(memory_space=pl.ANY)
WHOLE = pl.BlockSpec(memory_space=pltpu.VMEM)
SCALARS = pl.BlockSpec(memory_space=pltpu.SMEM)


def flip(value, *axes):
    count = 2 ** len(axes)
    return lax.ppermute(value, axes, [(i, count - 1 - i) for i in range(count)])


def hop(value, axis, bits):
    return lax.ppermute(value, axis, [(i, i ^ bits) for i in range(4)])


def fold_kernel(*refs):
    inputs, keep_ref, sends = refs[:4], refs[4], refs[5:]
    rows = keep_ref.shape[1]

    def add(mine_ref, theirs_ref):
        for which in range(2):
            for i in range(4):
                block = slice(i * rows, (i + 1) * rows)
                total = mine_ref[which, block, :].astype(F32) + theirs_ref[which, block, :].astype(F32)
                if i == 0:
                    keep_ref[which] = total
                else:
                    sends[i - 1][which] = total.astype(BF16)

    pl.when(pl.program_id(0) < 2)(lambda: add(inputs[0], inputs[1]))
    pl.when(pl.program_id(0) >= 2)(lambda: add(inputs[2], inputs[3]))


def fold(*halves):
    _, rows, half = halves[0].shape
    rows, tile = rows // 4, half // 2
    low = pl.BlockSpec((2, 4 * rows, tile), lambda j: (0, 0, jnp.minimum(j, 1)))
    high = pl.BlockSpec((2, 4 * rows, tile), lambda j: (0, 0, jnp.maximum(j - 2, 0)))
    keep, *sends = pl.pallas_call(
        fold_kernel,
        grid=(4,),
        in_specs=[low, low, high, high],
        out_specs=[pl.BlockSpec((2, rows, tile), lambda j: (0, 0, j))] * 4,
        out_shape=[like((2, rows, 2 * half), F32)] + [like((2, rows, 2 * half))] * 3,
        compiler_params=params(16),
        cost_estimate=cost(0, 52 * rows * half),
        name="fold",
    )(*halves)
    return keep, sends


def heads_kernel(
    pair_ref,
    weights_ref,
    bias_ref,
    trig_ref,
    segment_col,
    segment_row,
    index_col,
    index_row,
    right_ref,
    linear_ref,
    query_ref,
    key_ref,
    value_ref,
    grad_ref,
    grad_query_ref,
    grad_key_ref,
    attended_ref,
):
    width = grad_ref.shape[1]
    length = grad_ref.shape[0]
    scale = HEAD_DIM ** (-0.5)
    linear_ref[...] = (
        jnp.dot(pair_ref[0], weights_ref[:, : 3 * width], preferred_element_type=F32)
        + bias_ref[...]
    )
    grad_ref[...] = jnp.dot(
        pair_ref[1], weights_ref[:, 3 * width :], preferred_element_type=F32
    ).astype(BF16)

    def rotated(tile, sign):
        ahead = pltpu.roll(tile, LANES - HALF, 1)
        behind = pltpu.roll(tile, HALF, 1)
        turned = ahead * trig_ref[:, LANES : 2 * LANES] + behind * trig_ref[:, 2 * LANES :]
        return tile * trig_ref[:, :LANES] + turned * sign

    for start in range(0, width, LANES):
        lanes = slice(start, start + LANES)
        query_ref[:, lanes] = (rotated(linear_ref[:, lanes], 1.0) * scale).astype(BF16)
        keys = linear_ref[:, width + start : width + start + LANES]
        key_ref[:, lanes] = rotated(keys, 1.0).astype(BF16)
        value_ref[:, lanes] = linear_ref[:, 2 * width + start : 2 * width + start + LANES].astype(BF16)
    allowed = (segment_row[0] == segment_col[...]) & (index_row[0] >= index_col[...])
    both = (((1,), (1,)), ((), ()))
    value_t, key_t = value_ref[...].T, key_ref[...].T
    for start in range(0, width, HEAD_DIM):
        lanes = slice(start, start + HEAD_DIM)
        query, key, value = query_ref[:, lanes], key_ref[:, lanes], value_ref[:, lanes]
        grad = grad_ref[:, lanes]
        scores = lax.dot_general(key, query, both, preferred_element_type=F32)
        scores = jnp.where(allowed, scores, -1000000000.0)
        expo = jnp.exp(scores - jnp.max(scores, axis=0, keepdims=True))
        probs = expo * (1.0 / jnp.sum(expo, axis=0, keepdims=True))
        low_probs = probs.astype(BF16)
        attended_ref[lanes, :] = jnp.dot(value_t[lanes], low_probs, preferred_element_type=F32)
        grad_probs = lax.dot_general(value, grad, both, preferred_element_type=F32)
        grad_values = jnp.dot(low_probs, grad, preferred_element_type=F32)
        weighted = probs * grad_probs
        delta = jnp.sum(weighted, axis=0, keepdims=True)
        grad_scores = (weighted - probs * delta).astype(BF16)
        grad_query_ref[lanes, :] = jnp.dot(key_t[lanes], grad_scores, preferred_element_type=F32) * scale
        grad_key_ref[:, lanes] = jnp.dot(grad_scores, query, preferred_element_type=F32)
        right_ref[:, 2 * width + start : 2 * width + start + HEAD_DIM] = grad_values.astype(BF16)
    right_ref[:, 3 * width :] = attended_ref[...].T.astype(BF16)
    linear_ref[:, :width] = grad_query_ref[...].T
    for start in range(0, width, LANES):
        lanes = slice(start, start + LANES)
        right_ref[:, lanes] = rotated(linear_ref[:, lanes], -1.0).astype(BF16)
        right_ref[:, width + start : width + start + LANES] = rotated(
            grad_key_ref[:, lanes], -1.0
        ).astype(BF16)


def heads(pair, weights, bias, tables, length):
    _, rows, depth = pair.shape
    width = bias.shape[0] // 3
    blocks = lambda lanes: pl.BlockSpec((length, lanes), lambda i: (i, 0))
    rowwise = pl.BlockSpec((1, 1, length), lambda i: (i, 0, 0))
    return pl.pallas_call(
        heads_kernel,
        grid=(rows // length,),
        in_specs=[
            pl.BlockSpec((2, length, depth), lambda i: (0, i, 0)),
            pl.BlockSpec((depth, 4 * width), lambda i: (0, 0), pipeline_mode=pl.Buffered(1)),
            pl.BlockSpec((1, 3 * width), lambda i: (0, 0)),
            blocks(3 * LANES),
            blocks(1),
            rowwise,
            blocks(1),
            rowwise,
        ],
        out_specs=blocks(4 * width),
        out_shape=like((rows, 4 * width)),
        scratch_shapes=[pltpu.VMEM((length, 3 * width), F32)]
        + [pltpu.VMEM((length, width), BF16)] * 4
        + [
            pltpu.VMEM((width, length), F32),
            pltpu.VMEM((length, width), F32),
            pltpu.VMEM((width, length), F32),
        ],
        compiler_params=params(32),
        cost_estimate=cost(26 * GIGA, 10 * MIB),
        name="heads",
    )(pair, weights, bias.reshape(1, -1), *tables)


def tables_kernel(cos_ref, sin_ref, *refs):
    inputs, outputs = refs[:4], refs[5:]
    trig_ref = refs[4]
    cos, sin = cos_ref[...], sin_ref[...]
    trig_ref[...] = jnp.zeros_like(trig_ref)
    for start in range(0, LANES, HEAD_DIM):
        rest = (cos.shape[0], HEAD_DIM - ROT)
        trig_ref[:, start : start + HALF] = cos
        trig_ref[:, start + HALF : start + ROT] = cos
        trig_ref[:, start + ROT : start + HEAD_DIM] = jnp.ones(rest, F32)
        trig_ref[:, LANES + start : LANES + start + HALF] = -sin
        trig_ref[:, 2 * LANES + start + HALF : 2 * LANES + start + ROT] = sin
    for source, target in zip(inputs, outputs):
        target[...] = source[...]


def rotary_tables(doc, index):
    count, length = doc.shape
    rows = count * length
    same_doc = doc[:, :, None] == doc[:, None, :]
    doc_start = jnp.min(jnp.where(same_doc, index[:, None, :], length), axis=2)
    positions = (index - doc_start).astype(F32).reshape(-1)
    inv_freq = 10000.0 ** (-(jnp.arange(HALF, dtype=F32) * 2.0 / ROT))
    angles = positions[:, None] * inv_freq
    column, row = (rows, 1), (count, 1, length)
    shapes = [column, row, column, row]
    passed = [value.reshape(shape) for value, shape in zip((doc, doc, index, index), shapes)]
    return pl.pallas_call(
        tables_kernel,
        in_specs=[WHOLE] * 6,
        out_specs=[WHOLE] * 5,
        out_shape=[like((rows, 3 * LANES), F32)] + [like(shape, jnp.int32) for shape in shapes],
        compiler_params=params(16),
        name="tables",
    )(jnp.cos(angles), jnp.sin(angles), *passed)


def like(shape, dtype=BF16):
    return jax.ShapeDtypeStruct(shape, dtype)


def params(mib):
    return pltpu.CompilerParams(vmem_limit_bytes=mib * MIB)


def cost(flops, moved):
    return pl.CostEstimate(flops=flops, bytes_accessed=moved, transcendentals=0)


def slot_of(coords, bits):
    return (coords[0] * 2 + coords[3]) ^ bits


def pack_kernel(coords, up_ref, down_ref, qkv_ref, out_ref, segment_ref, *refs):
    parts, sems = refs[:4], refs[4]
    hidden, width = up_ref.shape[1] // 4, out_ref.shape[1] // 4
    copies = []

    def copy(source, target):
        copies.append(pltpu.make_async_copy(source, target, sems.at[len(copies)]))
        copies[-1].start()

    for bits in (1, 2, 3, 0):
        slot = slot_of(coords, bits)
        wide = pl.ds(pl.multiple_of(slot * hidden, hidden), hidden)
        narrow = pl.ds(pl.multiple_of(slot * width, width), width)
        part = parts[bits]
        for kind in range(3):
            copy(qkv_ref.at[kind, :, narrow], part.at[:, pl.ds(kind * width, width)])
        copy(out_ref.at[:, narrow], part.at[:, pl.ds(3 * width, width)])
        copy(up_ref.at[:, wide], part.at[:, pl.ds(4 * width, hidden)])
        copy(down_ref.at[:, wide], part.at[:, pl.ds(4 * width + hidden, hidden)])
    segments = segment_ref[...].astype(F32).astype(BF16)
    segments = jnp.broadcast_to(segments, (up_ref.shape[0], segments.shape[1]))
    for part in parts:
        part[:, 4 * width + 2 * hidden :] = segments
    for each in copies:
        each.wait()


def pack(coords, w_up, down_t, qkv_t, out_t, segments):
    rows, hidden, width = w_up.shape[0], w_up.shape[1] // 4, out_t.shape[1] // 4
    return pl.pallas_call(
        pack_kernel,
        in_specs=[SCALARS] + [ANY] * 4 + [WHOLE],
        out_specs=[WHOLE] * 4,
        out_shape=[like((rows, 2 * hidden + 4 * width + segments.shape[0]))] * 4,
        scratch_shapes=[pltpu.SemaphoreType.DMA((24,))],
        compiler_params=params(60),
        name="pack",
    )(coords, w_up, down_t, qkv_t, out_t, segments.reshape(1, -1))


def order_kernel(coords, *refs):
    parts, out = refs[:4], refs[4]
    for bits in range(4):
        out[coords[0] ^ (bits >> 1), coords[3] ^ (bits & 1)] = parts[bits][:, : out.shape[3]]


def order(coords, parts, columns):
    rows = parts[0].shape[0]
    out = pl.pallas_call(
        order_kernel,
        in_specs=[SCALARS] + [WHOLE] * 4,
        out_specs=WHOLE,
        out_shape=like((2, 2, rows, columns)),
        compiler_params=params(16),
        name="order",
    )(coords, *parts)
    return out.reshape(4 * rows, columns)


def join_kernel(*refs):
    parts, out, sem = refs[:-2], refs[-2], refs[-1]
    copies = []
    for i, part in enumerate(parts):
        copies.append(pltpu.make_async_copy(part, out.at[i], sem.at[i]))
        copies[-1].start()
    for copy in copies:
        copy.wait()


def join(*parts):
    return pl.pallas_call(
        join_kernel,
        in_specs=[ANY] * len(parts),
        out_specs=ANY,
        out_shape=like((len(parts),) + parts[0].shape),
        scratch_shapes=[pltpu.SemaphoreType.DMA((len(parts),))],
        compiler_params=params(16),
        name="join",
    )(*parts)


def tokens_kernel(mine_ref, other_ref, rows_ref, columns_ref):
    @pl.when(pl.program_id(1) == 0)
    def _():
        rows_ref[0] = mine_ref[0, 0]
        columns_ref[0] = mine_ref[0, 0].T

    @pl.when(pl.program_id(1) == 1)
    def _():
        rows_ref[0] = other_ref[0, 0]
        columns_ref[0] = other_ref[0, 0].T


def gather_tokens(*pairs):
    mine = join(*pairs)
    other = flip(mine, "c")
    _, _, rows, depth = mine.shape
    block = (1, 1, rows, depth)
    return pl.pallas_call(
        tokens_kernel,
        grid=(2, 2, 4),
        in_specs=[
            pl.BlockSpec(block, lambda w, c, z: (jnp.where(c == 0, z, 3), w, 0, 0)),
            pl.BlockSpec(block, lambda w, c, z: (jnp.where(c == 1, z, 0), w, 0, 0)),
        ],
        out_specs=[
            pl.BlockSpec((1, rows, depth), lambda w, c, z: (w, 4 * c + z, 0)),
            pl.BlockSpec((1, depth, rows), lambda w, c, z: (w, 0, 4 * c + z)),
        ],
        out_shape=[like((2, 8 * rows, depth)), like((2, depth, 8 * rows))],
        compiler_params=params(32),
        cost_estimate=cost(0, 8 * mine.size * 2),
        name="tokens",
    )(mine, other)


def across(columns):
    ones = jnp.ones((8, columns.shape[1]), F32)
    contract = (((1,), (1,)), ((), ()))
    return lax.dot_general(
        ones, columns, contract, precision=lax.Precision.HIGHEST, preferred_element_type=F32
    )[:1]


def lane_sums(value):
    total = value[:, :LANES]
    for start in range(LANES, value.shape[1], LANES):
        total = total + value[:, start : start + LANES]
    return total


def mlp_kernel(pair_hbm, pair_t_hbm, bias_ref, up_ref, down_ref, *refs):
    hidden_ref, grads_ref, bias_sums_ref, sums_ref, product_ref, level_ref, pair_ref, pair_t_ref, sems = refs
    step, tile = pl.program_id(0), up_ref.shape[1]
    slope = 0.7978845608028654
    loads = [
        pltpu.make_async_copy(source.at[i], target.at[i], sems.at[k, i])
        for k, (source, target) in enumerate(((pair_hbm, pair_ref), (pair_t_hbm, pair_t_ref)))
        for i in range(2)
    ]

    def begin():
        for load in loads:
            load.start()

    def wait(*which):
        def body():
            for i in which:
                loads[i].wait()

        pl.when(step == 0)(body)

    pl.when(step == 0)(begin)
    wait(0)
    up = jnp.dot(pair_ref[0], up_ref[...], preferred_element_type=F32) + bias_ref[...]
    square = up * up
    wave = jnp.tanh(up * (slope + (slope * 0.044715) * square))
    half = 0.5 + 0.5 * wave
    activated = (up * half).astype(BF16)
    hidden_ref[1] = activated
    rise = half + up * (1.0 - wave * wave) * (0.5 * slope + (1.5 * slope * 0.044715) * square)
    wait(1)
    grad = jnp.dot(pair_ref[1], down_ref[...], preferred_element_type=F32) * rise
    low = grad.astype(BF16)
    hidden_ref[0] = low
    wait(2, 3)
    bias_sums = jnp.sum(low.astype(F32), axis=0, keepdims=True)
    bias_sums_ref[...] = bias_sums
    grads_ref[:, tile:] = jnp.dot(pair_t_ref[1], activated, preferred_element_type=F32).astype(BF16)
    grads = jnp.dot(pair_t_ref[0], low, preferred_element_type=F32)
    grads_ref[:, :tile] = grads.astype(BF16)
    weights = up_ref[...].astype(F32)
    products, levels = lane_sums(weights * grads), lane_sums(weights * bias_sums)

    @pl.when(step == 0)
    def _():
        product_ref[...] = products
        level_ref[...] = levels

    @pl.when(step > 0)
    def _():
        product_ref[...] += products
        level_ref[...] += levels

    @pl.when(step == pl.num_programs(0) - 1)
    def _():
        sums_ref[0:1, :] = across(level_ref[...])
        sums_ref[1:2, :] = across(product_ref[...])


def mlp(pair, pair_t, bias, weights, tile):
    rows, depth = pair.shape[1:]
    hidden = bias.shape[0]
    tiles = hidden // tile
    start = (weights.shape[1] - 2 * hidden) // tile
    column = lambda j: (0, j)
    return pl.pallas_call(
        mlp_kernel,
        grid=(tiles,),
        in_specs=[
            ANY,
            ANY,
            pl.BlockSpec((1, tile), column),
            pl.BlockSpec((depth, tile), lambda j: (0, start + j)),
            pl.BlockSpec((depth, tile), lambda j: (0, start + tiles + j)),
        ],
        out_specs=[
            pl.BlockSpec((2, rows, tile), lambda j: (0, 0, j)),
            pl.BlockSpec((depth, 2 * tile), column),
            pl.BlockSpec((1, tile), column),
            pl.BlockSpec((2, depth), lambda j: (0, 0)),
        ],
        out_shape=[
            like((2, rows, hidden)),
            like((depth, 2 * hidden)),
            like((1, hidden), F32),
            like((2, depth), F32),
        ],
        scratch_shapes=[pltpu.VMEM((depth, LANES), F32)] * 2
        + [
            pltpu.VMEM((2, rows, depth), BF16),
            pltpu.VMEM((2, depth, rows), BF16),
            pltpu.SemaphoreType.DMA((2, 2)),
        ],
        compiler_params=params(48),
        cost_estimate=cost(8 * rows * depth * hidden, 40 * MIB),
        name="mlp",
    )(pair, pair_t, bias.reshape(1, -1), weights, weights)


def split(rows):
    high = rows.astype(BF16)
    return high, (rows - high.astype(F32)).astype(BF16)


def whole(rows):
    count = rows.shape[0] // 2
    return rows[:count].astype(F32) + rows[count:].astype(F32)


def head_grads_kernel(
    coords, left_ref, right_ref, weights_ref, gain_ref, bias_ref, mlp_sums_ref, up_sums_ref, cot_ref, *refs
):
    outs, (product_ref, turned_ref, rows_ref, product_sums, level_sums) = refs[:5], refs[5:]
    x, y = coords[1], coords[2]
    step, tile = pl.program_id(0), right_ref.shape[1]
    block = product_ref.shape[1]
    lanes = pl.ds(pl.multiple_of(step * tile, tile), tile)
    product = jnp.dot(left_ref[step // 3], right_ref[...], preferred_element_type=F32)
    product_ref[...] = product.astype(BF16).reshape(product_ref.shape)
    targets = []
    for y_bits in range(4):
        for x_bits in range(4):
            out, i = outs[(0, 1, None, 2)[y_bits] or 0], x_bits
            if y_bits == 2:
                out, i = outs[3 + x_bits // 2], x_bits % 2
            chip = (x ^ x_bits) * 4 + (y ^ y_bits)
            out[i, :block, lanes] = product_ref[chip]
            targets.append(out.at[i])

    @pl.when(step == 0)
    def _():
        product_sums[...] = jnp.zeros_like(product_sums)
        level_sums[...] = jnp.zeros_like(level_sums)
        rows_ref[...] = jnp.zeros_like(rows_ref)

    @pl.when(step < 3)
    def _():
        sums = jnp.sum(right_ref[...].astype(F32), axis=0, keepdims=True)
        rows_ref[7:8, lanes] = sums
        weights = weights_ref[...].astype(F32)
        product_sums[...] += lane_sums(weights * product)
        level_sums[...] += lane_sums(weights * sums)

    @pl.when(step == 3)
    def _():
        wide = rows_ref.shape[1]
        level = mlp_sums_ref[0:1, :] + across(level_sums[...])
        product = mlp_sums_ref[1:2, :] + across(product_sums[...])
        turn(turned_ref, jnp.concatenate([product, level], axis=0), True)
        level = turned_ref[1:2, :]
        by_gain = (turned_ref[0:1, :] - bias_ref[...] * level) / gain_ref[...]
        for i, row in enumerate((by_gain, level, cot_ref[...])):
            rows_ref[2 * i : 2 * i + 1, :] = row[:, :wide]
            rows_ref[2 * i + 1 : 2 * i + 2, :] = row[:, wide:]
        rows_ref[6:7, :] = up_sums_ref[...]
        high, low = split(rows_ref[...])
        both = jnp.concatenate([high.astype(F32), low.astype(F32)], axis=0).astype(BF16)
        for target in targets:
            target[block:, :] = both


def head_grads(coords, pair_t, right, weights, gain, bias, mlp_sums, up_sums, cot_sums):
    _, depth, rows = pair_t.shape
    columns = right.shape[1]
    tile, block = columns // 4, depth // 16
    full, half = like((4, block + 16, columns)), like((2, block + 16, columns))
    first = lambda j: (0, jnp.minimum(j, 2))
    return pl.pallas_call(
        head_grads_kernel,
        grid=(4,),
        in_specs=[
            SCALARS,
            WHOLE,
            pl.BlockSpec((rows, tile), lambda j: (0, j)),
            pl.BlockSpec((depth, tile), first),
        ]
        + [WHOLE] * 5,
        out_specs=[WHOLE] * 5,
        out_shape=[full, full, full, half, half],
        scratch_shapes=[
            pltpu.VMEM((16, block, tile), BF16),
            pltpu.VMEM((2, depth), F32),
            pltpu.VMEM((8, columns), F32),
            pltpu.VMEM((depth, LANES), F32),
            pltpu.VMEM((depth, LANES), F32),
        ],
        compiler_params=params(28),
        cost_estimate=cost(2 * depth * rows * columns, 16 * MIB),
        name="head_grads",
    )(coords, pair_t, right, weights, gain.reshape(1, -1), bias.reshape(1, -1), mlp_sums, up_sums, cot_sums)


def put(target, data, rows):
    block = data.shape[0]
    target[:block, :] = data.astype(BF16)
    high, low = split(rows)
    target[block:, :] = jnp.concatenate([high.astype(F32), low.astype(F32)], axis=0).astype(BF16)


def bump_kernel(chunk_ref, part_ref, out_ref):
    block = chunk_ref.shape[1] - 16
    for i in range(2):
        data = chunk_ref[i, :block].astype(F32) + part_ref[i, :block].astype(F32)
        put(out_ref.at[i], data, whole(chunk_ref[i, block:]) + whole(part_ref[i, block:]))


def bump(chunk, part, half):
    spec = pl.BlockSpec(part.shape, lambda i: (half, 0, 0))
    return pl.pallas_call(
        bump_kernel,
        grid=(1,),
        in_specs=[spec, pl.BlockSpec(part.shape, lambda i: (0, 0, 0))],
        out_specs=spec,
        out_shape=like(chunk.shape),
        input_output_aliases={0: 0},
        compiler_params=params(16),
        name="bump",
    )(chunk, part)


def near_kernel(own_ref, one_ref, three_ref, keep_ref, *sends):
    block = own_ref.shape[1] - 16
    for i in range(4):
        data = own_ref[i, :block].astype(F32)
        data = data + (one_ref[i, :block].astype(F32) + three_ref[i, :block].astype(F32))
        rows = whole(own_ref[i, block:]) + (whole(one_ref[i, block:]) + whole(three_ref[i, block:]))
        if i == 0:
            keep_ref[:block, :] = data
            keep_ref[block:, :] = rows
        else:
            put(sends[i - 1], data, rows)


def near_sums(own, one, three):
    rows, columns = own.shape[1:]
    return pl.pallas_call(
        near_kernel,
        in_specs=[WHOLE] * 3,
        out_specs=[WHOLE] * 4,
        out_shape=[like((rows - 8, columns), F32)] + [like((rows, columns))] * 3,
        compiler_params=params(16),
        name="near",
    )(own, one, three)


def cut_kernel(coords, mlp_ref, *refs):
    blocks, outs = refs[:4], refs[4:]
    rows, columns = outs[0].shape[0], mlp_ref.shape[1]
    block, wide = 4 * rows, blocks[0].shape[1]
    vectors = blocks[0][block:, :]
    for other in blocks[1:]:
        vectors = vectors + whole(other[block:, :])
    high, low = split(vectors)
    vectors = jnp.concatenate([high.astype(F32), low.astype(F32)], axis=0).astype(BF16)
    for bits in range(4):
        some = pl.ds(pl.multiple_of(slot_of(coords, bits) * rows, rows), rows)
        out = outs[bits]
        out[:, :columns] = mlp_ref[some, :]
        total = blocks[0][some, :]
        for other in blocks[1:]:
            total = total + other[some, :].astype(F32)
        out[:, columns : columns + wide] = total.astype(BF16)
        out[:16, columns + wide :] = vectors[:, : wide // 2]
        out[16:, columns + wide :] = vectors[:, wide // 2 :]


def cut(coords, mlp_grads, blocks):
    rows, columns = mlp_grads.shape[0] // 4, mlp_grads.shape[1]
    wide = blocks[0].shape[1]
    return pl.pallas_call(
        cut_kernel,
        in_specs=[SCALARS] + [WHOLE] * 5,
        out_specs=[WHOLE] * 4,
        out_shape=[like((rows, columns + wide + wide // 2))] * 4,
        compiler_params=params(16),
        name="cut",
    )(coords, mlp_grads, *blocks)


def combine_kernel(hidden_ref, right_ref, weights_ref, mine_ref, theirs_ref):
    contract = (((1,), (1,)), ((), ()))
    hidden, columns = hidden_ref.shape[2], right_ref.shape[1]
    inner = columns * 3 // 4
    half = mine_ref.shape[1]

    def product(left, start):
        weights = weights_ref[:, start : start + left.shape[1]]
        return lax.dot_general(left, weights, contract, preferred_element_type=F32)

    total = product(hidden_ref[0], columns) + product(right_ref[:, :inner], 0)
    mine_ref[0] = total[:half].astype(BF16)
    theirs_ref[0] = total[half:].astype(BF16)
    total = product(hidden_ref[1], columns + hidden) + product(right_ref[:, inner:], inner)
    mine_ref[1] = total[:half].astype(BF16)
    theirs_ref[1] = total[half:].astype(BF16)


def combine(hidden_pair, right, weights, part):
    _, rows, hidden = hidden_pair.shape
    depth, columns = weights.shape
    tile = depth // 4
    block = pl.BlockSpec((2, rows // 2, tile), lambda i: (0, 0, i))
    return pl.pallas_call(
        combine_kernel,
        grid=(2,),
        in_specs=[
            WHOLE,
            WHOLE,
            pl.BlockSpec((tile, columns), lambda i: (2 * part + i, 0)),
        ],
        out_specs=[block] * 2,
        out_shape=[like((2, rows // 2, depth // 2))] * 2,
        compiler_params=params(40),
        cost_estimate=cost(rows * depth * columns, 16 * MIB),
        name="combine",
    )(hidden_pair, right, weights)


def exchange(parts):
    return [parts[0], flip(parts[1], "c"), flip(parts[2], "zl"), flip(parts[3], "zl", "c")]


def unpack_kernel(coords, *refs):
    parts, (up_ref, down_ref, qkv_ref, out_ref, rows_ref, up_sums_ref, qkv_sums_ref) = refs[:4], refs[4:]
    hidden, width = up_ref.shape[1] // 4, out_ref.shape[1] // 4
    tile = hidden // 4
    for bits in range(4):
        slot = slot_of(coords, bits)
        wide = pl.ds(pl.multiple_of(slot * hidden, hidden), hidden)
        narrow = pl.ds(pl.multiple_of(slot * width, width), width)
        part = parts[bits]
        for j in range(4):
            some = pl.ds(pl.multiple_of(slot * hidden + j * tile, tile), tile)
            up_ref[:, some] = part[:, 2 * j * tile : (2 * j + 1) * tile].astype(F32)
            down_ref[:, some] = part[:, (2 * j + 1) * tile : (2 * j + 2) * tile].astype(F32)
        start = 2 * hidden
        for kind in range(3):
            qkv_ref[kind, :, narrow] = part[:, start + kind * width : start + (kind + 1) * width].astype(F32)
        out_ref[:, narrow] = part[:, start + 3 * width : start + 4 * width].astype(F32)
        start += 4 * width
        vectors = jnp.concatenate([whole(part[:16, start:]), whole(part[16:, start:])], axis=1)
        rows_ref[...] = vectors if bits == 0 else rows_ref[...] + vectors
        up_sums_ref[:, wide] = vectors[6:7, :]
        for kind in range(3):
            qkv_sums_ref[kind : kind + 1, narrow] = vectors[7:8, kind * width : (kind + 1) * width]


def unpack(coords, parts, hidden, width):
    rows = parts[0].shape[0]
    wide, narrow = (rows, 4 * hidden), (rows, 4 * width)
    shapes = [wide, wide, (3,) + narrow, narrow, (8, 4 * width), (1, 4 * hidden), (3, 4 * width)]
    return pl.pallas_call(
        unpack_kernel,
        in_specs=[SCALARS] + [WHOLE] * 4,
        out_specs=[WHOLE] * 7,
        out_shape=[like(shape, F32) for shape in shapes],
        compiler_params=params(16),
        name="unpack",
    )(coords, *parts)


def turn(dest, value, back):
    block = value.shape[1] // 32
    for chip in range(16):
        for zl in range(2):
            natural, inside = (zl * 16 + chip) * block, (chip * 2 + zl) * block
            source, target = (inside, natural) if back else (natural, inside)
            dest[:, target : target + block] = value[:, source : source + block].astype(dest.dtype)


def standardize(tokens):
    rows = tokens.astype(F32)
    centered = rows - jnp.mean(rows, axis=1, keepdims=True)
    scale = lax.rsqrt(jnp.mean(centered * centered, axis=1, keepdims=True) + EPSILON)
    return rows, centered * scale, scale


def enter_kernel(tokens_ref, cot_ref, gain_ref, bias_ref, pair_ref, sums_ref):
    _, standard, _ = standardize(tokens_ref[...])
    turn(pair_ref.at[0], (standard * gain_ref[...] + bias_ref[...]).astype(BF16), False)
    turn(pair_ref.at[1], cot_ref[...], False)
    sums_ref[...] = jnp.sum(cot_ref[...].astype(F32), axis=0, keepdims=True)


def enter(tokens, cotangent, gain, bias):
    return pl.pallas_call(
        enter_kernel,
        in_specs=[WHOLE] * 4,
        out_specs=[WHOLE] * 2,
        out_shape=[like((2,) + tokens.shape), like((1, tokens.shape[1]), F32)],
        compiler_params=params(16),
        name="enter",
    )(tokens, cotangent, gain.reshape(1, -1), bias.reshape(1, -1))


def leave_kernel(tokens_ref, cot_ref, gain_ref, bias_ref, *refs):
    mixed_ref, grad_ref, branch_ref, normed_ref = refs[-4:]
    for which, target in ((0, normed_ref), (1, branch_ref)):
        total = refs[0][which]
        for part in refs[1:4]:
            total = total + part[which].astype(F32)
        turn(target, total, True)
    rows, standard, scale = standardize(tokens_ref[...])
    mixed_ref[...] = (rows + branch_ref[...] + bias_ref[...]).astype(BF16)
    grad = normed_ref[...] * gain_ref[...]
    level = jnp.mean(grad, axis=1, keepdims=True)
    slope = jnp.mean(grad * standard, axis=1, keepdims=True)
    grad_ref[...] = cot_ref[...].astype(F32) + scale * (grad - level - standard * slope)


def leave(tokens, cotangent, gain, bias, sums):
    shape = tokens.shape
    return pl.pallas_call(
        leave_kernel,
        in_specs=[WHOLE] * 8,
        out_specs=[WHOLE] * 2,
        out_shape=[like(shape), like(shape, F32)],
        scratch_shapes=[pltpu.VMEM(shape, F32)] * 2,
        compiler_params=params(24),
        name="leave",
    )(tokens, cotangent, gain.reshape(1, -1), bias.reshape(1, -1), *sums)


def scatter_plane(grads):
    return lax.psum_scatter(grads, PLANE, scatter_dimension=0, tiled=True)


def per_device(
    tokens,
    layernorm_gain,
    layernorm_bias,
    w_qkv,
    b_qkv,
    w_out,
    b_out,
    w_up,
    b_up,
    w_down,
    b_down,
    segments,
    cotangent,
):
    depth = tokens.shape[1]
    length = segments.shape[0]
    half_rows = tokens.shape[0]
    width = w_out.shape[0] // 4
    hidden = w_down.shape[0] // 4
    rows = w_up.shape[0]
    coords = jnp.stack([lax.axis_index(axis) for axis in AXES]).astype(jnp.int32)
    place_here = coords[0] * 2 + coords[3]
    this_half = coords[4]

    parts = exchange(pack(coords, w_up, w_down.T, w_qkv.transpose(1, 0, 2), w_out.T, segments))
    shard = order(coords, parts, 2 * hidden + 4 * width)
    weights = lax.all_gather(shard, PLANE, axis=0, tiled=True)

    pair, cot_sums = enter(tokens, cotangent, layernorm_gain, layernorm_bias)
    _, pair = lax.optimization_barrier((shard, pair))
    near, far, opposite = flip(pair, "zl"), flip(pair, "zl", "mp"), flip(pair, "mp")
    pair, pair_t = gather_tokens(pair, opposite, near, far)

    doc = jnp.stack([parts[k][0, -length:] for k in (0, 2, 1, 3)]).astype(jnp.int32)
    doc = doc.reshape(4, 2, half_rows)
    doc = jnp.where(this_half == 0, doc, doc[:, ::-1]).reshape(4, length)
    halves = jnp.stack([this_half, 1 - this_half]) * half_rows
    index = (halves[:, None] + jnp.arange(half_rows, dtype=jnp.int32)).reshape(1, length)
    index = jnp.broadcast_to(index, (4, length)).astype(jnp.int32)
    b_up_here = lax.dynamic_slice_in_dim(b_up, place_here * hidden, hidden)
    b_qkv_here = lax.dynamic_slice_in_dim(b_qkv, place_here * width, width, axis=1).reshape(-1)

    tables = rotary_tables(doc, index)

    pair, pair_t, tables = lax.optimization_barrier((pair, pair_t, tables))
    hidden_pair, mlp_grads, up_sums, mlp_sums = mlp(pair, pair_t, b_up_here, weights, hidden // 4)
    mlp_grads = scatter_plane(mlp_grads)

    pair, pair_t, hidden_pair = lax.optimization_barrier((pair, pair_t, hidden_pair))
    right = heads(pair, weights, b_qkv_here, tables, length)

    chunks = head_grads(
        coords, pair_t, right, weights, layernorm_gain, layernorm_bias, mlp_sums, up_sums, cot_sums
    )
    chunks, hidden_pair = lax.optimization_barrier((chunks, hidden_pair))
    own, one, three, two_low, two_high = chunks
    low, high = hop(two_low, "y", 1), hop(two_high, "y", 3)
    first, first_theirs = combine(hidden_pair, right, weights, 0)
    first_theirs = flip(first_theirs, "c")
    first, hidden_pair = lax.optimization_barrier((first, hidden_pair))
    second, second_theirs = combine(hidden_pair, right, weights, 1)

    low, high, first_theirs, second, second_theirs = lax.optimization_barrier(
        (low, high, first_theirs, second, second_theirs)
    )
    second_theirs = flip(second_theirs, "c")
    one, three = hop(bump(one, high, 1), "y", 1), hop(bump(three, low, 0), "y", 3)
    keep, sends = fold(first, first_theirs, second, second_theirs)
    near, far = flip(sends[1], "zl"), flip(sends[2], "zl", "mp")
    one, three, near, far, keep, opposite = lax.optimization_barrier(
        (one, three, near, far, keep, sends[0])
    )
    along_z = [near, far, flip(opposite, "mp")]
    blocks = near_sums(own, one, three)
    blocks = [blocks[0]] + [hop(part, "x", bits) for part, bits in zip(blocks[1:], (1, 2, 3))]
    parts = exchange(cut(coords, mlp_grads, blocks))
    mixed, d_tokens = leave(
        tokens, cotangent, layernorm_gain, b_out + b_down, [keep] + along_z
    )
    grad_up_w, grad_down_w, grad_qkv_w, grad_out_w, vectors, grad_b_up, grad_b_qkv = unpack(
        coords, parts, hidden, width
    )
    vectors = (vectors + flip(vectors, "mp"))[:6].reshape(3, depth)
    return (
        mixed,
        d_tokens,
        vectors[0],
        vectors[1],
        grad_qkv_w.transpose(1, 0, 2),
        grad_b_qkv,
        grad_out_w.T,
        vectors[2],
        grad_up_w,
        grad_b_up[0],
        grad_down_w.T,
        vectors[2],
    )


def solution(mesh):
    fine = Mesh(mesh.devices.reshape(SIZES), AXES)
    dp = ("zl", "x", "y", "c")
    in_specs = (
        P(AXES, None),
        P(),
        P(),
        P(dp, None, "mp"),
        P(None, "mp"),
        P("mp", dp),
        P(),
        P(dp, "mp"),
        P("mp"),
        P("mp", dp),
        P(),
        P(dp),
        P(AXES, None),
    )
    out_specs = (
        P(AXES, None),
        P(AXES, None),
        P(),
        P(),
        P(dp, None, "mp"),
        P(None, "mp"),
        P("mp", dp),
        P(),
        P(dp, "mp"),
        P("mp"),
        P("mp", dp),
        P(),
    )
    return jax.shard_map(
        per_device, mesh=fine, in_specs=in_specs, out_specs=out_specs, check_vma=False
    )
```

time: 358 us -> 322 us (0.90)
  Pallas kernels: 132 us -> 116 us
  starting transfers between devices: 45.1 us -> 30.1 us
  other arithmetic: 7.06 us -> 2.48 us
  waiting for transfers between devices: 128 us -> 132 us
  local copies, waits for them, and re-layouts: 29.4 us -> 25.8 us
    ppermute x13 -> x7, waiting for transfers between devices: 30.7 us -> 52.1 us  [hop(): return lax.ppermute(value, axis, [(i, i ^ bits) for i in range(4)])]
    ppermute x19 -> x16, waiting for transfers between devices: 83.8 us -> 67 us  [flip(): return lax.ppermute(value, axes, [(i, count - 1 - i) for i in range(count)])]
    pallas_call x9 -> x8, Pallas kernels: 102 us -> 90.8 us  [the longest x1 38 us: mlp(): pl.pallas_call(mlp_kernel, grid=(tiles,), in_specs=[ANY, ANY, pl.BlockSpe...]
    ppermute x19 -> x16, starting transfers between devices: 31 us -> 21 us  [flip(): return lax.ppermute(value, axes, [(i, count - 1 - i) for i in range(count)])]
    ppermute x13 -> x7, starting transfers between devices: 14 us -> 9.04 us  [hop(): return lax.ppermute(value, axis, [(i, i ^ bits) for i in range(4)])]
    unnamed x85 -> x75, local copies, waits for them, and re-layouts: 23 us -> 22.9 us
  transfers between devices with their start and end apart: 34 -> 25, of which waited for: 14 -> 15; matrix products, arithmetic and copies ran while one was open for 4% -> 1% of each run, Pallas kernels for 27% -> 23%
where the time goes in v4:
time: 322 us
  waiting for transfers between devices  132 us (41%)
  Pallas kernels  116 us (36%)
  starting transfers between devices  30.1 us (9%)
  local copies, waits for them, and re-layouts  25.8 us (8%)
  between operations  14.5 us (5%)
    ppermute x16, waiting for transfers between devices, flip(): return lax.ppermute(value, axes, [(i, count - 1 - i) for i in range(count)])  67 us
    ppermute x7, waiting for transfers between devices, hop(): return lax.ppermute(value, axis, [(i, i ^ bits) for i in range(4)])  52.1 us
    pallas_call x1, Pallas kernels, mlp(): pl.pallas_call(mlp_kernel, grid=(tiles,), in_specs=[ANY, ANY, pl.BlockSpe...  38 us
    unnamed x75, local copies, waits for them, and re-layouts  22.9 us
    ppermute x16, starting transfers between devices, flip(): return lax.ppermute(value, axes, [(i, count - 1 - i) for i in range(count)])  21 us
    pallas_call x2, Pallas kernels, combine(): pl.pallas_call(combine_kernel, grid=(2,), in_specs=[WHOLE, WHOLE, pl.Bloc...  18.3 us
    pallas_call x1, Pallas kernels, heads(): pl.pallas_call(heads_kernel, grid=(rows // length,), in_specs=[pl.BlockSp...  16.1 us
    pallas_call x1, Pallas kernels, gather_tokens(): pl.pallas_call(tokens_kernel, grid=(2, 2, 4), in_specs=[pl.BlockSpec(bloc...  13.5 us
  transfers between devices with their start and end apart: 25, of which 15 were waited for; matrix products, arithmetic and copies ran while one was open for 1% of the time, Pallas kernels for 23%

profile of v4, /device:TPU:1, one launch (start us, length us, event | category | flops | bytes accessed | tf_op | source)
XLA Modules:
  0.0 321.7 jit_solution(2951543092838575340)
XLA Ops:
  7.9 3.0 pack.1
  14.4 4.2 %collective-permute-done.1.refs_2_ = bf16[32,3328]{1,0:T(8,128)(2,1)S(1)} collective-permute-done((bf16[32,3328]{1,0:T(8,128)(2,1)}, bf16[32,3328]{1,0:T(8,128)(2,1)S(1)}, u32[]{:S(2)}, u32[]{:S(2)}) %collective-permute-start.1) | collective-permute-done | bytes 213024 | tf_op jit(solution)/shard_map/ppermute | solution.py:32
  18.6 5.1 %collective-permute-done.2.refs_3_ = bf16[32,3328]{1,0:T(8,128)(2,1)S(1)} collective-permute-done((bf16[32,3328]{1,0:T(8,128)(2,1)}, bf16[32,3328]{1,0:T(8,128)(2,1)S(1)}, u32[]{:S(2)}, u32[]{:S(2)}) %collective-permute-start.2) | collective-permute-done | bytes 213024 | tf_op jit(solution)/shard_map/ppermute | solution.py:32
  27.8 3.5 %collective-permute-start.3 = (bf16[2,128,2048]{2,1,0:T(8,128)(2,1)S(1)}, bf16[2,128,2048]{2,1,0:T(8,128)(2,1)S(1)}, u32[]{:S(2)}, u32[]{:S(2)}) collective-permute-start(bf16[2,128,2048]{2,1,0:T(8,128)(2,1)S(1)} %get-tuple-element.94.refs_0_), channel_id=1, source_target_pairs={{0,1},{1,0},{2,3},{3,2},{4,5},{5,4},{6,7},{7,6},{8,9},{9,8},{10,11... | collective-permute-start | bytes 3145736 | tf_op jit(solution)/shard_map/ppermute | solution.py:32
  32.0 22.9 %collective-permute-done.3.refs_1_ = bf16[2,128,2048]{2,1,0:T(8,128)(2,1)S(1)} collective-permute-done((bf16[2,128,2048]{2,1,0:T(8,128)(2,1)S(1)}, bf16[2,128,2048]{2,1,0:T(8,128)(2,1)S(1)}, u32[]{:S(2)}, u32[]{:S(2)}) %collective-permute-start.3) | collective-permute-done | bytes 1048608 | tf_op jit(solution)/shard_map/ppermute | solution.py:32
  54.9 23.4 %collective-permute-done.4.refs_2_ = bf16[2,128,2048]{2,1,0:T(8,128)(2,1)S(1)} collective-permute-done((bf16[2,128,2048]{2,1,0:T(8,128)(2,1)S(1)}, bf16[2,128,2048]{2,1,0:T(8,128)(2,1)S(1)}, u32[]{:S(2)}, u32[]{:S(2)}) %collective-permute-start.4) | collective-permute-done | bytes 1048608 | tf_op jit(solution)/shard_map/ppermute | solution.py:32
  88.3 13.5 %tokens.1 = (bf16[2,1024,2048]{2,1,0:T(8,128)(2,1)S(1)}, bf16[2,2048,1024]{2,1,0:T(8,128)(2,1)}) custom-call(bf16[4,2,128,2048]{3,2,1,0:T(8,128)(2,1)} %join.1.mine_ref, bf16[4,2,128,2048]{3,2,1,0:T(8,128)(2,1)} %collective-permute-done.6.other_ref), custom_call_target="tpu_custom_call" | custom-call | bytes 33554432 | tf_op jit(solution)/shard_map/tokens/pallas_call | solution.py:332
  101.8 3.4 %copy-done.20 = bf16[2,1024,2048]{2,1,0:T(8,128)(2,1)} copy-done((bf16[2,1024,2048]{2,1,0:T(8,128)(2,1)}, bf16[2,1024,2048]{2,1,0:T(8,128)(2,1)S(1)}, u32[]{:S(2)}) %copy-start.20) | copy-done | bytes 8388632
  105.1 13.4 %all-gather.2.cloned.1.call-done.up_ref.down_ref.weights_ref = bf16[2048,3072]{1,0:T(8,128)(2,1)} async-done(((bf16[128,3072]{1,0:T(8,128)(2,1)}), bf16[2048,3072]{1,0:T(8,128)(2,1)}) %all-gather.2.cloned.1.call-update) | async-done | bytes 12582928 | tf_op jit(solution)/shard_map/all_gather | solution.py:819
  118.5 38.0 %mlp.1 = (bf16[2,1024,1024]{2,1,0:T(8,128)(2,1)S(1)}, bf16[2048,2048]{1,0:T(8,128)(2,1)}, f32[1,1024]{1,0:T(1,128)S(1)}, f32[2,2048]{1,0:T(2,128)S(1)}) custom-call(bf16[2,1024,2048]{2,1,0:T(8,128)(2,1)} %copy-done.20, bf16[2,2048,1024]{2,1,0:T(8,128)(2,1)} %get-tuple-element.105.pair_t_hbm.left_ref, f32[1,1024]{1,0:T(1,128)S(1)} %bitcast.68, ...), custom_call_target="tpu_custom_call" | custom-call | flops 17179869184 | bytes 41943040 | tf_op jit(solution)/shard_map/mlp/pallas_call | solution.py:430
  159.9 3.7 %copy-done.21 = bf16[2,1024,2048]{2,1,0:T(8,128)(2,1)S(1)} copy-done((bf16[2,1024,2048]{2,1,0:T(8,128)(2,1)S(1)}, bf16[2,1024,2048]{2,1,0:T(8,128)(2,1)}, u32[]{:S(2)}) %copy-start.21) | copy-done | bytes 8388632
  164.6 16.1 %heads.1.right_ref = bf16[1024,1024]{1,0:T(8,128)(2,1)S(1)} custom-call(bf16[2,1024,2048]{2,1,0:T(8,128)(2,1)S(1)} %copy-done.21, bf16[2048,3072]{1,0:T(8,128)(2,1)} %all-gather.2.cloned.1.call-done.up_ref.down_ref.weights_ref, f32[1,768]{1,0:T(1,128)S(1)} %bitcast.69, f32[1024,384]{1,0:T(8,128)S(1)} %copy-done.23, ...), custom_call_target="tpu_custom_call" | custom-call | flops 27262976000 | bytes 10485760 | tf_op jit(solution)/shard_map/heads/pallas_call | solution.py:153
  180.7 11.6 %head_grads.1 = (bf16[4,144,1024]{2,1,0:T(8,128)(2,1)S(1)}, bf16[4,144,1024]{2,1,0:T(8,128)(2,1)S(1)}, bf16[4,144,1024]{2,1,0:T(8,128)(2,1)S(1)}, bf16[2,144,102...) custom-call(s32[5]{0:T(128)S(1)} %copy-done.19, bf16[2,2048,1024]{2,1,0:T(8,128)(2,1)S(1)} %bitcast.58, ...), custom_call_target="tpu_custom_call" | custom-call | flops 4294967296 | bytes 16777216 | tf_op jit(solution)/shard_map/head_grads/pallas_call | solution.py:532
  192.3 9.1 %combine.2 = (bf16[2,512,1024]{2,1,0:T(8,128)(2,1)S(1)}, bf16[2,512,1024]{2,1,0:T(8,128)(2,1)S(1)}) custom-call(bf16[2,1024,1024]{2,1,0:T(8,128)(2,1)S(1)} %copy-done.27, bf16[1024,1024]{1,0:T(8,128)(2,1)S(1)} %heads.1.right_ref, bf16[2048,3072]{1,0:T(8,128)(2,1)} %all-gather.2.cloned.1.call-done.up_ref.down_ref.weights_ref), custom_call_target="tpu_custom_call" | custom-call | flops 6442450944 | bytes 16777216 | tf_op jit(solution)/shard_map/combine/pallas_call | solution.py:667
  205.2 9.2 %combine.3 = (bf16[2,512,1024]{2,1,0:T(8,128)(2,1)S(1)}, bf16[2,512,1024]{2,1,0:T(8,128)(2,1)S(1)}) custom-call(bf16[2,1024,1024]{2,1,0:T(8,128)(2,1)S(1)} %copy-done.27, bf16[1024,1024]{1,0:T(8,128)(2,1)S(1)} %heads.1.right_ref, bf16[2048,3072]{1,0:T(8,128)(2,1)} %all-gather.2.cloned.1.call-done.up_ref.down_ref.weights_ref), custom_call_target="tpu_custom_call" | custom-call | flops 6442450944 | bytes 16777216 | tf_op jit(solution)/shard_map/combine/pallas_call | solution.py:667
  214.4 10.5 %collective-permute-done.7.part_ref = bf16[2,144,1024]{2,1,0:T(8,128)(2,1)S(1)} collective-permute-done((bf16[2,144,1024]{2,1,0:T(8,128)(2,1)S(1)}, bf16[2,144,1024]{2,1,0:T(8,128)(2,1)S(1)}, u32[]{:S(2)}, u32[]{:S(2)}) %collective-permute-start.7) | collective-permute-done | bytes 589856 | tf_op jit(solution)/shard_map/ppermute | solution.py:36
  230.6 2.9 fold.1
  236.9 27.7 %collective-permute-done.11.three_ref = bf16[4,144,1024]{2,1,0:T(8,128)(2,1)S(1)} collective-permute-done((bf16[4,144,1024]{2,1,0:T(8,128)(2,1)S(1)}, bf16[4,144,1024]{2,1,0:T(8,128)(2,1)S(1)}, u32[]{:S(2)}, u32[]{:S(2)}) %collective-permute-start.11) | collective-permute-done | bytes 1179680 | tf_op jit(solution)/shard_map/ppermute | solution.py:36
  265.6 3.0 collective-permute-start.15
  273.8 3.4 %collective-permute-done.16.refs_1_ = bf16[144,1024]{1,0:T(8,128)(2,1)S(1)} collective-permute-done((bf16[144,1024]{1,0:T(8,128)(2,1)S(1)}, bf16[144,1024]{1,0:T(8,128)(2,1)S(1)}, u32[]{:S(2)}, u32[]{:S(2)}) %collective-permute-start.16) | collective-permute-done | bytes 294944 | tf_op jit(solution)/shard_map/ppermute | solution.py:36
  277.1 7.0 %collective-permute-done.17.refs_2_ = bf16[144,1024]{1,0:T(8,128)(2,1)S(1)} collective-permute-done((bf16[144,1024]{1,0:T(8,128)(2,1)S(1)}, bf16[144,1024]{1,0:T(8,128)(2,1)S(1)}, u32[]{:S(2)}, u32[]{:S(2)}) %collective-permute-start.17) | collective-permute-done | bytes 294944 | tf_op jit(solution)/shard_map/ppermute | solution.py:36
  296.4 5.4 %collective-permute-done.20.refs_2_ = bf16[32,3584]{1,0:T(8,128)(2,1)S(1)} collective-permute-done((bf16[32,3584]{1,0:T(8,128)(2,1)S(1)}, bf16[32,3584]{1,0:T(8,128)(2,1)S(1)}, u32[]{:S(2)}, u32[]{:S(2)}) %collective-permute-start.20) | collective-permute-done | bytes 229408 | tf_op jit(solution)/shard_map/ppermute | solution.py:32
  301.8 5.1 %collective-permute-done.21.refs_3_ = bf16[32,3584]{1,0:T(8,128)(2,1)S(1)} collective-permute-done((bf16[32,3584]{1,0:T(8,128)(2,1)S(1)}, bf16[32,3584]{1,0:T(8,128)(2,1)S(1)}, u32[]{:S(2)}, u32[]{:S(2)}) %collective-permute-start.21) | collective-permute-done | bytes 229408 | tf_op jit(solution)/shard_map/ppermute | solution.py:32
  309.1 3.9 %leave.1 = (bf16[128,2048]{1,0:T(8,128)(2,1)}, f32[128,2048]{1,0:T(8,128)}) custom-call(bf16[128,2048]{1,0:T(8,128)(2,1)S(1)} %copy-done.2, bf16[128,2048]{1,0:T(8,128)(2,1)S(1)} %copy-done.3, f32[1,2048]{1,0:T(1,128)S(1)} %bitcast.62, f32[1,2048]{1,0:T(1,128)S(1)} %bitcast.67, f32[2,128,2048]{2,1,0:T(8,128)S(1)} %get-tuple-element.141.refs_0_, ...), custom_call_target="tpu_custom_call" | custom-call | tf_op jit(solution)/shard_map/leave/pallas_call | solution.py:777
  (143 shorter events, 58.3 us)
Async XLA Ops:
  7.2 111.3 %all-gather.2.cloned.1.call-start = ((), (), s32[]{:S(2)}) async-start(), calls=%async_computation.1 | async-start | bytes 13369344 | tf_op jit(solution)/shard_map/all_gather | solution.py:819
  10.9 7.7 %collective-permute-start.1 = (bf16[32,3328]{1,0:T(8,128)(2,1)}, bf16[32,3328]{1,0:T(8,128)(2,1)S(1)}, u32[]{:S(2)}, u32[]{:S(2)}) collective-permute-start(bf16[32,3328]{1,0:T(8,128)(2,1)} %get-tuple-element.91), channel_id=1, source_target_pairs={{0,64},{64,0},{1,65},{65,1},{2,66},{66,2},{3,67},{67,3},{4,68},{68... | collective-permute-start | bytes 638984 | tf_op jit(solution)/shard_map/ppermute | solution.py:32
  13.4 5.2 %collective-permute-start = (bf16[32,3328]{1,0:T(8,128)(2,1)}, bf16[32,3328]{1,0:T(8,128)(2,1)S(1)}, u32[]{:S(2)}, u32[]{:S(2)}) collective-permute-start(bf16[32,3328]{1,0:T(8,128)(2,1)} %get-tuple-element.90), channel_id=1, source_target_pairs={{0,2},{2,0},{1,3},{3,1},{4,6},{6,4},{5,7},{7,5},{8,10},{10,8},{9,1... | collective-permute-start | bytes 638984 | tf_op jit(solution)/shard_map/ppermute | solution.py:32
  14.4 9.3 %collective-permute-start.2 = (bf16[32,3328]{1,0:T(8,128)(2,1)}, bf16[32,3328]{1,0:T(8,128)(2,1)S(1)}, u32[]{:S(2)}, u32[]{:S(2)}) collective-permute-start(bf16[32,3328]{1,0:T(8,128)(2,1)} %get-tuple-element.92), channel_id=1, source_target_pairs={{0,66},{2,64},{64,2},{66,0},{1,67},{3,65},{65,3},{67,1},{4,70},{6,... | collective-permute-start | bytes 638984 | tf_op jit(solution)/shard_map/ppermute | solution.py:32
  26.8 260.4 %reduce-scatter.2.cloned.1.call-start = ((), (), s32[]{:S(2)}) async-start(), calls=%async_computation.2 | async-start | bytes 8912896 | tf_op jit(solution)/shard_map/reduce_scatter | solution.py:789
  27.8 27.1 %collective-permute-start.3 = (bf16[2,128,2048]{2,1,0:T(8,128)(2,1)S(1)}, bf16[2,128,2048]{2,1,0:T(8,128)(2,1)S(1)}, u32[]{:S(2)}, u32[]{:S(2)}) collective-permute-start(bf16[2,128,2048]{2,1,0:T(8,128)(2,1)S(1)} %get-tuple-element.94.refs_0_), channel_id=1, source_target_pairs={{0,1},{1,0},{2,3},{3,2},{4,5},{5,4},{6,7},{7,6},{8,9},{9,8},{10,11... | collective-permute-start | bytes 3145736 | tf_op jit(solution)/shard_map/ppermute | solution.py:32
  31.3 47.1 %collective-permute-start.4 = (bf16[2,128,2048]{2,1,0:T(8,128)(2,1)S(1)}, bf16[2,128,2048]{2,1,0:T(8,128)(2,1)S(1)}, u32[]{:S(2)}, u32[]{:S(2)}) collective-permute-start(bf16[2,128,2048]{2,1,0:T(8,128)(2,1)S(1)} %get-tuple-element.94.refs_0_), channel_id=1, source_target_pairs={{0,64},{64,0},{1,65},{65,1},{2,66},{66,2},{3,67},{67,3},{4,68},{68... | collective-permute-start | bytes 3145736 | tf_op jit(solution)/shard_map/ppermute | solution.py:32
  32.0 46.3 %collective-permute-start.5 = (bf16[2,128,2048]{2,1,0:T(8,128)(2,1)S(1)}, bf16[2,128,2048]{2,1,0:T(8,128)(2,1)S(1)}, u32[]{:S(2)}, u32[]{:S(2)}) collective-permute-start(bf16[2,128,2048]{2,1,0:T(8,128)(2,1)S(1)} %get-tuple-element.94.refs_0_), channel_id=1, source_target_pairs={{0,65},{1,64},{64,1},{65,0},{2,67},{3,66},{66,3},{67,2},{4,69},{5,... | collective-permute-start | bytes 3145736 | tf_op jit(solution)/shard_map/ppermute | solution.py:32
  80.4 7.9 %collective-permute-start.6 = (bf16[4,2,128,2048]{3,2,1,0:T(8,128)(2,1)}, bf16[4,2,128,2048]{3,2,1,0:T(8,128)(2,1)}, u32[]{:S(2)}, u32[]{:S(2)}) collective-permute-start(bf16[4,2,128,2048]{3,2,1,0:T(8,128)(2,1)} %join.1.mine_ref), channel_id=1, source_target_pairs={{0,2},{2,0},{1,3},{3,1},{4,6},{6,4},{5,7},{7,5},{8,10},{10,8},{9,1... | collective-permute-start | bytes 12582920 | tf_op jit(solution)/shard_map/ppermute | solution.py:32
  201.5 24.3 %collective-permute-start.9 = (bf16[2,512,1024]{2,1,0:T(8,128)(2,1)S(1)}, bf16[2,512,1024]{2,1,0:T(8,128)(2,1)S(1)}, u32[]{:S(2)}, u32[]{:S(2)}) collective-permute-start(bf16[2,512,1024]{2,1,0:T(8,128)(2,1)S(1)} %get-tuple-element.125), channel_id=1, source_target_pairs={{0,2},{2,0},{1,3},{3,1},{4,6},{6,4},{5,7},{7,5},{8,10},{10,8},{9,1... | collective-permute-start | bytes 6291464 | tf_op jit(solution)/shard_map/ppermute | solution.py:32
  202.1 22.8 %collective-permute-start.7 = (bf16[2,144,1024]{2,1,0:T(8,128)(2,1)S(1)}, bf16[2,144,1024]{2,1,0:T(8,128)(2,1)S(1)}, u32[]{:S(2)}, u32[]{:S(2)}) collective-permute-start(bf16[2,144,1024]{2,1,0:T(8,128)(2,1)S(1)} %get-tuple-element.122), channel_id=1, source_target_pairs={{0,4},{4,0},{8,12},{12,8},{1,5},{5,1},{9,13},{13,9},{2,6},{6,2},{1... | collective-permute-start | bytes 1769480 | tf_op jit(solution)/shard_map/ppermute | solution.py:36
  203.4 22.3 %collective-permute-start.8 = (bf16[2,144,1024]{2,1,0:T(8,128)(2,1)S(1)}, bf16[2,144,1024]{2,1,0:T(8,128)(2,1)S(1)}, u32[]{:S(2)}, u32[]{:S(2)}) collective-permute-start(bf16[2,144,1024]{2,1,0:T(8,128)(2,1)S(1)} %get-tuple-element.123), channel_id=1, source_target_pairs={{0,12},{4,8},{8,4},{12,0},{1,13},{5,9},{9,5},{13,1},{2,14},{6,10},... | collective-permute-start | bytes 1769480 | tf_op jit(solution)/shard_map/ppermute | solution.py:36
  225.8 4.8 %collective-permute-start.12 = (bf16[2,512,1024]{2,1,0:T(8,128)(2,1)S(1)}, bf16[2,512,1024]{2,1,0:T(8,128)(2,1)S(1)}, u32[]{:S(2)}, u32[]{:S(2)}) collective-permute-start(bf16[2,512,1024]{2,1,0:T(8,128)(2,1)S(1)} %get-tuple-element.136), channel_id=1, source_target_pairs={{0,2},{2,0},{1,3},{3,1},{4,6},{6,4},{5,7},{7,5},{8,10},{10,8},{9,1... | collective-permute-start | bytes 6291464 | tf_op jit(solution)/shard_map/ppermute | solution.py:32
  227.3 37.3 %collective-permute-start.11 = (bf16[4,144,1024]{2,1,0:T(8,128)(2,1)S(1)}, bf16[4,144,1024]{2,1,0:T(8,128)(2,1)S(1)}, u32[]{:S(2)}, u32[]{:S(2)}) collective-permute-start(bf16[4,144,1024]{2,1,0:T(8,128)(2,1)S(1)} %bump.3), channel_id=1, source_target_pairs={{0,12},{4,8},{8,4},{12,0},{1,13},{5,9},{9,5},{13,1},{2,14},{6,10},... | collective-permute-start | bytes 3538952 | tf_op jit(solution)/shard_map/ppermute | solution.py:36
  229.8 35.8 %collective-permute-start.10 = (bf16[4,144,1024]{2,1,0:T(8,128)(2,1)S(1)}, bf16[4,144,1024]{2,1,0:T(8,128)(2,1)S(1)}, u32[]{:S(2)}, u32[]{:S(2)}) collective-permute-start(bf16[4,144,1024]{2,1,0:T(8,128)(2,1)S(1)} %bump.2), channel_id=1, source_target_pairs={{0,4},{4,0},{8,12},{12,8},{1,5},{5,1},{9,13},{13,9},{2,6},{6,2},{1... | collective-permute-start | bytes 3538952 | tf_op jit(solution)/shard_map/ppermute | solution.py:36
  233.5 32.0 %collective-permute-start.13 = (bf16[2,128,2048]{2,1,0:T(8,128)(2,1)S(1)}, bf16[2,128,2048]{2,1,0:T(8,128)(2,1)S(1)}, u32[]{:S(2)}, u32[]{:S(2)}) collective-permute-start(bf16[2,128,2048]{2,1,0:T(8,128)(2,1)S(1)} %get-tuple-element.137), channel_id=1, source_target_pairs={{0,64},{64,0},{1,65},{65,1},{2,66},{66,2},{3,67},{67,3},{4,68},{68... | collective-permute-start | bytes 3145736 | tf_op jit(solution)/shard_map/ppermute | solution.py:32
  235.0 30.6 %collective-permute-start.14 = (bf16[2,128,2048]{2,1,0:T(8,128)(2,1)S(1)}, bf16[2,128,2048]{2,1,0:T(8,128)(2,1)S(1)}, u32[]{:S(2)}, u32[]{:S(2)}) collective-permute-start(bf16[2,128,2048]{2,1,0:T(8,128)(2,1)S(1)} %get-tuple-element.138), channel_id=1, source_target_pairs={{0,65},{1,64},{64,1},{65,0},{2,67},{3,66},{66,3},{67,2},{4,69},{5,... | collective-permute-start | bytes 3145736 | tf_op jit(solution)/shard_map/ppermute | solution.py:32
  265.6 43.5 %collective-permute-start.15 = (bf16[2,128,2048]{2,1,0:T(8,128)(2,1)}, bf16[2,128,2048]{2,1,0:T(8,128)(2,1)}, u32[]{:S(2)}, u32[]{:S(2)}) collective-permute-start(bf16[2,128,2048]{2,1,0:T(8,128)(2,1)} %get-tuple-element.144), channel_id=1, source_target_pairs={{0,1},{1,0},{2,3},{3,2},{4,5},{5,4},{6,7},{7,6},{8,9},{9,8},{10,11... | collective-permute-start | bytes 3145736 | tf_op jit(solution)/shard_map/ppermute | solution.py:32
  269.9 7.2 %collective-permute-start.16 = (bf16[144,1024]{1,0:T(8,128)(2,1)S(1)}, bf16[144,1024]{1,0:T(8,128)(2,1)S(1)}, u32[]{:S(2)}, u32[]{:S(2)}) collective-permute-start(bf16[144,1024]{1,0:T(8,128)(2,1)S(1)} %get-tuple-element.152), channel_id=1, source_target_pairs={{0,16},{16,0},{32,48},{48,32},{1,17},{17,1},{33,49},{49,33},{2,18}... | collective-permute-start | bytes 884744 | tf_op jit(solution)/shard_map/ppermute | solution.py:36
  269.9 14.2 %collective-permute-start.17 = (bf16[144,1024]{1,0:T(8,128)(2,1)S(1)}, bf16[144,1024]{1,0:T(8,128)(2,1)S(1)}, u32[]{:S(2)}, u32[]{:S(2)}) collective-permute-start(bf16[144,1024]{1,0:T(8,128)(2,1)S(1)} %get-tuple-element.153), channel_id=1, source_target_pairs={{0,32},{16,48},{32,0},{48,16},{1,33},{17,49},{33,1},{49,17},{2,34}... | collective-permute-start | bytes 884744 | tf_op jit(solution)/shard_map/ppermute | solution.py:36
  272.0 14.5 %collective-permute-start.18 = (bf16[144,1024]{1,0:T(8,128)(2,1)S(1)}, bf16[144,1024]{1,0:T(8,128)(2,1)S(1)}, u32[]{:S(2)}, u32[]{:S(2)}) collective-permute-start(bf16[144,1024]{1,0:T(8,128)(2,1)S(1)} %get-tuple-element.154), channel_id=1, source_target_pairs={{0,48},{16,32},{32,16},{48,0},{1,49},{17,33},{33,17},{49,1},{2,50}... | collective-permute-start | bytes 884744 | tf_op jit(solution)/shard_map/ppermute | solution.py:36
  294.6 7.2 %collective-permute-start.20 = (bf16[32,3584]{1,0:T(8,128)(2,1)S(1)}, bf16[32,3584]{1,0:T(8,128)(2,1)S(1)}, u32[]{:S(2)}, u32[]{:S(2)}) collective-permute-start(bf16[32,3584]{1,0:T(8,128)(2,1)S(1)} %get-tuple-element.157), channel_id=1, source_target_pairs={{0,64},{64,0},{1,65},{65,1},{2,66},{66,2},{3,67},{67,3},{4,68},{68... | collective-permute-start | bytes 688136 | tf_op jit(solution)/shard_map/ppermute | solution.py:32
  295.0 11.9 %collective-permute-start.21 = (bf16[32,3584]{1,0:T(8,128)(2,1)S(1)}, bf16[32,3584]{1,0:T(8,128)(2,1)S(1)}, u32[]{:S(2)}, u32[]{:S(2)}) collective-permute-start(bf16[32,3584]{1,0:T(8,128)(2,1)S(1)} %get-tuple-element.158), channel_id=1, source_target_pairs={{0,66},{2,64},{64,2},{66,0},{1,67},{3,65},{65,3},{67,1},{4,70},{6,... | collective-permute-start | bytes 688136 | tf_op jit(solution)/shard_map/ppermute | solution.py:32
  308.6 4.4 %collective-permute-start.22 = (f32[8,1024]{1,0:T(8,128)S(1)}, f32[8,1024]{1,0:T(8,128)S(1)}, u32[]{:S(2)}, u32[]{:S(2)}) collective-permute-start(f32[8,1024]{1,0:T(8,128)S(1)} %get-tuple-element.159), channel_id=1, source_target_pairs={{0,1},{1,0},{2,3},{3,2},{4,5},{5,4},{6,7},{7,6},{8,9},{9,8},{10,11... | collective-permute-start | bytes 98312 | tf_op jit(solution)/shard_map/ppermute | solution.py:32
  (34 other events, 424.9 us)
Sparse Core Ops, SparseCore 0:
  26.9 91.5 all-gather.1
  158.6 94.8 reduce-scatter.1

commit v5 on v4

--- a/solution.py
+++ b/solution.py
@@ -36,39 +36,31 @@
     return lax.ppermute(value, axis, [(i, i ^ bits) for i in range(4)])
 
 
-def fold_kernel(*refs):
-    inputs, keep_ref, sends = refs[:4], refs[4], refs[5:]
+def fold_kernel(mine_ref, theirs_ref, keep_ref, *sends):
     rows = keep_ref.shape[1]
-
-    def add(mine_ref, theirs_ref):
-        for which in range(2):
-            for i in range(4):
-                block = slice(i * rows, (i + 1) * rows)
-                total = mine_ref[which, block, :].astype(F32) + theirs_ref[which, block, :].astype(F32)
-                if i == 0:
-                    keep_ref[which] = total
-                else:
-                    sends[i - 1][which] = total.astype(BF16)
-
-    pl.when(pl.program_id(0) < 2)(lambda: add(inputs[0], inputs[1]))
-    pl.when(pl.program_id(0) >= 2)(lambda: add(inputs[2], inputs[3]))
-
-
-def fold(*halves):
-    _, rows, half = halves[0].shape
-    rows, tile = rows // 4, half // 2
-    low = pl.BlockSpec((2, 4 * rows, tile), lambda j: (0, 0, jnp.minimum(j, 1)))
-    high = pl.BlockSpec((2, 4 * rows, tile), lambda j: (0, 0, jnp.maximum(j - 2, 0)))
+    for which in range(2):
+        for i in range(4):
+            block = slice(i * rows, (i + 1) * rows)
+            total = mine_ref[which, block, :].astype(F32) + theirs_ref[which, block, :].astype(F32)
+            if i == 0:
+                keep_ref[which] = total
+            else:
+                sends[i - 1][which] = total.astype(BF16)
+
+
+def fold(mine, theirs):
+    _, rows, depth = mine.shape
+    rows, tile = rows // 4, depth // 4
     keep, *sends = pl.pallas_call(
         fold_kernel,
         grid=(4,),
-        in_specs=[low, low, high, high],
+        in_specs=[pl.BlockSpec((2, 4 * rows, tile), lambda j: (0, 0, j))] * 2,
         out_specs=[pl.BlockSpec((2, rows, tile), lambda j: (0, 0, j))] * 4,
-        out_shape=[like((2, rows, 2 * half), F32)] + [like((2, rows, 2 * half))] * 3,
+        out_shape=[like((2, rows, depth), F32)] + [like((2, rows, depth))] * 3,
         compiler_params=params(16),
-        cost_estimate=cost(0, 52 * rows * half),
+        cost_estimate=cost(0, 26 * rows * depth),
         name="fold",
-    )(*halves)
+    )(mine, theirs)
     return keep, sends
 
 
@@ -341,7 +333,7 @@
             pl.BlockSpec((1, depth, rows), lambda w, c, z: (w, 0, 4 * c + z)),
         ],
         out_shape=[like((2, 8 * rows, depth)), like((2, depth, 8 * rows))],
-        compiler_params=params(32),
+        compiler_params=params(12),
         cost_estimate=cost(0, 8 * mine.size * 2),
         name="tokens",
     )(mine, other)
@@ -362,58 +354,52 @@
     return total
 
 
-def mlp_kernel(pair_hbm, pair_t_hbm, bias_ref, up_ref, down_ref, *refs):
-    hidden_ref, grads_ref, bias_sums_ref, sums_ref, product_ref, level_ref, pair_ref, pair_t_ref, sems = refs
-    step, tile = pl.program_id(0), up_ref.shape[1]
+def hidden_kernel(pair_ref, bias_ref, up_ref, down_ref, hidden_ref, sums_ref):
     slope = 0.7978845608028654
-    loads = [
-        pltpu.make_async_copy(source.at[i], target.at[i], sems.at[k, i])
-        for k, (source, target) in enumerate(((pair_hbm, pair_ref), (pair_t_hbm, pair_t_ref)))
-        for i in range(2)
-    ]
-
-    def begin():
-        for load in loads:
-            load.start()
-
-    def wait(*which):
-        def body():
-            for i in which:
-                loads[i].wait()
-
-        pl.when(step == 0)(body)
-
-    pl.when(step == 0)(begin)
-    wait(0)
     up = jnp.dot(pair_ref[0], up_ref[...], preferred_element_type=F32) + bias_ref[...]
     square = up * up
     wave = jnp.tanh(up * (slope + (slope * 0.044715) * square))
     half = 0.5 + 0.5 * wave
-    activated = (up * half).astype(BF16)
-    hidden_ref[1] = activated
+    hidden_ref[1] = (up * half).astype(BF16)
     rise = half + up * (1.0 - wave * wave) * (0.5 * slope + (1.5 * slope * 0.044715) * square)
-    wait(1)
     grad = jnp.dot(pair_ref[1], down_ref[...], preferred_element_type=F32) * rise
     low = grad.astype(BF16)
     hidden_ref[0] = low
-    wait(2, 3)
-    bias_sums = jnp.sum(low.astype(F32), axis=0, keepdims=True)
-    bias_sums_ref[...] = bias_sums
-    grads_ref[:, tile:] = jnp.dot(pair_t_ref[1], activated, preferred_element_type=F32).astype(BF16)
-    grads = jnp.dot(pair_t_ref[0], low, preferred_element_type=F32)
+    sums_ref[...] = jnp.sum(low.astype(F32), axis=0, keepdims=True)
+
+
+def hidden_units(pair, bias, weights):
+    rows, depth = pair.shape[1:]
+    hidden = bias.shape[0]
+    tile = hidden // 4
+    start = (weights.shape[1] - 2 * hidden) // tile
+    column = lambda j: (0, j)
+    return pl.pallas_call(
+        hidden_kernel,
+        grid=(4,),
+        in_specs=[
+            WHOLE,
+            pl.BlockSpec((1, tile), column),
+            pl.BlockSpec((depth, tile), lambda j: (0, start + j)),
+            pl.BlockSpec((depth, tile), lambda j: (0, start + 4 + j)),
+        ],
+        out_specs=[pl.BlockSpec((2, rows, tile), lambda j: (0, 0, j)), pl.BlockSpec((1, tile), column)],
+        out_shape=[like((2, rows, hidden)), like((1, hidden), F32)],
+        compiler_params=params(40),
+        cost_estimate=cost(4 * rows * depth * hidden, 20 * MIB),
+        name="hidden",
+    )(pair, bias.reshape(1, -1), weights, weights)
+
+
+def mlp_grads_kernel(pair_t_ref, hidden_ref, bias_sums_ref, weights_ref, grads_ref, sums_ref, product_ref, level_ref):
+    step, tile = pl.program_id(0), weights_ref.shape[1]
+    grads = jnp.dot(pair_t_ref[0], hidden_ref[0], preferred_element_type=F32)
     grads_ref[:, :tile] = grads.astype(BF16)
-    weights = up_ref[...].astype(F32)
-    products, levels = lane_sums(weights * grads), lane_sums(weights * bias_sums)
-
-    @pl.when(step == 0)
-    def _():
-        product_ref[...] = products
-        level_ref[...] = levels
-
-    @pl.when(step > 0)
-    def _():
-        product_ref[...] += products
-        level_ref[...] += levels
+    weights = weights_ref[...].astype(F32)
+    products, levels = lane_sums(weights * grads), lane_sums(weights * bias_sums_ref[...])
+    product_ref[...] = jnp.where(step == 0, products, product_ref[...] + products)
+    level_ref[...] = jnp.where(step == 0, levels, level_ref[...] + levels)
+    grads_ref[:, tile:] = jnp.dot(pair_t_ref[1], hidden_ref[1], preferred_element_type=F32).astype(BF16)
 
     @pl.when(step == pl.num_programs(0) - 1)
     def _():
@@ -421,44 +407,28 @@
         sums_ref[1:2, :] = across(product_ref[...])
 
 
-def mlp(pair, pair_t, bias, weights, tile):
-    rows, depth = pair.shape[1:]
-    hidden = bias.shape[0]
-    tiles = hidden // tile
+def mlp_weight_grads(pair_t, hidden_pair, bias_sums, weights):
+    _, depth, rows = pair_t.shape
+    hidden = hidden_pair.shape[2]
+    tile = hidden // 4
     start = (weights.shape[1] - 2 * hidden) // tile
     column = lambda j: (0, j)
     return pl.pallas_call(
-        mlp_kernel,
-        grid=(tiles,),
+        mlp_grads_kernel,
+        grid=(4,),
         in_specs=[
-            ANY,
-            ANY,
+            WHOLE,
+            pl.BlockSpec((2, rows, tile), lambda j: (0, 0, j)),
             pl.BlockSpec((1, tile), column),
             pl.BlockSpec((depth, tile), lambda j: (0, start + j)),
-            pl.BlockSpec((depth, tile), lambda j: (0, start + tiles + j)),
         ],
-        out_specs=[
-            pl.BlockSpec((2, rows, tile), lambda j: (0, 0, j)),
-            pl.BlockSpec((depth, 2 * tile), column),
-            pl.BlockSpec((1, tile), column),
-            pl.BlockSpec((2, depth), lambda j: (0, 0)),
-        ],
-        out_shape=[
-            like((2, rows, hidden)),
-            like((depth, 2 * hidden)),
-            like((1, hidden), F32),
-            like((2, depth), F32),
-        ],
-        scratch_shapes=[pltpu.VMEM((depth, LANES), F32)] * 2
-        + [
-            pltpu.VMEM((2, rows, depth), BF16),
-            pltpu.VMEM((2, depth, rows), BF16),
-            pltpu.SemaphoreType.DMA((2, 2)),
-        ],
-        compiler_params=params(48),
-        cost_estimate=cost(8 * rows * depth * hidden, 40 * MIB),
-        name="mlp",
-    )(pair, pair_t, bias.reshape(1, -1), weights, weights)
+        out_specs=[pl.BlockSpec((depth, 2 * tile), column), pl.BlockSpec((2, depth), lambda j: (0, 0))],
+        out_shape=[like((depth, 2 * hidden)), like((2, depth), F32)],
+        scratch_shapes=[pltpu.VMEM((depth, LANES), F32)] * 2,
+        compiler_params=params(40),
+        cost_estimate=cost(4 * rows * depth * hidden, 20 * MIB),
+        name="mlp_grads",
+    )(pair_t, hidden_pair, bias_sums, weights)
 
 
 def split(rows):
@@ -491,19 +461,13 @@
             out[i, :block, lanes] = product_ref[chip]
             targets.append(out.at[i])
 
-    @pl.when(step == 0)
-    def _():
-        product_sums[...] = jnp.zeros_like(product_sums)
-        level_sums[...] = jnp.zeros_like(level_sums)
-        rows_ref[...] = jnp.zeros_like(rows_ref)
-
-    @pl.when(step < 3)
-    def _():
-        sums = jnp.sum(right_ref[...].astype(F32), axis=0, keepdims=True)
-        rows_ref[7:8, lanes] = sums
-        weights = weights_ref[...].astype(F32)
-        product_sums[...] += lane_sums(weights * product)
-        level_sums[...] += lane_sums(weights * sums)
+    sums = jnp.sum(right_ref[...].astype(F32), axis=0, keepdims=True)
+    weights = weights_ref[...].astype(F32)
+    fresh, inner = step == 0, jnp.where(step < 3, 1.0, 0.0)
+    products, levels = lane_sums(weights * product) * inner, lane_sums(weights * sums) * inner
+    product_sums[...] = jnp.where(fresh, products, product_sums[...] + products)
+    level_sums[...] = jnp.where(fresh, levels, level_sums[...] + levels)
+    rows_ref[7:8, lanes] = sums * inner
 
     @pl.when(step == 3)
     def _():
@@ -607,8 +571,15 @@
     )(own, one, three)
 
 
-def cut_kernel(coords, mlp_ref, *refs):
-    blocks, outs = refs[:4], refs[4:]
+def cut_kernel(coords, *refs):
+    sources, outs, targets, sems = refs[:5], refs[5:9], refs[9:14], refs[14]
+    copies = []
+    for i, (source, target) in enumerate(zip(sources, targets)):
+        copies.append(pltpu.make_async_copy(source, target, sems.at[i]))
+        copies[-1].start()
+    for copy in copies:
+        copy.wait()
+    mlp_ref, blocks = targets[0], targets[1:]
     rows, columns = outs[0].shape[0], mlp_ref.shape[1]
     block, wide = 4 * rows, blocks[0].shape[1]
     vectors = blocks[0][block:, :]
@@ -631,14 +602,17 @@
 def cut(coords, mlp_grads, blocks):
     rows, columns = mlp_grads.shape[0] // 4, mlp_grads.shape[1]
     wide = blocks[0].shape[1]
+    arrays = [mlp_grads, *blocks]
     return pl.pallas_call(
         cut_kernel,
-        in_specs=[SCALARS] + [WHOLE] * 5,
+        in_specs=[SCALARS] + [ANY] * 5,
         out_specs=[WHOLE] * 4,
         out_shape=[like((rows, columns + wide + wide // 2))] * 4,
+        scratch_shapes=[pltpu.VMEM(array.shape, array.dtype) for array in arrays]
+        + [pltpu.SemaphoreType.DMA((5,))],
         compiler_params=params(16),
         name="cut",
-    )(coords, mlp_grads, *blocks)
+    )(coords, *arrays)
 
 
 def combine_kernel(hidden_ref, right_ref, weights_ref, mine_ref, theirs_ref):
@@ -659,23 +633,19 @@
     theirs_ref[1] = total[half:].astype(BF16)
 
 
-def combine(hidden_pair, right, weights, part):
+def combine(hidden_pair, right, weights):
     _, rows, hidden = hidden_pair.shape
     depth, columns = weights.shape
     tile = depth // 4
     block = pl.BlockSpec((2, rows // 2, tile), lambda i: (0, 0, i))
     return pl.pallas_call(
         combine_kernel,
-        grid=(2,),
-        in_specs=[
-            WHOLE,
-            WHOLE,
-            pl.BlockSpec((tile, columns), lambda i: (2 * part + i, 0)),
-        ],
+        grid=(4,),
+        in_specs=[WHOLE, WHOLE, pl.BlockSpec((tile, columns), lambda i: (i, 0))],
         out_specs=[block] * 2,
-        out_shape=[like((2, rows // 2, depth // 2))] * 2,
+        out_shape=[like((2, rows // 2, depth))] * 2,
         compiler_params=params(40),
-        cost_estimate=cost(rows * depth * columns, 16 * MIB),
+        cost_estimate=cost(2 * rows * depth * columns, 16 * MIB),
         name="combine",
     )(hidden_pair, right, weights)
 
@@ -835,7 +805,8 @@
     tables = rotary_tables(doc, index)
 
     pair, pair_t, tables = lax.optimization_barrier((pair, pair_t, tables))
-    hidden_pair, mlp_grads, up_sums, mlp_sums = mlp(pair, pair_t, b_up_here, weights, hidden // 4)
+    hidden_pair, up_sums = hidden_units(pair, b_up_here, weights)
+    mlp_grads, mlp_sums = mlp_weight_grads(pair_t, hidden_pair, up_sums, weights)
     mlp_grads = scatter_plane(mlp_grads)
 
     pair, pair_t, hidden_pair = lax.optimization_barrier((pair, pair_t, hidden_pair))
@@ -847,17 +818,11 @@
     chunks, hidden_pair = lax.optimization_barrier((chunks, hidden_pair))
     own, one, three, two_low, two_high = chunks
     low, high = hop(two_low, "y", 1), hop(two_high, "y", 3)
-    first, first_theirs = combine(hidden_pair, right, weights, 0)
-    first_theirs = flip(first_theirs, "c")
-    first, hidden_pair = lax.optimization_barrier((first, hidden_pair))
-    second, second_theirs = combine(hidden_pair, right, weights, 1)
-
-    low, high, first_theirs, second, second_theirs = lax.optimization_barrier(
-        (low, high, first_theirs, second, second_theirs)
-    )
-    second_theirs = flip(second_theirs, "c")
+    mine, theirs = combine(hidden_pair, right, weights)
+    low, high, mine, theirs = lax.optimization_barrier((low, high, mine, theirs))
+    theirs = flip(theirs, "c")
     one, three = hop(bump(one, high, 1), "y", 1), hop(bump(three, low, 0), "y", 3)
-    keep, sends = fold(first, first_theirs, second, second_theirs)
+    keep, sends = fold(mine, theirs)
     near, far = flip(sends[1], "zl"), flip(sends[2], "zl", "mp")
     one, three, near, far, keep, opposite = lax.optimization_barrier(
         (one, three, near, far, keep, sends[0])

time: 322 us -> 319 us (level)
  local copies, waits for them, and re-layouts: 25.8 us -> 37 us
  Pallas kernels: 116 us -> 107 us
  waiting for transfers between devices: 132 us -> 126 us
    unnamed x75 -> x83, local copies, waits for them, and re-layouts: 22.9 us -> 34.1 us
    pallas_call x5, Pallas kernels: 59.9 us -> 52.9 us  [the longest x1 18 us: mlp_weight_grads(): pl.pallas_call(mlp_grads_kernel, grid=(4,), in_specs=[WHOLE, pl.BlockSpec...]
    all_gather x1, waiting for transfers between devices: 13.4 us -> 7.81 us  [per_device(): weights = lax.all_gather(shard, PLANE, axis=0, tiled=True)]
    ppermute x7, waiting for transfers between devices: 52.1 us -> 46.7 us  [hop(): return lax.ppermute(value, axis, [(i, i ^ bits) for i in range(4)])]
    ppermute x16 -> x15, waiting for transfers between devices: 67 us -> 71.6 us  [flip(): return lax.ppermute(value, axes, [(i, count - 1 - i) for i in range(count)])]
    ppermute x16 -> x15, starting transfers between devices: 21 us -> 22.3 us  [flip(): return lax.ppermute(value, axes, [(i, count - 1 - i) for i in range(count)])]
  transfers between devices with their start and end apart: 25 -> 24, of which waited for: 15 -> 16; matrix products, arithmetic and copies ran while one was open for 1% -> 1% of each run, Pallas kernels for 23% -> 22%
where the time goes in v5:
time: 319 us; the launch traced here: 318 us
  waiting for transfers between devices  126 us (39%)
  Pallas kernels  107 us (34%)
  local copies, waits for them, and re-layouts  37 us (12%)
  starting transfers between devices  30.6 us (10%)
  between operations  14.5 us (5%)
    ppermute x15, waiting for transfers between devices, flip(): return lax.ppermute(value, axes, [(i, count - 1 - i) for i in range(count)])  71.6 us
    ppermute x7, waiting for transfers between devices, hop(): return lax.ppermute(value, axis, [(i, i ^ bits) for i in range(4)])  46.7 us
    unnamed x83, local copies, waits for them, and re-layouts  34.1 us
    ppermute x15, starting transfers between devices, flip(): return lax.ppermute(value, axes, [(i, count - 1 - i) for i in range(count)])  22.3 us
    pallas_call x1, Pallas kernels, mlp_weight_grads(): pl.pallas_call(mlp_grads_kernel, grid=(4,), in_specs=[WHOLE, pl.BlockSpec...  18 us
    pallas_call x1, Pallas kernels, combine(): pl.pallas_call(combine_kernel, grid=(4,), in_specs=[WHOLE, WHOLE, pl.Bloc...  17.7 us
    pallas_call x1, Pallas kernels, heads(): pl.pallas_call(heads_kernel, grid=(rows // length,), in_specs=[pl.BlockSp...  16.1 us
    pallas_call x1, Pallas kernels, hidden_units(): pl.pallas_call(hidden_kernel, grid=(4,), in_specs=[WHOLE, pl.BlockSpec((1...  13.4 us
  transfers between devices with their start and end apart: 24, of which 16 were waited for; matrix products, arithmetic and copies ran while one was open for 1% of the time, Pallas kernels for 22%

profile of v5, /device:TPU:1, one launch (start us, length us, event | category | flops | bytes accessed | tf_op | source)
XLA Modules:
  0.0 317.7 jit_solution(15165885332195721988)
XLA Ops:
  14.1 5.7 %collective-permute-done.1.refs_2_ = bf16[32,3328]{1,0:T(8,128)(2,1)S(1)} collective-permute-done((bf16[32,3328]{1,0:T(8,128)(2,1)}, bf16[32,3328]{1,0:T(8,128)(2,1)S(1)}, u32[]{:S(2)}, u32[]{:S(2)}) %collective-permute-start.1) | collective-permute-done | bytes 213024 | tf_op jit(solution)/shard_map/ppermute | solution.py:32
  19.8 4.6 %collective-permute-done.2.refs_3_ = bf16[32,3328]{1,0:T(8,128)(2,1)S(1)} collective-permute-done((bf16[32,3328]{1,0:T(8,128)(2,1)}, bf16[32,3328]{1,0:T(8,128)(2,1)S(1)}, u32[]{:S(2)}, u32[]{:S(2)}) %collective-permute-start.2) | collective-permute-done | bytes 213024 | tf_op jit(solution)/shard_map/ppermute | solution.py:32
  31.9 3.7 %collective-permute-start.5 = (bf16[2,128,2048]{2,1,0:T(8,128)(2,1)S(1)}, bf16[2,128,2048]{2,1,0:T(8,128)(2,1)S(1)}, u32[]{:S(2)}, u32[]{:S(2)}) collective-permute-start(bf16[2,128,2048]{2,1,0:T(8,128)(2,1)S(1)} %get-tuple-element.89.refs_0_), channel_id=1, source_target_pairs={{0,65},{1,64},{64,1},{65,0},{2,67},{3,66},{66,3},{67,2},{4,69},{5,... | collective-permute-start | bytes 3145736 | tf_op jit(solution)/shard_map/ppermute | solution.py:32
  36.8 22.1 %collective-permute-done.5.refs_3_ = bf16[2,128,2048]{2,1,0:T(8,128)(2,1)S(1)} collective-permute-done((bf16[2,128,2048]{2,1,0:T(8,128)(2,1)S(1)}, bf16[2,128,2048]{2,1,0:T(8,128)(2,1)S(1)}, u32[]{:S(2)}, u32[]{:S(2)}) %collective-permute-start.5) | collective-permute-done | bytes 1048608 | tf_op jit(solution)/shard_map/ppermute | solution.py:32
  59.8 22.6 %collective-permute-done.3.refs_1_ = bf16[2,128,2048]{2,1,0:T(8,128)(2,1)S(1)} collective-permute-done((bf16[2,128,2048]{2,1,0:T(8,128)(2,1)S(1)}, bf16[2,128,2048]{2,1,0:T(8,128)(2,1)S(1)}, u32[]{:S(2)}, u32[]{:S(2)}) %collective-permute-start.3) | collective-permute-done | bytes 1048608 | tf_op jit(solution)/shard_map/ppermute | solution.py:32
  92.7 12.1 %tokens.1 = (bf16[2,1024,2048]{2,1,0:T(8,128)(2,1)S(1)}, bf16[2,2048,1024]{2,1,0:T(8,128)(2,1)S(1)}) custom-call(bf16[4,2,128,2048]{3,2,1,0:T(8,128)(2,1)} %join.1.mine_ref, bf16[4,2,128,2048]{3,2,1,0:T(8,128)(2,1)} %collective-permute-done.6.other_ref), custom_call_target="tpu_custom_call" | custom-call | bytes 33554432 | tf_op jit(solution)/shard_map/tokens/pallas_call | solution.py:324
  104.8 3.3 %copy-done.2 = bf16[2,2048,1024]{2,1,0:T(8,128)(2,1)} copy-done((bf16[2,2048,1024]{2,1,0:T(8,128)(2,1)}, bf16[2,2048,1024]{2,1,0:T(8,128)(2,1)S(1)}, u32[]{:S(2)}) %copy-start.2) | copy-done | bytes 8388632
  108.1 3.4 %copy-done.3 = bf16[2,1024,2048]{2,1,0:T(8,128)(2,1)} copy-done((bf16[2,1024,2048]{2,1,0:T(8,128)(2,1)}, bf16[2,1024,2048]{2,1,0:T(8,128)(2,1)S(1)}, u32[]{:S(2)}) %copy-start.3) | copy-done | bytes 8388632
  111.4 7.8 %all-gather.2.cloned.1.call-done.up_ref.down_ref.weights_ref = bf16[2048,3072]{1,0:T(8,128)(2,1)} async-done(((bf16[128,3072]{1,0:T(8,128)(2,1)}), bf16[2048,3072]{1,0:T(8,128)(2,1)}) %all-gather.2.cloned.1.call-update) | async-done | bytes 12582928 | tf_op jit(solution)/shard_map/all_gather | solution.py:789
  119.2 3.4 %copy-done.4 = bf16[2,1024,2048]{2,1,0:T(8,128)(2,1)S(1)} copy-done((bf16[2,1024,2048]{2,1,0:T(8,128)(2,1)S(1)}, bf16[2,1024,2048]{2,1,0:T(8,128)(2,1)}, u32[]{:S(2)}) %copy-start.4) | copy-done | bytes 8388632
  122.6 13.4 %hidden.1 = (bf16[2,1024,1024]{2,1,0:T(8,128)(2,1)S(1)}, f32[1,1024]{1,0:T(1,128)S(1)}) custom-call(bf16[2,1024,2048]{2,1,0:T(8,128)(2,1)S(1)} %copy-done.4, f32[1,1024]{1,0:T(1,128)S(1)} %bitcast.68, bf16[2048,3072]{1,0:T(8,128)(2,1)} %all-gather.2.cloned.1.call-done.up_ref.down_ref.weights_ref, ...), custom_call_target="tpu_custom_call" | custom-call | flops 8589934592 | bytes 20971520 | tf_op jit(solution)/shard_map/hidden/pallas_call | solution.py:377
  136.0 18.0 %mlp_grads.1 = (bf16[2048,2048]{1,0:T(8,128)(2,1)S(1)}, f32[2,2048]{1,0:T(2,128)S(1)}) custom-call(bf16[2,2048,1024]{2,1,0:T(8,128)(2,1)} %copy-done.2, bf16[2,1024,1024]{2,1,0:T(8,128)(2,1)S(1)} %get-tuple-element.119.hidden_ref, f32[1,1024]{1,0:T(1,128)S(1)} %get-tuple-element.107.bias_sums_ref.up_sums_ref, ...), custom_call_target="tpu_custom_call" | custom-call | flops 8589934592 | bytes 20971520 | tf_op jit(solution)/shard_map/mlp_grads/pallas_call | solution.py:416
  158.3 3.8 %copy-done.5 = bf16[2,1024,2048]{2,1,0:T(8,128)(2,1)S(1)} copy-done((bf16[2,1024,2048]{2,1,0:T(8,128)(2,1)S(1)}, bf16[2,1024,2048]{2,1,0:T(8,128)(2,1)}, u32[]{:S(2)}) %copy-start.5) | copy-done | bytes 8388632
  162.1 16.1 %heads.1.right_ref = bf16[1024,1024]{1,0:T(8,128)(2,1)S(1)} custom-call(bf16[2,1024,2048]{2,1,0:T(8,128)(2,1)S(1)} %copy-done.5, bf16[2048,3072]{1,0:T(8,128)(2,1)} %all-gather.2.cloned.1.call-done.up_ref.down_ref.weights_ref, f32[1,768]{1,0:T(1,128)S(1)} %bitcast.69, f32[1024,384]{1,0:T(8,128)S(1)} %get-tuple-element.102.trig_ref, ...), custom_call_target="tpu_custom_call" | custom-call | flops 27262976000 | bytes 10485760 | tf_op jit(solution)/shard_map/heads/pallas_call | solution.py:145
  178.2 10.5 %head_grads.1 = (bf16[4,144,1024]{2,1,0:T(8,128)(2,1)S(1)}, bf16[4,144,1024]{2,1,0:T(8,128)(2,1)S(1)}, bf16[4,144,1024]{2,1,0:T(8,128)(2,1)S(1)}, bf16[2,144,102...) custom-call(s32[5]{0:T(128)S(1)} %copy-done.28, bf16[2,2048,1024]{2,1,0:T(8,128)(2,1)S(1)} %bitcast.58, ...), custom_call_target="tpu_custom_call" | custom-call | flops 4294967296 | bytes 16777216 | tf_op jit(solution)/shard_map/head_grads/pallas_call | solution.py:496
  191.7 17.7 %combine.1 = (bf16[2,512,2048]{2,1,0:T(8,128)(2,1)S(1)}, bf16[2,512,2048]{2,1,0:T(8,128)(2,1)S(1)}) custom-call(bf16[2,1024,1024]{2,1,0:T(8,128)(2,1)} %copy-done.29, bf16[1024,1024]{1,0:T(8,128)(2,1)S(1)} %heads.1.right_ref, bf16[2048,3072]{1,0:T(8,128)(2,1)} %all-gather.2.cloned.1.call-done.up_ref.down_ref.weights_ref), custom_call_target="tpu_custom_call" | custom-call | flops 12884901888 | bytes 16777216 | tf_op jit(solution)/shard_map/combine/pallas_call | solution.py:641
  209.4 7.0 %collective-permute-done.7.part_ref = bf16[2,144,1024]{2,1,0:T(8,128)(2,1)S(1)} collective-permute-done((bf16[2,144,1024]{2,1,0:T(8,128)(2,1)S(1)}, bf16[2,144,1024]{2,1,0:T(8,128)(2,1)S(1)}, u32[]{:S(2)}, u32[]{:S(2)}) %collective-permute-start.7) | collective-permute-done | bytes 589856 | tf_op jit(solution)/shard_map/ppermute | solution.py:36
  222.8 4.5 %collective-permute-done.11.theirs_ref = bf16[2,512,2048]{2,1,0:T(8,128)(2,1)S(1)} collective-permute-done((bf16[2,512,2048]{2,1,0:T(8,128)(2,1)S(1)}, bf16[2,512,2048]{2,1,0:T(8,128)(2,1)S(1)}, u32[]{:S(2)}, u32[]{:S(2)}) %collective-permute-start.11) | collective-permute-done | bytes 4194336 | tf_op jit(solution)/shard_map/ppermute | solution.py:32
  233.3 25.3 %collective-permute-done.10.three_ref = bf16[4,144,1024]{2,1,0:T(8,128)(2,1)S(1)} collective-permute-done((bf16[4,144,1024]{2,1,0:T(8,128)(2,1)S(1)}, bf16[4,144,1024]{2,1,0:T(8,128)(2,1)S(1)}, u32[]{:S(2)}, u32[]{:S(2)}) %collective-permute-start.10) | collective-permute-done | bytes 1179680 | tf_op jit(solution)/shard_map/ppermute | solution.py:36
  266.7 3.5 %collective-permute-done.15.refs_2_ = bf16[144,1024]{1,0:T(8,128)(2,1)S(1)} collective-permute-done((bf16[144,1024]{1,0:T(8,128)(2,1)S(1)}, bf16[144,1024]{1,0:T(8,128)(2,1)S(1)}, u32[]{:S(2)}, u32[]{:S(2)}) %collective-permute-start.15) | collective-permute-done | bytes 294944 | tf_op jit(solution)/shard_map/ppermute | solution.py:36
  270.2 7.2 %collective-permute-done.16.refs_3_ = bf16[144,1024]{1,0:T(8,128)(2,1)S(1)} collective-permute-done((bf16[144,1024]{1,0:T(8,128)(2,1)S(1)}, bf16[144,1024]{1,0:T(8,128)(2,1)S(1)}, u32[]{:S(2)}, u32[]{:S(2)}) %collective-permute-start.16) | collective-permute-done | bytes 294944 | tf_op jit(solution)/shard_map/ppermute | solution.py:36
  289.9 5.4 %collective-permute-done.19.refs_2_ = bf16[32,3584]{1,0:T(8,128)(2,1)S(1)} collective-permute-done((bf16[32,3584]{1,0:T(8,128)(2,1)S(1)}, bf16[32,3584]{1,0:T(8,128)(2,1)S(1)}, u32[]{:S(2)}, u32[]{:S(2)}) %collective-permute-start.19) | collective-permute-done | bytes 229408 | tf_op jit(solution)/shard_map/ppermute | solution.py:32
  295.3 5.1 %collective-permute-done.20.refs_3_ = bf16[32,3584]{1,0:T(8,128)(2,1)S(1)} collective-permute-done((bf16[32,3584]{1,0:T(8,128)(2,1)S(1)}, bf16[32,3584]{1,0:T(8,128)(2,1)S(1)}, u32[]{:S(2)}, u32[]{:S(2)}) %collective-permute-start.20) | collective-permute-done | bytes 229408 | tf_op jit(solution)/shard_map/ppermute | solution.py:32
  305.1 4.0 %leave.1 = (bf16[128,2048]{1,0:T(8,128)(2,1)}, f32[128,2048]{1,0:T(8,128)}) custom-call(bf16[128,2048]{1,0:T(8,128)(2,1)S(1)} %copy-done.8, bf16[128,2048]{1,0:T(8,128)(2,1)S(1)} %copy-done.10, f32[1,2048]{1,0:T(1,128)S(1)} %bitcast.62, f32[1,2048]{1,0:T(1,128)S(1)} %bitcast.67, f32[2,128,2048]{2,1,0:T(8,128)S(1)} %get-tuple-element.131.refs_0_, ...), custom_call_target="tpu_custom_call" | custom-call | tf_op jit(solution)/shard_map/leave/pallas_call | solution.py:747
  (149 shorter events, 73.3 us)
Async XLA Ops:
  7.2 112.0 %all-gather.2.cloned.1.call-start = ((), (), s32[]{:S(2)}) async-start(), calls=%async_computation.1 | async-start | bytes 13369344 | tf_op jit(solution)/shard_map/all_gather | solution.py:789
  10.8 3.3 %collective-permute-start = (bf16[32,3328]{1,0:T(8,128)(2,1)}, bf16[32,3328]{1,0:T(8,128)(2,1)S(1)}, u32[]{:S(2)}, u32[]{:S(2)}) collective-permute-start(bf16[32,3328]{1,0:T(8,128)(2,1)} %get-tuple-element.85), channel_id=1, source_target_pairs={{0,2},{2,0},{1,3},{3,1},{4,6},{6,4},{5,7},{7,5},{8,10},{10,8},{9,1... | collective-permute-start | bytes 638984 | tf_op jit(solution)/shard_map/ppermute | solution.py:32
  12.3 7.4 %collective-permute-start.1 = (bf16[32,3328]{1,0:T(8,128)(2,1)}, bf16[32,3328]{1,0:T(8,128)(2,1)S(1)}, u32[]{:S(2)}, u32[]{:S(2)}) collective-permute-start(bf16[32,3328]{1,0:T(8,128)(2,1)} %get-tuple-element.86), channel_id=1, source_target_pairs={{0,64},{64,0},{1,65},{65,1},{2,66},{66,2},{3,67},{67,3},{4,68},{68... | collective-permute-start | bytes 638984 | tf_op jit(solution)/shard_map/ppermute | solution.py:32
  14.1 10.3 %collective-permute-start.2 = (bf16[32,3328]{1,0:T(8,128)(2,1)}, bf16[32,3328]{1,0:T(8,128)(2,1)S(1)}, u32[]{:S(2)}, u32[]{:S(2)}) collective-permute-start(bf16[32,3328]{1,0:T(8,128)(2,1)} %get-tuple-element.87), channel_id=1, source_target_pairs={{0,66},{2,64},{64,2},{66,0},{1,67},{3,65},{65,3},{67,1},{4,70},{6,... | collective-permute-start | bytes 638984 | tf_op jit(solution)/shard_map/ppermute | solution.py:32
  27.4 253.1 %reduce-scatter.2.cloned.1.call-start = ((), (), s32[]{:S(2)}) async-start(), calls=%async_computation.2 | async-start | bytes 8912896 | tf_op jit(solution)/shard_map/reduce_scatter | solution.py:759
  31.9 27.1 %collective-permute-start.5 = (bf16[2,128,2048]{2,1,0:T(8,128)(2,1)S(1)}, bf16[2,128,2048]{2,1,0:T(8,128)(2,1)S(1)}, u32[]{:S(2)}, u32[]{:S(2)}) collective-permute-start(bf16[2,128,2048]{2,1,0:T(8,128)(2,1)S(1)} %get-tuple-element.89.refs_0_), channel_id=1, source_target_pairs={{0,65},{1,64},{64,1},{65,0},{2,67},{3,66},{66,3},{67,2},{4,69},{5,... | collective-permute-start | bytes 3145736 | tf_op jit(solution)/shard_map/ppermute | solution.py:32
  35.6 24.2 %collective-permute-start.4 = (bf16[2,128,2048]{2,1,0:T(8,128)(2,1)S(1)}, bf16[2,128,2048]{2,1,0:T(8,128)(2,1)S(1)}, u32[]{:S(2)}, u32[]{:S(2)}) collective-permute-start(bf16[2,128,2048]{2,1,0:T(8,128)(2,1)S(1)} %get-tuple-element.89.refs_0_), channel_id=1, source_target_pairs={{0,64},{64,0},{1,65},{65,1},{2,66},{66,2},{3,67},{67,3},{4,68},{68... | collective-permute-start | bytes 3145736 | tf_op jit(solution)/shard_map/ppermute | solution.py:32
  35.6 46.8 %collective-permute-start.3 = (bf16[2,128,2048]{2,1,0:T(8,128)(2,1)S(1)}, bf16[2,128,2048]{2,1,0:T(8,128)(2,1)S(1)}, u32[]{:S(2)}, u32[]{:S(2)}) collective-permute-start(bf16[2,128,2048]{2,1,0:T(8,128)(2,1)S(1)} %get-tuple-element.89.refs_0_), channel_id=1, source_target_pairs={{0,1},{1,0},{2,3},{3,2},{4,5},{5,4},{6,7},{7,6},{8,9},{9,8},{10,11... | collective-permute-start | bytes 3145736 | tf_op jit(solution)/shard_map/ppermute | solution.py:32
  84.4 8.2 %collective-permute-start.6 = (bf16[4,2,128,2048]{3,2,1,0:T(8,128)(2,1)}, bf16[4,2,128,2048]{3,2,1,0:T(8,128)(2,1)}, u32[]{:S(2)}, u32[]{:S(2)}) collective-permute-start(bf16[4,2,128,2048]{3,2,1,0:T(8,128)(2,1)} %join.1.mine_ref), channel_id=1, source_target_pairs={{0,2},{2,0},{1,3},{3,1},{4,6},{6,4},{5,7},{7,5},{8,10},{10,8},{9,1... | collective-permute-start | bytes 12582920 | tf_op jit(solution)/shard_map/ppermute | solution.py:32
  188.8 27.6 %collective-permute-start.7 = (bf16[2,144,1024]{2,1,0:T(8,128)(2,1)S(1)}, bf16[2,144,1024]{2,1,0:T(8,128)(2,1)S(1)}, u32[]{:S(2)}, u32[]{:S(2)}) collective-permute-start(bf16[2,144,1024]{2,1,0:T(8,128)(2,1)S(1)} %get-tuple-element.117), channel_id=1, source_target_pairs={{0,4},{4,0},{8,12},{12,8},{1,5},{5,1},{9,13},{13,9},{2,6},{6,2},{1... | collective-permute-start | bytes 1769480 | tf_op jit(solution)/shard_map/ppermute | solution.py:36
  189.9 28.5 %collective-permute-start.8 = (bf16[2,144,1024]{2,1,0:T(8,128)(2,1)S(1)}, bf16[2,144,1024]{2,1,0:T(8,128)(2,1)S(1)}, u32[]{:S(2)}, u32[]{:S(2)}) collective-permute-start(bf16[2,144,1024]{2,1,0:T(8,128)(2,1)S(1)} %get-tuple-element.118), channel_id=1, source_target_pairs={{0,12},{4,8},{8,4},{12,0},{1,13},{5,9},{9,5},{13,1},{2,14},{6,10},... | collective-permute-start | bytes 1769480 | tf_op jit(solution)/shard_map/ppermute | solution.py:36
  218.4 8.8 %collective-permute-start.11 = (bf16[2,512,2048]{2,1,0:T(8,128)(2,1)S(1)}, bf16[2,512,2048]{2,1,0:T(8,128)(2,1)S(1)}, u32[]{:S(2)}, u32[]{:S(2)}) collective-permute-start(bf16[2,512,2048]{2,1,0:T(8,128)(2,1)S(1)} %get-tuple-element.126), channel_id=1, source_target_pairs={{0,2},{2,0},{1,3},{3,1},{4,6},{6,4},{5,7},{7,5},{8,10},{10,8},{9,1... | collective-permute-start | bytes 12582920 | tf_op jit(solution)/shard_map/ppermute | solution.py:32
  220.9 37.7 %collective-permute-start.10 = (bf16[4,144,1024]{2,1,0:T(8,128)(2,1)S(1)}, bf16[4,144,1024]{2,1,0:T(8,128)(2,1)S(1)}, u32[]{:S(2)}, u32[]{:S(2)}) collective-permute-start(bf16[4,144,1024]{2,1,0:T(8,128)(2,1)S(1)} %bump.3), channel_id=1, source_target_pairs={{0,12},{4,8},{8,4},{12,0},{1,13},{5,9},{9,5},{13,1},{2,14},{6,10},... | collective-permute-start | bytes 3538952 | tf_op jit(solution)/shard_map/ppermute | solution.py:36
  222.7 36.0 %collective-permute-start.9 = (bf16[4,144,1024]{2,1,0:T(8,128)(2,1)S(1)}, bf16[4,144,1024]{2,1,0:T(8,128)(2,1)S(1)}, u32[]{:S(2)}, u32[]{:S(2)}) collective-permute-start(bf16[4,144,1024]{2,1,0:T(8,128)(2,1)S(1)} %bump.2), channel_id=1, source_target_pairs={{0,4},{4,0},{8,12},{12,8},{1,5},{5,1},{9,13},{13,9},{2,6},{6,2},{1... | collective-permute-start | bytes 3538952 | tf_op jit(solution)/shard_map/ppermute | solution.py:36
  230.1 28.5 %collective-permute-start.12 = (bf16[2,128,2048]{2,1,0:T(8,128)(2,1)S(1)}, bf16[2,128,2048]{2,1,0:T(8,128)(2,1)S(1)}, u32[]{:S(2)}, u32[]{:S(2)}) collective-permute-start(bf16[2,128,2048]{2,1,0:T(8,128)(2,1)S(1)} %get-tuple-element.127), channel_id=1, source_target_pairs={{0,64},{64,0},{1,65},{65,1},{2,66},{66,2},{3,67},{67,3},{4,68},{68... | collective-permute-start | bytes 3145736 | tf_op jit(solution)/shard_map/ppermute | solution.py:32
  231.3 27.4 %collective-permute-start.13 = (bf16[2,128,2048]{2,1,0:T(8,128)(2,1)S(1)}, bf16[2,128,2048]{2,1,0:T(8,128)(2,1)S(1)}, u32[]{:S(2)}, u32[]{:S(2)}) collective-permute-start(bf16[2,128,2048]{2,1,0:T(8,128)(2,1)S(1)} %get-tuple-element.128), channel_id=1, source_target_pairs={{0,65},{1,64},{64,1},{65,0},{2,67},{3,66},{66,3},{67,2},{4,69},{5,... | collective-permute-start | bytes 3145736 | tf_op jit(solution)/shard_map/ppermute | solution.py:32
  258.7 44.0 %collective-permute-start.14 = (bf16[2,128,2048]{2,1,0:T(8,128)(2,1)}, bf16[2,128,2048]{2,1,0:T(8,128)(2,1)}, u32[]{:S(2)}, u32[]{:S(2)}) collective-permute-start(bf16[2,128,2048]{2,1,0:T(8,128)(2,1)} %get-tuple-element.134), channel_id=1, source_target_pairs={{0,1},{1,0},{2,3},{3,2},{4,5},{5,4},{6,7},{7,6},{8,9},{9,8},{10,11... | collective-permute-start | bytes 3145736 | tf_op jit(solution)/shard_map/ppermute | solution.py:32
  262.9 7.3 %collective-permute-start.15 = (bf16[144,1024]{1,0:T(8,128)(2,1)S(1)}, bf16[144,1024]{1,0:T(8,128)(2,1)S(1)}, u32[]{:S(2)}, u32[]{:S(2)}) collective-permute-start(bf16[144,1024]{1,0:T(8,128)(2,1)S(1)} %get-tuple-element.142), channel_id=1, source_target_pairs={{0,16},{16,0},{32,48},{48,32},{1,17},{17,1},{33,49},{49,33},{2,18}... | collective-permute-start | bytes 884744 | tf_op jit(solution)/shard_map/ppermute | solution.py:36
  262.9 14.5 %collective-permute-start.16 = (bf16[144,1024]{1,0:T(8,128)(2,1)S(1)}, bf16[144,1024]{1,0:T(8,128)(2,1)S(1)}, u32[]{:S(2)}, u32[]{:S(2)}) collective-permute-start(bf16[144,1024]{1,0:T(8,128)(2,1)S(1)} %get-tuple-element.143), channel_id=1, source_target_pairs={{0,32},{16,48},{32,0},{48,16},{1,33},{17,49},{33,1},{49,17},{2,34}... | collective-permute-start | bytes 884744 | tf_op jit(solution)/shard_map/ppermute | solution.py:36
  265.3 14.5 %collective-permute-start.17 = (bf16[144,1024]{1,0:T(8,128)(2,1)S(1)}, bf16[144,1024]{1,0:T(8,128)(2,1)S(1)}, u32[]{:S(2)}, u32[]{:S(2)}) collective-permute-start(bf16[144,1024]{1,0:T(8,128)(2,1)S(1)} %get-tuple-element.144), channel_id=1, source_target_pairs={{0,48},{16,32},{32,16},{48,0},{1,49},{17,33},{33,17},{49,1},{2,50}... | collective-permute-start | bytes 884744 | tf_op jit(solution)/shard_map/ppermute | solution.py:36
  285.6 4.2 %collective-permute-start.18 = (bf16[32,3584]{1,0:T(8,128)(2,1)S(1)}, bf16[32,3584]{1,0:T(8,128)(2,1)S(1)}, u32[]{:S(2)}, u32[]{:S(2)}) collective-permute-start(bf16[32,3584]{1,0:T(8,128)(2,1)S(1)} %get-tuple-element.146), channel_id=1, source_target_pairs={{0,2},{2,0},{1,3},{3,1},{4,6},{6,4},{5,7},{7,5},{8,10},{10,8},{9,1... | collective-permute-start | bytes 688136 | tf_op jit(solution)/shard_map/ppermute | solution.py:32
  288.2 7.2 %collective-permute-start.19 = (bf16[32,3584]{1,0:T(8,128)(2,1)S(1)}, bf16[32,3584]{1,0:T(8,128)(2,1)S(1)}, u32[]{:S(2)}, u32[]{:S(2)}) collective-permute-start(bf16[32,3584]{1,0:T(8,128)(2,1)S(1)} %get-tuple-element.147), channel_id=1, source_target_pairs={{0,64},{64,0},{1,65},{65,1},{2,66},{66,2},{3,67},{67,3},{4,68},{68... | collective-permute-start | bytes 688136 | tf_op jit(solution)/shard_map/ppermute | solution.py:32
  288.3 12.2 %collective-permute-start.20 = (bf16[32,3584]{1,0:T(8,128)(2,1)S(1)}, bf16[32,3584]{1,0:T(8,128)(2,1)S(1)}, u32[]{:S(2)}, u32[]{:S(2)}) collective-permute-start(bf16[32,3584]{1,0:T(8,128)(2,1)S(1)} %get-tuple-element.148), channel_id=1, source_target_pairs={{0,66},{2,64},{64,2},{66,0},{1,67},{3,65},{65,3},{67,1},{4,70},{6,... | collective-permute-start | bytes 688136 | tf_op jit(solution)/shard_map/ppermute | solution.py:32
  302.1 6.9 %collective-permute-start.21 = (f32[8,1024]{1,0:T(8,128)S(1)}, f32[8,1024]{1,0:T(8,128)S(1)}, u32[]{:S(2)}, u32[]{:S(2)}) collective-permute-start(f32[8,1024]{1,0:T(8,128)S(1)} %get-tuple-element.149), channel_id=1, source_target_pairs={{0,1},{1,0},{2,3},{3,2},{4,5},{5,4},{6,7},{7,6},{8,9},{9,8},{10,11... | collective-permute-start | bytes 98312 | tf_op jit(solution)/shard_map/ppermute | solution.py:32
  (37 other events, 611.4 us)
Sparse Core Ops, SparseCore 0:
  27.6 91.6 all-gather.1
  157.4 97.8 reduce-scatter.1

commit v6 on v5

v6 whole, which is shorter than its diff:
```python
import functools

import jax
import jax.numpy as jnp
from jax import lax
from jax.experimental import pallas as pl
from jax.experimental.pallas import tpu as pltpu
from jax.sharding import Mesh, PartitionSpec as P

HEAD_DIM = 64
ROT = 32
HALF = ROT // 2
LANES = 128
EPSILON = 1e-05

AXES = ("zl", "x", "y", "c", "mp")
SIZES = (2, 4, 4, 2, 2)
PLANE = ("x", "y")
PAIR = ("zl", "c")

BF16 = jnp.bfloat16
F32 = jnp.float32
MIB = 1024 * 1024
GIGA = 1000 * MIB
ANY = pl.BlockSpec(memory_space=pl.ANY)
WHOLE = pl.BlockSpec(memory_space=pltpu.VMEM)
SCALARS = pl.BlockSpec(memory_space=pltpu.SMEM)


def flip(value, *axes):
    count = 2 ** len(axes)
    return lax.ppermute(value, axes, [(i, count - 1 - i) for i in range(count)])


def hop(value, axis, bits):
    return lax.ppermute(value, axis, [(i, i ^ bits) for i in range(4)])


def fold_kernel(mine_ref, theirs_ref, keep_ref, *sends):
    rows = keep_ref.shape[1]
    for which in range(2):
        for i in range(4):
            block = slice(i * rows, (i + 1) * rows)
            total = mine_ref[which, block, :].astype(F32) + theirs_ref[which, block, :].astype(F32)
            if i == 0:
                keep_ref[which] = total
            else:
                sends[i - 1][which] = total.astype(BF16)


def fold(mine, theirs):
    _, rows, depth = mine.shape
    rows, tile = rows // 4, depth // 4
    keep, *sends = pl.pallas_call(
        fold_kernel,
        grid=(4,),
        in_specs=[pl.BlockSpec((2, 4 * rows, tile), lambda j: (0, 0, j))] * 2,
        out_specs=[pl.BlockSpec((2, rows, tile), lambda j: (0, 0, j))] * 4,
        out_shape=[like((2, rows, depth), F32)] + [like((2, rows, depth))] * 3,
        compiler_params=params(16),
        cost_estimate=cost(0, 26 * rows * depth),
        name="fold",
    )(mine, theirs)
    return keep, sends


def lane_sums(value):
    total = value[:, :LANES]
    for start in range(LANES, value.shape[1], LANES):
        total = total + value[:, start : start + LANES]
    return total


def across(columns):
    ones = jnp.ones((8, columns.shape[1]), F32)
    contract = (((1,), (1,)), ((), ()))
    return lax.dot_general(
        ones, columns, contract, precision=lax.Precision.HIGHEST, preferred_element_type=F32
    )[:1]


def heads_kernel(
    pair_hbm,
    pair_t_hbm,
    weights_hbm,
    bias_ref,
    trig_ref,
    segment_col,
    segment_row,
    index_col,
    index_row,
    right_hbm,
    grads_hbm,
    bias_sums_ref,
    sums_ref,
    pair_ref,
    pair_t_ref,
    weights_ref,
    right_ref,
    grads_ref,
    linear_ref,
    query_ref,
    key_ref,
    value_ref,
    grad_ref,
    grad_query_ref,
    grad_key_ref,
    attended_ref,
    product_ref,
    level_ref,
    sems,
):
    length, width = grad_ref.shape
    count, columns = segment_row.shape[0], weights_ref.shape[1]
    tile = grads_ref.shape[2]
    scale = HEAD_DIM ** (-0.5)

    def rows_of(i):
        return pl.ds(pl.multiple_of(i * length, length), length)

    def load_tokens(i):
        some = rows_of(i)
        return pltpu.make_async_copy(pair_hbm.at[:, some, :], pair_ref.at[:, some, :], sems.at[i])

    load_weights = pltpu.make_async_copy(
        weights_hbm.at[:, pl.ds(0, columns)], weights_ref, sems.at[count]
    )
    load_features = [
        pltpu.make_async_copy(pair_t_hbm.at[i], pair_t_ref.at[i], sems.at[count + 1 + i]) for i in range(2)
    ]
    store_right = pltpu.make_async_copy(right_ref, right_hbm, sems.at[count + 3])

    def store_grads(j):
        lanes = pl.ds(pl.multiple_of(j * tile, tile), tile)
        return pltpu.make_async_copy(grads_ref.at[j], grads_hbm.at[:, lanes], sems.at[count + 4 + j])

    load_weights.start()
    for i in range(count):
        load_tokens(i).start()
    for load in load_features:
        load.start()
    load_weights.wait()
    both = (((1,), (1,)), ((), ()))

    def one_sequence(i, carry):
        some = rows_of(i)
        load_tokens(i).wait()
        linear_ref[...] = (
            jnp.dot(pair_ref[0, some, :], weights_ref[:, : 3 * width], preferred_element_type=F32)
            + bias_ref[...]
        )
        grad_ref[...] = jnp.dot(
            pair_ref[1, some, :], weights_ref[:, 3 * width :], preferred_element_type=F32
        ).astype(BF16)
        trig = trig_ref[some, :]

        def rotated(value, sign):
            ahead = pltpu.roll(value, LANES - HALF, 1)
            behind = pltpu.roll(value, HALF, 1)
            turned = ahead * trig[:, LANES : 2 * LANES] + behind * trig[:, 2 * LANES :]
            return value * trig[:, :LANES] + turned * sign

        for start in range(0, width, LANES):
            lanes = slice(start, start + LANES)
            query_ref[:, lanes] = (rotated(linear_ref[:, lanes], 1.0) * scale).astype(BF16)
            keys = linear_ref[:, width + start : width + start + LANES]
            key_ref[:, lanes] = rotated(keys, 1.0).astype(BF16)
            values = linear_ref[:, 2 * width + start : 2 * width + start + LANES]
            value_ref[:, lanes] = values.astype(BF16)
        allowed = (segment_row[i] == segment_col[some, :]) & (index_row[i] >= index_col[some, :])
        value_t, key_t = value_ref[...].T, key_ref[...].T
        for start in range(0, width, HEAD_DIM):
            lanes = slice(start, start + HEAD_DIM)
            query, key, value = query_ref[:, lanes], key_ref[:, lanes], value_ref[:, lanes]
            grad = grad_ref[:, lanes]
            scores = lax.dot_general(key, query, both, preferred_element_type=F32)
            scores = jnp.where(allowed, scores, -1000000000.0)
            expo = jnp.exp(scores - jnp.max(scores, axis=0, keepdims=True))
            probs = expo * (1.0 / jnp.sum(expo, axis=0, keepdims=True))
            low_probs = probs.astype(BF16)
            attended_ref[lanes, :] = jnp.dot(value_t[lanes], low_probs, preferred_element_type=F32)
            grad_probs = lax.dot_general(value, grad, both, preferred_element_type=F32)
            grad_values = jnp.dot(low_probs, grad, preferred_element_type=F32)
            weighted = probs * grad_probs
            delta = jnp.sum(weighted, axis=0, keepdims=True)
            grad_scores = (weighted - probs * delta).astype(BF16)
            grad_queries = jnp.dot(key_t[lanes], grad_scores, preferred_element_type=F32)
            grad_query_ref[lanes, :] = grad_queries * scale
            grad_key_ref[:, lanes] = jnp.dot(grad_scores, query, preferred_element_type=F32)
            right_ref[some, 2 * width + start : 2 * width + start + HEAD_DIM] = grad_values.astype(BF16)
        right_ref[some, 3 * width :] = attended_ref[...].T.astype(BF16)
        linear_ref[:, :width] = grad_query_ref[...].T
        for start in range(0, width, LANES):
            lanes = slice(start, start + LANES)
            right_ref[some, lanes] = rotated(linear_ref[:, lanes], -1.0).astype(BF16)
            right_ref[some, width + start : width + start + LANES] = rotated(
                grad_key_ref[:, lanes], -1.0
            ).astype(BF16)
        return carry

    lax.fori_loop(0, count, one_sequence, 0)
    store_right.start()
    for load in load_features:
        load.wait()
    product_ref[...] = jnp.zeros_like(product_ref)
    level_ref[...] = jnp.zeros_like(level_ref)

    def one_tile(j, carry):
        lanes = pl.ds(pl.multiple_of(j * tile, tile), tile)
        right = right_ref[:, lanes]
        product = jnp.dot(pair_t_ref[j // 3], right, preferred_element_type=F32)
        grads_ref[j] = product.astype(BF16)
        store_grads(j).start()
        inner = jnp.where(j < 3, 1.0, 0.0)
        sums = jnp.sum(right.astype(F32), axis=0, keepdims=True) * inner
        bias_sums_ref[:, lanes] = sums
        weights = weights_ref[:, lanes].astype(F32)
        product_ref[...] += lane_sums(weights * product) * inner
        level_ref[...] += lane_sums(weights * sums)
        return carry

    lax.fori_loop(0, 4, one_tile, 0)
    sums_ref[0:1, :] = across(level_ref[...])
    sums_ref[1:2, :] = across(product_ref[...])
    store_right.wait()
    for j in range(4):
        store_grads(j).wait()


def heads(pair, pair_t, weights, bias, tables, length):
    _, rows, depth = pair.shape
    width = bias.shape[0] // 3
    columns, count = 4 * width, rows // length
    return pl.pallas_call(
        heads_kernel,
        in_specs=[ANY] * 3 + [WHOLE] * 6,
        out_specs=[ANY, ANY, WHOLE, WHOLE],
        out_shape=[
            like((rows, columns)),
            like((depth, columns)),
            like((1, columns), F32),
            like((2, depth), F32),
        ],
        scratch_shapes=[
            pltpu.VMEM((2, rows, depth), BF16),
            pltpu.VMEM((2, depth, rows), BF16),
            pltpu.VMEM((depth, columns), BF16),
            pltpu.VMEM((rows, columns), BF16),
            pltpu.VMEM((4, depth, width), BF16),
            pltpu.VMEM((length, 3 * width), F32),
        ]
        + [pltpu.VMEM((length, width), BF16)] * 4
        + [
            pltpu.VMEM((width, length), F32),
            pltpu.VMEM((length, width), F32),
            pltpu.VMEM((width, length), F32),
            pltpu.VMEM((depth, LANES), F32),
            pltpu.VMEM((depth, LANES), F32),
            pltpu.SemaphoreType.DMA((count + 8,)),
        ],
        compiler_params=params(60),
        cost_estimate=cost(30 * GIGA, 10 * MIB),
        name="heads",
    )(pair, pair_t, weights, bias.reshape(1, -1), *tables)


def tables_kernel(cos_ref, sin_ref, *refs):
    inputs, outputs = refs[:4], refs[5:]
    trig_ref = refs[4]
    cos, sin = cos_ref[...], sin_ref[...]
    trig_ref[...] = jnp.zeros_like(trig_ref)
    for start in range(0, LANES, HEAD_DIM):
        rest = (cos.shape[0], HEAD_DIM - ROT)
        trig_ref[:, start : start + HALF] = cos
        trig_ref[:, start + HALF : start + ROT] = cos
        trig_ref[:, start + ROT : start + HEAD_DIM] = jnp.ones(rest, F32)
        trig_ref[:, LANES + start : LANES + start + HALF] = -sin
        trig_ref[:, 2 * LANES + start + HALF : 2 * LANES + start + ROT] = sin
    for source, target in zip(inputs, outputs):
        target[...] = source[...]


def rotary_tables(doc, index):
    count, length = doc.shape
    rows = count * length
    same_doc = doc[:, :, None] == doc[:, None, :]
    doc_start = jnp.min(jnp.where(same_doc, index[:, None, :], length), axis=2)
    positions = (index - doc_start).astype(F32).reshape(-1)
    inv_freq = 10000.0 ** (-(jnp.arange(HALF, dtype=F32) * 2.0 / ROT))
    angles = positions[:, None] * inv_freq
    column, row = (rows, 1), (count, 1, length)
    shapes = [column, row, column, row]
    passed = [value.reshape(shape) for value, shape in zip((doc, doc, index, index), shapes)]
    return pl.pallas_call(
        tables_kernel,
        in_specs=[WHOLE] * 6,
        out_specs=[WHOLE] * 5,
        out_shape=[like((rows, 3 * LANES), F32)] + [like(shape, jnp.int32) for shape in shapes],
        compiler_params=params(16),
        name="tables",
    )(jnp.cos(angles), jnp.sin(angles), *passed)


def like(shape, dtype=BF16):
    return jax.ShapeDtypeStruct(shape, dtype)


def params(mib):
    return pltpu.CompilerParams(vmem_limit_bytes=mib * MIB)


def cost(flops, moved):
    return pl.CostEstimate(flops=flops, bytes_accessed=moved, transcendentals=0)


def slot_of(coords, bits):
    return (coords[0] * 2 + coords[3]) ^ bits


def pack_kernel(coords, up_ref, down_ref, qkv_ref, out_ref, segment_ref, *refs):
    parts, sems = refs[:4], refs[4]
    hidden, width = up_ref.shape[1] // 4, out_ref.shape[1] // 4
    copies = []

    def copy(source, target):
        copies.append(pltpu.make_async_copy(source, target, sems.at[len(copies)]))
        copies[-1].start()

    for bits in (1, 2, 3, 0):
        slot = slot_of(coords, bits)
        wide = pl.ds(pl.multiple_of(slot * hidden, hidden), hidden)
        narrow = pl.ds(pl.multiple_of(slot * width, width), width)
        part = parts[bits]
        for kind in range(3):
            copy(qkv_ref.at[kind, :, narrow], part.at[:, pl.ds(kind * width, width)])
        copy(out_ref.at[:, narrow], part.at[:, pl.ds(3 * width, width)])
        copy(up_ref.at[:, wide], part.at[:, pl.ds(4 * width, hidden)])
        copy(down_ref.at[:, wide], part.at[:, pl.ds(4 * width + hidden, hidden)])
    segments = segment_ref[...].astype(F32).astype(BF16)
    segments = jnp.broadcast_to(segments, (up_ref.shape[0], segments.shape[1]))
    for part in parts:
        part[:, 4 * width + 2 * hidden :] = segments
    for each in copies:
        each.wait()


def pack(coords, w_up, down_t, qkv_t, out_t, segments):
    rows, hidden, width = w_up.shape[0], w_up.shape[1] // 4, out_t.shape[1] // 4
    return pl.pallas_call(
        pack_kernel,
        in_specs=[SCALARS] + [ANY] * 4 + [WHOLE],
        out_specs=[WHOLE] * 4,
        out_shape=[like((rows, 2 * hidden + 4 * width + segments.shape[0]))] * 4,
        scratch_shapes=[pltpu.SemaphoreType.DMA((24,))],
        compiler_params=params(60),
        name="pack",
    )(coords, w_up, down_t, qkv_t, out_t, segments.reshape(1, -1))


def order_kernel(coords, *refs):
    parts, out = refs[:4], refs[4]
    for bits in range(4):
        out[coords[0] ^ (bits >> 1), coords[3] ^ (bits & 1)] = parts[bits][:, : out.shape[3]]


def order(coords, parts, columns):
    rows = parts[0].shape[0]
    out = pl.pallas_call(
        order_kernel,
        in_specs=[SCALARS] + [WHOLE] * 4,
        out_specs=WHOLE,
        out_shape=like((2, 2, rows, columns)),
        compiler_params=params(16),
        name="order",
    )(coords, *parts)
    return out.reshape(4 * rows, columns)


def join_kernel(*refs):
    parts, out, sem = refs[:-2], refs[-2], refs[-1]
    copies = []
    for i, part in enumerate(parts):
        copies.append(pltpu.make_async_copy(part, out.at[i], sem.at[i]))
        copies[-1].start()
    for copy in copies:
        copy.wait()


def join(*parts):
    return pl.pallas_call(
        join_kernel,
        in_specs=[ANY] * len(parts),
        out_specs=ANY,
        out_shape=like((len(parts),) + parts[0].shape),
        scratch_shapes=[pltpu.SemaphoreType.DMA((len(parts),))],
        compiler_params=params(16),
        name="join",
    )(*parts)


def tokens_kernel(mine_ref, other_ref, rows_ref, columns_ref):
    @pl.when(pl.program_id(1) == 0)
    def _():
        rows_ref[0] = mine_ref[0, 0]
        columns_ref[0] = mine_ref[0, 0].T

    @pl.when(pl.program_id(1) == 1)
    def _():
        rows_ref[0] = other_ref[0, 0]
        columns_ref[0] = other_ref[0, 0].T


def gather_tokens(*pairs):
    mine = join(*pairs)
    other = flip(mine, "c")
    _, _, rows, depth = mine.shape
    block = (1, 1, rows, depth)
    return pl.pallas_call(
        tokens_kernel,
        grid=(2, 2, 4),
        in_specs=[
            pl.BlockSpec(block, lambda w, c, z: (jnp.where(c == 0, z, 3), w, 0, 0)),
            pl.BlockSpec(block, lambda w, c, z: (jnp.where(c == 1, z, 0), w, 0, 0)),
        ],
        out_specs=[
            pl.BlockSpec((1, rows, depth), lambda w, c, z: (w, 4 * c + z, 0)),
            pl.BlockSpec((1, depth, rows), lambda w, c, z: (w, 0, 4 * c + z)),
        ],
        out_shape=[like((2, 8 * rows, depth)), like((2, depth, 8 * rows))],
        compiler_params=params(12),
        cost_estimate=cost(0, 8 * mine.size * 2),
        name="tokens",
    )(mine, other)


def split(rows):
    high = rows.astype(BF16)
    return high, (rows - high.astype(F32)).astype(BF16)


def whole(rows):
    count = rows.shape[0] // 2
    return rows[:count].astype(F32) + rows[count:].astype(F32)


GROUPS = ((0, 4), (4, 4), (8, 4), (12, 2), (14, 2))


def place_of(first_bits, second_bits):
    return (0, 4, 12, 8)[first_bits] + second_bits


def mlp_kernel(
    coords,
    pair_hbm,
    pair_t_hbm,
    weights_hbm,
    bias_ref,
    gain_ref,
    shift_ref,
    cot_ref,
    head_sums_ref,
    head_bias_ref,
    hidden_hbm,
    *refs,
):
    up_outs, down_outs = refs[:5], refs[5:10]
    (
        pair_ref,
        pair_t_ref,
        up_ref,
        down_ref,
        hidden_ref,
        up_blocks,
        down_blocks,
        staged_ref,
        bias_sums_ref,
        rows_ref,
        turned_ref,
        product_ref,
        level_ref,
        load_sems,
        store_sems,
    ) = refs[10:]
    x, y = coords[1], coords[2]
    tiles, depth, tile = up_ref.shape
    hidden, half = tiles * tile, pair_ref.shape[1] // 2
    block = down_blocks.shape[1]
    start = weights_hbm.shape[1] - 2 * hidden
    slope = 0.7978845608028654

    def load_weights(j, which):
        lanes = pl.ds(pl.multiple_of(start + which * hidden + j * tile, tile), tile)
        target = (up_ref, down_ref)[which].at[j]
        return pltpu.make_async_copy(weights_hbm.at[:, lanes], target, load_sems.at[2 * j + which])

    def load_tokens(i):
        some = pl.ds(i * half, half)
        return pltpu.make_async_copy(
            pair_hbm.at[:, some, :], pair_ref.at[:, some, :], load_sems.at[2 * tiles + i]
        )

    load_features = [
        pltpu.make_async_copy(pair_t_hbm.at[i], pair_t_ref.at[i], load_sems.at[2 * tiles + 2 + i])
        for i in range(2)
    ]
    store_hidden = pltpu.make_async_copy(hidden_ref, hidden_hbm, store_sems.at[tiles, 0])

    def store_blocks(j):
        lanes = pl.ds(pl.multiple_of(j * tile, tile), tile)
        some = pl.ds(0, block)
        copies = []
        for blocks, outs in ((up_blocks, up_outs), (down_blocks, down_outs)):
            for (first, count), out in zip(GROUPS, outs):
                source = blocks.at[pl.ds(first, count), some, lanes]
                sem = store_sems.at[j, len(copies)]
                copies.append(pltpu.make_async_copy(source, out.at[:, some, lanes], sem))
        return copies

    load_tokens(0).start()
    for j in range(tiles):
        for which in range(2):
            load_weights(j, which).start()
        if j == 0:
            load_tokens(1).start()
    for load in load_features:
        load.start()

    def units(i):
        some = pl.ds(i * half, half)
        load_tokens(i).wait()

        def one_tile(j, carry):
            if i == 0:
                load_weights(j, 0).wait()
                load_weights(j, 1).wait()
            lanes = pl.ds(pl.multiple_of(j * tile, tile), tile)
            up = jnp.dot(pair_ref[0, some, :], up_ref[j], preferred_element_type=F32) + bias_ref[:, lanes]
            square = up * up
            wave = jnp.tanh(up * (slope + (slope * 0.044715) * square))
            gate = 0.5 + 0.5 * wave
            hidden_ref[1, some, lanes] = (up * gate).astype(BF16)
            rise = gate + up * (1.0 - wave * wave) * (0.5 * slope + (1.5 * slope * 0.044715) * square)
            grad = jnp.dot(pair_ref[1, some, :], down_ref[j], preferred_element_type=F32) * rise
            low = grad.astype(BF16)
            hidden_ref[0, some, lanes] = low
            sums = jnp.sum(low.astype(F32), axis=0, keepdims=True)
            bias_sums_ref[:, lanes] = sums if i == 0 else bias_sums_ref[:, lanes] + sums
            return carry

        lax.fori_loop(0, tiles, one_tile, 0)

    units(0)
    units(1)
    store_hidden.start()
    for load in load_features:
        load.wait()
    product_ref[...] = jnp.zeros_like(product_ref)
    level_ref[...] = jnp.zeros_like(level_ref)

    def one_tile(j, carry):
        lanes = pl.ds(pl.multiple_of(j * tile, tile), tile)
        product = jnp.dot(pair_t_ref[0], hidden_ref[0, :, lanes], preferred_element_type=F32)
        staged_ref[0] = product.astype(BF16).reshape(staged_ref.shape[1:])
        weights = up_ref[j].astype(F32)
        product_ref[...] += lane_sums(weights * product)
        level_ref[...] += lane_sums(weights * bias_sums_ref[:, lanes])
        product = jnp.dot(pair_t_ref[1], hidden_ref[1, :, lanes], preferred_element_type=F32)
        staged_ref[1] = product.astype(BF16).reshape(staged_ref.shape[1:])
        for x_bits in range(4):
            for y_bits in range(4):
                chip = (x ^ x_bits) * 4 + (y ^ y_bits)
                up_blocks[place_of(y_bits, x_bits), :block, lanes] = staged_ref[0, chip]
                down_blocks[place_of(x_bits, y_bits), :, lanes] = staged_ref[1, chip]
        for copy in store_blocks(j):
            copy.start()
        return carry

    lax.fori_loop(0, tiles, one_tile, 0)

    level = head_sums_ref[0:1, :] + across(level_ref[...])
    product = head_sums_ref[1:2, :] + across(product_ref[...])
    turn(turned_ref, jnp.concatenate([product, level], axis=0), True)
    level = turned_ref[1:2, :]
    by_gain = (turned_ref[0:1, :] - shift_ref[...] * level) / gain_ref[...]
    for i, row in enumerate((by_gain, level, cot_ref[...])):
        rows_ref[2 * i : 2 * i + 1, :] = row[:, :hidden]
        rows_ref[2 * i + 1 : 2 * i + 2, :] = row[:, hidden:]
    rows_ref[6:7, :] = bias_sums_ref[...]
    rows_ref[7:8, :] = head_bias_ref[...]
    high, low = split(rows_ref[...])
    vectors = jnp.concatenate([high.astype(F32), low.astype(F32)], axis=0).astype(BF16)
    for i in range(16):
        up_blocks[i, block:, :] = vectors
    copies = []
    for (first, count), out in zip(GROUPS, up_outs):
        source = up_blocks.at[pl.ds(first, count), pl.ds(block, 16), :]
        sem = store_sems.at[tiles, 1 + len(copies)]
        copies.append(pltpu.make_async_copy(source, out.at[:, pl.ds(block, 16), :], sem))
        copies[-1].start()
    store_hidden.wait()
    for j in range(tiles):
        copies += store_blocks(j)
    for copy in copies:
        copy.wait()


def mlp(coords, pair, pair_t, weights, bias, gain, shift, cot_sums, head_sums, head_bias):
    _, rows, depth = pair.shape
    hidden = bias.shape[0]
    tiles, block = 4, depth // 16
    tile = hidden // tiles
    ups = [like((count, block + 16, hidden)) for _, count in GROUPS]
    downs = [like((count, block, hidden)) for _, count in GROUPS]
    outs = pl.pallas_call(
        mlp_kernel,
        in_specs=[SCALARS] + [ANY] * 3 + [WHOLE] * 6,
        out_specs=[ANY] * 11,
        out_shape=[like((2, rows, hidden)), *ups, *downs],
        scratch_shapes=[
            pltpu.VMEM((2, rows, depth), BF16),
            pltpu.VMEM((2, depth, rows), BF16),
            pltpu.VMEM((tiles, depth, tile), BF16),
            pltpu.VMEM((tiles, depth, tile), BF16),
            pltpu.VMEM((2, rows, hidden), BF16),
            pltpu.VMEM((16, block + 16, hidden), BF16),
            pltpu.VMEM((16, block, hidden), BF16),
            pltpu.VMEM((2, 16, block, tile), BF16),
            pltpu.VMEM((1, hidden), F32),
            pltpu.VMEM((8, hidden), F32),
            pltpu.VMEM((2, depth), F32),
            pltpu.VMEM((depth, LANES), F32),
            pltpu.VMEM((depth, LANES), F32),
            pltpu.SemaphoreType.DMA((2 * tiles + 4,)),
            pltpu.SemaphoreType.DMA((tiles + 1, 10)),
        ],
        compiler_params=params(60),
        cost_estimate=cost(8 * rows * depth * hidden, 40 * MIB),
        name="mlp",
    )(
        coords,
        pair,
        pair_t,
        weights,
        bias.reshape(1, -1),
        gain.reshape(1, -1),
        shift.reshape(1, -1),
        cot_sums,
        head_sums,
        head_bias,
    )
    return outs[0], outs[1:6], outs[6:]


def add_blocks(parts, target, vectors):
    end = parts[0].shape[0] - 16 if vectors else parts[0].shape[0]
    data = parts[0][:end].astype(F32)
    for part in parts[1:]:
        data = data + part[:end].astype(F32)
    target[:end, :] = data.astype(target.dtype)
    if vectors:
        rows = whole(parts[0][end:])
        for part in parts[1:]:
            rows = rows + whole(part[end:])
        if target.dtype == F32:
            target[end:, :] = rows
        else:
            high, low = split(rows)
            target[end:, :] = jnp.concatenate([high.astype(F32), low.astype(F32)], axis=0).astype(BF16)


def bump_kernel(*refs):
    for i in range(4):
        chunk, part, out = refs[2 * i], refs[2 * i + 1], refs[8 + i]
        for k in range(2):
            add_blocks([chunk[k], part[k]], out.at[k], i < 2)


def bump(*chunks):
    specs, arrays, outs = [], [], []
    for chunk, part, half in chunks:
        shape = part.shape
        spec = pl.BlockSpec(shape, lambda i, half=half: (half, 0, 0))
        specs += [spec, pl.BlockSpec(shape, lambda i: (0, 0, 0))]
        arrays += [chunk, part]
        outs.append(spec)
    return pl.pallas_call(
        bump_kernel,
        grid=(1,),
        in_specs=specs,
        out_specs=outs,
        out_shape=[like(chunk.shape) for chunk, _, _ in chunks],
        input_output_aliases={0: 0, 2: 1, 4: 2, 6: 3},
        compiler_params=params(24),
        name="bump",
    )(*arrays)


def near_kernel(*refs):
    for side in range(2):
        own, one, three = refs[3 * side : 3 * side + 3]
        outs = refs[6 + 4 * side : 10 + 4 * side]
        for i in range(4):
            add_blocks([own[i], one[i], three[i]], outs[i], side == 0)


def near_sums(*chunks):
    shapes = []
    for chunk, less in ((chunks[0], 8), (chunks[3], 0)):
        rows, columns = chunk.shape[1:]
        shapes += [like((rows - less, columns), F32)] + [like((rows, columns))] * 3
    outs = pl.pallas_call(
        near_kernel,
        in_specs=[WHOLE] * 6,
        out_specs=[WHOLE] * 8,
        out_shape=shapes,
        compiler_params=params(24),
        name="near",
    )(*chunks)
    return outs[:4], outs[4:]


def cut_heads_kernel(coords, heads_ref, *outs):
    rows = outs[0].shape[0]
    for bits in range(4):
        some = pl.ds(pl.multiple_of(slot_of(coords, bits) * rows, rows), rows)
        outs[bits][...] = heads_ref[some, :]


def cut_heads(coords, grads):
    rows, columns = grads.shape[0] // 4, grads.shape[1]
    return pl.pallas_call(
        cut_heads_kernel,
        in_specs=[SCALARS, WHOLE],
        out_specs=[WHOLE] * 4,
        out_shape=[like((rows, columns))] * 4,
        compiler_params=params(16),
        name="cut_heads",
    )(coords, grads)


def cut_kernel(coords, *refs):
    up, down, heads, outs = refs[:4], refs[4:8], refs[8:12], refs[12:]
    rows, hidden = outs[0].shape[0], up[0].shape[1]
    block = 4 * rows
    vectors = up[0][block:, :]
    for other in up[1:]:
        vectors = vectors + whole(other[block:, :])
    high, low = split(vectors)
    vectors = jnp.concatenate([high.astype(F32), low.astype(F32)], axis=0).astype(BF16)
    for bits in range(4):
        some = pl.ds(pl.multiple_of(slot_of(coords, bits) * rows, rows), rows)
        out = outs[bits]
        for side, blocks in enumerate((up, down)):
            total = blocks[0][some, :]
            for other in blocks[1:]:
                total = total + other[some, :].astype(F32)
            out[:, side * hidden : (side + 1) * hidden] = total.astype(BF16)
        end = 2 * hidden + heads[bits].shape[1]
        out[:, 2 * hidden : end] = heads[bits][...]
        out[:16, end:] = vectors[:, : hidden // 2]
        out[16:, end:] = vectors[:, hidden // 2 :]


def cut(coords, up, down, heads):
    rows, hidden = heads[0].shape[0], up[0].shape[1]
    columns = 2 * hidden + heads[0].shape[1] + hidden // 2
    return pl.pallas_call(
        cut_kernel,
        in_specs=[SCALARS] + [WHOLE] * 12,
        out_specs=[WHOLE] * 4,
        out_shape=[like((rows, columns))] * 4,
        compiler_params=params(16),
        name="cut",
    )(coords, *up, *down, *heads)


def combine_kernel(hidden_ref, right_ref, weights_ref, mine_ref, theirs_ref):
    contract = (((1,), (1,)), ((), ()))
    hidden, columns = hidden_ref.shape[2], right_ref.shape[1]
    inner = columns * 3 // 4
    half = mine_ref.shape[1]

    def product(left, start):
        weights = weights_ref[:, start : start + left.shape[1]]
        return lax.dot_general(left, weights, contract, preferred_element_type=F32)

    total = product(hidden_ref[0], columns) + product(right_ref[:, :inner], 0)
    mine_ref[0] = total[:half].astype(BF16)
    theirs_ref[0] = total[half:].astype(BF16)
    total = product(hidden_ref[1], columns + hidden) + product(right_ref[:, inner:], inner)
    mine_ref[1] = total[:half].astype(BF16)
    theirs_ref[1] = total[half:].astype(BF16)


def combine(hidden_pair, right, weights):
    _, rows, hidden = hidden_pair.shape
    depth, columns = weights.shape
    tile = depth // 4
    block = pl.BlockSpec((2, rows // 2, tile), lambda i: (0, 0, i))
    return pl.pallas_call(
        combine_kernel,
        grid=(4,),
        in_specs=[WHOLE, WHOLE, pl.BlockSpec((tile, columns), lambda i: (i, 0))],
        out_specs=[block] * 2,
        out_shape=[like((2, rows // 2, depth))] * 2,
        compiler_params=params(40),
        cost_estimate=cost(2 * rows * depth * columns, 16 * MIB),
        name="combine",
    )(hidden_pair, right, weights)


def exchange(parts):
    return [parts[0], flip(parts[1], "c"), flip(parts[2], "zl"), flip(parts[3], "zl", "c")]


def unpack_kernel(coords, *refs):
    parts, (up_ref, down_ref, qkv_ref, out_ref, rows_ref, up_sums_ref, qkv_sums_ref) = refs[:4], refs[4:]
    hidden, width = up_ref.shape[1] // 4, out_ref.shape[1] // 4
    for bits in range(4):
        slot, part = slot_of(coords, bits), parts[bits]
        wide = pl.ds(pl.multiple_of(slot * hidden, hidden), hidden)
        narrow = pl.ds(pl.multiple_of(slot * width, width), width)
        up_ref[:, wide] = part[:, :hidden].astype(F32)
        down_ref[:, wide] = part[:, hidden : 2 * hidden].astype(F32)
        start = 2 * hidden
        for kind in range(3):
            qkv_ref[kind, :, narrow] = part[:, start + kind * width : start + (kind + 1) * width].astype(F32)
        out_ref[:, narrow] = part[:, start + 3 * width : start + 4 * width].astype(F32)
        start += 4 * width
        vectors = jnp.concatenate([whole(part[:16, start:]), whole(part[16:, start:])], axis=1)
        rows_ref[...] = vectors if bits == 0 else rows_ref[...] + vectors
        up_sums_ref[:, wide] = vectors[6:7, :]
        for kind in range(3):
            qkv_sums_ref[kind : kind + 1, narrow] = vectors[7:8, kind * width : (kind + 1) * width]


def unpack(coords, parts, hidden, width):
    rows = parts[0].shape[0]
    wide, narrow = (rows, 4 * hidden), (rows, 4 * width)
    shapes = [wide, wide, (3,) + narrow, narrow, (8, hidden), (1, 4 * hidden), (3, 4 * width)]
    return pl.pallas_call(
        unpack_kernel,
        in_specs=[SCALARS] + [WHOLE] * 4,
        out_specs=[WHOLE] * 7,
        out_shape=[like(shape, F32) for shape in shapes],
        compiler_params=params(16),
        name="unpack",
    )(coords, *parts)


def turn(dest, value, back):
    block = value.shape[1] // 32
    for chip in range(16):
        for zl in range(2):
            natural, inside = (zl * 16 + chip) * block, (chip * 2 + zl) * block
            source, target = (inside, natural) if back else (natural, inside)
            dest[:, target : target + block] = value[:, source : source + block].astype(dest.dtype)


def standardize(tokens):
    rows = tokens.astype(F32)
    centered = rows - jnp.mean(rows, axis=1, keepdims=True)
    scale = lax.rsqrt(jnp.mean(centered * centered, axis=1, keepdims=True) + EPSILON)
    return rows, centered * scale, scale


def enter_kernel(tokens_ref, cot_ref, gain_ref, bias_ref, pair_ref, sums_ref):
    _, standard, _ = standardize(tokens_ref[...])
    turn(pair_ref.at[0], (standard * gain_ref[...] + bias_ref[...]).astype(BF16), False)
    turn(pair_ref.at[1], cot_ref[...], False)
    sums_ref[...] = jnp.sum(cot_ref[...].astype(F32), axis=0, keepdims=True)


def enter(tokens, cotangent, gain, bias):
    return pl.pallas_call(
        enter_kernel,
        in_specs=[WHOLE] * 4,
        out_specs=[WHOLE] * 2,
        out_shape=[like((2,) + tokens.shape), like((1, tokens.shape[1]), F32)],
        compiler_params=params(16),
        name="enter",
    )(tokens, cotangent, gain.reshape(1, -1), bias.reshape(1, -1))


def leave_kernel(tokens_ref, cot_ref, gain_ref, bias_ref, *refs):
    mixed_ref, grad_ref, branch_ref, normed_ref = refs[-4:]
    for which, target in ((0, normed_ref), (1, branch_ref)):
        total = refs[0][which]
        for part in refs[1:4]:
            total = total + part[which].astype(F32)
        turn(target, total, True)
    rows, standard, scale = standardize(tokens_ref[...])
    mixed_ref[...] = (rows + branch_ref[...] + bias_ref[...]).astype(BF16)
    grad = normed_ref[...] * gain_ref[...]
    level = jnp.mean(grad, axis=1, keepdims=True)
    slope = jnp.mean(grad * standard, axis=1, keepdims=True)
    grad_ref[...] = cot_ref[...].astype(F32) + scale * (grad - level - standard * slope)


def leave(tokens, cotangent, gain, bias, sums):
    shape = tokens.shape
    return pl.pallas_call(
        leave_kernel,
        in_specs=[WHOLE] * 8,
        out_specs=[WHOLE] * 2,
        out_shape=[like(shape), like(shape, F32)],
        scratch_shapes=[pltpu.VMEM(shape, F32)] * 2,
        compiler_params=params(24),
        name="leave",
    )(tokens, cotangent, gain.reshape(1, -1), bias.reshape(1, -1), *sums)


def scatter_plane(grads):
    return lax.psum_scatter(grads, PLANE, scatter_dimension=0, tiled=True)


def per_device(
    tokens,
    layernorm_gain,
    layernorm_bias,
    w_qkv,
    b_qkv,
    w_out,
    b_out,
    w_up,
    b_up,
    w_down,
    b_down,
    segments,
    cotangent,
):
    depth = tokens.shape[1]
    length = segments.shape[0]
    half_rows = tokens.shape[0]
    width = w_out.shape[0] // 4
    hidden = w_down.shape[0] // 4
    rows = w_up.shape[0]
    coords = jnp.stack([lax.axis_index(axis) for axis in AXES]).astype(jnp.int32)
    place_here = coords[0] * 2 + coords[3]
    this_half = coords[4]

    parts = exchange(pack(coords, w_up, w_down.T, w_qkv.transpose(1, 0, 2), w_out.T, segments))
    shard = order(coords, parts, 2 * hidden + 4 * width)
    weights = lax.all_gather(shard, PLANE, axis=0, tiled=True)

    pair, cot_sums = enter(tokens, cotangent, layernorm_gain, layernorm_bias)
    _, pair = lax.optimization_barrier((shard, pair))
    near, far, opposite = flip(pair, "zl"), flip(pair, "zl", "mp"), flip(pair, "mp")
    pair, pair_t = gather_tokens(pair, opposite, near, far)

    doc = jnp.stack([parts[k][0, -length:] for k in (0, 2, 1, 3)]).astype(jnp.int32)
    doc = doc.reshape(4, 2, half_rows)
    doc = jnp.where(this_half == 0, doc, doc[:, ::-1]).reshape(4, length)
    halves = jnp.stack([this_half, 1 - this_half]) * half_rows
    index = (halves[:, None] + jnp.arange(half_rows, dtype=jnp.int32)).reshape(1, length)
    index = jnp.broadcast_to(index, (4, length)).astype(jnp.int32)
    b_up_here = lax.dynamic_slice_in_dim(b_up, place_here * hidden, hidden)
    b_qkv_here = lax.dynamic_slice_in_dim(b_qkv, place_here * width, width, axis=1).reshape(-1)

    tables = rotary_tables(doc, index)

    pair, pair_t, tables = lax.optimization_barrier((pair, pair_t, tables))
    right, head_grads, head_bias, head_sums = heads(pair, pair_t, weights, b_qkv_here, tables, length)
    head_grads = scatter_plane(head_grads)

    right, pair, pair_t = lax.optimization_barrier((right, pair, pair_t))
    hidden_pair, up_blocks, down_blocks = mlp(
        coords,
        pair,
        pair_t,
        weights,
        b_up_here,
        layernorm_gain,
        layernorm_bias,
        cot_sums,
        head_sums,
        head_bias,
    )

    up_blocks, down_blocks, hidden_pair = lax.optimization_barrier((up_blocks, down_blocks, hidden_pair))
    up_own, up_one, up_three, up_low, up_high = up_blocks
    down_own, down_one, down_three, down_low, down_high = down_blocks
    low = [hop(up_low, "y", 1), hop(down_low, "x", 1)]
    high = [hop(up_high, "y", 3), hop(down_high, "x", 3)]
    mine, theirs = combine(hidden_pair, right, weights)
    low, high, mine, theirs = lax.optimization_barrier((low, high, mine, theirs))
    theirs = flip(theirs, "c")
    up_one, up_three, down_one, down_three = bump(
        (up_one, high[0], 1), (up_three, low[0], 0), (down_one, high[1], 1), (down_three, low[1], 0)
    )
    up_one, up_three = hop(up_one, "y", 1), hop(up_three, "y", 3)
    down_one, down_three = hop(down_one, "x", 1), hop(down_three, "x", 3)
    keep, sends = fold(mine, theirs)
    near = flip(sends[1], "zl")
    head_parts = cut_heads(coords, head_grads)
    up_one, up_three, down_one, down_three, near, keep, far, opposite, head_parts = lax.optimization_barrier(
        (up_one, up_three, down_one, down_three, near, keep, sends[2], sends[0], head_parts)
    )
    along_z = [near, flip(far, "zl", "mp"), flip(opposite, "mp")]
    up_sums, down_sums = near_sums(up_own, up_one, up_three, down_own, down_one, down_three)
    up_sums = [up_sums[0]] + [hop(part, "x", bits) for part, bits in zip(up_sums[1:], (1, 2, 3))]
    down_sums = [down_sums[0]] + [hop(part, "y", bits) for part, bits in zip(down_sums[1:], (1, 2, 3))]
    parts = exchange(cut(coords, up_sums, down_sums, head_parts))
    mixed, d_tokens = leave(
        tokens, cotangent, layernorm_gain, b_out + b_down, [keep] + along_z
    )
    grad_up_w, grad_down_w, grad_qkv_w, grad_out_w, vectors, grad_b_up, grad_b_qkv = unpack(
        coords, parts, hidden, width
    )
    swapped, mixed, d_tokens = lax.optimization_barrier((flip(vectors, "mp"), mixed, d_tokens))
    vectors = (vectors + swapped)[:6].reshape(3, depth)
    return (
        mixed,
        d_tokens,
        vectors[0],
        vectors[1],
        grad_qkv_w.transpose(1, 0, 2),
        grad_b_qkv,
        grad_out_w.T,
        vectors[2],
        grad_up_w,
        grad_b_up[0],
        grad_down_w.T,
        vectors[2],
    )


def solution(mesh):
    fine = Mesh(mesh.devices.reshape(SIZES), AXES)
    dp = ("zl", "x", "y", "c")
    in_specs = (
        P(AXES, None),
        P(),
        P(),
        P(dp, None, "mp"),
        P(None, "mp"),
        P("mp", dp),
        P(),
        P(dp, "mp"),
        P("mp"),
        P("mp", dp),
        P(),
        P(dp),
        P(AXES, None),
    )
    out_specs = (
        P(AXES, None),
        P(AXES, None),
        P(),
        P(),
        P(dp, None, "mp"),
        P(None, "mp"),
        P("mp", dp),
        P(),
        P(dp, "mp"),
        P("mp"),
        P("mp", dp),
        P(),
    )
    return jax.shard_map(
        per_device, mesh=fine, in_specs=in_specs, out_specs=out_specs, check_vma=False
    )
```

time: 319 us -> 308 us (0.966)
  local copies, waits for them, and re-layouts: 37 us -> 24.7 us
  waiting for transfers between devices: 126 us -> 119 us
  Pallas kernels: 107 us -> 112 us
  starting transfers between devices: 30.6 us -> 33.9 us
    unnamed x83 -> x67, local copies, waits for them, and re-layouts: 34.1 us -> 21.2 us
    ppermute x7 -> x14, waiting for transfers between devices: 46.7 us -> 35.3 us  [hop(): return lax.ppermute(value, axis, [(i, i ^ bits) for i in range(4)])]
    reduce_scatter x1, waiting for transfers between devices: 0.01 us -> 11.2 us  [scatter_plane(): return lax.psum_scatter(grads, PLANE, scatter_dimension=0, tiled=True)]
    ppermute x7 -> x14, starting transfers between devices: 8.22 us -> 15.2 us  [hop(): return lax.ppermute(value, axis, [(i, i ^ bits) for i in range(4)])]
    ppermute x15, waiting for transfers between devices: 71.6 us -> 66.2 us  [flip(): return lax.ppermute(value, axes, [(i, count - 1 - i) for i in range(count)])]
    pallas_call x8 -> x6, Pallas kernels: 60.3 us -> 64.7 us  [the longest x1 30.9 us: mlp(): pl.pallas_call(mlp_kernel, in_specs=[SCALARS] + [ANY] * 3 + [WHOLE] * 6,...]
    ppermute x15, starting transfers between devices: 22.3 us -> 18.7 us  [flip(): return lax.ppermute(value, axes, [(i, count - 1 - i) for i in range(count)])]
  transfers between devices with their start and end apart: 24 -> 31, of which waited for: 16 -> 17; matrix products, arithmetic and copies ran while one was open for 1% -> 2% of each run, Pallas kernels for 22% -> 26%
where the time goes in v6:
time: 308 us; the launch traced here: 307 us
  waiting for transfers between devices  119 us (39%)
  Pallas kernels  112 us (36%)
  starting transfers between devices  33.9 us (11%)
  local copies, waits for them, and re-layouts  24.7 us (8%)
  between operations  14.4 us (5%)
    ppermute x15, waiting for transfers between devices, flip(): return lax.ppermute(value, axes, [(i, count - 1 - i) for i in range(count)])  66.2 us
    ppermute x14, waiting for transfers between devices, hop(): return lax.ppermute(value, axis, [(i, i ^ bits) for i in range(4)])  35.3 us
    pallas_call x1, Pallas kernels, mlp(): pl.pallas_call(mlp_kernel, in_specs=[SCALARS] + [ANY] * 3 + [WHOLE] * 6,...  30.9 us
    pallas_call x1, Pallas kernels, heads(): pl.pallas_call(heads_kernel, in_specs=[ANY] * 3 + [WHOLE] * 6, out_specs=...  26.3 us
    unnamed x67, local copies, waits for them, and re-layouts  21.2 us
    ppermute x15, starting transfers between devices, flip(): return lax.ppermute(value, axes, [(i, count - 1 - i) for i in range(count)])  18.7 us
    pallas_call x1, Pallas kernels, combine(): pl.pallas_call(combine_kernel, grid=(4,), in_specs=[WHOLE, WHOLE, pl.Bloc...  17.8 us
    ppermute x14, starting transfers between devices, hop(): return lax.ppermute(value, axis, [(i, i ^ bits) for i in range(4)])  15.2 us
  transfers between devices with their start and end apart: 31, of which 17 were waited for; matrix products, arithmetic and copies ran while one was open for 2% of the time, Pallas kernels for 26%

profile of v6, /device:TPU:1, one launch (start us, length us, event | category | flops | bytes accessed | tf_op | source)
XLA Modules:
  0.0 306.8 jit_solution(1190679630818071708)
XLA Ops:
  7.8 3.0 pack.1
  14.4 4.2 %collective-permute-done.1.refs_2_ = bf16[32,3328]{1,0:T(8,128)(2,1)S(1)} collective-permute-done((bf16[32,3328]{1,0:T(8,128)(2,1)}, bf16[32,3328]{1,0:T(8,128)(2,1)S(1)}, u32[]{:S(2)}, u32[]{:S(2)}) %collective-permute-start.1) | collective-permute-done | bytes 213024 | tf_op jit(solution)/shard_map/ppermute | solution.py:32
  18.6 5.1 %collective-permute-done.2.refs_3_ = bf16[32,3328]{1,0:T(8,128)(2,1)S(1)} collective-permute-done((bf16[32,3328]{1,0:T(8,128)(2,1)}, bf16[32,3328]{1,0:T(8,128)(2,1)S(1)}, u32[]{:S(2)}, u32[]{:S(2)}) %collective-permute-start.2) | collective-permute-done | bytes 213024 | tf_op jit(solution)/shard_map/ppermute | solution.py:32
  31.8 3.4 %collective-permute-start.3 = (bf16[2,128,2048]{2,1,0:T(8,128)(2,1)S(1)}, bf16[2,128,2048]{2,1,0:T(8,128)(2,1)S(1)}, u32[]{:S(2)}, u32[]{:S(2)}) collective-permute-start(bf16[2,128,2048]{2,1,0:T(8,128)(2,1)S(1)} %get-tuple-element.123.refs_0_), channel_id=1, source_target_pairs={{0,1},{1,0},{2,3},{3,2},{4,5},{5,4},{6,7},{7,6},{8,9},{9,8},{10,11... | collective-permute-start | bytes 3145736 | tf_op jit(solution)/shard_map/ppermute | solution.py:32
  36.0 22.9 %collective-permute-done.3.refs_1_ = bf16[2,128,2048]{2,1,0:T(8,128)(2,1)S(1)} collective-permute-done((bf16[2,128,2048]{2,1,0:T(8,128)(2,1)S(1)}, bf16[2,128,2048]{2,1,0:T(8,128)(2,1)S(1)}, u32[]{:S(2)}, u32[]{:S(2)}) %collective-permute-start.3) | collective-permute-done | bytes 1048608 | tf_op jit(solution)/shard_map/ppermute | solution.py:32
  58.9 23.4 %collective-permute-done.4.refs_2_ = bf16[2,128,2048]{2,1,0:T(8,128)(2,1)S(1)} collective-permute-done((bf16[2,128,2048]{2,1,0:T(8,128)(2,1)S(1)}, bf16[2,128,2048]{2,1,0:T(8,128)(2,1)S(1)}, u32[]{:S(2)}, u32[]{:S(2)}) %collective-permute-start.4) | collective-permute-done | bytes 1048608 | tf_op jit(solution)/shard_map/ppermute | solution.py:32
  92.9 12.3 %tokens.1 = (bf16[2,1024,2048]{2,1,0:T(8,128)(2,1)S(1)}, bf16[2,2048,1024]{2,1,0:T(8,128)(2,1)S(1)}) custom-call(bf16[4,2,128,2048]{3,2,1,0:T(8,128)(2,1)} %join.1.mine_ref, bf16[4,2,128,2048]{3,2,1,0:T(8,128)(2,1)} %collective-permute-done.6.other_ref), custom_call_target="tpu_custom_call" | custom-call | bytes 33554432 | tf_op jit(solution)/shard_map/tokens/pallas_call | solution.py:418
  105.2 3.2 %copy-done.15 = bf16[2,1024,2048]{2,1,0:T(8,128)(2,1)} copy-done((bf16[2,1024,2048]{2,1,0:T(8,128)(2,1)}, bf16[2,1024,2048]{2,1,0:T(8,128)(2,1)S(1)}, u32[]{:S(2)}) %copy-start.15) | copy-done | bytes 8388632
  108.4 3.3 %copy-done.16 = bf16[2,2048,1024]{2,1,0:T(8,128)(2,1)} copy-done((bf16[2,2048,1024]{2,1,0:T(8,128)(2,1)}, bf16[2,2048,1024]{2,1,0:T(8,128)(2,1)S(1)}, u32[]{:S(2)}) %copy-start.16) | copy-done | bytes 8388632
  111.8 6.7 %all-gather.2.cloned.1.call-done.weights_hbm.weights_ref = bf16[2048,3072]{1,0:T(8,128)(2,1)} async-done(((bf16[128,3072]{1,0:T(8,128)(2,1)}), bf16[2048,3072]{1,0:T(8,128)(2,1)}) %all-gather.2.cloned.1.call-update) | async-done | bytes 12582928 | tf_op jit(solution)/shard_map/all_gather | solution.py:945
  118.5 26.3 %heads.1 = (bf16[1024,1024]{1,0:T(8,128)(2,1)}, bf16[2048,1024]{1,0:T(8,128)(2,1)}, f32[1,1024]{1,0:T(1,128)}, f32[2,2048]{1,0:T(2,128)}) custom-call(bf16[2,1024,2048]{2,1,0:T(8,128)(2,1)} %copy-done.15, bf16[2,2048,1024]{2,1,0:T(8,128)(2,1)} %copy-done.16, bf16[2048,3072]{1,0:T(8,128)(2,1)} %all-gather.2.cloned.1.call-done.weights_hbm.weights_ref, ...), custom_call_target="tpu_custom_call" | custom-call | flops 31457280000 | bytes 10485760 | tf_op jit(solution)/shard_map/heads/pallas_call | solution.py:234
  146.1 30.9 %mlp.1 = (bf16[2,1024,1024]{2,1,0:T(8,128)(2,1)}, bf16[4,144,1024]{2,1,0:T(8,128)(2,1)}, bf16[4,144,1024]{2,1,0:T(8,128)(2,1)}, bf16[4,144,1024]{2,1,0:T(8,128)(...) custom-call(s32[5]{0:T(128)} %stack.40.coords, ...), custom_call_target="tpu_custom_call" | custom-call | flops 17179869184 | bytes 41943040 | tf_op jit(solution)/shard_map/mlp/pallas_call | solution.py:615
  180.9 17.8 %combine.1 = (bf16[2,512,2048]{2,1,0:T(8,128)(2,1)S(1)}, bf16[2,512,2048]{2,1,0:T(8,128)(2,1)S(1)}) custom-call(bf16[2,1024,1024]{2,1,0:T(8,128)(2,1)} %get-tuple-element.161.hidden_ref, bf16[1024,1024]{1,0:T(8,128)(2,1)S(1)} %copy-done.25, bf16[2048,3072]{1,0:T(8,128)(2,1)} %all-gather.2.cloned.1.call-done.weights_hbm.weights_ref), custom_call_target="tpu_custom_call" | custom-call | flops 12884901888 | bytes 16777216 | tf_op jit(solution)/shard_map/combine/pallas_call | solution.py:801
  200.7 3.1 %bump.1 = (bf16[4,144,1024]{2,1,0:T(8,128)(2,1)}, bf16[4,144,1024]{2,1,0:T(8,128)(2,1)}, bf16[4,128,1024]{2,1,0:T(8,128)(2,1)}, bf16[4,128,1024]{2,1,0:T(8,128)(2,1)}) custom-call(bf16[4,144,1024]{2,1,0:T(8,128)(2,1)} %get-tuple-element.156.refs_0_, ...), custom_call_target="tpu_custom_call", output_to_operand_aliasing={{0}: (0, {}), {1}: (2, {}), {2}: (4, {}), {3}: (6, {})} | custom-call | tf_op jit(solution)/shard_map/bump/pallas_call | solution.py:687
  213.9 11.2 %reduce-scatter.2.cloned.1.call-done.heads_ref = bf16[128,1024]{1,0:T(8,128)(2,1)} async-done(((bf16[2048,1024]{1,0:T(8,128)(2,1)}), bf16[128,1024]{1,0:T(8,128)(2,1)}) %reduce-scatter.2.cloned.1.call-update) | async-done | bytes 262160 | tf_op jit(solution)/shard_map/reduce_scatter | solution.py:915
  226.6 8.2 %collective-permute-done.13.refs_4_ = bf16[4,128,1024]{2,1,0:T(8,128)(2,1)} collective-permute-done((bf16[4,128,1024]{2,1,0:T(8,128)(2,1)}, bf16[4,128,1024]{2,1,0:T(8,128)(2,1)}, u32[]{:S(2)}, u32[]{:S(2)}) %collective-permute-start.13) | collective-permute-done | bytes 1048608 | tf_op jit(solution)/shard_map/ppermute | solution.py:36
  241.5 3.1 near.1
  244.7 3.2 %collective-permute-start.21 = (bf16[128,1024]{1,0:T(8,128)(2,1)S(1)}, bf16[128,1024]{1,0:T(8,128)(2,1)S(1)}, u32[]{:S(2)}, u32[]{:S(2)}) collective-permute-start(bf16[128,1024]{1,0:T(8,128)(2,1)S(1)} %get-tuple-element.198), channel_id=1, source_target_pairs={{0,8},{4,12},{8,0},{12,4},{1,9},{5,13},{9,1},{13,5},{2,10},{6,14},... | collective-permute-start | bytes 786440 | tf_op jit(solution)/shard_map/ppermute | solution.py:36
  251.8 6.1 %collective-permute-done.21.refs_6_ = bf16[128,1024]{1,0:T(8,128)(2,1)S(1)} collective-permute-done((bf16[128,1024]{1,0:T(8,128)(2,1)S(1)}, bf16[128,1024]{1,0:T(8,128)(2,1)S(1)}, u32[]{:S(2)}, u32[]{:S(2)}) %collective-permute-start.21) | collective-permute-done | bytes 262176 | tf_op jit(solution)/shard_map/ppermute | solution.py:36
  262.0 6.2 %collective-permute-done.18.refs_2_ = bf16[144,1024]{1,0:T(8,128)(2,1)S(1)} collective-permute-done((bf16[144,1024]{1,0:T(8,128)(2,1)S(1)}, bf16[144,1024]{1,0:T(8,128)(2,1)S(1)}, u32[]{:S(2)}, u32[]{:S(2)}) %collective-permute-start.18) | collective-permute-done | bytes 294944 | tf_op jit(solution)/shard_map/ppermute | solution.py:36
  268.2 7.9 %collective-permute-done.19.refs_3_ = bf16[144,1024]{1,0:T(8,128)(2,1)S(1)} collective-permute-done((bf16[144,1024]{1,0:T(8,128)(2,1)S(1)}, bf16[144,1024]{1,0:T(8,128)(2,1)S(1)}, u32[]{:S(2)}, u32[]{:S(2)}) %collective-permute-start.19) | collective-permute-done | bytes 294944 | tf_op jit(solution)/shard_map/ppermute | solution.py:36
  279.3 5.4 %collective-permute-done.24.refs_2_ = bf16[32,3584]{1,0:T(8,128)(2,1)S(1)} collective-permute-done((bf16[32,3584]{1,0:T(8,128)(2,1)S(1)}, bf16[32,3584]{1,0:T(8,128)(2,1)S(1)}, u32[]{:S(2)}, u32[]{:S(2)}) %collective-permute-start.24) | collective-permute-done | bytes 229408 | tf_op jit(solution)/shard_map/ppermute | solution.py:32
  284.8 5.1 %collective-permute-done.25.refs_3_ = bf16[32,3584]{1,0:T(8,128)(2,1)S(1)} collective-permute-done((bf16[32,3584]{1,0:T(8,128)(2,1)S(1)}, bf16[32,3584]{1,0:T(8,128)(2,1)S(1)}, u32[]{:S(2)}, u32[]{:S(2)}) %collective-permute-start.25) | collective-permute-done | bytes 229408 | tf_op jit(solution)/shard_map/ppermute | solution.py:32
  294.1 4.0 %leave.1 = (bf16[128,2048]{1,0:T(8,128)(2,1)}, f32[128,2048]{1,0:T(8,128)}) custom-call(bf16[128,2048]{1,0:T(8,128)(2,1)S(1)} %copy-done.3, bf16[128,2048]{1,0:T(8,128)(2,1)S(1)} %copy-done.5, f32[1,2048]{1,0:T(1,128)S(1)} %bitcast.62, f32[1,2048]{1,0:T(1,128)S(1)} %bitcast.63, f32[2,128,2048]{2,1,0:T(8,128)S(1)} %get-tuple-element.209.refs_0_, ...), custom_call_target="tpu_custom_call" | custom-call | tf_op jit(solution)/shard_map/leave/pallas_call | solution.py:903
  (144 shorter events, 66.4 us)
Async XLA Ops:
  7.2 111.3 %all-gather.2.cloned.1.call-start = ((), (), s32[]{:S(2)}) async-start(), calls=%async_computation.1 | async-start | bytes 13369344 | tf_op jit(solution)/shard_map/all_gather | solution.py:945
  14.4 9.3 %collective-permute-start.2 = (bf16[32,3328]{1,0:T(8,128)(2,1)}, bf16[32,3328]{1,0:T(8,128)(2,1)S(1)}, u32[]{:S(2)}, u32[]{:S(2)}) collective-permute-start(bf16[32,3328]{1,0:T(8,128)(2,1)} %get-tuple-element.121), channel_id=1, source_target_pairs={{0,66},{2,64},{64,2},{66,0},{1,67},{3,65},{65,3},{67,1},{4,70},{6,... | collective-permute-start | bytes 638984 | tf_op jit(solution)/shard_map/ppermute | solution.py:32
  26.8 198.3 %reduce-scatter.2.cloned.1.call-start = ((), (), s32[]{:S(2)}) async-start(), calls=%async_computation.2 | async-start | bytes 4456448 | tf_op jit(solution)/shard_map/reduce_scatter | solution.py:915
  31.8 27.1 %collective-permute-start.3 = (bf16[2,128,2048]{2,1,0:T(8,128)(2,1)S(1)}, bf16[2,128,2048]{2,1,0:T(8,128)(2,1)S(1)}, u32[]{:S(2)}, u32[]{:S(2)}) collective-permute-start(bf16[2,128,2048]{2,1,0:T(8,128)(2,1)S(1)} %get-tuple-element.123.refs_0_), channel_id=1, source_target_pairs={{0,1},{1,0},{2,3},{3,2},{4,5},{5,4},{6,7},{7,6},{8,9},{9,8},{10,11... | collective-permute-start | bytes 3145736 | tf_op jit(solution)/shard_map/ppermute | solution.py:32
  35.2 47.1 %collective-permute-start.4 = (bf16[2,128,2048]{2,1,0:T(8,128)(2,1)S(1)}, bf16[2,128,2048]{2,1,0:T(8,128)(2,1)S(1)}, u32[]{:S(2)}, u32[]{:S(2)}) collective-permute-start(bf16[2,128,2048]{2,1,0:T(8,128)(2,1)S(1)} %get-tuple-element.123.refs_0_), channel_id=1, source_target_pairs={{0,64},{64,0},{1,65},{65,1},{2,66},{66,2},{3,67},{67,3},{4,68},{68... | collective-permute-start | bytes 3145736 | tf_op jit(solution)/shard_map/ppermute | solution.py:32
  36.0 46.3 %collective-permute-start.5 = (bf16[2,128,2048]{2,1,0:T(8,128)(2,1)S(1)}, bf16[2,128,2048]{2,1,0:T(8,128)(2,1)S(1)}, u32[]{:S(2)}, u32[]{:S(2)}) collective-permute-start(bf16[2,128,2048]{2,1,0:T(8,128)(2,1)S(1)} %get-tuple-element.123.refs_0_), channel_id=1, source_target_pairs={{0,65},{1,64},{64,1},{65,0},{2,67},{3,66},{66,3},{67,2},{4,69},{5,... | collective-permute-start | bytes 3145736 | tf_op jit(solution)/shard_map/ppermute | solution.py:32
  84.3 8.6 %collective-permute-start.6 = (bf16[4,2,128,2048]{3,2,1,0:T(8,128)(2,1)}, bf16[4,2,128,2048]{3,2,1,0:T(8,128)(2,1)}, u32[]{:S(2)}, u32[]{:S(2)}) collective-permute-start(bf16[4,2,128,2048]{3,2,1,0:T(8,128)(2,1)} %join.1.mine_ref), channel_id=1, source_target_pairs={{0,2},{2,0},{1,3},{3,1},{4,6},{6,4},{5,7},{7,5},{8,10},{10,8},{9,1... | collective-permute-start | bytes 12582920 | tf_op jit(solution)/shard_map/ppermute | solution.py:32
  176.9 22.4 %collective-permute-start.7 = (bf16[2,144,1024]{2,1,0:T(8,128)(2,1)}, bf16[2,144,1024]{2,1,0:T(8,128)(2,1)S(1)}, u32[]{:S(2)}, u32[]{:S(2)}) collective-permute-start(bf16[2,144,1024]{2,1,0:T(8,128)(2,1)} %get-tuple-element.157), channel_id=1, source_target_pairs={{0,4},{4,0},{8,12},{12,8},{1,5},{5,1},{9,13},{13,9},{2,6},{6,2},{1... | collective-permute-start | bytes 1769480 | tf_op jit(solution)/shard_map/ppermute | solution.py:36
  178.2 21.2 %collective-permute-start.9 = (bf16[2,144,1024]{2,1,0:T(8,128)(2,1)}, bf16[2,144,1024]{2,1,0:T(8,128)(2,1)S(1)}, u32[]{:S(2)}, u32[]{:S(2)}) collective-permute-start(bf16[2,144,1024]{2,1,0:T(8,128)(2,1)} %get-tuple-element.159), channel_id=1, source_target_pairs={{0,12},{4,8},{8,4},{12,0},{1,13},{5,9},{9,5},{13,1},{2,14},{6,10},... | collective-permute-start | bytes 1769480 | tf_op jit(solution)/shard_map/ppermute | solution.py:36
  179.9 19.4 %collective-permute-start.10 = (bf16[2,128,1024]{2,1,0:T(8,128)(2,1)}, bf16[2,128,1024]{2,1,0:T(8,128)(2,1)S(1)}, u32[]{:S(2)}, u32[]{:S(2)}) collective-permute-start(bf16[2,128,1024]{2,1,0:T(8,128)(2,1)} %get-tuple-element.160), channel_id=1, source_target_pairs={{0,48},{16,32},{32,16},{48,0},{1,49},{17,33},{33,17},{49,1},{2,50}... | collective-permute-start | bytes 1572872 | tf_op jit(solution)/shard_map/ppermute | solution.py:36
  180.9 18.5 %collective-permute-start.8 = (bf16[2,128,1024]{2,1,0:T(8,128)(2,1)}, bf16[2,128,1024]{2,1,0:T(8,128)(2,1)S(1)}, u32[]{:S(2)}, u32[]{:S(2)}) collective-permute-start(bf16[2,128,1024]{2,1,0:T(8,128)(2,1)} %get-tuple-element.158), channel_id=1, source_target_pairs={{0,16},{16,0},{32,48},{48,32},{1,17},{17,1},{33,49},{49,33},{2,18}... | collective-permute-start | bytes 1572872 | tf_op jit(solution)/shard_map/ppermute | solution.py:36
  203.9 32.7 %collective-permute-start.11 = (bf16[4,144,1024]{2,1,0:T(8,128)(2,1)}, bf16[4,144,1024]{2,1,0:T(8,128)(2,1)}, u32[]{:S(2)}, u32[]{:S(2)}) collective-permute-start(bf16[4,144,1024]{2,1,0:T(8,128)(2,1)} %get-tuple-element.172), channel_id=1, source_target_pairs={{0,4},{4,0},{8,12},{12,8},{1,5},{5,1},{9,13},{13,9},{2,6},{6,2},{1... | collective-permute-start | bytes 3538952 | tf_op jit(solution)/shard_map/ppermute | solution.py:36
  204.2 33.0 %collective-permute-start.12 = (bf16[4,144,1024]{2,1,0:T(8,128)(2,1)}, bf16[4,144,1024]{2,1,0:T(8,128)(2,1)}, u32[]{:S(2)}, u32[]{:S(2)}) collective-permute-start(bf16[4,144,1024]{2,1,0:T(8,128)(2,1)} %get-tuple-element.173), channel_id=1, source_target_pairs={{0,12},{4,8},{8,4},{12,0},{1,13},{5,9},{9,5},{13,1},{2,14},{6,10},... | collective-permute-start | bytes 3538952 | tf_op jit(solution)/shard_map/ppermute | solution.py:36
  205.8 28.9 %collective-permute-start.13 = (bf16[4,128,1024]{2,1,0:T(8,128)(2,1)}, bf16[4,128,1024]{2,1,0:T(8,128)(2,1)}, u32[]{:S(2)}, u32[]{:S(2)}) collective-permute-start(bf16[4,128,1024]{2,1,0:T(8,128)(2,1)} %get-tuple-element.174), channel_id=1, source_target_pairs={{0,16},{16,0},{32,48},{48,32},{1,17},{17,1},{33,49},{49,33},{2,18}... | collective-permute-start | bytes 3145736 | tf_op jit(solution)/shard_map/ppermute | solution.py:36
  207.1 29.5 %collective-permute-start.14 = (bf16[4,128,1024]{2,1,0:T(8,128)(2,1)}, bf16[4,128,1024]{2,1,0:T(8,128)(2,1)}, u32[]{:S(2)}, u32[]{:S(2)}) collective-permute-start(bf16[4,128,1024]{2,1,0:T(8,128)(2,1)} %get-tuple-element.175), channel_id=1, source_target_pairs={{0,48},{16,32},{32,16},{48,0},{1,49},{17,33},{33,17},{49,1},{2,50}... | collective-permute-start | bytes 3145736 | tf_op jit(solution)/shard_map/ppermute | solution.py:36
  212.6 24.5 %collective-permute-start.16 = (bf16[2,128,2048]{2,1,0:T(8,128)(2,1)}, bf16[2,128,2048]{2,1,0:T(8,128)(2,1)}, u32[]{:S(2)}, u32[]{:S(2)}) collective-permute-start(bf16[2,128,2048]{2,1,0:T(8,128)(2,1)} %get-tuple-element.178), channel_id=1, source_target_pairs={{0,64},{64,0},{1,65},{65,1},{2,66},{66,2},{3,67},{67,3},{4,68},{68... | collective-permute-start | bytes 3145736 | tf_op jit(solution)/shard_map/ppermute | solution.py:32
  237.1 57.0 %collective-permute-start.27 = (bf16[2,128,2048]{2,1,0:T(8,128)(2,1)}, bf16[2,128,2048]{2,1,0:T(8,128)(2,1)S(1)}, u32[]{:S(2)}, u32[]{:S(2)}) collective-permute-start(bf16[2,128,2048]{2,1,0:T(8,128)(2,1)} %copy-done.19), channel_id=1, source_target_pairs={{0,65},{1,64},{64,1},{65,0},{2,67},{3,66},{66,3},{67,2},{4,69},{5,... | collective-permute-start | bytes 3145736 | tf_op jit(solution)/shard_map/ppermute | solution.py:32
  239.9 54.2 %collective-permute-start.28 = (bf16[2,128,2048]{2,1,0:T(8,128)(2,1)}, bf16[2,128,2048]{2,1,0:T(8,128)(2,1)S(1)}, u32[]{:S(2)}, u32[]{:S(2)}) collective-permute-start(bf16[2,128,2048]{2,1,0:T(8,128)(2,1)} %copy-done.18), channel_id=1, source_target_pairs={{0,1},{1,0},{2,3},{3,2},{4,5},{5,4},{6,7},{7,6},{8,9},{9,8},{10,11... | collective-permute-start | bytes 3145736 | tf_op jit(solution)/shard_map/ppermute | solution.py:32
  244.7 13.2 %collective-permute-start.21 = (bf16[128,1024]{1,0:T(8,128)(2,1)S(1)}, bf16[128,1024]{1,0:T(8,128)(2,1)S(1)}, u32[]{:S(2)}, u32[]{:S(2)}) collective-permute-start(bf16[128,1024]{1,0:T(8,128)(2,1)S(1)} %get-tuple-element.198), channel_id=1, source_target_pairs={{0,8},{4,12},{8,0},{12,4},{1,9},{5,13},{9,1},{13,5},{2,10},{6,14},... | collective-permute-start | bytes 786440 | tf_op jit(solution)/shard_map/ppermute | solution.py:36
  247.9 13.4 %collective-permute-start.22 = (bf16[128,1024]{1,0:T(8,128)(2,1)S(1)}, bf16[128,1024]{1,0:T(8,128)(2,1)S(1)}, u32[]{:S(2)}, u32[]{:S(2)}) collective-permute-start(bf16[128,1024]{1,0:T(8,128)(2,1)S(1)} %get-tuple-element.199), channel_id=1, source_target_pairs={{0,12},{4,8},{8,4},{12,0},{1,13},{5,9},{9,5},{13,1},{2,14},{6,10},... | collective-permute-start | bytes 786440 | tf_op jit(solution)/shard_map/ppermute | solution.py:36
  250.7 11.3 %collective-permute-start.17 = (bf16[144,1024]{1,0:T(8,128)(2,1)S(1)}, bf16[144,1024]{1,0:T(8,128)(2,1)S(1)}, u32[]{:S(2)}, u32[]{:S(2)}) collective-permute-start(bf16[144,1024]{1,0:T(8,128)(2,1)S(1)} %get-tuple-element.193), channel_id=1, source_target_pairs={{0,16},{16,0},{32,48},{48,32},{1,17},{17,1},{33,49},{49,33},{2,18}... | collective-permute-start | bytes 884744 | tf_op jit(solution)/shard_map/ppermute | solution.py:36
  257.9 10.3 %collective-permute-start.18 = (bf16[144,1024]{1,0:T(8,128)(2,1)S(1)}, bf16[144,1024]{1,0:T(8,128)(2,1)S(1)}, u32[]{:S(2)}, u32[]{:S(2)}) collective-permute-start(bf16[144,1024]{1,0:T(8,128)(2,1)S(1)} %get-tuple-element.194), channel_id=1, source_target_pairs={{0,32},{16,48},{32,0},{48,16},{1,33},{17,49},{33,1},{49,17},{2,34}... | collective-permute-start | bytes 884744 | tf_op jit(solution)/shard_map/ppermute | solution.py:36
  261.3 14.9 %collective-permute-start.19 = (bf16[144,1024]{1,0:T(8,128)(2,1)S(1)}, bf16[144,1024]{1,0:T(8,128)(2,1)S(1)}, u32[]{:S(2)}, u32[]{:S(2)}) collective-permute-start(bf16[144,1024]{1,0:T(8,128)(2,1)S(1)} %get-tuple-element.195), channel_id=1, source_target_pairs={{0,48},{16,32},{32,16},{48,0},{1,49},{17,33},{33,17},{49,1},{2,50}... | collective-permute-start | bytes 884744 | tf_op jit(solution)/shard_map/ppermute | solution.py:36
  277.9 12.0 %collective-permute-start.25 = (bf16[32,3584]{1,0:T(8,128)(2,1)S(1)}, bf16[32,3584]{1,0:T(8,128)(2,1)S(1)}, u32[]{:S(2)}, u32[]{:S(2)}) collective-permute-start(bf16[32,3584]{1,0:T(8,128)(2,1)S(1)} %get-tuple-element.207), channel_id=1, source_target_pairs={{0,66},{2,64},{64,2},{66,0},{1,67},{3,65},{65,3},{67,1},{4,70},{6,... | collective-permute-start | bytes 688136 | tf_op jit(solution)/shard_map/ppermute | solution.py:32
  (36 other events, 560.4 us)
Sparse Core Ops, SparseCore 0:
  26.9 91.5 all-gather.1
  144.9 80.1 reduce-scatter.1

commit v7 on v6

--- a/solution.py
+++ b/solution.py
@@ -696,51 +696,65 @@
     )(*arrays)
 
 
-def near_kernel(*refs):
+def near_kernel(coords, *refs):
     for side in range(2):
         own, one, three = refs[3 * side : 3 * side + 3]
-        outs = refs[6 + 4 * side : 10 + 4 * side]
         for i in range(4):
-            add_blocks([own[i], one[i], three[i]], outs[i], side == 0)
-
-
-def near_sums(*chunks):
-    shapes = []
-    for chunk, less in ((chunks[0], 8), (chunks[3], 0)):
-        rows, columns = chunk.shape[1:]
-        shapes += [like((rows - less, columns), F32)] + [like((rows, columns))] * 3
+            target = refs[6 + i] if side == 0 else refs[10].at[coords[2] ^ i]
+            add_blocks([own[i], one[i], three[i]], target, side == 0)
+
+
+def near_sums(coords, *chunks):
+    rows, columns = chunks[0].shape[1:]
+    shapes = [like((rows - 8, columns), F32)] + [like((rows, columns))] * 3 + [like(chunks[3].shape)]
     outs = pl.pallas_call(
         near_kernel,
-        in_specs=[WHOLE] * 6,
-        out_specs=[WHOLE] * 8,
+        in_specs=[SCALARS] + [WHOLE] * 6,
+        out_specs=[WHOLE] * 5,
         out_shape=shapes,
-        compiler_params=params(24),
+        compiler_params=params(60),
         name="near",
-    )(*chunks)
-    return outs[:4], outs[4:]
-
-
-def cut_heads_kernel(coords, heads_ref, *outs):
-    rows = outs[0].shape[0]
+    )(coords, *chunks)
+    return outs[:4], outs[4]
+
+
+def settle_kernel(sum_ref, out_ref):
+    out_ref[...] = sum_ref[...]
+
+
+def settle(summed):
+    return pl.pallas_call(
+        settle_kernel,
+        in_specs=[WHOLE],
+        out_specs=WHOLE,
+        out_shape=like(summed.shape),
+        compiler_params=params(60),
+        name="settle",
+    )(summed)
+
+
+def cut_summed_kernel(coords, down_ref, heads_ref, *outs):
+    rows, wide = outs[0].shape[0], down_ref.shape[1]
     for bits in range(4):
         some = pl.ds(pl.multiple_of(slot_of(coords, bits) * rows, rows), rows)
-        outs[bits][...] = heads_ref[some, :]
-
-
-def cut_heads(coords, grads):
-    rows, columns = grads.shape[0] // 4, grads.shape[1]
-    return pl.pallas_call(
-        cut_heads_kernel,
-        in_specs=[SCALARS, WHOLE],
+        outs[bits][:, :wide] = down_ref[some, :]
+        outs[bits][:, wide:] = heads_ref[some, :]
+
+
+def cut_summed(coords, down, heads):
+    rows = down.shape[0] // 4
+    return pl.pallas_call(
+        cut_summed_kernel,
+        in_specs=[SCALARS] + [WHOLE] * 2,
         out_specs=[WHOLE] * 4,
-        out_shape=[like((rows, columns))] * 4,
+        out_shape=[like((rows, down.shape[1] + heads.shape[1]))] * 4,
         compiler_params=params(16),
-        name="cut_heads",
-    )(coords, grads)
+        name="cut_summed",
+    )(coords, down, heads)
 
 
 def cut_kernel(coords, *refs):
-    up, down, heads, outs = refs[:4], refs[4:8], refs[8:12], refs[12:]
+    up, summed, outs = refs[:4], refs[4:8], refs[8:]
     rows, hidden = outs[0].shape[0], up[0].shape[1]
     block = 4 * rows
     vectors = up[0][block:, :]
@@ -751,28 +765,27 @@
     for bits in range(4):
         some = pl.ds(pl.multiple_of(slot_of(coords, bits) * rows, rows), rows)
         out = outs[bits]
-        for side, blocks in enumerate((up, down)):
-            total = blocks[0][some, :]
-            for other in blocks[1:]:
-                total = total + other[some, :].astype(F32)
-            out[:, side * hidden : (side + 1) * hidden] = total.astype(BF16)
-        end = 2 * hidden + heads[bits].shape[1]
-        out[:, 2 * hidden : end] = heads[bits][...]
+        total = up[0][some, :]
+        for other in up[1:]:
+            total = total + other[some, :].astype(F32)
+        out[:, :hidden] = total.astype(BF16)
+        end = hidden + summed[bits].shape[1]
+        out[:, hidden:end] = summed[bits][...]
         out[:16, end:] = vectors[:, : hidden // 2]
         out[16:, end:] = vectors[:, hidden // 2 :]
 
 
-def cut(coords, up, down, heads):
-    rows, hidden = heads[0].shape[0], up[0].shape[1]
-    columns = 2 * hidden + heads[0].shape[1] + hidden // 2
+def cut(coords, up, summed):
+    rows, hidden = summed[0].shape[0], up[0].shape[1]
+    columns = hidden + summed[0].shape[1] + hidden // 2
     return pl.pallas_call(
         cut_kernel,
-        in_specs=[SCALARS] + [WHOLE] * 12,
+        in_specs=[SCALARS] + [WHOLE] * 8,
         out_specs=[WHOLE] * 4,
         out_shape=[like((rows, columns))] * 4,
         compiler_params=params(16),
         name="cut",
-    )(coords, *up, *down, *heads)
+    )(coords, *up, *summed)
 
 
 def combine_kernel(hidden_ref, right_ref, weights_ref, mine_ref, theirs_ref):
@@ -907,6 +920,7 @@
         out_shape=[like(shape), like(shape, F32)],
         scratch_shapes=[pltpu.VMEM(shape, F32)] * 2,
         compiler_params=params(24),
+        cost_estimate=cost(5 * GIGA, 4 * MIB),
         name="leave",
     )(tokens, cotangent, gain.reshape(1, -1), bias.reshape(1, -1), *sums)
 
@@ -992,24 +1006,26 @@
     up_one, up_three = hop(up_one, "y", 1), hop(up_three, "y", 3)
     down_one, down_three = hop(down_one, "x", 1), hop(down_three, "x", 3)
     keep, sends = fold(mine, theirs)
-    near = flip(sends[1], "zl")
-    head_parts = cut_heads(coords, head_grads)
-    up_one, up_three, down_one, down_three, near, keep, far, opposite, head_parts = lax.optimization_barrier(
-        (up_one, up_three, down_one, down_three, near, keep, sends[2], sends[0], head_parts)
-    )
-    along_z = [near, flip(far, "zl", "mp"), flip(opposite, "mp")]
-    up_sums, down_sums = near_sums(up_own, up_one, up_three, down_own, down_one, down_three)
+    opposite = flip(sends[0], "mp")
+    up_one, up_three, down_one, down_three, opposite, keep, near, far, head_grads = lax.optimization_barrier(
+        (up_one, up_three, down_one, down_three, opposite, keep, sends[1], sends[2], settle(head_grads))
+    )
+    along_z = [opposite, flip(near, "zl"), flip(far, "zl", "mp")]
+    up_sums, down_sums = near_sums(coords, up_own, up_one, up_three, down_own, down_one, down_three)
     up_sums = [up_sums[0]] + [hop(part, "x", bits) for part, bits in zip(up_sums[1:], (1, 2, 3))]
-    down_sums = [down_sums[0]] + [hop(part, "y", bits) for part, bits in zip(down_sums[1:], (1, 2, 3))]
-    parts = exchange(cut(coords, up_sums, down_sums, head_parts))
+    down_sums = lax.psum_scatter(
+        down_sums.reshape(-1, hidden), "y", scatter_dimension=0, tiled=True
+    )
+    up_sums, summed = lax.optimization_barrier((up_sums, cut_summed(coords, down_sums, head_grads)))
+    parts = exchange(cut(coords, up_sums, summed))
     mixed, d_tokens = leave(
         tokens, cotangent, layernorm_gain, b_out + b_down, [keep] + along_z
     )
+    mixed, d_tokens, *parts = lax.optimization_barrier((mixed, d_tokens, *parts))
     grad_up_w, grad_down_w, grad_qkv_w, grad_out_w, vectors, grad_b_up, grad_b_qkv = unpack(
         coords, parts, hidden, width
     )
-    swapped, mixed, d_tokens = lax.optimization_barrier((flip(vectors, "mp"), mixed, d_tokens))
-    vectors = (vectors + swapped)[:6].reshape(3, depth)
+    vectors = (vectors + flip(vectors, "mp"))[:6].reshape(3, depth)
     return (
         mixed,
         d_tokens,

time: 308 us -> 300 us (0.974)
  waiting for transfers between devices: 119 us -> 103 us
  local copies, waits for them, and re-layouts: 24.7 us -> 28.2 us
    ppermute x14 -> x11, waiting for transfers between devices: 35.3 us -> 10.8 us  [hop(): return lax.ppermute(value, axis, [(i, i ^ bits) for i in range(4)])]
    reduce_scatter x0 -> x1, waiting for transfers between devices: none -> 15.1 us  [per_device(): lax.psum_scatter(down_sums.reshape(-1, hidden), 'y', scatter_dimension=0,...]
    ppermute x15, starting transfers between devices: 18.7 us -> 23 us  [flip(): return lax.ppermute(value, axes, [(i, count - 1 - i) for i in range(count)])]
    ppermute x15, waiting for transfers between devices: 66.2 us -> 62.6 us  [flip(): return lax.ppermute(value, axes, [(i, count - 1 - i) for i in range(count)])]
    unnamed x67 -> x73, local copies, waits for them, and re-layouts: 21.2 us -> 24.7 us
    pallas_call x3 -> x4, Pallas kernels: 4.44 us -> 7.84 us  [the longest x1 4.9 us: near_sums(): pl.pallas_call(near_kernel, in_specs=[SCALARS] + [WHOLE] * 6, out_specs=[...]
    ppermute x14 -> x11, starting transfers between devices: 15.2 us -> 12.7 us  [hop(): return lax.ppermute(value, axis, [(i, i ^ bits) for i in range(4)])]
  transfers between devices with their start and end apart: 31 -> 29, of which waited for: 17 -> 12; matrix products, arithmetic and copies ran while one was open for 2% -> 2% of each run, Pallas kernels for 26% -> 26%
where the time goes in v7:
time: 300 us; the launch traced here: 299 us
  Pallas kernels  115 us (38%)
  waiting for transfers between devices  103 us (34%)
  starting transfers between devices  36.1 us (12%)
  local copies, waits for them, and re-layouts  28.2 us (9%)
  between operations  14.1 us (5%)
    ppermute x15, waiting for transfers between devices, flip(): return lax.ppermute(value, axes, [(i, count - 1 - i) for i in range(count)])  62.6 us
    pallas_call x1, Pallas kernels, mlp(): pl.pallas_call(mlp_kernel, in_specs=[SCALARS] + [ANY] * 3 + [WHOLE] * 6,...  30.5 us
    pallas_call x1, Pallas kernels, heads(): pl.pallas_call(heads_kernel, in_specs=[ANY] * 3 + [WHOLE] * 6, out_specs=...  26.3 us
    unnamed x73, local copies, waits for them, and re-layouts  24.7 us
    ppermute x15, starting transfers between devices, flip(): return lax.ppermute(value, axes, [(i, count - 1 - i) for i in range(count)])  23 us
    pallas_call x1, Pallas kernels, combine(): pl.pallas_call(combine_kernel, grid=(4,), in_specs=[WHOLE, WHOLE, pl.Bloc...  17.8 us
    reduce_scatter x1, waiting for transfers between devices, per_device(): lax.psum_scatter(down_sums.reshape(-1, hidden), 'y', scatter_dimension=0,...  15.1 us
    ppermute x11, starting transfers between devices, hop(): return lax.ppermute(value, axis, [(i, i ^ bits) for i in range(4)])  12.7 us
  transfers between devices with their start and end apart: 29, of which 12 were waited for; matrix products, arithmetic and copies ran while one was open for 2% of the time, Pallas kernels for 26%

profile of v7, /device:TPU:1, one launch (start us, length us, event | category | flops | bytes accessed | tf_op | source)
XLA Modules:
  0.0 299.0 jit_solution(15771155748366404632)
XLA Ops:
  7.8 3.0 %pack.1 = (bf16[32,3328]{1,0:T(8,128)(2,1)}, bf16[32,3328]{1,0:T(8,128)(2,1)}, bf16[32,3328]{1,0:T(8,128)(2,1)}, bf16[32,3328]{1,0:T(8,128)(2,1)}) custom-call(s32[5]{0:T(128)} %stack.40.coords, bf16[32,4096]{1,0:T(8,128)(2,1)} %up_ref.1, bf16[32,4096]{1,0:T(8,128)(2,1)} %bitcast.68, bf16[3,32,1024]{2,1,0:T(8,128)(2,1)} %bitcast.69, ...), custom_call_target="tpu_custom_call" | custom-call | tf_op jit(solution)/shard_map/pack/pallas_call | solution.py:349
  10.8 2.5 collective-permute-start.1
  14.4 4.2 %collective-permute-done.1.refs_2_ = bf16[32,3328]{1,0:T(8,128)(2,1)S(1)} collective-permute-done((bf16[32,3328]{1,0:T(8,128)(2,1)}, bf16[32,3328]{1,0:T(8,128)(2,1)S(1)}, u32[]{:S(2)}, u32[]{:S(2)}) %collective-permute-start.1) | collective-permute-done | bytes 213024 | tf_op jit(solution)/shard_map/ppermute | solution.py:32
  18.6 5.1 %collective-permute-done.2.refs_3_ = bf16[32,3328]{1,0:T(8,128)(2,1)S(1)} collective-permute-done((bf16[32,3328]{1,0:T(8,128)(2,1)}, bf16[32,3328]{1,0:T(8,128)(2,1)S(1)}, u32[]{:S(2)}, u32[]{:S(2)}) %collective-permute-start.2) | collective-permute-done | bytes 213024 | tf_op jit(solution)/shard_map/ppermute | solution.py:32
  31.8 3.4 %collective-permute-start.3 = (bf16[2,128,2048]{2,1,0:T(8,128)(2,1)S(1)}, bf16[2,128,2048]{2,1,0:T(8,128)(2,1)S(1)}, u32[]{:S(2)}, u32[]{:S(2)}) collective-permute-start(bf16[2,128,2048]{2,1,0:T(8,128)(2,1)S(1)} %get-tuple-element.128.refs_0_), channel_id=1, source_target_pairs={{0,1},{1,0},{2,3},{3,2},{4,5},{5,4},{6,7},{7,6},{8,9},{9,8},{10,11... | collective-permute-start | bytes 3145736 | tf_op jit(solution)/shard_map/ppermute | solution.py:32
  36.0 22.9 %collective-permute-done.3.refs_1_ = bf16[2,128,2048]{2,1,0:T(8,128)(2,1)S(1)} collective-permute-done((bf16[2,128,2048]{2,1,0:T(8,128)(2,1)S(1)}, bf16[2,128,2048]{2,1,0:T(8,128)(2,1)S(1)}, u32[]{:S(2)}, u32[]{:S(2)}) %collective-permute-start.3) | collective-permute-done | bytes 1048608 | tf_op jit(solution)/shard_map/ppermute | solution.py:32
  58.9 23.4 %collective-permute-done.4.refs_2_ = bf16[2,128,2048]{2,1,0:T(8,128)(2,1)S(1)} collective-permute-done((bf16[2,128,2048]{2,1,0:T(8,128)(2,1)S(1)}, bf16[2,128,2048]{2,1,0:T(8,128)(2,1)S(1)}, u32[]{:S(2)}, u32[]{:S(2)}) %collective-permute-start.4) | collective-permute-done | bytes 1048608 | tf_op jit(solution)/shard_map/ppermute | solution.py:32
  94.3 12.1 %tokens.1 = (bf16[2,1024,2048]{2,1,0:T(8,128)(2,1)S(1)}, bf16[2,2048,1024]{2,1,0:T(8,128)(2,1)S(1)}) custom-call(bf16[4,2,128,2048]{3,2,1,0:T(8,128)(2,1)} %join.1.mine_ref, bf16[4,2,128,2048]{3,2,1,0:T(8,128)(2,1)} %collective-permute-done.6.other_ref), custom_call_target="tpu_custom_call" | custom-call | bytes 33554432 | tf_op jit(solution)/shard_map/tokens/pallas_call | solution.py:418
  106.4 3.2 %copy-done.18 = bf16[2,1024,2048]{2,1,0:T(8,128)(2,1)} copy-done((bf16[2,1024,2048]{2,1,0:T(8,128)(2,1)}, bf16[2,1024,2048]{2,1,0:T(8,128)(2,1)S(1)}, u32[]{:S(2)}) %copy-start.18) | copy-done | bytes 8388632
  109.6 3.3 %copy-done.19 = bf16[2,2048,1024]{2,1,0:T(8,128)(2,1)} copy-done((bf16[2,2048,1024]{2,1,0:T(8,128)(2,1)}, bf16[2,2048,1024]{2,1,0:T(8,128)(2,1)S(1)}, u32[]{:S(2)}) %copy-start.19) | copy-done | bytes 8388632
  112.9 5.5 %all-gather.2.cloned.1.call-done.weights_hbm.weights_ref = bf16[2048,3072]{1,0:T(8,128)(2,1)} async-done(((bf16[128,3072]{1,0:T(8,128)(2,1)}), bf16[2048,3072]{1,0:T(8,128)(2,1)}) %all-gather.2.cloned.1.call-update) | async-done | bytes 12582928 | tf_op jit(solution)/shard_map/all_gather | solution.py:959
  118.5 26.3 %heads.1 = (bf16[1024,1024]{1,0:T(8,128)(2,1)}, bf16[2048,1024]{1,0:T(8,128)(2,1)}, f32[1,1024]{1,0:T(1,128)}, f32[2,2048]{1,0:T(2,128)}) custom-call(bf16[2,1024,2048]{2,1,0:T(8,128)(2,1)} %copy-done.18, bf16[2,2048,1024]{2,1,0:T(8,128)(2,1)} %copy-done.19, bf16[2048,3072]{1,0:T(8,128)(2,1)} %all-gather.2.cloned.1.call-done.weights_hbm.weights_ref, ...), custom_call_target="tpu_custom_call" | custom-call | flops 31457280000 | bytes 10485760 | tf_op jit(solution)/shard_map/heads/pallas_call | solution.py:234
  146.3 30.5 %mlp.1 = (bf16[2,1024,1024]{2,1,0:T(8,128)(2,1)}, bf16[4,144,1024]{2,1,0:T(8,128)(2,1)}, bf16[4,144,1024]{2,1,0:T(8,128)(2,1)}, bf16[4,144,1024]{2,1,0:T(8,128)(...) custom-call(s32[5]{0:T(128)} %stack.40.coords, ...), custom_call_target="tpu_custom_call" | custom-call | flops 17179869184 | bytes 41943040 | tf_op jit(solution)/shard_map/mlp/pallas_call | solution.py:615
  182.4 17.8 %combine.1 = (bf16[2,512,2048]{2,1,0:T(8,128)(2,1)S(1)}, bf16[2,512,2048]{2,1,0:T(8,128)(2,1)S(1)}) custom-call(bf16[2,1024,1024]{2,1,0:T(8,128)(2,1)} %get-tuple-element.165.hidden_ref, bf16[1024,1024]{1,0:T(8,128)(2,1)S(1)} %copy-done.28, bf16[2048,3072]{1,0:T(8,128)(2,1)} %all-gather.2.cloned.1.call-done.weights_hbm.weights_ref), custom_call_target="tpu_custom_call" | custom-call | flops 12884901888 | bytes 16777216 | tf_op jit(solution)/shard_map/combine/pallas_call | solution.py:814
  202.0 2.5 bump.1
  209.0 3.3 %fold.1 = (f32[2,128,2048]{2,1,0:T(8,128)S(1)}, bf16[2,128,2048]{2,1,0:T(8,128)(2,1)}, bf16[2,128,2048]{2,1,0:T(8,128)(2,1)}, bf16[2,128,2048]{2,1,0:T(8,128)(2,1)}) custom-call(bf16[2,512,2048]{2,1,0:T(8,128)(2,1)S(1)} %get-tuple-element.180.mine_ref, bf16[2,512,2048]{2,1,0:T(8,128)(2,1)S(1)} %collective-permute-done.15.theirs_ref), custom_call_target="tpu_custom_call" | custom-call | bytes 6815744 | tf_op jit(solution)/shard_map/fold/pallas_call | solution.py:54
  213.6 2.9 collective-permute-start.16
  216.5 8.9 %reduce-scatter.3.cloned.1.call-done.sum_ref = bf16[128,1024]{1,0:T(8,128)(2,1)} async-done(((bf16[2048,1024]{1,0:T(8,128)(2,1)}), bf16[128,1024]{1,0:T(8,128)(2,1)}) %reduce-scatter.3.cloned.1.call-update) | async-done | bytes 262160 | tf_op jit(solution)/shard_map/reduce_scatter | solution.py:929
  227.1 8.3 %collective-permute-done.13.refs_4_ = bf16[4,128,1024]{2,1,0:T(8,128)(2,1)} collective-permute-done((bf16[4,128,1024]{2,1,0:T(8,128)(2,1)S(1)}, bf16[4,128,1024]{2,1,0:T(8,128)(2,1)}, u32[]{:S(2)}, u32[]{:S(2)}) %collective-permute-start.13) | collective-permute-done | bytes 1048608 | tf_op jit(solution)/shard_map/ppermute | solution.py:36
  239.2 4.9 %near.1 = (f32[136,1024]{1,0:T(8,128)}, bf16[144,1024]{1,0:T(8,128)(2,1)}, bf16[144,1024]{1,0:T(8,128)(2,1)}, bf16[144,1024]{1,0:T(8,128)(2,1)}, bf16[4,128,1024]{2,1,0:T(8,128)(2,1)}) custom-call(s32[5]{0:T(128)} %stack.40.coords, bf16[4,144,1024]{2,1,0:T(8,128)(2,1)} %get-tuple-element.193.refs_0_, bf16[4,144,1024]{2,1,0:T(8,128)(2,1)} %collective-permute-done.11.refs_1_, ...), custom_call_target="tpu_custom_call" | custom-call | tf_op jit(solution)/shard_map/near/pallas_call | solution.py:710
  251.7 15.1 %reduce-scatter.5.cloned.1.call-done.down_ref = bf16[128,1024]{1,0:T(8,128)(2,1)} async-done(((bf16[512,1024]{1,0:T(8,128)(2,1)}), bf16[128,1024]{1,0:T(8,128)(2,1)}) %reduce-scatter.5.cloned.1.call-update) | async-done | bytes 262160 | tf_op jit(solution)/shard_map/reduce_scatter | solution.py:1016
  275.8 4.6 %leave.1 = (bf16[128,2048]{1,0:T(8,128)(2,1)}, f32[128,2048]{1,0:T(8,128)}) custom-call(bf16[128,2048]{1,0:T(8,128)(2,1)S(1)} %copy-done.8, bf16[128,2048]{1,0:T(8,128)(2,1)S(1)} %copy-done.10, f32[1,2048]{1,0:T(1,128)S(1)} %bitcast.65, f32[1,2048]{1,0:T(1,128)S(1)} %bitcast.66, f32[2,128,2048]{2,1,0:T(8,128)S(1)} %copy-done.21, ...), custom_call_target="tpu_custom_call" | custom-call | flops 5242880000 | bytes 4194304 | tf_op jit(solution)/shard_map/leave/pallas_call | solution.py:916
  280.4 4.3 %collective-permute-done.24.refs_3_ = bf16[32,3584]{1,0:T(8,128)(2,1)S(1)} collective-permute-done((bf16[32,3584]{1,0:T(8,128)(2,1)S(1)}, bf16[32,3584]{1,0:T(8,128)(2,1)S(1)}, u32[]{:S(2)}, u32[]{:S(2)}) %collective-permute-start.24) | collective-permute-done | bytes 229408 | tf_op jit(solution)/shard_map/ppermute | solution.py:32
  286.4 2.9 collective-permute-start.25
  (148 shorter events, 63.8 us)
Async XLA Ops:
  7.2 111.3 %all-gather.2.cloned.1.call-start = ((), (), s32[]{:S(2)}) async-start(), calls=%async_computation.2 | async-start | bytes 13369344 | tf_op jit(solution)/shard_map/all_gather | solution.py:959
  14.4 9.3 %collective-permute-start.2 = (bf16[32,3328]{1,0:T(8,128)(2,1)}, bf16[32,3328]{1,0:T(8,128)(2,1)S(1)}, u32[]{:S(2)}, u32[]{:S(2)}) collective-permute-start(bf16[32,3328]{1,0:T(8,128)(2,1)} %get-tuple-element.126), channel_id=1, source_target_pairs={{0,66},{2,64},{64,2},{66,0},{1,67},{3,65},{65,3},{67,1},{4,70},{6,... | collective-permute-start | bytes 638984 | tf_op jit(solution)/shard_map/ppermute | solution.py:32
  26.8 198.6 %reduce-scatter.3.cloned.1.call-start = ((), (), s32[]{:S(2)}) async-start(), calls=%async_computation.3 | async-start | bytes 4456448 | tf_op jit(solution)/shard_map/reduce_scatter | solution.py:929
  31.8 27.1 %collective-permute-start.3 = (bf16[2,128,2048]{2,1,0:T(8,128)(2,1)S(1)}, bf16[2,128,2048]{2,1,0:T(8,128)(2,1)S(1)}, u32[]{:S(2)}, u32[]{:S(2)}) collective-permute-start(bf16[2,128,2048]{2,1,0:T(8,128)(2,1)S(1)} %get-tuple-element.128.refs_0_), channel_id=1, source_target_pairs={{0,1},{1,0},{2,3},{3,2},{4,5},{5,4},{6,7},{7,6},{8,9},{9,8},{10,11... | collective-permute-start | bytes 3145736 | tf_op jit(solution)/shard_map/ppermute | solution.py:32
  35.2 47.1 %collective-permute-start.4 = (bf16[2,128,2048]{2,1,0:T(8,128)(2,1)S(1)}, bf16[2,128,2048]{2,1,0:T(8,128)(2,1)S(1)}, u32[]{:S(2)}, u32[]{:S(2)}) collective-permute-start(bf16[2,128,2048]{2,1,0:T(8,128)(2,1)S(1)} %get-tuple-element.128.refs_0_), channel_id=1, source_target_pairs={{0,64},{64,0},{1,65},{65,1},{2,66},{66,2},{3,67},{67,3},{4,68},{68... | collective-permute-start | bytes 3145736 | tf_op jit(solution)/shard_map/ppermute | solution.py:32
  36.0 46.3 %collective-permute-start.5 = (bf16[2,128,2048]{2,1,0:T(8,128)(2,1)S(1)}, bf16[2,128,2048]{2,1,0:T(8,128)(2,1)S(1)}, u32[]{:S(2)}, u32[]{:S(2)}) collective-permute-start(bf16[2,128,2048]{2,1,0:T(8,128)(2,1)S(1)} %get-tuple-element.128.refs_0_), channel_id=1, source_target_pairs={{0,65},{1,64},{64,1},{65,0},{2,67},{3,66},{66,3},{67,2},{4,69},{5,... | collective-permute-start | bytes 3145736 | tf_op jit(solution)/shard_map/ppermute | solution.py:32
  84.3 9.9 %collective-permute-start.6 = (bf16[4,2,128,2048]{3,2,1,0:T(8,128)(2,1)}, bf16[4,2,128,2048]{3,2,1,0:T(8,128)(2,1)}, u32[]{:S(2)}, u32[]{:S(2)}) collective-permute-start(bf16[4,2,128,2048]{3,2,1,0:T(8,128)(2,1)} %join.1.mine_ref), channel_id=1, source_target_pairs={{0,2},{2,0},{1,3},{3,1},{4,6},{6,4},{5,7},{7,5},{8,10},{10,8},{9,1... | collective-permute-start | bytes 12582920 | tf_op jit(solution)/shard_map/ppermute | solution.py:32
  144.8 122.0 %reduce-scatter.5.cloned.1.call-start = ((), (), s32[]{:S(2)}) async-start(), calls=%async_computation.4 | async-start | bytes 1310720 | tf_op jit(solution)/shard_map/reduce_scatter | solution.py:1016
  176.9 23.4 %collective-permute-start.7 = (bf16[2,144,1024]{2,1,0:T(8,128)(2,1)}, bf16[2,144,1024]{2,1,0:T(8,128)(2,1)S(1)}, u32[]{:S(2)}, u32[]{:S(2)}) collective-permute-start(bf16[2,144,1024]{2,1,0:T(8,128)(2,1)} %get-tuple-element.161), channel_id=1, source_target_pairs={{0,4},{4,0},{8,12},{12,8},{1,5},{5,1},{9,13},{13,9},{2,6},{6,2},{1... | collective-permute-start | bytes 1769480 | tf_op jit(solution)/shard_map/ppermute | solution.py:36
  178.1 22.2 %collective-permute-start.9 = (bf16[2,144,1024]{2,1,0:T(8,128)(2,1)}, bf16[2,144,1024]{2,1,0:T(8,128)(2,1)S(1)}, u32[]{:S(2)}, u32[]{:S(2)}) collective-permute-start(bf16[2,144,1024]{2,1,0:T(8,128)(2,1)} %get-tuple-element.163), channel_id=1, source_target_pairs={{0,12},{4,8},{8,4},{12,0},{1,13},{5,9},{9,5},{13,1},{2,14},{6,10},... | collective-permute-start | bytes 1769480 | tf_op jit(solution)/shard_map/ppermute | solution.py:36
  179.9 20.3 %collective-permute-start.10 = (bf16[2,128,1024]{2,1,0:T(8,128)(2,1)}, bf16[2,128,1024]{2,1,0:T(8,128)(2,1)S(1)}, u32[]{:S(2)}, u32[]{:S(2)}) collective-permute-start(bf16[2,128,1024]{2,1,0:T(8,128)(2,1)} %get-tuple-element.164), channel_id=1, source_target_pairs={{0,48},{16,32},{32,16},{48,0},{1,49},{17,33},{33,17},{49,1},{2,50}... | collective-permute-start | bytes 1572872 | tf_op jit(solution)/shard_map/ppermute | solution.py:36
  180.8 19.4 %collective-permute-start.8 = (bf16[2,128,1024]{2,1,0:T(8,128)(2,1)}, bf16[2,128,1024]{2,1,0:T(8,128)(2,1)S(1)}, u32[]{:S(2)}, u32[]{:S(2)}) collective-permute-start(bf16[2,128,1024]{2,1,0:T(8,128)(2,1)} %get-tuple-element.162), channel_id=1, source_target_pairs={{0,16},{16,0},{32,48},{48,32},{1,17},{17,1},{33,49},{49,33},{2,18}... | collective-permute-start | bytes 1572872 | tf_op jit(solution)/shard_map/ppermute | solution.py:36
  204.4 33.4 %collective-permute-start.11 = (bf16[4,144,1024]{2,1,0:T(8,128)(2,1)S(1)}, bf16[4,144,1024]{2,1,0:T(8,128)(2,1)}, u32[]{:S(2)}, u32[]{:S(2)}) collective-permute-start(bf16[4,144,1024]{2,1,0:T(8,128)(2,1)S(1)} %get-tuple-element.176), channel_id=1, source_target_pairs={{0,4},{4,0},{8,12},{12,8},{1,5},{5,1},{9,13},{13,9},{2,6},{6,2},{1... | collective-permute-start | bytes 3538952 | tf_op jit(solution)/shard_map/ppermute | solution.py:36
  205.0 32.8 %collective-permute-start.12 = (bf16[4,144,1024]{2,1,0:T(8,128)(2,1)S(1)}, bf16[4,144,1024]{2,1,0:T(8,128)(2,1)}, u32[]{:S(2)}, u32[]{:S(2)}) collective-permute-start(bf16[4,144,1024]{2,1,0:T(8,128)(2,1)S(1)} %get-tuple-element.177), channel_id=1, source_target_pairs={{0,12},{4,8},{8,4},{12,0},{1,13},{5,9},{9,5},{13,1},{2,14},{6,10},... | collective-permute-start | bytes 3538952 | tf_op jit(solution)/shard_map/ppermute | solution.py:36
  206.8 28.6 %collective-permute-start.13 = (bf16[4,128,1024]{2,1,0:T(8,128)(2,1)S(1)}, bf16[4,128,1024]{2,1,0:T(8,128)(2,1)}, u32[]{:S(2)}, u32[]{:S(2)}) collective-permute-start(bf16[4,128,1024]{2,1,0:T(8,128)(2,1)S(1)} %get-tuple-element.178), channel_id=1, source_target_pairs={{0,16},{16,0},{32,48},{48,32},{1,17},{17,1},{33,49},{49,33},{2,18}... | collective-permute-start | bytes 3145736 | tf_op jit(solution)/shard_map/ppermute | solution.py:36
  208.3 29.5 %collective-permute-start.14 = (bf16[4,128,1024]{2,1,0:T(8,128)(2,1)}, bf16[4,128,1024]{2,1,0:T(8,128)(2,1)}, u32[]{:S(2)}, u32[]{:S(2)}) collective-permute-start(bf16[4,128,1024]{2,1,0:T(8,128)(2,1)} %get-tuple-element.179), channel_id=1, source_target_pairs={{0,48},{16,32},{32,16},{48,0},{1,49},{17,33},{33,17},{49,1},{2,50}... | collective-permute-start | bytes 3145736 | tf_op jit(solution)/shard_map/ppermute | solution.py:36
  213.6 25.6 %collective-permute-start.16 = (bf16[2,128,2048]{2,1,0:T(8,128)(2,1)}, bf16[2,128,2048]{2,1,0:T(8,128)(2,1)}, u32[]{:S(2)}, u32[]{:S(2)}) collective-permute-start(bf16[2,128,2048]{2,1,0:T(8,128)(2,1)} %get-tuple-element.182), channel_id=1, source_target_pairs={{0,1},{1,0},{2,3},{3,2},{4,5},{5,4},{6,7},{7,6},{8,9},{9,8},{10,11... | collective-permute-start | bytes 3145736 | tf_op jit(solution)/shard_map/ppermute | solution.py:32
  244.1 30.0 %collective-permute-start.17 = (bf16[2,128,2048]{2,1,0:T(8,128)(2,1)}, bf16[2,128,2048]{2,1,0:T(8,128)(2,1)}, u32[]{:S(2)}, u32[]{:S(2)}) collective-permute-start(bf16[2,128,2048]{2,1,0:T(8,128)(2,1)} %get-tuple-element.189), channel_id=1, source_target_pairs={{0,64},{64,0},{1,65},{65,1},{2,66},{66,2},{3,67},{67,3},{4,68},{68... | collective-permute-start | bytes 3145736 | tf_op jit(solution)/shard_map/ppermute | solution.py:32
  245.5 28.7 %collective-permute-start.18 = (bf16[2,128,2048]{2,1,0:T(8,128)(2,1)}, bf16[2,128,2048]{2,1,0:T(8,128)(2,1)}, u32[]{:S(2)}, u32[]{:S(2)}) collective-permute-start(bf16[2,128,2048]{2,1,0:T(8,128)(2,1)} %get-tuple-element.190), channel_id=1, source_target_pairs={{0,65},{1,64},{64,1},{65,0},{2,67},{3,66},{66,3},{67,2},{4,69},{5,... | collective-permute-start | bytes 3145736 | tf_op jit(solution)/shard_map/ppermute | solution.py:32
  247.4 21.0 %collective-permute-start.19 = (bf16[144,1024]{1,0:T(8,128)(2,1)}, bf16[144,1024]{1,0:T(8,128)(2,1)S(1)}, u32[]{:S(2)}, u32[]{:S(2)}) collective-permute-start(bf16[144,1024]{1,0:T(8,128)(2,1)} %get-tuple-element.200), channel_id=1, source_target_pairs={{0,16},{16,0},{32,48},{48,32},{1,17},{17,1},{33,49},{49,33},{2,18}... | collective-permute-start | bytes 884744 | tf_op jit(solution)/shard_map/ppermute | solution.py:36
  249.3 19.1 %collective-permute-start.20 = (bf16[144,1024]{1,0:T(8,128)(2,1)}, bf16[144,1024]{1,0:T(8,128)(2,1)S(1)}, u32[]{:S(2)}, u32[]{:S(2)}) collective-permute-start(bf16[144,1024]{1,0:T(8,128)(2,1)} %get-tuple-element.201), channel_id=1, source_target_pairs={{0,32},{16,48},{32,0},{48,16},{1,33},{17,49},{33,1},{49,17},{2,34}... | collective-permute-start | bytes 884744 | tf_op jit(solution)/shard_map/ppermute | solution.py:36
  250.7 17.6 %collective-permute-start.21 = (bf16[144,1024]{1,0:T(8,128)(2,1)}, bf16[144,1024]{1,0:T(8,128)(2,1)S(1)}, u32[]{:S(2)}, u32[]{:S(2)}) collective-permute-start(bf16[144,1024]{1,0:T(8,128)(2,1)} %get-tuple-element.202), channel_id=1, source_target_pairs={{0,48},{16,32},{32,16},{48,0},{1,49},{17,33},{33,17},{49,1},{2,50}... | collective-permute-start | bytes 884744 | tf_op jit(solution)/shard_map/ppermute | solution.py:36
  270.1 10.3 %collective-permute-start.22 = (bf16[32,3584]{1,0:T(8,128)(2,1)S(1)}, bf16[32,3584]{1,0:T(8,128)(2,1)S(1)}, u32[]{:S(2)}, u32[]{:S(2)}) collective-permute-start(bf16[32,3584]{1,0:T(8,128)(2,1)S(1)} %get-tuple-element.218), channel_id=1, source_target_pairs={{0,2},{2,0},{1,3},{3,1},{4,6},{6,4},{5,7},{7,5},{8,10},{10,8},{9,1... | collective-permute-start | bytes 688136 | tf_op jit(solution)/shard_map/ppermute | solution.py:32
  273.8 10.9 %collective-permute-start.24 = (bf16[32,3584]{1,0:T(8,128)(2,1)S(1)}, bf16[32,3584]{1,0:T(8,128)(2,1)S(1)}, u32[]{:S(2)}, u32[]{:S(2)}) collective-permute-start(bf16[32,3584]{1,0:T(8,128)(2,1)S(1)} %get-tuple-element.220), channel_id=1, source_target_pairs={{0,66},{2,64},{64,2},{66,0},{1,67},{3,65},{65,3},{67,1},{4,70},{6,... | collective-permute-start | bytes 688136 | tf_op jit(solution)/shard_map/ppermute | solution.py:32
  (37 other events, 493.1 us)
Sparse Core Ops, SparseCore 0:
  26.9 91.5 all-gather.1
  144.9 80.4 reduce-scatter.2
  244.3 22.5 reduce-scatter.4

commit v8 on v7

--- a/solution.py
+++ b/solution.py
@@ -43,7 +43,7 @@
             block = slice(i * rows, (i + 1) * rows)
             total = mine_ref[which, block, :].astype(F32) + theirs_ref[which, block, :].astype(F32)
             if i == 0:
-                keep_ref[which] = total
+                keep_ref[which] = total.astype(BF16)
             else:
                 sends[i - 1][which] = total.astype(BF16)
 
@@ -56,7 +56,7 @@
         grid=(4,),
         in_specs=[pl.BlockSpec((2, 4 * rows, tile), lambda j: (0, 0, j))] * 2,
         out_specs=[pl.BlockSpec((2, rows, tile), lambda j: (0, 0, j))] * 4,
-        out_shape=[like((2, rows, depth), F32)] + [like((2, rows, depth))] * 3,
+        out_shape=[like((2, rows, depth))] * 4,
         compiler_params=params(16),
         cost_estimate=cost(0, 26 * rows * depth),
         name="fold",
@@ -696,26 +696,37 @@
     )(*arrays)
 
 
-def near_kernel(coords, *refs):
-    for side in range(2):
-        own, one, three = refs[3 * side : 3 * side + 3]
-        for i in range(4):
-            target = refs[6 + i] if side == 0 else refs[10].at[coords[2] ^ i]
-            add_blocks([own[i], one[i], three[i]], target, side == 0)
-
-
-def near_sums(coords, *chunks):
-    rows, columns = chunks[0].shape[1:]
-    shapes = [like((rows - 8, columns), F32)] + [like((rows, columns))] * 3 + [like(chunks[3].shape)]
-    outs = pl.pallas_call(
-        near_kernel,
-        in_specs=[SCALARS] + [WHOLE] * 6,
-        out_specs=[WHOLE] * 5,
-        out_shape=shapes,
+def near_up_kernel(own, one, three, *outs):
+    for i in range(4):
+        add_blocks([own[i], one[i], three[i]], outs[i], True)
+
+
+def near_up(own, one, three):
+    rows, columns = own.shape[1:]
+    return pl.pallas_call(
+        near_up_kernel,
+        in_specs=[WHOLE] * 3,
+        out_specs=[WHOLE] * 4,
+        out_shape=[like((rows - 8, columns), F32)] + [like((rows, columns))] * 3,
         compiler_params=params(60),
-        name="near",
-    )(coords, *chunks)
-    return outs[:4], outs[4]
+        name="near_up",
+    )(own, one, three)
+
+
+def near_down_kernel(coords, own, one, three, out):
+    for i in range(4):
+        add_blocks([own[i], one[i], three[i]], out.at[coords[2] ^ i], False)
+
+
+def near_down(coords, own, one, three):
+    return pl.pallas_call(
+        near_down_kernel,
+        in_specs=[SCALARS] + [WHOLE] * 3,
+        out_specs=WHOLE,
+        out_shape=like(own.shape),
+        compiler_params=params(60),
+        name="near_down",
+    )(coords, own, one, three)
 
 
 def settle_kernel(sum_ref, out_ref):
@@ -828,7 +839,7 @@
 
 
 def unpack_kernel(coords, *refs):
-    parts, (up_ref, down_ref, qkv_ref, out_ref, rows_ref, up_sums_ref, qkv_sums_ref) = refs[:4], refs[4:]
+    parts, (up_ref, down_ref, qkv_ref, out_ref) = refs[:4], refs[4:]
     hidden, width = up_ref.shape[1] // 4, out_ref.shape[1] // 4
     for bits in range(4):
         slot, part = slot_of(coords, bits), parts[bits]
@@ -840,25 +851,48 @@
         for kind in range(3):
             qkv_ref[kind, :, narrow] = part[:, start + kind * width : start + (kind + 1) * width].astype(F32)
         out_ref[:, narrow] = part[:, start + 3 * width : start + 4 * width].astype(F32)
-        start += 4 * width
-        vectors = jnp.concatenate([whole(part[:16, start:]), whole(part[16:, start:])], axis=1)
+
+
+def unpack(coords, parts, hidden, width):
+    rows = parts[0].shape[0]
+    wide, narrow = (rows, 4 * hidden), (rows, 4 * width)
+    return pl.pallas_call(
+        unpack_kernel,
+        in_specs=[SCALARS] + [WHOLE] * 4,
+        out_specs=[WHOLE] * 4,
+        out_shape=[like(shape, F32) for shape in (wide, wide, (3,) + narrow, narrow)],
+        compiler_params=params(16),
+        name="unpack",
+    )(coords, *parts)
+
+
+def vectors_kernel(coords, *refs):
+    parts, (rows_ref, up_sums_ref, qkv_sums_ref) = refs[:4], refs[4:]
+    hidden, width = up_sums_ref.shape[1] // 4, qkv_sums_ref.shape[1] // 4
+    for bits in range(4):
+        slot, part = slot_of(coords, bits), parts[bits]
+        wide = pl.ds(pl.multiple_of(slot * hidden, hidden), hidden)
+        narrow = pl.ds(pl.multiple_of(slot * width, width), width)
+        vectors = jnp.concatenate([whole(part[:16, :]), whole(part[16:, :])], axis=1)
         rows_ref[...] = vectors if bits == 0 else rows_ref[...] + vectors
         up_sums_ref[:, wide] = vectors[6:7, :]
         for kind in range(3):
             qkv_sums_ref[kind : kind + 1, narrow] = vectors[7:8, kind * width : (kind + 1) * width]
 
 
-def unpack(coords, parts, hidden, width):
-    rows = parts[0].shape[0]
-    wide, narrow = (rows, 4 * hidden), (rows, 4 * width)
-    shapes = [wide, wide, (3,) + narrow, narrow, (8, hidden), (1, 4 * hidden), (3, 4 * width)]
-    return pl.pallas_call(
-        unpack_kernel,
-        in_specs=[SCALARS] + [WHOLE] * 4,
-        out_specs=[WHOLE] * 7,
+def unpack_vectors(coords, parts, hidden, width):
+    rows, columns = parts[0].shape
+    half = hidden // 2
+    last = columns // half - 1
+    shapes = [(8, hidden), (1, 4 * hidden), (3, 4 * width)]
+    return pl.pallas_call(
+        vectors_kernel,
+        grid=(1,),
+        in_specs=[SCALARS] + [pl.BlockSpec((rows, half), lambda i: (0, last))] * 4,
+        out_specs=[pl.BlockSpec(shape, lambda i: (0, 0)) for shape in shapes],
         out_shape=[like(shape, F32) for shape in shapes],
         compiler_params=params(16),
-        name="unpack",
+        name="vectors",
     )(coords, *parts)
 
 
@@ -899,7 +933,7 @@
 def leave_kernel(tokens_ref, cot_ref, gain_ref, bias_ref, *refs):
     mixed_ref, grad_ref, branch_ref, normed_ref = refs[-4:]
     for which, target in ((0, normed_ref), (1, branch_ref)):
-        total = refs[0][which]
+        total = refs[0][which].astype(F32)
         for part in refs[1:4]:
             total = total + part[which].astype(F32)
         turn(target, total, True)
@@ -1011,7 +1045,8 @@
         (up_one, up_three, down_one, down_three, opposite, keep, sends[1], sends[2], settle(head_grads))
     )
     along_z = [opposite, flip(near, "zl"), flip(far, "zl", "mp")]
-    up_sums, down_sums = near_sums(coords, up_own, up_one, up_three, down_own, down_one, down_three)
+    down_sums = near_down(coords, down_own, down_one, down_three)
+    up_sums = near_up(up_own, up_one, up_three)
     up_sums = [up_sums[0]] + [hop(part, "x", bits) for part, bits in zip(up_sums[1:], (1, 2, 3))]
     down_sums = lax.psum_scatter(
         down_sums.reshape(-1, hidden), "y", scatter_dimension=0, tiled=True
@@ -1022,10 +1057,11 @@
         tokens, cotangent, layernorm_gain, b_out + b_down, [keep] + along_z
     )
     mixed, d_tokens, *parts = lax.optimization_barrier((mixed, d_tokens, *parts))
-    grad_up_w, grad_down_w, grad_qkv_w, grad_out_w, vectors, grad_b_up, grad_b_qkv = unpack(
-        coords, parts, hidden, width
-    )
-    vectors = (vectors + flip(vectors, "mp"))[:6].reshape(3, depth)
+    vectors, grad_b_up, grad_b_qkv = unpack_vectors(coords, parts, hidden, width)
+    swapped = flip(vectors, "mp")
+    grad_up_w, grad_down_w, grad_qkv_w, grad_out_w = unpack(coords, parts, hidden, width)
+    vectors, swapped, grad_up_w = lax.optimization_barrier((vectors, swapped, grad_up_w))
+    vectors = (vectors + swapped)[:6].reshape(3, depth)
     return (
         mixed,
         d_tokens,

time: 300 us -> 298 us (level)
  local copies, waits for them, and re-layouts: 28.2 us -> 25.1 us
  Pallas kernels: 115 us -> 118 us
    unnamed x73, local copies, waits for them, and re-layouts: 24.7 us -> 21.6 us
    pallas_call x1 -> x3, Pallas kernels: 4.9 us -> 7.62 us  [the longest x1 3.25 us: near_down(): pl.pallas_call(near_down_kernel, in_specs=[SCALARS] + [WHOLE] * 3, out_sp...]
  transfers between devices with their start and end apart: 29 -> 29, of which waited for: 12 -> 14; matrix products, arithmetic and copies ran while one was open for 2% -> 2% of each run, Pallas kernels for 26% -> 28%
where the time goes in v8:
time: 298 us; the launch traced here: 297 us
  Pallas kernels  118 us (40%)
  waiting for transfers between devices  102 us (34%)
  starting transfers between devices  35.8 us (12%)
  local copies, waits for them, and re-layouts  25.1 us (8%)
  between operations  14.1 us (5%)
    ppermute x15, waiting for transfers between devices, flip(): return lax.ppermute(value, axes, [(i, count - 1 - i) for i in range(count)])  62.5 us
    pallas_call x1, Pallas kernels, mlp(): pl.pallas_call(mlp_kernel, in_specs=[SCALARS] + [ANY] * 3 + [WHOLE] * 6,...  30.4 us
    pallas_call x1, Pallas kernels, heads(): pl.pallas_call(heads_kernel, in_specs=[ANY] * 3 + [WHOLE] * 6, out_specs=...  26.3 us
    ppermute x15, starting transfers between devices, flip(): return lax.ppermute(value, axes, [(i, count - 1 - i) for i in range(count)])  22.7 us
    unnamed x73, local copies, waits for them, and re-layouts  21.6 us
    pallas_call x1, Pallas kernels, combine(): pl.pallas_call(combine_kernel, grid=(4,), in_specs=[WHOLE, WHOLE, pl.Bloc...  17.8 us
    ppermute x11, starting transfers between devices, hop(): return lax.ppermute(value, axis, [(i, i ^ bits) for i in range(4)])  12.7 us
    reduce_scatter x1, waiting for transfers between devices, per_device(): lax.psum_scatter(down_sums.reshape(-1, hidden), 'y', scatter_dimension=0,...  12.1 us
  transfers between devices with their start and end apart: 29, of which 14 were waited for; matrix products, arithmetic and copies ran while one was open for 2% of the time, Pallas kernels for 28%

profile of v8, /device:TPU:1, one launch (start us, length us, event | category | flops | bytes accessed | tf_op | source)
XLA Modules:
  0.0 296.8 jit_solution(5286085389371425742)
XLA Ops:
  7.8 3.0 %pack.1 = (bf16[32,3328]{1,0:T(8,128)(2,1)}, bf16[32,3328]{1,0:T(8,128)(2,1)}, bf16[32,3328]{1,0:T(8,128)(2,1)}, bf16[32,3328]{1,0:T(8,128)(2,1)}) custom-call(s32[5]{0:T(128)} %stack.40.coords, bf16[32,4096]{1,0:T(8,128)(2,1)} %up_ref.1, bf16[32,4096]{1,0:T(8,128)(2,1)} %bitcast.68, bf16[3,32,1024]{2,1,0:T(8,128)(2,1)} %bitcast.69, ...), custom_call_target="tpu_custom_call" | custom-call | tf_op jit(solution)/shard_map/pack/pallas_call | solution.py:349
  10.8 2.5 collective-permute-start.1
  14.4 4.2 %collective-permute-done.1.refs_2_ = bf16[32,3328]{1,0:T(8,128)(2,1)S(1)} collective-permute-done((bf16[32,3328]{1,0:T(8,128)(2,1)}, bf16[32,3328]{1,0:T(8,128)(2,1)S(1)}, u32[]{:S(2)}, u32[]{:S(2)}) %collective-permute-start.1) | collective-permute-done | bytes 213024 | tf_op jit(solution)/shard_map/ppermute | solution.py:32
  18.6 5.1 %collective-permute-done.2.refs_3_ = bf16[32,3328]{1,0:T(8,128)(2,1)S(1)} collective-permute-done((bf16[32,3328]{1,0:T(8,128)(2,1)}, bf16[32,3328]{1,0:T(8,128)(2,1)S(1)}, u32[]{:S(2)}, u32[]{:S(2)}) %collective-permute-start.2) | collective-permute-done | bytes 213024 | tf_op jit(solution)/shard_map/ppermute | solution.py:32
  31.8 3.4 %collective-permute-start.3 = (bf16[2,128,2048]{2,1,0:T(8,128)(2,1)S(1)}, bf16[2,128,2048]{2,1,0:T(8,128)(2,1)S(1)}, u32[]{:S(2)}, u32[]{:S(2)}) collective-permute-start(bf16[2,128,2048]{2,1,0:T(8,128)(2,1)S(1)} %get-tuple-element.130.refs_0_), channel_id=1, source_target_pairs={{0,1},{1,0},{2,3},{3,2},{4,5},{5,4},{6,7},{7,6},{8,9},{9,8},{10,11... | collective-permute-start | bytes 3145736 | tf_op jit(solution)/shard_map/ppermute | solution.py:32
  36.0 22.9 %collective-permute-done.3.refs_1_ = bf16[2,128,2048]{2,1,0:T(8,128)(2,1)S(1)} collective-permute-done((bf16[2,128,2048]{2,1,0:T(8,128)(2,1)S(1)}, bf16[2,128,2048]{2,1,0:T(8,128)(2,1)S(1)}, u32[]{:S(2)}, u32[]{:S(2)}) %collective-permute-start.3) | collective-permute-done | bytes 1048608 | tf_op jit(solution)/shard_map/ppermute | solution.py:32
  58.9 23.4 %collective-permute-done.4.refs_2_ = bf16[2,128,2048]{2,1,0:T(8,128)(2,1)S(1)} collective-permute-done((bf16[2,128,2048]{2,1,0:T(8,128)(2,1)S(1)}, bf16[2,128,2048]{2,1,0:T(8,128)(2,1)S(1)}, u32[]{:S(2)}, u32[]{:S(2)}) %collective-permute-start.4) | collective-permute-done | bytes 1048608 | tf_op jit(solution)/shard_map/ppermute | solution.py:32
  93.1 12.1 %tokens.1 = (bf16[2,1024,2048]{2,1,0:T(8,128)(2,1)S(1)}, bf16[2,2048,1024]{2,1,0:T(8,128)(2,1)S(1)}) custom-call(bf16[4,2,128,2048]{3,2,1,0:T(8,128)(2,1)} %join.1.mine_ref, bf16[4,2,128,2048]{3,2,1,0:T(8,128)(2,1)} %collective-permute-done.6.other_ref), custom_call_target="tpu_custom_call" | custom-call | bytes 33554432 | tf_op jit(solution)/shard_map/tokens/pallas_call | solution.py:418
  105.2 3.2 %copy-done.18 = bf16[2,1024,2048]{2,1,0:T(8,128)(2,1)} copy-done((bf16[2,1024,2048]{2,1,0:T(8,128)(2,1)}, bf16[2,1024,2048]{2,1,0:T(8,128)(2,1)S(1)}, u32[]{:S(2)}) %copy-start.18) | copy-done | bytes 8388632
  108.4 3.3 %copy-done.19 = bf16[2,2048,1024]{2,1,0:T(8,128)(2,1)} copy-done((bf16[2,2048,1024]{2,1,0:T(8,128)(2,1)}, bf16[2,2048,1024]{2,1,0:T(8,128)(2,1)S(1)}, u32[]{:S(2)}) %copy-start.19) | copy-done | bytes 8388632
  111.8 6.7 %all-gather.2.cloned.1.call-done.weights_hbm.weights_ref = bf16[2048,3072]{1,0:T(8,128)(2,1)} async-done(((bf16[128,3072]{1,0:T(8,128)(2,1)}), bf16[2048,3072]{1,0:T(8,128)(2,1)}) %all-gather.2.cloned.1.call-update) | async-done | bytes 12582928 | tf_op jit(solution)/shard_map/all_gather | solution.py:993
  118.5 26.3 %heads.1 = (bf16[1024,1024]{1,0:T(8,128)(2,1)}, bf16[2048,1024]{1,0:T(8,128)(2,1)}, f32[1,1024]{1,0:T(1,128)}, f32[2,2048]{1,0:T(2,128)}) custom-call(bf16[2,1024,2048]{2,1,0:T(8,128)(2,1)} %copy-done.18, bf16[2,2048,1024]{2,1,0:T(8,128)(2,1)} %copy-done.19, bf16[2048,3072]{1,0:T(8,128)(2,1)} %all-gather.2.cloned.1.call-done.weights_hbm.weights_ref, ...), custom_call_target="tpu_custom_call" | custom-call | flops 31457280000 | bytes 10485760 | tf_op jit(solution)/shard_map/heads/pallas_call | solution.py:234
  146.3 30.4 %mlp.1 = (bf16[2,1024,1024]{2,1,0:T(8,128)(2,1)}, bf16[4,144,1024]{2,1,0:T(8,128)(2,1)}, bf16[4,144,1024]{2,1,0:T(8,128)(2,1)}, bf16[4,144,1024]{2,1,0:T(8,128)(...) custom-call(s32[5]{0:T(128)} %stack.40.coords, ...), custom_call_target="tpu_custom_call" | custom-call | flops 17179869184 | bytes 41943040 | tf_op jit(solution)/shard_map/mlp/pallas_call | solution.py:615
  182.3 17.8 %combine.1 = (bf16[2,512,2048]{2,1,0:T(8,128)(2,1)S(1)}, bf16[2,512,2048]{2,1,0:T(8,128)(2,1)S(1)}) custom-call(bf16[2,1024,1024]{2,1,0:T(8,128)(2,1)} %get-tuple-element.167.hidden_ref, bf16[1024,1024]{1,0:T(8,128)(2,1)S(1)} %copy-done.28, bf16[2048,3072]{1,0:T(8,128)(2,1)} %all-gather.2.cloned.1.call-done.weights_hbm.weights_ref), custom_call_target="tpu_custom_call" | custom-call | flops 12884901888 | bytes 16777216 | tf_op jit(solution)/shard_map/combine/pallas_call | solution.py:825
  208.8 3.2 %fold.1 = (bf16[2,128,2048]{2,1,0:T(8,128)(2,1)S(1)}, bf16[2,128,2048]{2,1,0:T(8,128)(2,1)}, bf16[2,128,2048]{2,1,0:T(8,128)(2,1)}, bf16[2,128,2048]{2,1,0:T(8,128)(2,1)}) custom-call(bf16[2,512,2048]{2,1,0:T(8,128)(2,1)S(1)} %get-tuple-element.182.mine_ref, bf16[2,512,2048]{2,1,0:T(8,128)(2,1)S(1)} %collective-permute-done.15.theirs_ref), custom_call_target="tpu_custom_call" | custom-call | bytes 6815744 | tf_op jit(solution)/shard_map/fold/pallas_call | solution.py:54
  213.0 2.9 collective-permute-start.16
  215.9 9.4 %reduce-scatter.3.cloned.1.call-done.sum_ref = bf16[128,1024]{1,0:T(8,128)(2,1)} async-done(((bf16[2048,1024]{1,0:T(8,128)(2,1)}), bf16[128,1024]{1,0:T(8,128)(2,1)}) %reduce-scatter.3.cloned.1.call-update) | async-done | bytes 262160 | tf_op jit(solution)/shard_map/reduce_scatter | solution.py:963
  227.0 8.3 %collective-permute-done.13.one = bf16[4,128,1024]{2,1,0:T(8,128)(2,1)} collective-permute-done((bf16[4,128,1024]{2,1,0:T(8,128)(2,1)S(1)}, bf16[4,128,1024]{2,1,0:T(8,128)(2,1)}, u32[]{:S(2)}, u32[]{:S(2)}) %collective-permute-start.13) | collective-permute-done | bytes 1048608 | tf_op jit(solution)/shard_map/ppermute | solution.py:36
  238.6 3.2 %near_down.1 = bf16[4,128,1024]{2,1,0:T(8,128)(2,1)} custom-call(s32[5]{0:T(128)} %stack.40.coords, bf16[4,128,1024]{2,1,0:T(8,128)(2,1)} %get-tuple-element.202.own, bf16[4,128,1024]{2,1,0:T(8,128)(2,1)} %collective-permute-done.13.one, bf16[4,128,1024]{2,1,0:T(8,128)(2,1)} %collective-permute-done.14.three), custom_call_target="tpu_custom_call" | custom-call | tf_op jit(solution)/shard_map/near_down/pallas_call | solution.py:722
  245.2 3.2 %near_up.1 = (f32[136,1024]{1,0:T(8,128)}, bf16[144,1024]{1,0:T(8,128)(2,1)}, bf16[144,1024]{1,0:T(8,128)(2,1)}, bf16[144,1024]{1,0:T(8,128)(2,1)}) custom-call(bf16[4,144,1024]{2,1,0:T(8,128)(2,1)} %get-tuple-element.195.own, bf16[4,144,1024]{2,1,0:T(8,128)(2,1)} %collective-permute-done.11.one, bf16[4,144,1024]{2,1,0:T(8,128)(2,1)} %collective-permute-done.12.three), custom_call_target="tpu_custom_call" | custom-call | tf_op jit(solution)/shard_map/near_up/pallas_call | solution.py:706
  252.7 12.1 %reduce-scatter.5.cloned.1.call-done.down_ref = bf16[128,1024]{1,0:T(8,128)(2,1)} async-done(((bf16[512,1024]{1,0:T(8,128)(2,1)}), bf16[128,1024]{1,0:T(8,128)(2,1)}) %reduce-scatter.5.cloned.1.call-update) | async-done | bytes 262160 | tf_op jit(solution)/shard_map/reduce_scatter | solution.py:1051
  268.2 2.5 collective-permute-start.22
  272.5 4.6 %leave.1 = (bf16[128,2048]{1,0:T(8,128)(2,1)}, f32[128,2048]{1,0:T(8,128)}) custom-call(bf16[128,2048]{1,0:T(8,128)(2,1)S(1)} %copy-done.8, bf16[128,2048]{1,0:T(8,128)(2,1)S(1)} %copy-done.10, f32[1,2048]{1,0:T(1,128)S(1)} %bitcast.65, f32[1,2048]{1,0:T(1,128)S(1)} %bitcast.66, bf16[2,128,2048]{2,1,0:T(8,128)(2,1)S(1)} %copy-done.22, ...), custom_call_target="tpu_custom_call" | custom-call | flops 5242880000 | bytes 4194304 | tf_op jit(solution)/shard_map/leave/pallas_call | solution.py:950
  277.9 5.1 %collective-permute-done.24.refs_3_ = bf16[32,3584]{1,0:T(8,128)(2,1)S(1)} collective-permute-done((bf16[32,3584]{1,0:T(8,128)(2,1)S(1)}, bf16[32,3584]{1,0:T(8,128)(2,1)S(1)}, u32[]{:S(2)}, u32[]{:S(2)}) %collective-permute-start.24) | collective-permute-done | bytes 229408 | tf_op jit(solution)/shard_map/ppermute | solution.py:32
  (150 shorter events, 63.6 us)
Async XLA Ops:
  7.2 111.3 %all-gather.2.cloned.1.call-start = ((), (), s32[]{:S(2)}) async-start(), calls=%async_computation.2 | async-start | bytes 13369344 | tf_op jit(solution)/shard_map/all_gather | solution.py:993
  14.4 9.3 %collective-permute-start.2 = (bf16[32,3328]{1,0:T(8,128)(2,1)}, bf16[32,3328]{1,0:T(8,128)(2,1)S(1)}, u32[]{:S(2)}, u32[]{:S(2)}) collective-permute-start(bf16[32,3328]{1,0:T(8,128)(2,1)} %get-tuple-element.128), channel_id=1, source_target_pairs={{0,66},{2,64},{64,2},{66,0},{1,67},{3,65},{65,3},{67,1},{4,70},{6,... | collective-permute-start | bytes 638984 | tf_op jit(solution)/shard_map/ppermute | solution.py:32
  26.8 198.6 %reduce-scatter.3.cloned.1.call-start = ((), (), s32[]{:S(2)}) async-start(), calls=%async_computation.3 | async-start | bytes 4456448 | tf_op jit(solution)/shard_map/reduce_scatter | solution.py:963
  31.8 27.1 %collective-permute-start.3 = (bf16[2,128,2048]{2,1,0:T(8,128)(2,1)S(1)}, bf16[2,128,2048]{2,1,0:T(8,128)(2,1)S(1)}, u32[]{:S(2)}, u32[]{:S(2)}) collective-permute-start(bf16[2,128,2048]{2,1,0:T(8,128)(2,1)S(1)} %get-tuple-element.130.refs_0_), channel_id=1, source_target_pairs={{0,1},{1,0},{2,3},{3,2},{4,5},{5,4},{6,7},{7,6},{8,9},{9,8},{10,11... | collective-permute-start | bytes 3145736 | tf_op jit(solution)/shard_map/ppermute | solution.py:32
  35.2 47.1 %collective-permute-start.4 = (bf16[2,128,2048]{2,1,0:T(8,128)(2,1)S(1)}, bf16[2,128,2048]{2,1,0:T(8,128)(2,1)S(1)}, u32[]{:S(2)}, u32[]{:S(2)}) collective-permute-start(bf16[2,128,2048]{2,1,0:T(8,128)(2,1)S(1)} %get-tuple-element.130.refs_0_), channel_id=1, source_target_pairs={{0,64},{64,0},{1,65},{65,1},{2,66},{66,2},{3,67},{67,3},{4,68},{68... | collective-permute-start | bytes 3145736 | tf_op jit(solution)/shard_map/ppermute | solution.py:32
  36.0 46.3 %collective-permute-start.5 = (bf16[2,128,2048]{2,1,0:T(8,128)(2,1)S(1)}, bf16[2,128,2048]{2,1,0:T(8,128)(2,1)S(1)}, u32[]{:S(2)}, u32[]{:S(2)}) collective-permute-start(bf16[2,128,2048]{2,1,0:T(8,128)(2,1)S(1)} %get-tuple-element.130.refs_0_), channel_id=1, source_target_pairs={{0,65},{1,64},{64,1},{65,0},{2,67},{3,66},{66,3},{67,2},{4,69},{5,... | collective-permute-start | bytes 3145736 | tf_op jit(solution)/shard_map/ppermute | solution.py:32
  84.3 8.7 %collective-permute-start.6 = (bf16[4,2,128,2048]{3,2,1,0:T(8,128)(2,1)}, bf16[4,2,128,2048]{3,2,1,0:T(8,128)(2,1)}, u32[]{:S(2)}, u32[]{:S(2)}) collective-permute-start(bf16[4,2,128,2048]{3,2,1,0:T(8,128)(2,1)} %join.1.mine_ref), channel_id=1, source_target_pairs={{0,2},{2,0},{1,3},{3,1},{4,6},{6,4},{5,7},{7,5},{8,10},{10,8},{9,1... | collective-permute-start | bytes 12582920 | tf_op jit(solution)/shard_map/ppermute | solution.py:32
  144.8 120.0 %reduce-scatter.5.cloned.1.call-start = ((), (), s32[]{:S(2)}) async-start(), calls=%async_computation.4 | async-start | bytes 1310720 | tf_op jit(solution)/shard_map/reduce_scatter | solution.py:1051
  176.8 23.4 %collective-permute-start.7 = (bf16[2,144,1024]{2,1,0:T(8,128)(2,1)}, bf16[2,144,1024]{2,1,0:T(8,128)(2,1)S(1)}, u32[]{:S(2)}, u32[]{:S(2)}) collective-permute-start(bf16[2,144,1024]{2,1,0:T(8,128)(2,1)} %get-tuple-element.163), channel_id=1, source_target_pairs={{0,4},{4,0},{8,12},{12,8},{1,5},{5,1},{9,13},{13,9},{2,6},{6,2},{1... | collective-permute-start | bytes 1769480 | tf_op jit(solution)/shard_map/ppermute | solution.py:36
  178.0 22.2 %collective-permute-start.9 = (bf16[2,144,1024]{2,1,0:T(8,128)(2,1)}, bf16[2,144,1024]{2,1,0:T(8,128)(2,1)S(1)}, u32[]{:S(2)}, u32[]{:S(2)}) collective-permute-start(bf16[2,144,1024]{2,1,0:T(8,128)(2,1)} %get-tuple-element.165), channel_id=1, source_target_pairs={{0,12},{4,8},{8,4},{12,0},{1,13},{5,9},{9,5},{13,1},{2,14},{6,10},... | collective-permute-start | bytes 1769480 | tf_op jit(solution)/shard_map/ppermute | solution.py:36
  179.8 20.4 %collective-permute-start.10 = (bf16[2,128,1024]{2,1,0:T(8,128)(2,1)}, bf16[2,128,1024]{2,1,0:T(8,128)(2,1)S(1)}, u32[]{:S(2)}, u32[]{:S(2)}) collective-permute-start(bf16[2,128,1024]{2,1,0:T(8,128)(2,1)} %get-tuple-element.166), channel_id=1, source_target_pairs={{0,48},{16,32},{32,16},{48,0},{1,49},{17,33},{33,17},{49,1},{2,50}... | collective-permute-start | bytes 1572872 | tf_op jit(solution)/shard_map/ppermute | solution.py:36
  180.7 19.5 %collective-permute-start.8 = (bf16[2,128,1024]{2,1,0:T(8,128)(2,1)}, bf16[2,128,1024]{2,1,0:T(8,128)(2,1)S(1)}, u32[]{:S(2)}, u32[]{:S(2)}) collective-permute-start(bf16[2,128,1024]{2,1,0:T(8,128)(2,1)} %get-tuple-element.164), channel_id=1, source_target_pairs={{0,16},{16,0},{32,48},{48,32},{1,17},{17,1},{33,49},{49,33},{2,18}... | collective-permute-start | bytes 1572872 | tf_op jit(solution)/shard_map/ppermute | solution.py:36
  204.3 33.5 %collective-permute-start.11 = (bf16[4,144,1024]{2,1,0:T(8,128)(2,1)S(1)}, bf16[4,144,1024]{2,1,0:T(8,128)(2,1)}, u32[]{:S(2)}, u32[]{:S(2)}) collective-permute-start(bf16[4,144,1024]{2,1,0:T(8,128)(2,1)S(1)} %get-tuple-element.178), channel_id=1, source_target_pairs={{0,4},{4,0},{8,12},{12,8},{1,5},{5,1},{9,13},{13,9},{2,6},{6,2},{1... | collective-permute-start | bytes 3538952 | tf_op jit(solution)/shard_map/ppermute | solution.py:36
  204.9 32.8 %collective-permute-start.12 = (bf16[4,144,1024]{2,1,0:T(8,128)(2,1)S(1)}, bf16[4,144,1024]{2,1,0:T(8,128)(2,1)}, u32[]{:S(2)}, u32[]{:S(2)}) collective-permute-start(bf16[4,144,1024]{2,1,0:T(8,128)(2,1)S(1)} %get-tuple-element.179), channel_id=1, source_target_pairs={{0,12},{4,8},{8,4},{12,0},{1,13},{5,9},{9,5},{13,1},{2,14},{6,10},... | collective-permute-start | bytes 3538952 | tf_op jit(solution)/shard_map/ppermute | solution.py:36
  206.6 28.6 %collective-permute-start.13 = (bf16[4,128,1024]{2,1,0:T(8,128)(2,1)S(1)}, bf16[4,128,1024]{2,1,0:T(8,128)(2,1)}, u32[]{:S(2)}, u32[]{:S(2)}) collective-permute-start(bf16[4,128,1024]{2,1,0:T(8,128)(2,1)S(1)} %get-tuple-element.180), channel_id=1, source_target_pairs={{0,16},{16,0},{32,48},{48,32},{1,17},{17,1},{33,49},{49,33},{2,18}... | collective-permute-start | bytes 3145736 | tf_op jit(solution)/shard_map/ppermute | solution.py:36
  208.2 29.5 %collective-permute-start.14 = (bf16[4,128,1024]{2,1,0:T(8,128)(2,1)}, bf16[4,128,1024]{2,1,0:T(8,128)(2,1)}, u32[]{:S(2)}, u32[]{:S(2)}) collective-permute-start(bf16[4,128,1024]{2,1,0:T(8,128)(2,1)} %get-tuple-element.181), channel_id=1, source_target_pairs={{0,48},{16,32},{32,16},{48,0},{1,49},{17,33},{33,17},{49,1},{2,50}... | collective-permute-start | bytes 3145736 | tf_op jit(solution)/shard_map/ppermute | solution.py:36
  213.0 25.6 %collective-permute-start.16 = (bf16[2,128,2048]{2,1,0:T(8,128)(2,1)}, bf16[2,128,2048]{2,1,0:T(8,128)(2,1)}, u32[]{:S(2)}, u32[]{:S(2)}) collective-permute-start(bf16[2,128,2048]{2,1,0:T(8,128)(2,1)} %get-tuple-element.184), channel_id=1, source_target_pairs={{0,1},{1,0},{2,3},{3,2},{4,5},{5,4},{6,7},{7,6},{8,9},{9,8},{10,11... | collective-permute-start | bytes 3145736 | tf_op jit(solution)/shard_map/ppermute | solution.py:32
  241.9 30.5 %collective-permute-start.17 = (bf16[2,128,2048]{2,1,0:T(8,128)(2,1)}, bf16[2,128,2048]{2,1,0:T(8,128)(2,1)}, u32[]{:S(2)}, u32[]{:S(2)}) collective-permute-start(bf16[2,128,2048]{2,1,0:T(8,128)(2,1)} %get-tuple-element.191), channel_id=1, source_target_pairs={{0,64},{64,0},{1,65},{65,1},{2,66},{66,2},{3,67},{67,3},{4,68},{68... | collective-permute-start | bytes 3145736 | tf_op jit(solution)/shard_map/ppermute | solution.py:32
  243.3 29.2 %collective-permute-start.18 = (bf16[2,128,2048]{2,1,0:T(8,128)(2,1)}, bf16[2,128,2048]{2,1,0:T(8,128)(2,1)}, u32[]{:S(2)}, u32[]{:S(2)}) collective-permute-start(bf16[2,128,2048]{2,1,0:T(8,128)(2,1)} %get-tuple-element.192), channel_id=1, source_target_pairs={{0,65},{1,64},{64,1},{65,0},{2,67},{3,66},{66,3},{67,2},{4,69},{5,... | collective-permute-start | bytes 3145736 | tf_op jit(solution)/shard_map/ppermute | solution.py:32
  248.4 18.0 %collective-permute-start.19 = (bf16[144,1024]{1,0:T(8,128)(2,1)}, bf16[144,1024]{1,0:T(8,128)(2,1)S(1)}, u32[]{:S(2)}, u32[]{:S(2)}) collective-permute-start(bf16[144,1024]{1,0:T(8,128)(2,1)} %get-tuple-element.199), channel_id=1, source_target_pairs={{0,16},{16,0},{32,48},{48,32},{1,17},{17,1},{33,49},{49,33},{2,18}... | collective-permute-start | bytes 884744 | tf_op jit(solution)/shard_map/ppermute | solution.py:36
  250.3 16.1 %collective-permute-start.20 = (bf16[144,1024]{1,0:T(8,128)(2,1)}, bf16[144,1024]{1,0:T(8,128)(2,1)S(1)}, u32[]{:S(2)}, u32[]{:S(2)}) collective-permute-start(bf16[144,1024]{1,0:T(8,128)(2,1)} %get-tuple-element.200), channel_id=1, source_target_pairs={{0,32},{16,48},{32,0},{48,16},{1,33},{17,49},{33,1},{49,17},{2,34}... | collective-permute-start | bytes 884744 | tf_op jit(solution)/shard_map/ppermute | solution.py:36
  251.7 14.7 %collective-permute-start.21 = (bf16[144,1024]{1,0:T(8,128)(2,1)}, bf16[144,1024]{1,0:T(8,128)(2,1)S(1)}, u32[]{:S(2)}, u32[]{:S(2)}) collective-permute-start(bf16[144,1024]{1,0:T(8,128)(2,1)} %get-tuple-element.201), channel_id=1, source_target_pairs={{0,48},{16,32},{32,16},{48,0},{1,49},{17,33},{33,17},{49,1},{2,50}... | collective-permute-start | bytes 884744 | tf_op jit(solution)/shard_map/ppermute | solution.py:36
  268.2 8.9 %collective-permute-start.22 = (bf16[32,3584]{1,0:T(8,128)(2,1)S(1)}, bf16[32,3584]{1,0:T(8,128)(2,1)S(1)}, u32[]{:S(2)}, u32[]{:S(2)}) collective-permute-start(bf16[32,3584]{1,0:T(8,128)(2,1)S(1)} %get-tuple-element.219), channel_id=1, source_target_pairs={{0,2},{2,0},{1,3},{3,1},{4,6},{6,4},{5,7},{7,5},{8,10},{10,8},{9,1... | collective-permute-start | bytes 688136 | tf_op jit(solution)/shard_map/ppermute | solution.py:32
  271.6 11.4 %collective-permute-start.24 = (bf16[32,3584]{1,0:T(8,128)(2,1)S(1)}, bf16[32,3584]{1,0:T(8,128)(2,1)S(1)}, u32[]{:S(2)}, u32[]{:S(2)}) collective-permute-start(bf16[32,3584]{1,0:T(8,128)(2,1)S(1)} %get-tuple-element.221), channel_id=1, source_target_pairs={{0,66},{2,64},{64,2},{66,0},{1,67},{3,65},{65,3},{67,1},{4,70},{6,... | collective-permute-start | bytes 688136 | tf_op jit(solution)/shard_map/ppermute | solution.py:32
  (37 other events, 464.5 us)
Sparse Core Ops, SparseCore 0:
  26.9 91.5 all-gather.1
  144.9 80.3 reduce-scatter.2
  242.0 22.7 reduce-scatter.4
